TPU v7x, 32 devices: a whole 2x2x4 slice. The times are simulated.
32 devices in a mesh: tm: 8 (over y, x, core), space: 4 (over z).
Axes of the slice: x: 2, y: 2, z: 4, core: 2. Of those that a mesh axis runs over, the one named last changes fastest.
Arguments:
- video_tokens: bfloat16 [8, 16, 64, 1152], P('tm', 'space'), may hold values from -6 to 6
- qkv_weight: bfloat16 [1152, 3456], P('space'), may hold values from -0.1875 to 0.1875
- out_weight: bfloat16 [1152, 1152], P('space'), may hold values from -0.1875 to 0.1875
- conv_weight: float32 [3, 3, 1152], replicated, may hold values from -2 to 2
- norm_gain: float32 [1152], replicated, may hold values from 0.1 to 1.9
Outputs:
- attended: bfloat16 [8, 16, 64, 1152], P('tm', 'space')
All inputs are finite; a program needn't handle non-finite values.
Results may differ from a plain program's by a relative error of at most 0.015.
Values may be sent and summed in bfloat16 or wider, within the bound.
No kernel may reach another device: no remote copies, remote signals or barrier semaphores. Data moves between devices by JAX's collectives and lax.ppermute only.
A program may use at most 64 MiB of HBM per device.

v0:
```python
import jax
import jax.numpy as jnp
from jax import lax
from jax.sharding import PartitionSpec as P

HEADS = 36
HEAD_DIM = 32


def entering(value, axis, combine, identity):
    devices, place = (lax.axis_size(axis), lax.axis_index(axis))
    everything = lax.all_gather(value.astype(jnp.bfloat16), axis)
    start = jnp.broadcast_to(jnp.asarray(identity, value.dtype), value.shape)

    def lap(k, before):
        reached = k < place
        new = combine(before, everything[k].astype(value.dtype))
        return jnp.where(reached, new, before)

    return lax.fori_loop(0, devices, lap, start)


def with_halo(block, sides, width):
    for axis, dim in sides:
        count = lax.axis_size(axis)
        forward = [(i, i + 1) for i in range(count - 1)]
        backward = [(target, source) for source, target in forward]
        low = lax.ppermute(
            lax.slice_in_dim(block, block.shape[dim] - width, None, axis=dim), axis, forward
        )
        high = lax.ppermute(lax.slice_in_dim(block, 0, width, axis=dim), axis, backward)
        block = jnp.concatenate([low, block, high], axis=dim)
    return block


def fold_product(left_side, block_rows):
    return jnp.dot(left_side, block_rows, preferred_element_type=jnp.float32)


def add_states(earlier, later):
    return earlier + later


def causal_states(key_feat, values):
    key_heads = key_feat.reshape(-1, HEADS, HEAD_DIM)
    value_heads = values.reshape(-1, HEADS, HEAD_DIM)
    frame_state = jnp.einsum(
        "thd,the->hde", key_heads, value_heads, preferred_element_type=jnp.float32
    )
    flat_state = frame_state.reshape(-1)
    frame_sum = lax.psum(flat_state.astype(jnp.bfloat16), "space").astype(jnp.float32)
    earlier = entering(frame_sum, "tm", add_states, jnp.zeros_like(frame_sum))
    whole_state = earlier + frame_sum
    return whole_state.reshape(HEADS, HEAD_DIM, HEAD_DIM)


def per_device(video_tokens, qkv_weight, out_weight, conv_weight, norm_gain):
    frame_now = video_tokens[0]
    row_count, col_count, feat_width = frame_now.shape
    tokens = frame_now.reshape(row_count * col_count, feat_width)
    projected = fold_product(tokens, lax.all_gather(qkv_weight, "space", axis=0, tiled=True))
    query_feat = jax.nn.relu(projected[:, :feat_width]).astype(jnp.bfloat16)
    key_feat = jax.nn.relu(projected[:, feat_width : 2 * feat_width]).astype(jnp.bfloat16)
    values = projected[:, 2 * feat_width :].astype(jnp.bfloat16)
    state_all = causal_states(key_feat, values)
    padded_rows = with_halo(values.reshape(row_count, col_count, feat_width), (("space", 0),), 1)
    padded = jnp.pad(padded_rows, ((0, 0), (1, 1), (0, 0))).astype(jnp.float32)
    local_term = jnp.zeros((row_count, col_count, feat_width), jnp.float32)
    for row_shift in range(3):
        for col_shift in range(3):
            local_term = (
                local_term
                + conv_weight[row_shift, col_shift]
                * padded[row_shift : row_shift + row_count, col_shift : col_shift + col_count]
            )
    state_low = state_all.astype(jnp.bfloat16)
    query_heads = query_feat.reshape(-1, HEADS, HEAD_DIM)
    readout = jnp.einsum("thd,hde->the", query_heads, state_low, preferred_element_type=jnp.float32)
    readout = readout.reshape(-1, feat_width)
    mean_square = jnp.mean(readout * readout, axis=-1, keepdims=True)
    normed = readout * lax.rsqrt(mean_square + 1e-06) * norm_gain
    mixture = (normed + local_term.reshape(-1, feat_width)).astype(jnp.bfloat16)
    result = fold_product(mixture, lax.all_gather(out_weight, "space", axis=0, tiled=True))
    return result.astype(jnp.bfloat16).reshape(1, row_count, col_count, feat_width)


def solution(mesh):
    in_specs = (P("tm", "space", None, None), P("space", None), P("space", None), P(), P())
    out_specs = P("tm", "space", None, None)
    return jax.shard_map(
        per_device, mesh=mesh, in_specs=in_specs, out_specs=out_specs, check_vma=False
    )
```

profile of v0, /device:TPU:0, one launch (start us, length us, event | category | flops | bytes accessed | tf_op | source)
XLA Modules:
  0.0 266.5 jit_solution(2047738377409590884)
XLA Ops:
  6.5 0.0 copy-start
  6.5 0.0 all-gather.4.cloned.1.call-start
  6.5 0.7 all-gather.4.cloned.1.call-update
  7.3 0.0 all-reduce.3.cloned.1.call-start
  7.3 147.0 %all-gather.4.cloned.1.call-done = bf16[1152,3456]{1,0:T(8,128)(2,1)} async-done(((bf16[288,3456]{1,0:T(8,128)(2,1)}), bf16[1152,3456]{1,0:T(8,128)(2,1)}) %all-gather.4.cloned.1.call-update) | async-done | bytes 7962640 | tf_op jit(solution)/shard_map/all_gather | solution.py:61
  154.3 0.0 copy-done
  154.3 5.8 %fusion.21 = bf16[256,3456]{1,0:T(8,128)(2,1)S(1)} fusion(bf16[256,1152]{1,0:T(8,128)(2,1)S(1)} %bitcast.35, bf16[1152,3456]{1,0:T(8,128)(2,1)} %all-gather.4.cloned.1.call-done), kind=kOutput, calls=%fused_computation.53 | convolution fusion | flops 2038431744 | bytes 10321920 | tf_op jit(solution)/shard_map/dot_general | solution.py:37
  160.1 1.2 fusion.9
  161.3 1.1 copy.16
  162.4 2.1 copy.15
  164.5 0.0 copy-start.9
  164.5 1.5 convolution_convert_fusion.1
  166.1 0.8 convert_element_type.46
  166.9 0.0 all-reduce.3.cloned.1.call-update
  166.9 0.0 all-gather.6.cloned.1.call-start
  167.0 0.7 all-gather.6.cloned.1.call-update
  167.7 0.0 copy-done.9
  167.7 0.7 slice_reduce_fusion.8
  168.4 0.7 slice_bitcast_fusion.1
  169.1 1.3 collective-permute-start
  170.4 1.3 collective-permute-start.1
  171.7 1.3 copy.17
  173.0 26.3 %all-reduce.3.cloned.1.call-done = bf16[36864]{0:T(1024)(128)(2,1)} async-done(((bf16[36864]{0:T(1024)(128)(2,1)}), bf16[36864]{0:T(1024)(128)(2,1)}) %all-reduce.3.cloned.1.call-update) | async-done | bytes 73744 | tf_op jit(solution)/shard_map/psum | solution.py:51
  199.3 10.3 %all-gather = bf16[294912]{0:T(1024)(128)(2,1)S(1)} all-gather(bf16[36864]{0:T(1024)(128)(2,1)} %all-reduce.3.cloned.1.call-done), channel_id=2, replica_groups=mesh['tm'=8,'space'=4] {'tm'}, dimensions={0}, use_global_device_ids=true | all-gather | bytes 663552 | tf_op jit(solution)/shard_map/all_gather | solution.py:12
  209.6 0.3 reshape.46
  209.8 0.0 copy-start.1
  209.9 1.6 while.14
  209.9 0.1 dynamic-slice_convert_fusion.2
  210.1 0.1 dynamic-slice_convert_fusion.2
  210.3 0.1 dynamic-slice_convert_fusion.2
  210.5 0.1 dynamic-slice_convert_fusion.2
  210.7 0.1 dynamic-slice_convert_fusion.2
  210.8 0.1 dynamic-slice_convert_fusion.2
  211.0 0.1 dynamic-slice_convert_fusion.2
  211.2 0.1 dynamic-slice_convert_fusion.2
  211.4 0.0 copy-done.1
  211.5 0.2 convert_element_type.49
  211.6 0.4 fusion.14
  212.0 0.0 collective-permute-done
  212.0 0.0 collective-permute-done.1
  212.0 0.0 copy-start.2
  212.1 0.0 copy-start.3
  212.1 0.0 copy-start.4
  212.1 0.0 copy-start.5
  212.1 0.0 copy-start.6
  212.1 0.0 copy-start.7
  212.1 0.0 copy-start.8
  212.1 1.2 fusion.20
  213.3 0.0 copy-done.2
  213.3 0.0 copy-done.3
  213.3 0.0 copy-done.4
  213.3 0.0 copy-done.5
  213.3 0.0 copy-done.6
  213.3 0.0 copy-done.7
  213.4 0.0 copy-done.8
  213.4 0.9 fusion.1
  214.3 0.0 copy-start.10
  214.3 1.4 copy.19
  215.7 0.0 copy-done.10
  215.7 1.5 fusion.13
  217.2 39.2 %all-gather.6.cloned.1.call-done = bf16[1152,1152]{1,0:T(8,128)(2,1)} async-done(((bf16[288,1152]{1,0:T(8,128)(2,1)}), bf16[1152,1152]{1,0:T(8,128)(2,1)}) %all-gather.6.cloned.1.call-update) | async-done | bytes 2654224 | tf_op jit(solution)/shard_map/all_gather | solution.py:83
  256.4 3.6 %convolution_convert_fusion = bf16[256,1152]{1,0:T(8,128)(2,1)} fusion(bf16[256,1152]{0,1:T(8,128)(2,1)S(1)} %fusion.13, bf16[1152,1152]{1,0:T(8,128)(2,1)} %all-gather.6.cloned.1.call-done), kind=kOutput, calls=%fused_computation.4 | convolution fusion | flops 679772160 | bytes 3833856 | tf_op jit(solution)/shard_map/dot_general | solution.py:37
  (11 shorter events, 0.4 us)
Async XLA Ops:
  6.5 147.8 %copy-start = (bf16[1,4,64,1152]{3,2,1,0:T(8,128)(2,1)S(1)}, bf16[1,4,64,1152]{3,2,1,0:T(8,128)(2,1)}, u32[]{:S(2)}) copy-start(bf16[1,4,64,1152]{3,2,1,0:T(8,128)(2,1)} %param.7) | copy-start | bytes 1769476
  6.5 147.8 %all-gather.4.cloned.1.call-start = ((), (), s32[]{:S(2)}) async-start(), calls=%async_computation | async-start | bytes 9953280 | tf_op jit(solution)/shard_map/all_gather | solution.py:61
  7.3 192.1 %all-reduce.3.cloned.1.call-start = ((), (), s32[]{:S(2)}) async-start(), calls=%async_computation.1 | async-start | bytes 147456 | tf_op jit(solution)/shard_map/psum | solution.py:51
  164.5 3.1 %copy-start.9 = (f32[3,3,1152]{2,1,0:T(4,128)S(1)}, f32[3,3,1152]{2,1,0:T(4,128)}, u32[]{:S(2)}) copy-start(f32[3,3,1152]{2,1,0:T(4,128)} %param.10) | copy-start | bytes 124420
  166.9 89.4 %all-gather.6.cloned.1.call-start = ((), (), s32[]{:S(2)}) async-start(), calls=%async_computation.2 | async-start | bytes 3317760 | tf_op jit(solution)/shard_map/all_gather | solution.py:83
  169.1 42.9 %collective-permute-start = (bf16[1,64,1152]{2,1,0:T(8,128)(2,1)}, bf16[1,64,1152]{2,1,0:T(8,128)(2,1)S(1)}, u32[]{:S(2)}, u32[]{:S(2)}) collective-permute-start(bf16[1,64,1152]{2,1,0:T(8,128)(2,1)} %get-tuple-element.120), channel_id=1, source_target_pairs={{0,1},{1,2},{2,3},{4,5},{5,6},{6,7},{8,9},{9,10},{10,11},{12,13},{... | collective-permute-start | bytes 442376 | tf_op jit(solution)/shard_map/ppermute | solution.py:28
  170.4 41.6 %collective-permute-start.1 = (bf16[1,64,1152]{2,1,0:T(8,128)(2,1)}, bf16[1,64,1152]{2,1,0:T(8,128)(2,1)}, u32[]{:S(2)}, u32[]{:S(2)}) collective-permute-start(bf16[1,64,1152]{2,1,0:T(8,128)(2,1)} %get-tuple-element.121), channel_id=1, source_target_pairs={{1,0},{2,1},{3,2},{5,4},{6,5},{7,6},{9,8},{10,9},{11,10},{13,12},{... | collective-permute-start | bytes 442376 | tf_op jit(solution)/shard_map/ppermute | solution.py:31
  209.8 1.6 copy-start.1
  212.0 1.3 copy-start.2
  212.1 1.3 copy-start.3
  212.1 1.3 copy-start.4
  212.1 1.3 copy-start.5
  212.1 1.3 copy-start.6
  212.1 1.3 copy-start.7
  212.1 1.3 copy-start.8
  214.3 1.4 copy-start.10
Sparse Core Ops, SparseCore 0:
  8.9 145.3 all-gather.3
  167.1 32.2 all-reduce.2
  201.0 55.3 all-gather.5
where the time goes:
time: 267 us; the launch traced here: 266 us
  waiting for transfers between devices  214 us (80%)
  between operations  13.4 us (5%)
  matrix products  11.3 us (4%)
  blocking collectives  10.3 us (4%)
  local copies, waits for them, and re-layouts  8.64 us (3%)
  other arithmetic  6.1 us (2%)
    all_gather x1, waiting for transfers between devices, per_device(): lax.all_gather(qkv_weight, 'space', axis=0, tiled=True)  147 us
    all_gather x1, waiting for transfers between devices, per_device(): lax.all_gather(out_weight, 'space', axis=0, tiled=True)  39.2 us
    psum x1, waiting for transfers between devices, causal_states(): lax.psum(flat_state.astype(jnp.bfloat16), 'space').astype(jnp.float32)  26.3 us
    all_gather x1, blocking collectives, entering(): everything = lax.all_gather(value.astype(jnp.bfloat16), axis)  10.3 us
    dot_general x2, matrix products, fold_product(): return jnp.dot(left_side, block_rows, preferred_element_type=jnp.float32)  9.37 us
  transfers between devices with their start and end apart: 5, of which 3 were waited for; matrix products, arithmetic and copies ran while one was open for 4% of the time, Pallas kernels for 0%

commit v1 on v0

--- a/solution.py
+++ b/solution.py
@@ -1,10 +1,20 @@
+import functools
+
 import jax
 import jax.numpy as jnp
 from jax import lax
+from jax.experimental import pallas as pl
+from jax.experimental.pallas import tpu as pltpu
 from jax.sharding import PartitionSpec as P
 
 HEADS = 36
 HEAD_DIM = 32
+LANES = 128
+MAIN = 64
+REST = 16
+STEPS = (1, 2, 3)
+VMEM_LIMIT = 24 * 1024 * 1024
+WHOLE_VMEM = 63 * 1024 * 1024
 
 
 def entering(value, axis, combine, identity):
@@ -54,7 +64,7 @@
     return whole_state.reshape(HEADS, HEAD_DIM, HEAD_DIM)
 
 
-def per_device(video_tokens, qkv_weight, out_weight, conv_weight, norm_gain):
+def general_form(video_tokens, qkv_weight, out_weight, conv_weight, norm_gain):
     frame_now = video_tokens[0]
     row_count, col_count, feat_width = frame_now.shape
     tokens = frame_now.reshape(row_count * col_count, feat_width)
@@ -84,7 +94,467 @@
     return result.astype(jnp.bfloat16).reshape(1, row_count, col_count, feat_width)
 
 
+def coordinates():
+    place = lax.axis_index("tm")
+    return lax.rem(place // 4, 2), lax.rem(place // 2, 2), lax.rem(place, 2)
+
+
+def shifted(value, step):
+    count = lax.axis_size("space")
+    return lax.ppermute(value, "space", [(i, (i + step) % count) for i in range(count)])
+
+
+def flipped(value, bit_on_core):
+    return lax.ppermute(value, "tm", [(t, t ^ bit_on_core[t % 2]) for t in range(8)])
+
+
+def after(value, *earlier):
+    return lax.optimization_barrier((value,) + earlier)[0]
+
+
+def chip_places(y, x):
+    return (2 * y + x, 2 * y + (1 - x), 2 * (1 - y) + x, 2 * (1 - y) + (1 - x))
+
+
+def source_plane(step):
+    count = lax.axis_size("space")
+    return lax.rem(lax.axis_index("space") - step + count, count)
+
+
+def steps_through(within, size):
+    run = sum(jnp.where(within >= size * k, 1, 0) for k in range(1, len(STEPS)))
+    return run, within - size * run
+
+
+def landed_order(at, width, rows):
+    y, x, _ = coordinates()
+    planes = [source_plane(step) for step in STEPS]
+    row = at + lax.broadcasted_iota(jnp.int32, (1, width), 1)
+
+    def pick(choices, index):
+        chosen = choices[-1]
+        for k in range(len(choices) - 2, -1, -1):
+            chosen = jnp.where(index == k, choices[k], chosen)
+        return chosen
+
+    def landed(within, size, starts):
+        count = len(STEPS) * size
+        slot = sum(jnp.where(within >= count * k, 1, 0) for k in range(1, len(starts)))
+        run, left = steps_through(within - count * slot, size)
+        return pick(planes, run) * rows + pick(starts, slot) + left
+
+    main = landed(row - rows, MAIN, [place * MAIN for place in chip_places(y, x)])
+    rest_at = rows + 4 * len(STEPS) * MAIN
+    rest = landed(row - rest_at, REST, [4 * MAIN + tile * REST for tile in (y, 1 - y)])
+    own = lax.axis_index("space") * rows + row
+    return jnp.where(row < rows, own, jnp.where(row < rest_at, main, rest))
+
+
+def whole_vmem():
+    return pl.BlockSpec(memory_space=pltpu.VMEM)
+
+
+def anywhere():
+    return pl.BlockSpec(memory_space=pltpu.HBM)
+
+
+def kernel_call(
+    body, outputs, inputs, in_specs, scratch=(), flops=0, bytes_accessed=0, limit=VMEM_LIMIT
+):
+    return pl.pallas_call(
+        body,
+        out_shape=outputs,
+        in_specs=in_specs,
+        out_specs=jax.tree.map(lambda _: whole_vmem(), outputs),
+        scratch_shapes=list(scratch),
+        compiler_params=pltpu.CompilerParams(vmem_limit_bytes=limit),
+        cost_estimate=pl.CostEstimate(
+            flops=flops, bytes_accessed=bytes_accessed, transcendentals=0
+        ),
+    )(*inputs)
+
+
+def pieces_kernel(qkv_ref, out_ref, first_ref, second_ref, sems):
+    y, x, core = coordinates()
+    depth = out_ref.shape[1]
+    main = pl.ds(pl.multiple_of((2 * y + x) * MAIN, REST), MAIN)
+    rest = pl.ds(pl.multiple_of(4 * MAIN + y * REST, REST), REST)
+    first_columns = pl.ds(pl.multiple_of(depth * (1 + core), LANES), depth)
+    rest_columns = pl.ds(pl.multiple_of(jnp.where(x == 0, depth * (1 + core), 0), LANES), depth)
+
+    def copy(source, target, k):
+        return pltpu.make_async_copy(source, target, sems.at[k])
+
+    first_main = copy(qkv_ref.at[main, first_columns], first_ref.at[pl.ds(0, MAIN), :], 0)
+    first_main.start()
+    rest_target = first_ref.at[pl.ds(MAIN, REST), :]
+    from_out = (core == 1) & (x == 1)
+
+    @pl.when(from_out)
+    def _():
+        copy(out_ref.at[rest, :], rest_target, 1).start()
+
+    @pl.when(jnp.logical_not(from_out))
+    def _():
+        copy(qkv_ref.at[rest, rest_columns], rest_target, 1).start()
+
+    places = chip_places(y, x)
+    for k, place in enumerate((places[0], places[3])):
+        rows = pl.ds(pl.multiple_of(place * MAIN, REST), MAIN)
+
+        @pl.when(core == 0)
+        def _():
+            copy(qkv_ref.at[rows, pl.ds(0, depth)], second_ref.at[k], 2 + k).start()
+
+        @pl.when(core == 1)
+        def _():
+            copy(out_ref.at[rows, :], second_ref.at[k], 2 + k).start()
+
+    first_main.wait()
+    copy(out_ref.at[rest, :], rest_target, 1).wait()
+    for k in range(2):
+        copy(out_ref.at[main, :], second_ref.at[k], 2 + k).wait()
+
+
+def pieces_call(qkv_weight, out_weight):
+    depth = out_weight.shape[1]
+    outputs = [
+        jax.ShapeDtypeStruct((MAIN + REST, depth), jnp.bfloat16),
+        jax.ShapeDtypeStruct((2, MAIN, depth), jnp.bfloat16),
+    ]
+    return kernel_call(
+        pieces_kernel,
+        outputs,
+        (qkv_weight, out_weight),
+        [anywhere(), anywhere()],
+        [pltpu.SemaphoreType.DMA((4,))],
+        bytes_accessed=4 * (3 * MAIN + REST) * depth,
+        limit=WHOLE_VMEM,
+    )
+
+
+def reorder_kernel(rows, tokens_ref, moved_ref):
+    depth = tokens_ref.shape[1]
+    width = 3 * LANES
+    row = lax.broadcasted_iota(jnp.int32, (depth, width), 0)
+    for at in range(0, depth, width):
+        order = landed_order(at, width, rows)
+        chosen = jnp.where(row == order, 1.0, 0.0).astype(jnp.bfloat16)
+        moved = jnp.dot(tokens_ref[...], chosen, preferred_element_type=jnp.float32)
+        moved_ref[:, at : at + width] = moved.astype(jnp.bfloat16)
+
+
+def reorder_call(tokens, rows):
+    depth = tokens.shape[1]
+    return kernel_call(
+        functools.partial(reorder_kernel, rows),
+        jax.ShapeDtypeStruct(tokens.shape, jnp.bfloat16),
+        (tokens,),
+        [whole_vmem()],
+        flops=2 * tokens.size * depth,
+        bytes_accessed=2 * tokens.size,
+    )
+
+
+def first_kernel(*refs):
+    tokens_ref, other_ref, qkv_ref, near_ref, away_ref, first_ref, far_ref, mine_ref = refs
+    slots = (
+        ((near_ref, 0), (near_ref, 4), (near_ref, 1)),
+        ((near_ref, 2), (first_ref, 0), (near_ref, 3)),
+        ((away_ref, 0), (away_ref, 4), (away_ref, 1)),
+        ((away_ref, 2), (far_ref, 0), (away_ref, 3)),
+    )
+    _, x, core = coordinates()
+    count, depth = tokens_ref.shape
+    floor = jnp.where(core == 0, 0.0, -jnp.inf).astype(jnp.float32)
+    width = 3 * LANES
+
+    for at in range(0, depth, width):
+        lanes = slice(at, at + width)
+
+        def slot(k, low, high):
+            return jnp.concatenate([ref[at, low:high, lanes] for ref, at in slots[k]], axis=0)
+
+        def by_place(low, high):
+            own, first, second, far = [slot(k, low, high) for k in range(4)]
+            along_x = jnp.where(core == 0, first, second)
+            along_y = jnp.where(core == 0, second, first)
+            return own, along_x, along_y, far
+
+        keys, values = [qkv_ref[:, depth * k + at : depth * k + at + width] for k in (1, 2)]
+        own = jnp.where(core == 0, keys, values)
+        rest = by_place(MAIN, MAIN + REST)
+        even = jnp.concatenate([rest[0], rest[2]], axis=0)
+        odd = jnp.concatenate([rest[1], rest[3]], axis=0)
+        mine_ref[2 * count :, lanes] = jnp.where(x == 1, even, odd)
+        columns = jnp.concatenate(
+            (own,) + by_place(0, MAIN) + (jnp.where(x == 0, even, odd),), axis=0
+        )
+        for k, ref in enumerate((tokens_ref, other_ref)):
+            product = jnp.dot(ref[...], columns, preferred_element_type=jnp.float32)
+            product = jnp.maximum(product, floor).astype(jnp.bfloat16)
+            mine_ref[k * count : (k + 1) * count, lanes] = product
+
+
+def first_call(tokens, other, qkv_weight, *landed):
+    count, depth = tokens.shape
+    inputs = (tokens, other, qkv_weight) + landed
+    return kernel_call(
+        first_kernel,
+        jax.ShapeDtypeStruct((2 * count + 2 * len(STEPS) * REST, depth), jnp.bfloat16),
+        inputs,
+        [whole_vmem()] * len(inputs),
+        flops=4 * tokens.size * depth,
+        bytes_accessed=2 * depth * depth,
+    )
+
+
+def diagonal_mask():
+    rows = lax.broadcasted_iota(jnp.int32, (LANES, LANES), 0) // HEAD_DIM
+    columns = lax.broadcasted_iota(jnp.int32, (LANES, LANES), 1) // HEAD_DIM
+    return rows == columns
+
+
+def state_kernel(mine_ref, other_ref, values_ref, top_ref, bottom_ref, upto_ref, total_ref):
+    _, _, core = coordinates()
+    mask = diagonal_mask()
+    columns = top_ref.shape[1]
+    count = values_ref.shape[0]
+    later = jnp.where(core == 1, 1.0, 0.0).astype(jnp.float32)
+    for group in range(mine_ref.shape[1] // LANES):
+        at = slice(group * LANES, (group + 1) * LANES)
+
+        def state(mine, other):
+            keys = jnp.where(core == 0, mine, other)
+            values = jnp.where(core == 0, other, mine)
+            full = lax.dot_general(
+                keys, values, (((0,), (0,)), ((), ())), preferred_element_type=jnp.float32
+            )
+            full = jnp.where(mask, full, 0.0)
+            total = full[0:HEAD_DIM]
+            for k in range(1, LANES // HEAD_DIM):
+                total = total + full[k * HEAD_DIM : (k + 1) * HEAD_DIM]
+            return total, values
+
+        low, high = slice(0, count), slice(count, 2 * count)
+        here, values = state(mine_ref[low, at], other_ref[high, at])
+        there, _ = state(mine_ref[high, at], other_ref[low, at])
+        values_ref[:, at] = values
+        top_ref[0, :, at] = values[:columns]
+        bottom_ref[0, :, at] = values[-columns:]
+        upto_ref[group] = here + later * there
+        total_ref[group] = (here + there).astype(jnp.bfloat16)
+
+
+def state_call(mine, other, count, columns):
+    depth = mine.shape[1]
+    compact = (depth // LANES, HEAD_DIM, LANES)
+    edge = jax.ShapeDtypeStruct((1, columns, depth), jnp.bfloat16)
+    return kernel_call(
+        state_kernel,
+        [
+            jax.ShapeDtypeStruct((count, depth), jnp.bfloat16),
+            edge,
+            edge,
+            jax.ShapeDtypeStruct(compact, jnp.float32),
+            jax.ShapeDtypeStruct(compact, jnp.bfloat16),
+        ],
+        (mine, other),
+        [whole_vmem()] * 2,
+        flops=4 * count * depth * LANES,
+        bytes_accessed=8 * count * depth,
+    )
+
+
+def local_kernel(values_ref, above_ref, below_ref, conv_ref, local_ref):
+    rows, columns, depth = values_ref.shape
+    for at in range(0, depth, LANES):
+        lanes = slice(at, at + LANES)
+        taps = conv_ref[:, :, lanes]
+        sheet = jnp.concatenate(
+            [above_ref[:, :, lanes], values_ref[:, :, lanes], below_ref[:, :, lanes]], axis=0
+        ).astype(jnp.float32)
+        edge = jnp.zeros((rows + 2, 1, LANES), jnp.float32)
+        before = jnp.concatenate([edge, sheet[:, :-1]], axis=1)
+        behind = jnp.concatenate([sheet[:, 1:], edge], axis=1)
+        total = jnp.zeros((rows, columns, LANES), jnp.float32)
+        for col_shift, moved in enumerate((before, sheet, behind)):
+            for row_shift in range(3):
+                total = total + taps[row_shift, col_shift] * moved[row_shift : row_shift + rows]
+        local_ref[:, :, lanes] = total
+
+
+def local_call(values, above, below, conv_weight):
+    return kernel_call(
+        local_kernel,
+        jax.ShapeDtypeStruct(values.shape, jnp.float32),
+        (values, above, below, conv_weight),
+        [whole_vmem()] * 4,
+        flops=18 * values.size,
+        bytes_accessed=6 * values.size,
+    )
+
+
+def query_kernel(*refs):
+    tokens_ref, qkv_ref, out_ref, mine_ref, theirs_ref, ours_ref, other_ref, *results = refs
+    query_ref, weight_ref = results
+    y, x, core = coordinates()
+    depth = tokens_ref.shape[1]
+    rows = qkv_ref.shape[0]
+    steps = len(STEPS)
+    rest_at = ours_ref.shape[0] - 2 * steps * REST
+    places = chip_places(y, x)
+    width = 3 * LANES
+
+    def block(of_core, k, lanes):
+        return jnp.where(core == of_core, mine_ref[k, :, lanes], theirs_ref[k, :, lanes])
+
+    def rest(of_core, lanes):
+        return jnp.where(core == of_core, ours_ref[rest_at:, lanes], other_ref[rest_at:, lanes])
+
+    def put(row, value, lanes):
+        weight_ref[pl.ds(pl.multiple_of(row, REST), value.shape[0]), lanes] = value
+
+    for at in range(0, depth, width):
+        lanes = slice(at, at + width)
+        order = [2 * k for k in range(steps)] + [2 * steps + k for k in range(2 * steps)]
+        order += [2 * k + 1 for k in range(steps)]
+        columns = [qkv_ref[:, lanes]] + [block(0, k, lanes) for k in order] + [rest(0, lanes)]
+        queries = jnp.dot(
+            tokens_ref[...], jnp.concatenate(columns, axis=0), preferred_element_type=jnp.float32
+        )
+        query_ref[:, lanes] = jnp.maximum(queries, 0.0).astype(jnp.bfloat16)
+
+        put(lax.axis_index("space") * rows, out_ref[:, lanes], lanes)
+        tiles = rest(1, lanes)
+        for k, step in enumerate(STEPS):
+            base = source_plane(step) * rows
+            held = (2 * k, 3 * steps + k, 2 * steps + k, 2 * k + 1)
+            for place, index in zip(places, held):
+                put(base + place * MAIN, block(1, index, lanes), lanes)
+            for run, tile in enumerate((y, 1 - y)):
+                start = (run * steps + k) * REST
+                put(base + 4 * MAIN + tile * REST, tiles[start : start + REST], lanes)
+
+
+def query_call(tokens, qkv_weight, out_weight, mine, theirs, ours, other):
+    depth = tokens.shape[1]
+    inputs = (tokens, qkv_weight, out_weight, mine, theirs, ours, other)
+    return kernel_call(
+        query_kernel,
+        [
+            jax.ShapeDtypeStruct(tokens.shape, jnp.bfloat16),
+            jax.ShapeDtypeStruct((depth, depth), jnp.bfloat16),
+        ],
+        inputs,
+        [whole_vmem()] * len(inputs),
+        flops=2 * tokens.size * depth,
+        bytes_accessed=4 * depth * depth,
+    )
+
+
+def finish_kernel(queries_ref, weight_ref, state_ref, local_ref, gain_ref, result_ref, read_ref):
+    count, depth = queries_ref.shape
+    mask = diagonal_mask()
+    square = jnp.zeros((count, LANES), jnp.float32)
+    for group in range(depth // LANES):
+        lanes = slice(group * LANES, (group + 1) * LANES)
+        spread = jnp.concatenate([state_ref[group]] * (LANES // HEAD_DIM), axis=0)
+        spread = jnp.where(mask, spread, 0.0).astype(jnp.bfloat16)
+        read = jnp.dot(queries_ref[:, lanes], spread, preferred_element_type=jnp.float32)
+        read_ref[:, lanes] = read
+        square = square + read * read
+    scale = lax.rsqrt(jnp.sum(square, axis=1, keepdims=True) / depth + 1e-06)
+    mixture = read_ref[...] * scale * gain_ref[...] + local_ref[...]
+    mixture = mixture.astype(jnp.bfloat16)
+    width = 3 * LANES
+    for at in range(0, depth, width):
+        lanes = slice(at, at + width)
+        product = jnp.dot(mixture, weight_ref[:, lanes], preferred_element_type=jnp.float32)
+        result_ref[:, lanes] = product.astype(jnp.bfloat16)
+
+
+def finish_call(queries, weight, state, local_term, gain):
+    inputs = (queries, weight, state, local_term, gain)
+    return kernel_call(
+        finish_kernel,
+        jax.ShapeDtypeStruct(queries.shape, jnp.bfloat16),
+        inputs,
+        [whole_vmem()] * len(inputs),
+        [pltpu.VMEM(queries.shape, jnp.float32)],
+        flops=2 * queries.size * queries.shape[1],
+        bytes_accessed=2 * weight.size,
+    )
+
+
+def plane_form(video_tokens, qkv_weight, out_weight, conv_weight, norm_gain):
+    frame_now = video_tokens[0]
+    row_count, col_count, depth = frame_now.shape
+    tokens = frame_now.reshape(row_count * col_count, depth)
+
+    first_piece, second_piece = pieces_call(qkv_weight, out_weight)
+    first_piece = first_piece[None]
+    one = shifted(first_piece, 1)
+    three = shifted(first_piece, -1)
+    tokens = reorder_call(after(tokens, second_piece), qkv_weight.shape[0])
+    other_tokens = flipped(tokens, (1, 1))
+    one, three = after((one, three), tokens)
+
+    pair = jnp.concatenate([one, three])
+    two = shifted(one, 1)
+    pair_first = flipped(pair, (2, 4))
+    near = jnp.concatenate(after((pair, pair_first, two), other_tokens))
+    away = flipped(near, (4, 2))
+    two_first = flipped(two, (2, 4))
+    two_far = flipped(two, (6, 6))
+
+    second_ready = after(second_piece, near)
+    second_one = shifted(second_ready, 1)
+    second_three = shifted(second_ready, -1)
+    second_two = shifted(after(second_one, two_first, two_far), 1)
+
+    mine = first_call(after(tokens, second_one, second_three), other_tokens, qkv_weight, near, away, two_first, two_far)
+    other = flipped(mine, (1, 1))
+    values, top, bottom, upto, total = state_call(mine, other, tokens.shape[0], col_count)
+
+    second_two = after(second_two, total)
+    second_own = jnp.stack([second_one[0], second_two[0], second_three[0]])
+    second_first = flipped(second_own, (2, 4))
+    second_second = flipped(second_own, (4, 2))
+
+    for bit, guard in ((2, 2), (4, 4), (6, 4)):
+        pairs = [(t, t ^ bit) for t in range(8) if not t & guard]
+        upto = upto + lax.ppermute(total, "tm", pairs).astype(jnp.float32)
+    count = lax.axis_size("space")
+    state = upto
+    for bit in (1, 2):
+        share = state.astype(jnp.bfloat16)
+        if bit == 2:
+            top, bottom = after((top, bottom), share)
+        pairs = [(i, i ^ bit) for i in range(count)]
+        state = share.astype(jnp.float32) + lax.ppermute(share, "space", pairs).astype(jnp.float32)
+    forward = [(i, i + 1) for i in range(count - 1)]
+    backward = [(target, source) for source, target in forward]
+    above = lax.ppermute(bottom, "space", forward)
+    below = lax.ppermute(top, "space", backward)
+    grid = values.reshape(row_count, col_count, depth)
+    local_term = local_call(grid, above, below, conv_weight).reshape(-1, depth)
+
+    parts = (second_one, second_two, second_three, second_first, second_second)
+    held = jnp.concatenate(after(parts, state, above, below))
+    swapped = flipped(held, (1, 1))
+    queries, weight = query_call(tokens, qkv_weight, out_weight, held, swapped, mine, other)
+    result = finish_call(queries, weight, state, local_term, norm_gain[None])
+    return result.reshape(1, row_count, col_count, depth)
+
+
 def solution(mesh):
+    def per_device(video_tokens, qkv_weight, out_weight, conv_weight, norm_gain):
+        fits = mesh.shape["tm"] == 8 and mesh.shape["space"] == 4
+        fits = fits and qkv_weight.shape[0] == 4 * MAIN + 2 * REST
+        form = plane_form if fits else general_form
+        return form(video_tokens, qkv_weight, out_weight, conv_weight, norm_gain)
+
     in_specs = (P("tm", "space", None, None), P("space", None), P("space", None), P(), P())
     out_specs = P("tm", "space", None, None)
     return jax.shard_map(

time: 267 us -> 83.4 us (0.31)
  waiting for transfers between devices: 214 us -> 40.5 us
  starting transfers between devices: 2.66 us -> 30.8 us
  between operations: 13.4 us -> 0.33 us
  matrix products: 11.3 us -> 0 us
  Pallas kernels: 0 us -> 11 us
  blocking collectives: 10.3 us -> 0 us
  local copies, waits for them, and re-layouts: 8.64 us -> 0.39 us
  other arithmetic: 6.1 us -> 0.15 us
    all_gather x2 -> x0, waiting for transfers between devices: 186 us -> none  [the longest x1 147 us: per_device(): lax.all_gather(qkv_weight, 'space', axis=0, tiled=True)]
    ppermute x2 -> x22, waiting for transfers between devices: 0.01 us -> 40.5 us  [the longest x6 21.9 us: shifted(): lax.ppermute(value, 'space', [(i, (i + step) % count) for i in range(coun...]
    ppermute x2 -> x22, starting transfers between devices: 2.58 us -> 30.8 us  [the longest x6 10.2 us: shifted(): lax.ppermute(value, 'space', [(i, (i + step) % count) for i in range(coun...]
    psum x1 -> x0, waiting for transfers between devices: 26.3 us -> none  [causal_states(): lax.psum(flat_state.astype(jnp.bfloat16), 'space').astype(jnp.float32)]
    dot_general x4 -> x0, matrix products: 11.3 us -> none  [the longest x2 9.37 us: fold_product(): return jnp.dot(left_side, block_rows, preferred_element_type=jnp.float32)]
    pallas_call x0 -> x7, Pallas kernels: none -> 11 us  [kernel_call(): pl.pallas_call(body, out_shape=outputs, in_specs=in_specs, out_specs=jax....]
    all_gather x1 -> x0, blocking collectives: 10.3 us -> none  [entering(): everything = lax.all_gather(value.astype(jnp.bfloat16), axis)]
    convert_element_type x12 -> x2, other arithmetic: 4.84 us -> 0.07 us  [plane_form(): share = state.astype(jnp.bfloat16)]
  transfers between devices with their start and end apart: 5 -> 22, of which waited for: 3 -> 14; matrix products, arithmetic and copies ran while one was open for 4% -> 0% of each run, Pallas kernels for 0% -> 4%
where the time goes in v1:
time: 83.4 us; the launch traced here: 83.1 us
  waiting for transfers between devices  40.5 us (49%)
  starting transfers between devices  30.8 us (37%)
  Pallas kernels  11 us (13%)
    ppermute x6, waiting for transfers between devices, shifted(): lax.ppermute(value, 'space', [(i, (i + step) % count) for i in range(coun...  21.9 us
    pallas_call x7, Pallas kernels, kernel_call(): pl.pallas_call(body, out_shape=outputs, in_specs=in_specs, out_specs=jax....  11 us
    ppermute x6, starting transfers between devices, shifted(): lax.ppermute(value, 'space', [(i, (i + step) % count) for i in range(coun...  10.2 us
    ppermute x9, waiting for transfers between devices, flipped(): lax.ppermute(value, 'tm', [(t, t ^ bit_on_core[t % 2]) for t in range(8)])  9.17 us
    ppermute x3, starting transfers between devices, plane_form(): upto = upto + lax.ppermute(total, 'tm', pairs).astype(jnp.float32)  7.94 us
    ppermute x9, starting transfers between devices, flipped(): lax.ppermute(value, 'tm', [(t, t ^ bit_on_core[t % 2]) for t in range(8)])  7.76 us
    ppermute x1, waiting for transfers between devices, plane_form(): below = lax.ppermute(top, 'space', backward)  4.39 us
    ppermute x1, starting transfers between devices, plane_form(): above = lax.ppermute(bottom, 'space', forward)  3.44 us
  transfers between devices with their start and end apart: 22, of which 14 were waited for; matrix products, arithmetic and copies ran while one was open for 0% of the time, Pallas kernels for 4%

profile of v1, /device:TPU:0, one launch (start us, length us, event | category | flops | bytes accessed | tf_op | source)
XLA Modules:
  0.0 83.1 jit_solution(7418411561613801858)
XLA Ops:
  0.0 0.0 copy-start.3
  0.0 1.9 %shard_map.55 = (bf16[80,1152]{1,0:T(8,128)(2,1)}, bf16[2,64,1152]{2,1,0:T(8,128)(2,1)}) custom-call(bf16[288,3456]{1,0:T(8,128)(2,1)} %refs_1_.1, bf16[288,1152]{1,0:T(8,128)(2,1)} %refs_2_.3), custom_call_target="tpu_custom_call" | custom-call | bytes 958464 | tf_op jit(solution)/shard_map/pallas_call | solution.py:164
  2.0 3.1 %collective-permute-start = (bf16[1,80,1152]{2,1,0:T(8,128)(2,1)}, bf16[1,80,1152]{2,1,0:T(8,128)(2,1)S(1)}, u32[]{:S(2)}, u32[]{:S(2)}) collective-permute-start(bf16[1,80,1152]{2,1,0:T(8,128)(2,1)} %bitcast.8), channel_id=1, source_target_pairs={{0,1},{1,2},{2,3},{3,0},{4,5},{5,6},{6,7},{7,4},{8,9},{9,10},{10,1... | collective-permute-start | bytes 552968 | tf_op jit(solution)/shard_map/ppermute | solution.py:104
  5.0 2.1 %collective-permute-start.1 = (bf16[1,80,1152]{2,1,0:T(8,128)(2,1)}, bf16[1,80,1152]{2,1,0:T(8,128)(2,1)S(1)}, u32[]{:S(2)}, u32[]{:S(2)}) collective-permute-start(bf16[1,80,1152]{2,1,0:T(8,128)(2,1)} %bitcast.9), channel_id=1, source_target_pairs={{0,3},{1,0},{2,1},{3,2},{4,7},{5,4},{6,5},{7,6},{8,11},{9,8},{10,9... | collective-permute-start | bytes 552968 | tf_op jit(solution)/shard_map/ppermute | solution.py:104
  7.1 0.0 copy-done.3
  7.1 1.2 %shard_map.56.refs_0_ = bf16[256,1152]{1,0:T(8,128)(2,1)S(1)} custom-call(bf16[256,1152]{1,0:T(8,128)(2,1)S(1)} %bitcast.7), custom_call_target="tpu_custom_call" | custom-call | flops 679477248 | bytes 589824 | tf_op jit(solution)/shard_map/pallas_call | solution.py:164
  8.3 0.0 copy-start.5
  8.3 0.0 copy-start
  8.3 0.1 collective-permute-start.4
  8.4 4.4 %collective-permute-done = bf16[1,80,1152]{2,1,0:T(8,128)(2,1)S(1)} collective-permute-done((bf16[1,80,1152]{2,1,0:T(8,128)(2,1)}, bf16[1,80,1152]{2,1,0:T(8,128)(2,1)S(1)}, u32[]{:S(2)}, u32[]{:S(2)}) %collective-permute-start) | collective-permute-done | bytes 184352 | tf_op jit(solution)/shard_map/ppermute | solution.py:104
  12.8 2.5 %collective-permute-done.1 = bf16[1,80,1152]{2,1,0:T(8,128)(2,1)S(1)} collective-permute-done((bf16[1,80,1152]{2,1,0:T(8,128)(2,1)}, bf16[1,80,1152]{2,1,0:T(8,128)(2,1)S(1)}, u32[]{:S(2)}, u32[]{:S(2)}) %collective-permute-start.1) | collective-permute-done | bytes 184352 | tf_op jit(solution)/shard_map/ppermute | solution.py:104
  15.3 1.6 %collective-permute-start.2 = (bf16[2,80,1152]{2,1,0:T(8,128)(2,1)S(1)}, bf16[2,80,1152]{2,1,0:T(8,128)(2,1)S(1)}, u32[]{:S(2)}, u32[]{:S(2)}) collective-permute-start(bf16[2,80,1152]{2,1,0:T(8,128)(2,1)S(1)} %constant_dynamic-update-slice_fusion), channel_id=1, source_target_pairs={{0,8},{4,20},{8,0},{12,28},{16,24},{20,4},{24,16},{28,12},{1,9},{5... | collective-permute-start | bytes 1105928 | tf_op jit(solution)/shard_map/ppermute | solution.py:108
  16.9 1.1 %collective-permute-start.3 = (bf16[1,80,1152]{2,1,0:T(8,128)(2,1)S(1)}, bf16[1,80,1152]{2,1,0:T(8,128)(2,1)S(1)}, u32[]{:S(2)}, u32[]{:S(2)}) collective-permute-start(bf16[1,80,1152]{2,1,0:T(8,128)(2,1)S(1)} %collective-permute-done), channel_id=1, source_target_pairs={{0,1},{1,2},{2,3},{3,0},{4,5},{5,6},{6,7},{7,4},{8,9},{9,10},{10,1... | collective-permute-start | bytes 552968 | tf_op jit(solution)/shard_map/ppermute | solution.py:104
  18.0 6.4 %collective-permute-done.3 = bf16[1,80,1152]{2,1,0:T(8,128)(2,1)S(1)} collective-permute-done((bf16[1,80,1152]{2,1,0:T(8,128)(2,1)S(1)}, bf16[1,80,1152]{2,1,0:T(8,128)(2,1)S(1)}, u32[]{:S(2)}, u32[]{:S(2)}) %collective-permute-start.3) | collective-permute-done | bytes 184352 | tf_op jit(solution)/shard_map/ppermute | solution.py:104
  24.4 0.0 collective-permute-done.2
  24.4 0.0 collective-permute-done.4.refs_1_
  24.5 1.4 %collective-permute-start.10 = (bf16[5,80,1152]{2,1,0:T(8,128)(2,1)S(1)}, bf16[5,80,1152]{2,1,0:T(8,128)(2,1)S(1)}, u32[]{:S(2)}, u32[]{:S(2)}) collective-permute-start(bf16[5,80,1152]{2,1,0:T(8,128)(2,1)S(1)} %constant_dynamic-update-slice_fusion.2.refs_3_), channel_id=1, source_target_pairs={{0,16},{4,12},{8,24},{12,4},{16,0},{20,28},{24,8},{28,20},{1,17},{... | collective-permute-start | bytes 2764808 | tf_op jit(solution)/shard_map/ppermute | solution.py:108
  25.9 0.0 copy-done.5
  25.9 0.0 collective-permute-start.5
  25.9 3.8 %collective-permute-start.9 = (bf16[2,64,1152]{2,1,0:T(8,128)(2,1)S(1)}, bf16[2,64,1152]{2,1,0:T(8,128)(2,1)S(1)}, u32[]{:S(2)}, u32[]{:S(2)}) collective-permute-start(bf16[2,64,1152]{2,1,0:T(8,128)(2,1)S(1)} %copy-done.5), channel_id=1, source_target_pairs={{0,3},{1,0},{2,1},{3,2},{4,7},{5,4},{6,5},{7,6},{8,11},{9,8},{10,9... | collective-permute-start | bytes 884744 | tf_op jit(solution)/shard_map/ppermute | solution.py:104
  29.8 0.6 collective-permute-start.6
  30.4 1.5 %collective-permute-start.7 = (bf16[1,80,1152]{2,1,0:T(8,128)(2,1)S(1)}, bf16[1,80,1152]{2,1,0:T(8,128)(2,1)S(1)}, u32[]{:S(2)}, u32[]{:S(2)}) collective-permute-start(bf16[1,80,1152]{2,1,0:T(8,128)(2,1)S(1)} %collective-permute-done.3), channel_id=1, source_target_pairs={{0,24},{4,28},{8,16},{12,20},{16,8},{20,12},{24,0},{28,4},{1,25},{... | collective-permute-start | bytes 552968 | tf_op jit(solution)/shard_map/ppermute | solution.py:108
  31.9 5.8 %collective-permute-done.5 = bf16[2,64,1152]{2,1,0:T(8,128)(2,1)S(1)} collective-permute-done((bf16[2,64,1152]{2,1,0:T(8,128)(2,1)S(1)}, bf16[2,64,1152]{2,1,0:T(8,128)(2,1)S(1)}, u32[]{:S(2)}, u32[]{:S(2)}) %collective-permute-start.5) | collective-permute-done | bytes 294944 | tf_op jit(solution)/shard_map/ppermute | solution.py:104
  37.7 2.9 %collective-permute-done.9 = bf16[2,64,1152]{2,1,0:T(8,128)(2,1)S(1)} collective-permute-done((bf16[2,64,1152]{2,1,0:T(8,128)(2,1)S(1)}, bf16[2,64,1152]{2,1,0:T(8,128)(2,1)S(1)}, u32[]{:S(2)}, u32[]{:S(2)}) %collective-permute-start.9) | collective-permute-done | bytes 294944 | tf_op jit(solution)/shard_map/ppermute | solution.py:104
  40.5 0.0 collective-permute-done.6.refs_5_
  40.5 0.5 collective-permute-done.7.refs_6_
  41.1 2.8 %collective-permute-done.10.refs_4_ = bf16[5,80,1152]{2,1,0:T(8,128)(2,1)S(1)} collective-permute-done((bf16[5,80,1152]{2,1,0:T(8,128)(2,1)S(1)}, bf16[5,80,1152]{2,1,0:T(8,128)(2,1)S(1)}, u32[]{:S(2)}, u32[]{:S(2)}) %collective-permute-start.10) | collective-permute-done | bytes 921632 | tf_op jit(solution)/shard_map/ppermute | solution.py:108
  43.9 0.0 copy-done
  43.9 2.2 %shard_map.57.mine_ref.refs_5_ = bf16[608,1152]{1,0:T(8,128)(2,1)S(1)} custom-call(bf16[256,1152]{1,0:T(8,128)(2,1)S(1)} %shard_map.56.refs_0_, bf16[256,1152]{1,0:T(8,128)(2,1)S(1)} %collective-permute-done.4.refs_1_, bf16[288,3456]{1,0:T(8,128)(2,1)S(1)} %copy-done, bf16[5,80,1152]{2,1,0:T(8,128)(2,1)S(1)} %constant_dynamic-update-slice_fusion.2.refs_3_, ...), custom_call_target="tpu_custom_call" | custom-call | flops 1358954496 | bytes 2654208 | tf_op jit(solution)/shard_map/pallas_call | solution.py:164
  46.1 0.1 collective-permute-start.11
  46.2 0.1 collective-permute-start.8
  46.2 3.1 %collective-permute-done.11.other_ref.refs_6_ = bf16[608,1152]{1,0:T(8,128)(2,1)S(1)} collective-permute-done((bf16[608,1152]{1,0:T(8,128)(2,1)S(1)}, bf16[608,1152]{1,0:T(8,128)(2,1)S(1)}, u32[]{:S(2)}, u32[]{:S(2)}) %collective-permute-start.11) | collective-permute-done | bytes 1400864 | tf_op jit(solution)/shard_map/ppermute | solution.py:108
  49.3 0.9 %shard_map.58 = (bf16[256,1152]{1,0:T(8,128)(2,1)S(1)}, bf16[1,64,1152]{2,1,0:T(8,128)(2,1)S(1)}, bf16[1,64,1152]{2,1,0:T(8,128)(2,1)S(1)}, f32[9,32,128]{2,1,0:T(8,128)S(1)}, bf16[9,32,128]{2,1,0:T(8,128)(2,1)S(1)}) custom-call(bf16[608,1152]{1,0:T(8,128)(2,1)S(1)} %shard_map.57.mine_ref.refs_5_, bf16[608,1152]{1,0:T(8,128)(2,1)S(1)} %collective-permute-done.11.other_ref.refs_6_), custom_call_target="tpu_custom_call" | custom-call | flops 150994944 | bytes 2359296 | tf_op jit(solution)/shard_map/pallas_call | solution.py:164
  50.2 3.3 %collective-permute-start.16 = (bf16[9,32,128]{2,1,0:T(8,128)(2,1)S(1)}, bf16[9,32,128]{2,1,0:T(8,128)(2,1)S(1)}, u32[]{:S(2)}, u32[]{:S(2)}) collective-permute-start(bf16[9,32,128]{2,1,0:T(8,128)(2,1)S(1)} %get-tuple-element.42), channel_id=1, source_target_pairs={{0,24},{4,28},{8,16},{12,20},{1,25},{5,29},{9,17},{13,21},{2,26},{... | collective-permute-start | bytes 221192 | tf_op jit(solution)/shard_map/ppermute | solution.py:527
  53.5 1.3 %collective-permute-start.15 = (bf16[9,32,128]{2,1,0:T(8,128)(2,1)S(1)}, bf16[9,32,128]{2,1,0:T(8,128)(2,1)S(1)}, u32[]{:S(2)}, u32[]{:S(2)}) collective-permute-start(bf16[9,32,128]{2,1,0:T(8,128)(2,1)S(1)} %get-tuple-element.42), channel_id=1, source_target_pairs={{0,16},{4,20},{8,24},{12,28},{1,17},{5,21},{9,25},{13,29},{2,18},{... | collective-permute-start | bytes 221192 | tf_op jit(solution)/shard_map/ppermute | solution.py:527
  54.8 3.3 %collective-permute-start.14 = (bf16[9,32,128]{2,1,0:T(8,128)(2,1)S(1)}, bf16[9,32,128]{2,1,0:T(8,128)(2,1)S(1)}, u32[]{:S(2)}, u32[]{:S(2)}) collective-permute-start(bf16[9,32,128]{2,1,0:T(8,128)(2,1)S(1)} %get-tuple-element.42), channel_id=1, source_target_pairs={{0,8},{4,12},{16,24},{20,28},{1,9},{5,13},{17,25},{21,29},{2,10},{... | collective-permute-start | bytes 221192 | tf_op jit(solution)/shard_map/ppermute | solution.py:527
  58.2 0.0 collective-permute-done.8
  58.2 0.0 collective-permute-done.16
  58.2 0.0 collective-permute-done.15
  58.3 1.9 %collective-permute-done.14 = bf16[9,32,128]{2,1,0:T(8,128)(2,1)S(1)} collective-permute-done((bf16[9,32,128]{2,1,0:T(8,128)(2,1)S(1)}, bf16[9,32,128]{2,1,0:T(8,128)(2,1)S(1)}, u32[]{:S(2)}, u32[]{:S(2)}) %collective-permute-start.14) | collective-permute-done | bytes 73760 | tf_op jit(solution)/shard_map/ppermute | solution.py:527
  60.2 0.1 collective-permute-start.17
  60.2 0.1 pad_maximum_fusion
  60.3 2.4 %collective-permute-start.12 = (bf16[3,64,1152]{2,1,0:T(8,128)(2,1)S(1)}, bf16[3,64,1152]{2,1,0:T(8,128)(2,1)S(1)}, u32[]{:S(2)}, u32[]{:S(2)}) collective-permute-start(bf16[3,64,1152]{2,1,0:T(8,128)(2,1)S(1)} %pad_maximum_fusion), channel_id=1, source_target_pairs={{0,8},{4,20},{8,0},{12,28},{16,24},{20,4},{24,16},{28,12},{1,9},{5... | collective-permute-start | bytes 1327112 | tf_op jit(solution)/shard_map/ppermute | solution.py:108
  62.8 0.0 collective-permute-start.13
  62.8 1.8 %collective-permute-done.17 = bf16[9,32,128]{2,1,0:T(8,128)(2,1)S(1)} collective-permute-done((bf16[9,32,128]{2,1,0:T(8,128)(2,1)S(1)}, bf16[9,32,128]{2,1,0:T(8,128)(2,1)S(1)}, u32[]{:S(2)}, u32[]{:S(2)}) %collective-permute-start.17) | collective-permute-done | bytes 73760 | tf_op jit(solution)/shard_map/ppermute | solution.py:535
  64.6 0.1 collective-permute-start.18
  64.7 3.4 %collective-permute-start.19 = (bf16[1,64,1152]{2,1,0:T(8,128)(2,1)S(1)}, bf16[1,64,1152]{2,1,0:T(8,128)(2,1)S(1)}, u32[]{:S(2)}, u32[]{:S(2)}) collective-permute-start(bf16[1,64,1152]{2,1,0:T(8,128)(2,1)S(1)} %get-tuple-element.47), channel_id=1, source_target_pairs={{0,1},{1,2},{2,3},{4,5},{5,6},{6,7},{8,9},{9,10},{10,11},{12,13},{... | collective-permute-start | bytes 442376 | tf_op jit(solution)/shard_map/ppermute | solution.py:538
  68.1 1.3 %collective-permute-start.20 = (bf16[1,64,1152]{2,1,0:T(8,128)(2,1)S(1)}, bf16[1,64,1152]{2,1,0:T(8,128)(2,1)S(1)}, u32[]{:S(2)}, u32[]{:S(2)}) collective-permute-start(bf16[1,64,1152]{2,1,0:T(8,128)(2,1)S(1)} %get-tuple-element.48), channel_id=1, source_target_pairs={{1,0},{2,1},{3,2},{5,4},{6,5},{7,6},{9,8},{10,9},{11,10},{13,12},{... | collective-permute-start | bytes 442376 | tf_op jit(solution)/shard_map/ppermute | solution.py:539
  69.4 0.9 %collective-permute-done.18 = bf16[9,32,128]{2,1,0:T(8,128)(2,1)S(1)} collective-permute-done((bf16[9,32,128]{2,1,0:T(8,128)(2,1)S(1)}, bf16[9,32,128]{2,1,0:T(8,128)(2,1)S(1)}, u32[]{:S(2)}, u32[]{:S(2)}) %collective-permute-start.18) | collective-permute-done | bytes 73760 | tf_op jit(solution)/shard_map/ppermute | solution.py:535
  70.4 0.0 copy-start.4
  70.4 0.0 copy-start.2
  70.4 0.4 collective-permute-done.19.above_ref
  70.8 4.4 %collective-permute-done.20.below_ref = bf16[1,64,1152]{2,1,0:T(8,128)(2,1)S(1)} collective-permute-done((bf16[1,64,1152]{2,1,0:T(8,128)(2,1)S(1)}, bf16[1,64,1152]{2,1,0:T(8,128)(2,1)S(1)}, u32[]{:S(2)}, u32[]{:S(2)}) %collective-permute-start.20) | collective-permute-done | bytes 147488 | tf_op jit(solution)/shard_map/ppermute | solution.py:539
  75.2 0.0 collective-permute-done.12
  75.2 0.0 collective-permute-done.13
  75.3 0.0 copy-start.1
  75.4 0.1 collective-permute-start.21
  75.5 0.0 copy-done.4
  75.5 0.0 copy-done.2
  75.5 0.9 %shard_map.60 = f32[4,64,1152]{2,1,0:T(8,128)S(1)} custom-call(bf16[4,64,1152]{2,1,0:T(8,128)(2,1)S(1)} %bitcast.6, bf16[1,64,1152]{2,1,0:T(8,128)(2,1)S(1)} %collective-permute-done.19.above_ref, bf16[1,64,1152]{2,1,0:T(8,128)(2,1)S(1)} %collective-permute-done.20.below_ref, f32[3,3,1152]{2,1,0:T(4,128)S(1)} %copy-done.2), custom_call_target="tpu_custom_call" | custom-call | flops 5308416 | bytes 1769472 | tf_op jit(solution)/shard_map/pallas_call | solution.py:164
  76.5 2.7 %collective-permute-done.21.refs_4_ = bf16[12,64,1152]{2,1,0:T(8,128)(2,1)S(1)} collective-permute-done((bf16[12,64,1152]{2,1,0:T(8,128)(2,1)S(1)}, bf16[12,64,1152]{2,1,0:T(8,128)(2,1)S(1)}, u32[]{:S(2)}, u32[]{:S(2)}) %collective-permute-start.21) | collective-permute-done | bytes 1769504 | tf_op jit(solution)/shard_map/ppermute | solution.py:108
  79.2 0.0 copy-done.1
  79.2 1.6 %shard_map.59 = (bf16[256,1152]{1,0:T(8,128)(2,1)S(1)}, bf16[1152,1152]{1,0:T(8,128)(2,1)S(1)}) custom-call(bf16[256,1152]{1,0:T(8,128)(2,1)S(1)} %shard_map.56.refs_0_, bf16[288,3456]{1,0:T(8,128)(2,1)S(1)} %copy-done, bf16[288,1152]{1,0:T(8,128)(2,1)S(1)} %copy-done.1, bf16[12,64,1152]{2,1,0:T(8,128)(2,1)S(1)} %constant_dynamic-update-slice_fusion.5.refs_3_, ...), custom_call_target="tpu_custom_call" | custom-call | flops 679477248 | bytes 5308416 | tf_op jit(solution)/shard_map/pallas_call | solution.py:164
  80.7 2.3 %shard_map.61 = bf16[256,1152]{1,0:T(8,128)(2,1)} custom-call(bf16[256,1152]{1,0:T(8,128)(2,1)S(1)} %get-tuple-element.54.queries_ref, bf16[1152,1152]{1,0:T(8,128)(2,1)S(1)} %get-tuple-element.55.weight_ref, f32[9,32,128]{2,1,0:T(8,128)S(1)} %convert_add_fusion.state_ref, f32[256,1152]{1,0:T(8,128)S(1)} %bitcast.5, f32[1,1152]{1,0:T(1,128)S(1)} %broadcast_in_dim.7.gain_ref), custom_call_target="tpu_custom_call" | custom-call | flops 679477248 | bytes 2654208 | tf_op jit(solution)/shard_map/pallas_call | solution.py:164
  (17 shorter events, 0.4 us)
Async XLA Ops:
  0.0 7.1 %copy-start.3 = (bf16[1,4,64,1152]{3,2,1,0:T(8,128)(2,1)S(1)}, bf16[1,4,64,1152]{3,2,1,0:T(8,128)(2,1)}, u32[]{:S(2)}) copy-start(bf16[1,4,64,1152]{3,2,1,0:T(8,128)(2,1)} %param.5) | copy-start | bytes 1769476
  2.0 10.8 %collective-permute-start = (bf16[1,80,1152]{2,1,0:T(8,128)(2,1)}, bf16[1,80,1152]{2,1,0:T(8,128)(2,1)S(1)}, u32[]{:S(2)}, u32[]{:S(2)}) collective-permute-start(bf16[1,80,1152]{2,1,0:T(8,128)(2,1)} %bitcast.8), channel_id=1, source_target_pairs={{0,1},{1,2},{2,3},{3,0},{4,5},{5,6},{6,7},{7,4},{8,9},{9,10},{10,1... | collective-permute-start | bytes 552968 | tf_op jit(solution)/shard_map/ppermute | solution.py:104
  5.0 10.3 %collective-permute-start.1 = (bf16[1,80,1152]{2,1,0:T(8,128)(2,1)}, bf16[1,80,1152]{2,1,0:T(8,128)(2,1)S(1)}, u32[]{:S(2)}, u32[]{:S(2)}) collective-permute-start(bf16[1,80,1152]{2,1,0:T(8,128)(2,1)} %bitcast.9), channel_id=1, source_target_pairs={{0,3},{1,0},{2,1},{3,2},{4,7},{5,4},{6,5},{7,6},{8,11},{9,8},{10,9... | collective-permute-start | bytes 552968 | tf_op jit(solution)/shard_map/ppermute | solution.py:104
  8.3 17.6 %copy-start.5 = (bf16[2,64,1152]{2,1,0:T(8,128)(2,1)S(1)}, bf16[2,64,1152]{2,1,0:T(8,128)(2,1)}, u32[]{:S(2)}) copy-start(bf16[2,64,1152]{2,1,0:T(8,128)(2,1)} %get-tuple-element.39) | copy-start | bytes 884740
  8.3 35.6 %copy-start = (bf16[288,3456]{1,0:T(8,128)(2,1)S(1)}, bf16[288,3456]{1,0:T(8,128)(2,1)}, u32[]{:S(2)}) copy-start(bf16[288,3456]{1,0:T(8,128)(2,1)} %refs_1_.1) | copy-start | bytes 5971972
  8.3 16.1 %collective-permute-start.4 = (bf16[256,1152]{1,0:T(8,128)(2,1)S(1)}, bf16[256,1152]{1,0:T(8,128)(2,1)S(1)}, u32[]{:S(2)}, u32[]{:S(2)}) collective-permute-start(bf16[256,1152]{1,0:T(8,128)(2,1)S(1)} %shard_map.56.refs_0_), channel_id=1, source_target_pairs={{0,4},{4,0},{8,12},{12,8},{16,20},{20,16},{24,28},{28,24},{1,5},{5... | collective-permute-start | bytes 1769480 | tf_op jit(solution)/shard_map/ppermute | solution.py:108
  15.3 9.0 %collective-permute-start.2 = (bf16[2,80,1152]{2,1,0:T(8,128)(2,1)S(1)}, bf16[2,80,1152]{2,1,0:T(8,128)(2,1)S(1)}, u32[]{:S(2)}, u32[]{:S(2)}) collective-permute-start(bf16[2,80,1152]{2,1,0:T(8,128)(2,1)S(1)} %constant_dynamic-update-slice_fusion), channel_id=1, source_target_pairs={{0,8},{4,20},{8,0},{12,28},{16,24},{20,4},{24,16},{28,12},{1,9},{5... | collective-permute-start | bytes 1105928 | tf_op jit(solution)/shard_map/ppermute | solution.py:108
  16.9 7.5 %collective-permute-start.3 = (bf16[1,80,1152]{2,1,0:T(8,128)(2,1)S(1)}, bf16[1,80,1152]{2,1,0:T(8,128)(2,1)S(1)}, u32[]{:S(2)}, u32[]{:S(2)}) collective-permute-start(bf16[1,80,1152]{2,1,0:T(8,128)(2,1)S(1)} %collective-permute-done), channel_id=1, source_target_pairs={{0,1},{1,2},{2,3},{3,0},{4,5},{5,6},{6,7},{7,4},{8,9},{9,10},{10,1... | collective-permute-start | bytes 552968 | tf_op jit(solution)/shard_map/ppermute | solution.py:104
  24.5 19.4 %collective-permute-start.10 = (bf16[5,80,1152]{2,1,0:T(8,128)(2,1)S(1)}, bf16[5,80,1152]{2,1,0:T(8,128)(2,1)S(1)}, u32[]{:S(2)}, u32[]{:S(2)}) collective-permute-start(bf16[5,80,1152]{2,1,0:T(8,128)(2,1)S(1)} %constant_dynamic-update-slice_fusion.2.refs_3_), channel_id=1, source_target_pairs={{0,16},{4,12},{8,24},{12,4},{16,0},{20,28},{24,8},{28,20},{1,17},{... | collective-permute-start | bytes 2764808 | tf_op jit(solution)/shard_map/ppermute | solution.py:108
  25.9 11.7 %collective-permute-start.5 = (bf16[2,64,1152]{2,1,0:T(8,128)(2,1)S(1)}, bf16[2,64,1152]{2,1,0:T(8,128)(2,1)S(1)}, u32[]{:S(2)}, u32[]{:S(2)}) collective-permute-start(bf16[2,64,1152]{2,1,0:T(8,128)(2,1)S(1)} %copy-done.5), channel_id=1, source_target_pairs={{0,1},{1,2},{2,3},{3,0},{4,5},{5,6},{6,7},{7,4},{8,9},{9,10},{10,1... | collective-permute-start | bytes 884744 | tf_op jit(solution)/shard_map/ppermute | solution.py:104
  25.9 14.6 %collective-permute-start.9 = (bf16[2,64,1152]{2,1,0:T(8,128)(2,1)S(1)}, bf16[2,64,1152]{2,1,0:T(8,128)(2,1)S(1)}, u32[]{:S(2)}, u32[]{:S(2)}) collective-permute-start(bf16[2,64,1152]{2,1,0:T(8,128)(2,1)S(1)} %copy-done.5), channel_id=1, source_target_pairs={{0,3},{1,0},{2,1},{3,2},{4,7},{5,4},{6,5},{7,6},{8,11},{9,8},{10,9... | collective-permute-start | bytes 884744 | tf_op jit(solution)/shard_map/ppermute | solution.py:104
  29.8 10.8 %collective-permute-start.6 = (bf16[1,80,1152]{2,1,0:T(8,128)(2,1)S(1)}, bf16[1,80,1152]{2,1,0:T(8,128)(2,1)S(1)}, u32[]{:S(2)}, u32[]{:S(2)}) collective-permute-start(bf16[1,80,1152]{2,1,0:T(8,128)(2,1)S(1)} %collective-permute-done.3), channel_id=1, source_target_pairs={{0,8},{4,20},{8,0},{12,28},{16,24},{20,4},{24,16},{28,12},{1,9},{5... | collective-permute-start | bytes 552968 | tf_op jit(solution)/shard_map/ppermute | solution.py:108
  30.4 10.7 %collective-permute-start.7 = (bf16[1,80,1152]{2,1,0:T(8,128)(2,1)S(1)}, bf16[1,80,1152]{2,1,0:T(8,128)(2,1)S(1)}, u32[]{:S(2)}, u32[]{:S(2)}) collective-permute-start(bf16[1,80,1152]{2,1,0:T(8,128)(2,1)S(1)} %collective-permute-done.3), channel_id=1, source_target_pairs={{0,24},{4,28},{8,16},{12,20},{16,8},{20,12},{24,0},{28,4},{1,25},{... | collective-permute-start | bytes 552968 | tf_op jit(solution)/shard_map/ppermute | solution.py:108
  46.1 3.2 %collective-permute-start.11 = (bf16[608,1152]{1,0:T(8,128)(2,1)S(1)}, bf16[608,1152]{1,0:T(8,128)(2,1)S(1)}, u32[]{:S(2)}, u32[]{:S(2)}) collective-permute-start(bf16[608,1152]{1,0:T(8,128)(2,1)S(1)} %shard_map.57.mine_ref.refs_5_), channel_id=1, source_target_pairs={{0,4},{4,0},{8,12},{12,8},{16,20},{20,16},{24,28},{28,24},{1,5},{5... | collective-permute-start | bytes 4202504 | tf_op jit(solution)/shard_map/ppermute | solution.py:108
  46.2 12.0 %collective-permute-start.8 = (bf16[2,64,1152]{2,1,0:T(8,128)(2,1)S(1)}, bf16[2,64,1152]{2,1,0:T(8,128)(2,1)S(1)}, u32[]{:S(2)}, u32[]{:S(2)}) collective-permute-start(bf16[2,64,1152]{2,1,0:T(8,128)(2,1)S(1)} %collective-permute-done.5), channel_id=1, source_target_pairs={{0,1},{1,2},{2,3},{3,0},{4,5},{5,6},{6,7},{7,4},{8,9},{9,10},{10,1... | collective-permute-start | bytes 884744 | tf_op jit(solution)/shard_map/ppermute | solution.py:104
  50.2 8.0 %collective-permute-start.16 = (bf16[9,32,128]{2,1,0:T(8,128)(2,1)S(1)}, bf16[9,32,128]{2,1,0:T(8,128)(2,1)S(1)}, u32[]{:S(2)}, u32[]{:S(2)}) collective-permute-start(bf16[9,32,128]{2,1,0:T(8,128)(2,1)S(1)} %get-tuple-element.42), channel_id=1, source_target_pairs={{0,24},{4,28},{8,16},{12,20},{1,25},{5,29},{9,17},{13,21},{2,26},{... | collective-permute-start | bytes 221192 | tf_op jit(solution)/shard_map/ppermute | solution.py:527
  53.5 4.7 %collective-permute-start.15 = (bf16[9,32,128]{2,1,0:T(8,128)(2,1)S(1)}, bf16[9,32,128]{2,1,0:T(8,128)(2,1)S(1)}, u32[]{:S(2)}, u32[]{:S(2)}) collective-permute-start(bf16[9,32,128]{2,1,0:T(8,128)(2,1)S(1)} %get-tuple-element.42), channel_id=1, source_target_pairs={{0,16},{4,20},{8,24},{12,28},{1,17},{5,21},{9,25},{13,29},{2,18},{... | collective-permute-start | bytes 221192 | tf_op jit(solution)/shard_map/ppermute | solution.py:527
  54.8 5.3 %collective-permute-start.14 = (bf16[9,32,128]{2,1,0:T(8,128)(2,1)S(1)}, bf16[9,32,128]{2,1,0:T(8,128)(2,1)S(1)}, u32[]{:S(2)}, u32[]{:S(2)}) collective-permute-start(bf16[9,32,128]{2,1,0:T(8,128)(2,1)S(1)} %get-tuple-element.42), channel_id=1, source_target_pairs={{0,8},{4,12},{16,24},{20,28},{1,9},{5,13},{17,25},{21,29},{2,10},{... | collective-permute-start | bytes 221192 | tf_op jit(solution)/shard_map/ppermute | solution.py:527
  60.2 4.4 %collective-permute-start.17 = (bf16[9,32,128]{2,1,0:T(8,128)(2,1)S(1)}, bf16[9,32,128]{2,1,0:T(8,128)(2,1)S(1)}, u32[]{:S(2)}, u32[]{:S(2)}) collective-permute-start(bf16[9,32,128]{2,1,0:T(8,128)(2,1)S(1)} %add_convert_fusion.1), channel_id=1, source_target_pairs={{0,1},{1,0},{2,3},{3,2},{4,5},{5,4},{6,7},{7,6},{8,9},{9,8},{10,11... | collective-permute-start | bytes 221192 | tf_op jit(solution)/shard_map/ppermute | solution.py:535
  60.3 14.9 %collective-permute-start.12 = (bf16[3,64,1152]{2,1,0:T(8,128)(2,1)S(1)}, bf16[3,64,1152]{2,1,0:T(8,128)(2,1)S(1)}, u32[]{:S(2)}, u32[]{:S(2)}) collective-permute-start(bf16[3,64,1152]{2,1,0:T(8,128)(2,1)S(1)} %pad_maximum_fusion), channel_id=1, source_target_pairs={{0,8},{4,20},{8,0},{12,28},{16,24},{20,4},{24,16},{28,12},{1,9},{5... | collective-permute-start | bytes 1327112 | tf_op jit(solution)/shard_map/ppermute | solution.py:108
  62.8 12.4 %collective-permute-start.13 = (bf16[3,64,1152]{2,1,0:T(8,128)(2,1)S(1)}, bf16[3,64,1152]{2,1,0:T(8,128)(2,1)S(1)}, u32[]{:S(2)}, u32[]{:S(2)}) collective-permute-start(bf16[3,64,1152]{2,1,0:T(8,128)(2,1)S(1)} %pad_maximum_fusion), channel_id=1, source_target_pairs={{0,16},{4,12},{8,24},{12,4},{16,0},{20,28},{24,8},{28,20},{1,17},{... | collective-permute-start | bytes 1327112 | tf_op jit(solution)/shard_map/ppermute | solution.py:108
  64.6 5.7 %collective-permute-start.18 = (bf16[9,32,128]{2,1,0:T(8,128)(2,1)S(1)}, bf16[9,32,128]{2,1,0:T(8,128)(2,1)S(1)}, u32[]{:S(2)}, u32[]{:S(2)}) collective-permute-start(bf16[9,32,128]{2,1,0:T(8,128)(2,1)S(1)} %add_convert_fusion), channel_id=1, source_target_pairs={{0,2},{1,3},{2,0},{3,1},{4,6},{5,7},{6,4},{7,5},{8,10},{9,11},{10,... | collective-permute-start | bytes 221192 | tf_op jit(solution)/shard_map/ppermute | solution.py:535
  64.7 6.1 %collective-permute-start.19 = (bf16[1,64,1152]{2,1,0:T(8,128)(2,1)S(1)}, bf16[1,64,1152]{2,1,0:T(8,128)(2,1)S(1)}, u32[]{:S(2)}, u32[]{:S(2)}) collective-permute-start(bf16[1,64,1152]{2,1,0:T(8,128)(2,1)S(1)} %get-tuple-element.47), channel_id=1, source_target_pairs={{0,1},{1,2},{2,3},{4,5},{5,6},{6,7},{8,9},{9,10},{10,11},{12,13},{... | collective-permute-start | bytes 442376 | tf_op jit(solution)/shard_map/ppermute | solution.py:538
  68.1 7.0 %collective-permute-start.20 = (bf16[1,64,1152]{2,1,0:T(8,128)(2,1)S(1)}, bf16[1,64,1152]{2,1,0:T(8,128)(2,1)S(1)}, u32[]{:S(2)}, u32[]{:S(2)}) collective-permute-start(bf16[1,64,1152]{2,1,0:T(8,128)(2,1)S(1)} %get-tuple-element.48), channel_id=1, source_target_pairs={{1,0},{2,1},{3,2},{5,4},{6,5},{7,6},{9,8},{10,9},{11,10},{13,12},{... | collective-permute-start | bytes 442376 | tf_op jit(solution)/shard_map/ppermute | solution.py:539
  70.4 5.1 %copy-start.4 = (f32[1152]{0:T(1024)S(1)}, f32[1152]{0:T(1024)}, u32[]{:S(2)}) copy-start(f32[1152]{0:T(1024)} %param.9) | copy-start | bytes 13828
  70.4 5.1 %copy-start.2 = (f32[3,3,1152]{2,1,0:T(4,128)S(1)}, f32[3,3,1152]{2,1,0:T(4,128)}, u32[]{:S(2)}) copy-start(f32[3,3,1152]{2,1,0:T(4,128)} %conv_ref.1) | copy-start | bytes 124420
  75.3 3.9 %copy-start.1 = (bf16[288,1152]{1,0:T(8,128)(2,1)S(1)}, bf16[288,1152]{1,0:T(8,128)(2,1)}, u32[]{:S(2)}) copy-start(bf16[288,1152]{1,0:T(8,128)(2,1)} %refs_2_.3) | copy-start | bytes 1990660
  75.4 3.8 %collective-permute-start.21 = (bf16[12,64,1152]{2,1,0:T(8,128)(2,1)S(1)}, bf16[12,64,1152]{2,1,0:T(8,128)(2,1)S(1)}, u32[]{:S(2)}, u32[]{:S(2)}) collective-permute-start(bf16[12,64,1152]{2,1,0:T(8,128)(2,1)S(1)} %constant_dynamic-update-slice_fusion.5.refs_3_), channel_id=1, source_target_pairs={{0,4},{4,0},{8,12},{12,8},{16,20},{20,16},{24,28},{28,24},{1,5},{5... | collective-permute-start | bytes 5308424 | tf_op jit(solution)/shard_map/ppermute | solution.py:108

commit v2 on v1

--- a/solution.py
+++ b/solution.py
@@ -514,10 +514,9 @@
     second_two = shifted(after(second_one, two_first, two_far), 1)
 
     mine = first_call(after(tokens, second_one, second_three), other_tokens, qkv_weight, near, away, two_first, two_far)
-    other = flipped(mine, (1, 1))
+    other = flipped(after(mine, second_two), (1, 1))
     values, top, bottom, upto, total = state_call(mine, other, tokens.shape[0], col_count)
 
-    second_two = after(second_two, total)
     second_own = jnp.stack([second_one[0], second_two[0], second_three[0]])
     second_first = flipped(second_own, (2, 4))
     second_second = flipped(second_own, (4, 2))
@@ -526,22 +525,23 @@
         pairs = [(t, t ^ bit) for t in range(8) if not t & guard]
         upto = upto + lax.ppermute(total, "tm", pairs).astype(jnp.float32)
     count = lax.axis_size("space")
-    state = upto
-    for bit in (1, 2):
-        share = state.astype(jnp.bfloat16)
-        if bit == 2:
-            top, bottom = after((top, bottom), share)
-        pairs = [(i, i ^ bit) for i in range(count)]
-        state = share.astype(jnp.float32) + lax.ppermute(share, "space", pairs).astype(jnp.float32)
+    top, bottom = after((top, bottom), upto)
     forward = [(i, i + 1) for i in range(count - 1)]
     backward = [(target, source) for source, target in forward]
     above = lax.ppermute(bottom, "space", forward)
     below = lax.ppermute(top, "space", backward)
+    state = after(upto, second_first, second_second)
+    for bit in (1, 2):
+        share = state.astype(jnp.bfloat16)
+        if bit == 2:
+            share = after(share, above, below)
+        pairs = [(i, i ^ bit) for i in range(count)]
+        state = share.astype(jnp.float32) + lax.ppermute(share, "space", pairs).astype(jnp.float32)
     grid = values.reshape(row_count, col_count, depth)
     local_term = local_call(grid, above, below, conv_weight).reshape(-1, depth)
 
     parts = (second_one, second_two, second_three, second_first, second_second)
-    held = jnp.concatenate(after(parts, state, above, below))
+    held = jnp.concatenate(after(parts, share))
     swapped = flipped(held, (1, 1))
     queries, weight = query_call(tokens, qkv_weight, out_weight, held, swapped, mine, other)
     result = finish_call(queries, weight, state, local_term, norm_gain[None])

time: 83.4 us -> 87.5 us (1.049)
  starting transfers between devices: 30.8 us -> 34.7 us
    ppermute x6, waiting for transfers between devices: 21.9 us -> 17.9 us  [shifted(): lax.ppermute(value, 'space', [(i, (i + step) % count) for i in range(coun...]
    ppermute x9, starting transfers between devices: 7.76 us -> 11.1 us  [flipped(): lax.ppermute(value, 'tm', [(t, t ^ bit_on_core[t % 2]) for t in range(8)])]
    ppermute x2, waiting for transfers between devices: 2.75 us -> 5.94 us  [plane_form(): lax.ppermute(share, 'space', pairs).astype(jnp.float32)]
    ppermute x1, waiting for transfers between devices: 0.39 us -> 2.1 us  [plane_form(): above = lax.ppermute(bottom, 'space', forward)]
    ppermute x9, waiting for transfers between devices: 9.17 us -> 7.6 us  [flipped(): lax.ppermute(value, 'tm', [(t, t ^ bit_on_core[t % 2]) for t in range(8)])]
    ppermute x3, waiting for transfers between devices: 1.87 us -> 3 us  [plane_form(): upto = upto + lax.ppermute(total, 'tm', pairs).astype(jnp.float32)]
  transfers between devices with their start and end apart: 22 -> 22, of which waited for: 14 -> 15; matrix products, arithmetic and copies ran while one was open for 0% -> 0% of each run, Pallas kernels for 4% -> 6%
where the time goes in v2:
time: 87.5 us; the launch traced here: 87.3 us
  waiting for transfers between devices  40.7 us (47%)
  starting transfers between devices  34.7 us (40%)
  Pallas kernels  11 us (13%)
    ppermute x6, waiting for transfers between devices, shifted(): lax.ppermute(value, 'space', [(i, (i + step) % count) for i in range(coun...  17.9 us
    ppermute x9, starting transfers between devices, flipped(): lax.ppermute(value, 'tm', [(t, t ^ bit_on_core[t % 2]) for t in range(8)])  11.1 us
    pallas_call x7, Pallas kernels, kernel_call(): pl.pallas_call(body, out_shape=outputs, in_specs=in_specs, out_specs=jax....  11 us
    ppermute x6, starting transfers between devices, shifted(): lax.ppermute(value, 'space', [(i, (i + step) % count) for i in range(coun...  10.4 us
    ppermute x3, starting transfers between devices, plane_form(): upto = upto + lax.ppermute(total, 'tm', pairs).astype(jnp.float32)  7.71 us
    ppermute x9, waiting for transfers between devices, flipped(): lax.ppermute(value, 'tm', [(t, t ^ bit_on_core[t % 2]) for t in range(8)])  7.6 us
    ppermute x2, waiting for transfers between devices, plane_form(): lax.ppermute(share, 'space', pairs).astype(jnp.float32)  5.94 us
    ppermute x1, waiting for transfers between devices, plane_form(): below = lax.ppermute(top, 'space', backward)  4.12 us
  transfers between devices with their start and end apart: 22, of which 15 were waited for; matrix products, arithmetic and copies ran while one was open for 0% of the time, Pallas kernels for 6%

profile of v2, /device:TPU:0, one launch (start us, length us, event | category | flops | bytes accessed | tf_op | source)
XLA Modules:
  0.0 87.3 jit_solution(14527582554381270365)
XLA Ops:
  0.0 0.0 copy-start.3
  0.0 1.9 %shard_map.55 = (bf16[80,1152]{1,0:T(8,128)(2,1)}, bf16[2,64,1152]{2,1,0:T(8,128)(2,1)}) custom-call(bf16[288,3456]{1,0:T(8,128)(2,1)} %refs_1_.1, bf16[288,1152]{1,0:T(8,128)(2,1)} %refs_2_.3), custom_call_target="tpu_custom_call" | custom-call | bytes 958464 | tf_op jit(solution)/shard_map/pallas_call | solution.py:164
  2.0 3.1 %collective-permute-start = (bf16[1,80,1152]{2,1,0:T(8,128)(2,1)}, bf16[1,80,1152]{2,1,0:T(8,128)(2,1)S(1)}, u32[]{:S(2)}, u32[]{:S(2)}) collective-permute-start(bf16[1,80,1152]{2,1,0:T(8,128)(2,1)} %bitcast.8), channel_id=1, source_target_pairs={{0,1},{1,2},{2,3},{3,0},{4,5},{5,6},{6,7},{7,4},{8,9},{9,10},{10,1... | collective-permute-start | bytes 552968 | tf_op jit(solution)/shard_map/ppermute | solution.py:104
  5.0 2.1 %collective-permute-start.1 = (bf16[1,80,1152]{2,1,0:T(8,128)(2,1)}, bf16[1,80,1152]{2,1,0:T(8,128)(2,1)S(1)}, u32[]{:S(2)}, u32[]{:S(2)}) collective-permute-start(bf16[1,80,1152]{2,1,0:T(8,128)(2,1)} %bitcast.9), channel_id=1, source_target_pairs={{0,3},{1,0},{2,1},{3,2},{4,7},{5,4},{6,5},{7,6},{8,11},{9,8},{10,9... | collective-permute-start | bytes 552968 | tf_op jit(solution)/shard_map/ppermute | solution.py:104
  7.1 0.0 copy-done.3
  7.1 1.2 %shard_map.56.refs_0_ = bf16[256,1152]{1,0:T(8,128)(2,1)S(1)} custom-call(bf16[256,1152]{1,0:T(8,128)(2,1)S(1)} %bitcast.7), custom_call_target="tpu_custom_call" | custom-call | flops 679477248 | bytes 589824 | tf_op jit(solution)/shard_map/pallas_call | solution.py:164
  8.3 0.0 copy-start.5
  8.3 0.0 copy-start
  8.3 0.1 collective-permute-start.4
  8.4 4.4 %collective-permute-done = bf16[1,80,1152]{2,1,0:T(8,128)(2,1)S(1)} collective-permute-done((bf16[1,80,1152]{2,1,0:T(8,128)(2,1)}, bf16[1,80,1152]{2,1,0:T(8,128)(2,1)S(1)}, u32[]{:S(2)}, u32[]{:S(2)}) %collective-permute-start) | collective-permute-done | bytes 184352 | tf_op jit(solution)/shard_map/ppermute | solution.py:104
  12.8 2.5 %collective-permute-done.1 = bf16[1,80,1152]{2,1,0:T(8,128)(2,1)S(1)} collective-permute-done((bf16[1,80,1152]{2,1,0:T(8,128)(2,1)}, bf16[1,80,1152]{2,1,0:T(8,128)(2,1)S(1)}, u32[]{:S(2)}, u32[]{:S(2)}) %collective-permute-start.1) | collective-permute-done | bytes 184352 | tf_op jit(solution)/shard_map/ppermute | solution.py:104
  15.3 1.6 %collective-permute-start.2 = (bf16[2,80,1152]{2,1,0:T(8,128)(2,1)S(1)}, bf16[2,80,1152]{2,1,0:T(8,128)(2,1)S(1)}, u32[]{:S(2)}, u32[]{:S(2)}) collective-permute-start(bf16[2,80,1152]{2,1,0:T(8,128)(2,1)S(1)} %constant_dynamic-update-slice_fusion), channel_id=1, source_target_pairs={{0,8},{4,20},{8,0},{12,28},{16,24},{20,4},{24,16},{28,12},{1,9},{5... | collective-permute-start | bytes 1105928 | tf_op jit(solution)/shard_map/ppermute | solution.py:108
  16.9 1.1 %collective-permute-start.3 = (bf16[1,80,1152]{2,1,0:T(8,128)(2,1)S(1)}, bf16[1,80,1152]{2,1,0:T(8,128)(2,1)S(1)}, u32[]{:S(2)}, u32[]{:S(2)}) collective-permute-start(bf16[1,80,1152]{2,1,0:T(8,128)(2,1)S(1)} %collective-permute-done), channel_id=1, source_target_pairs={{0,1},{1,2},{2,3},{3,0},{4,5},{5,6},{6,7},{7,4},{8,9},{9,10},{10,1... | collective-permute-start | bytes 552968 | tf_op jit(solution)/shard_map/ppermute | solution.py:104
  18.0 6.4 %collective-permute-done.3 = bf16[1,80,1152]{2,1,0:T(8,128)(2,1)S(1)} collective-permute-done((bf16[1,80,1152]{2,1,0:T(8,128)(2,1)S(1)}, bf16[1,80,1152]{2,1,0:T(8,128)(2,1)S(1)}, u32[]{:S(2)}, u32[]{:S(2)}) %collective-permute-start.3) | collective-permute-done | bytes 184352 | tf_op jit(solution)/shard_map/ppermute | solution.py:104
  24.4 0.0 collective-permute-done.2
  24.4 0.0 collective-permute-done.4.refs_1_
  24.5 1.4 %collective-permute-start.12 = (bf16[5,80,1152]{2,1,0:T(8,128)(2,1)S(1)}, bf16[5,80,1152]{2,1,0:T(8,128)(2,1)S(1)}, u32[]{:S(2)}, u32[]{:S(2)}) collective-permute-start(bf16[5,80,1152]{2,1,0:T(8,128)(2,1)S(1)} %constant_dynamic-update-slice_fusion.2.refs_3_), channel_id=1, source_target_pairs={{0,16},{4,12},{8,24},{12,4},{16,0},{20,28},{24,8},{28,20},{1,17},{... | collective-permute-start | bytes 2764808 | tf_op jit(solution)/shard_map/ppermute | solution.py:108
  25.9 0.0 copy-done.5
  25.9 0.0 collective-permute-start.5
  25.9 1.3 %collective-permute-start.6 = (bf16[1,80,1152]{2,1,0:T(8,128)(2,1)S(1)}, bf16[1,80,1152]{2,1,0:T(8,128)(2,1)S(1)}, u32[]{:S(2)}, u32[]{:S(2)}) collective-permute-start(bf16[1,80,1152]{2,1,0:T(8,128)(2,1)S(1)} %collective-permute-done.3), channel_id=1, source_target_pairs={{0,8},{4,20},{8,0},{12,28},{16,24},{20,4},{24,16},{28,12},{1,9},{5... | collective-permute-start | bytes 552968 | tf_op jit(solution)/shard_map/ppermute | solution.py:108
  27.2 0.8 collective-permute-start.7
  28.1 3.8 %collective-permute-start.9 = (bf16[2,64,1152]{2,1,0:T(8,128)(2,1)S(1)}, bf16[2,64,1152]{2,1,0:T(8,128)(2,1)S(1)}, u32[]{:S(2)}, u32[]{:S(2)}) collective-permute-start(bf16[2,64,1152]{2,1,0:T(8,128)(2,1)S(1)} %copy-done.5), channel_id=1, source_target_pairs={{0,3},{1,0},{2,1},{3,2},{4,7},{5,4},{6,5},{7,6},{8,11},{9,8},{10,9... | collective-permute-start | bytes 884744 | tf_op jit(solution)/shard_map/ppermute | solution.py:104
  31.9 1.6 %collective-permute-done.6.refs_5_ = bf16[1,80,1152]{2,1,0:T(8,128)(2,1)S(1)} collective-permute-done((bf16[1,80,1152]{2,1,0:T(8,128)(2,1)S(1)}, bf16[1,80,1152]{2,1,0:T(8,128)(2,1)S(1)}, u32[]{:S(2)}, u32[]{:S(2)}) %collective-permute-start.6) | collective-permute-done | bytes 184352 | tf_op jit(solution)/shard_map/ppermute | solution.py:108
  33.5 4.0 %collective-permute-done.7.refs_6_ = bf16[1,80,1152]{2,1,0:T(8,128)(2,1)S(1)} collective-permute-done((bf16[1,80,1152]{2,1,0:T(8,128)(2,1)S(1)}, bf16[1,80,1152]{2,1,0:T(8,128)(2,1)S(1)}, u32[]{:S(2)}, u32[]{:S(2)}) %collective-permute-start.7) | collective-permute-done | bytes 184352 | tf_op jit(solution)/shard_map/ppermute | solution.py:108
  37.6 0.1 collective-permute-done.5
  37.7 0.3 collective-permute-start.8
  37.9 3.8 %collective-permute-done.9 = bf16[2,64,1152]{2,1,0:T(8,128)(2,1)S(1)} collective-permute-done((bf16[2,64,1152]{2,1,0:T(8,128)(2,1)S(1)}, bf16[2,64,1152]{2,1,0:T(8,128)(2,1)S(1)}, u32[]{:S(2)}, u32[]{:S(2)}) %collective-permute-start.9) | collective-permute-done | bytes 294944 | tf_op jit(solution)/shard_map/ppermute | solution.py:104
  41.8 1.9 %collective-permute-done.12.refs_4_ = bf16[5,80,1152]{2,1,0:T(8,128)(2,1)S(1)} collective-permute-done((bf16[5,80,1152]{2,1,0:T(8,128)(2,1)S(1)}, bf16[5,80,1152]{2,1,0:T(8,128)(2,1)S(1)}, u32[]{:S(2)}, u32[]{:S(2)}) %collective-permute-start.12) | collective-permute-done | bytes 921632 | tf_op jit(solution)/shard_map/ppermute | solution.py:108
  43.7 0.0 copy-done
  43.7 2.2 %shard_map.57.mine_ref.refs_5_ = bf16[608,1152]{1,0:T(8,128)(2,1)S(1)} custom-call(bf16[256,1152]{1,0:T(8,128)(2,1)S(1)} %shard_map.56.refs_0_, bf16[256,1152]{1,0:T(8,128)(2,1)S(1)} %collective-permute-done.4.refs_1_, bf16[288,3456]{1,0:T(8,128)(2,1)S(1)} %copy-done, bf16[5,80,1152]{2,1,0:T(8,128)(2,1)S(1)} %constant_dynamic-update-slice_fusion.2.refs_3_, ...), custom_call_target="tpu_custom_call" | custom-call | flops 1358954496 | bytes 2654208 | tf_op jit(solution)/shard_map/pallas_call | solution.py:164
  45.9 0.7 collective-permute-done.8
  46.6 2.6 %collective-permute-start.13 = (bf16[608,1152]{1,0:T(8,128)(2,1)S(1)}, bf16[608,1152]{1,0:T(8,128)(2,1)S(1)}, u32[]{:S(2)}, u32[]{:S(2)}) collective-permute-start(bf16[608,1152]{1,0:T(8,128)(2,1)S(1)} %shard_map.57.mine_ref.refs_5_), channel_id=1, source_target_pairs={{0,4},{4,0},{8,12},{12,8},{16,20},{20,16},{24,28},{28,24},{1,5},{5... | collective-permute-start | bytes 4202504 | tf_op jit(solution)/shard_map/ppermute | solution.py:108
  49.2 0.1 pad_maximum_fusion
  49.3 1.5 %collective-permute-start.10 = (bf16[3,64,1152]{2,1,0:T(8,128)(2,1)S(1)}, bf16[3,64,1152]{2,1,0:T(8,128)(2,1)S(1)}, u32[]{:S(2)}, u32[]{:S(2)}) collective-permute-start(bf16[3,64,1152]{2,1,0:T(8,128)(2,1)S(1)} %pad_maximum_fusion), channel_id=1, source_target_pairs={{0,8},{4,20},{8,0},{12,28},{16,24},{20,4},{24,16},{28,12},{1,9},{5... | collective-permute-start | bytes 1327112 | tf_op jit(solution)/shard_map/ppermute | solution.py:108
  50.8 1.7 %collective-permute-start.11 = (bf16[3,64,1152]{2,1,0:T(8,128)(2,1)S(1)}, bf16[3,64,1152]{2,1,0:T(8,128)(2,1)S(1)}, u32[]{:S(2)}, u32[]{:S(2)}) collective-permute-start(bf16[3,64,1152]{2,1,0:T(8,128)(2,1)S(1)} %pad_maximum_fusion), channel_id=1, source_target_pairs={{0,16},{4,12},{8,24},{12,4},{16,0},{20,28},{24,8},{28,20},{1,17},{... | collective-permute-start | bytes 1327112 | tf_op jit(solution)/shard_map/ppermute | solution.py:108
  52.6 0.0 collective-permute-done.13.other_ref.refs_6_
  52.6 0.9 %shard_map.58 = (bf16[256,1152]{1,0:T(8,128)(2,1)S(1)}, bf16[1,64,1152]{2,1,0:T(8,128)(2,1)S(1)}, bf16[1,64,1152]{2,1,0:T(8,128)(2,1)S(1)}, f32[9,32,128]{2,1,0:T(8,128)S(1)}, bf16[9,32,128]{2,1,0:T(8,128)(2,1)S(1)}) custom-call(bf16[608,1152]{1,0:T(8,128)(2,1)S(1)} %shard_map.57.mine_ref.refs_5_, bf16[608,1152]{1,0:T(8,128)(2,1)S(1)} %collective-permute-done.13.other_ref.refs_6_), custom_call_target="tpu_custom_call" | custom-call | flops 150994944 | bytes 2359296 | tf_op jit(solution)/shard_map/pallas_call | solution.py:164
  53.4 4.0 %collective-permute-start.16 = (bf16[9,32,128]{2,1,0:T(8,128)(2,1)S(1)}, bf16[9,32,128]{2,1,0:T(8,128)(2,1)S(1)}, u32[]{:S(2)}, u32[]{:S(2)}) collective-permute-start(bf16[9,32,128]{2,1,0:T(8,128)(2,1)S(1)} %get-tuple-element.46), channel_id=1, source_target_pairs={{0,24},{4,28},{8,16},{12,20},{1,25},{5,29},{9,17},{13,21},{2,26},{... | collective-permute-start | bytes 221192 | tf_op jit(solution)/shard_map/ppermute | solution.py:526
  57.4 1.3 %collective-permute-start.15 = (bf16[9,32,128]{2,1,0:T(8,128)(2,1)S(1)}, bf16[9,32,128]{2,1,0:T(8,128)(2,1)S(1)}, u32[]{:S(2)}, u32[]{:S(2)}) collective-permute-start(bf16[9,32,128]{2,1,0:T(8,128)(2,1)S(1)} %get-tuple-element.46), channel_id=1, source_target_pairs={{0,16},{4,20},{8,24},{12,28},{1,17},{5,21},{9,25},{13,29},{2,18},{... | collective-permute-start | bytes 221192 | tf_op jit(solution)/shard_map/ppermute | solution.py:526
  58.7 2.5 %collective-permute-start.14 = (bf16[9,32,128]{2,1,0:T(8,128)(2,1)S(1)}, bf16[9,32,128]{2,1,0:T(8,128)(2,1)S(1)}, u32[]{:S(2)}, u32[]{:S(2)}) collective-permute-start(bf16[9,32,128]{2,1,0:T(8,128)(2,1)S(1)} %get-tuple-element.46), channel_id=1, source_target_pairs={{0,8},{4,12},{16,24},{20,28},{1,9},{5,13},{17,25},{21,29},{2,10},{... | collective-permute-start | bytes 221192 | tf_op jit(solution)/shard_map/ppermute | solution.py:526
  61.2 1.4 %collective-permute-done.16 = bf16[9,32,128]{2,1,0:T(8,128)(2,1)S(1)} collective-permute-done((bf16[9,32,128]{2,1,0:T(8,128)(2,1)S(1)}, bf16[9,32,128]{2,1,0:T(8,128)(2,1)S(1)}, u32[]{:S(2)}, u32[]{:S(2)}) %collective-permute-start.16) | collective-permute-done | bytes 73760 | tf_op jit(solution)/shard_map/ppermute | solution.py:526
  62.6 1.1 %collective-permute-done.15 = bf16[9,32,128]{2,1,0:T(8,128)(2,1)S(1)} collective-permute-done((bf16[9,32,128]{2,1,0:T(8,128)(2,1)S(1)}, bf16[9,32,128]{2,1,0:T(8,128)(2,1)S(1)}, u32[]{:S(2)}, u32[]{:S(2)}) %collective-permute-start.15) | collective-permute-done | bytes 73760 | tf_op jit(solution)/shard_map/ppermute | solution.py:526
  63.7 0.5 collective-permute-done.14
  64.2 0.0 collective-permute-done.10
  64.2 0.0 collective-permute-done.11
  64.2 0.1 collective-permute-start.17
  64.3 3.9 %collective-permute-start.18 = (bf16[1,64,1152]{2,1,0:T(8,128)(2,1)S(1)}, bf16[1,64,1152]{2,1,0:T(8,128)(2,1)S(1)}, u32[]{:S(2)}, u32[]{:S(2)}) collective-permute-start(bf16[1,64,1152]{2,1,0:T(8,128)(2,1)S(1)} %get-tuple-element.50), channel_id=1, source_target_pairs={{0,1},{1,2},{2,3},{4,5},{5,6},{6,7},{8,9},{9,10},{10,11},{12,13},{... | collective-permute-start | bytes 442376 | tf_op jit(solution)/shard_map/ppermute | solution.py:531
  68.2 1.3 %collective-permute-start.19 = (bf16[1,64,1152]{2,1,0:T(8,128)(2,1)S(1)}, bf16[1,64,1152]{2,1,0:T(8,128)(2,1)S(1)}, u32[]{:S(2)}, u32[]{:S(2)}) collective-permute-start(bf16[1,64,1152]{2,1,0:T(8,128)(2,1)S(1)} %get-tuple-element.51), channel_id=1, source_target_pairs={{1,0},{2,1},{3,2},{5,4},{6,5},{7,6},{9,8},{10,9},{11,10},{13,12},{... | collective-permute-start | bytes 442376 | tf_op jit(solution)/shard_map/ppermute | solution.py:532
  69.5 0.0 collective-permute-done.17
  69.6 0.0 copy-start.4
  69.6 0.0 copy-start.2
  69.6 2.1 %collective-permute-done.18.above_ref = bf16[1,64,1152]{2,1,0:T(8,128)(2,1)S(1)} collective-permute-done((bf16[1,64,1152]{2,1,0:T(8,128)(2,1)S(1)}, bf16[1,64,1152]{2,1,0:T(8,128)(2,1)S(1)}, u32[]{:S(2)}, u32[]{:S(2)}) %collective-permute-start.18) | collective-permute-done | bytes 147488 | tf_op jit(solution)/shard_map/ppermute | solution.py:531
  71.7 4.1 %collective-permute-done.19.below_ref = bf16[1,64,1152]{2,1,0:T(8,128)(2,1)S(1)} collective-permute-done((bf16[1,64,1152]{2,1,0:T(8,128)(2,1)S(1)}, bf16[1,64,1152]{2,1,0:T(8,128)(2,1)S(1)}, u32[]{:S(2)}, u32[]{:S(2)}) %collective-permute-start.19) | collective-permute-done | bytes 147488 | tf_op jit(solution)/shard_map/ppermute | solution.py:532
  76.0 0.0 copy-start.1
  76.1 0.1 collective-permute-start.20
  76.1 0.3 collective-permute-start.21
  76.4 0.0 copy-done.4
  76.4 0.0 copy-done.2
  76.4 0.9 %shard_map.60 = f32[4,64,1152]{2,1,0:T(8,128)S(1)} custom-call(bf16[4,64,1152]{2,1,0:T(8,128)(2,1)S(1)} %bitcast.6, bf16[1,64,1152]{2,1,0:T(8,128)(2,1)S(1)} %collective-permute-done.18.above_ref, bf16[1,64,1152]{2,1,0:T(8,128)(2,1)S(1)} %collective-permute-done.19.below_ref, f32[3,3,1152]{2,1,0:T(4,128)S(1)} %copy-done.2), custom_call_target="tpu_custom_call" | custom-call | flops 5308416 | bytes 1769472 | tf_op jit(solution)/shard_map/pallas_call | solution.py:164
  77.4 5.9 %collective-permute-done.21 = bf16[9,32,128]{2,1,0:T(8,128)(2,1)S(1)} collective-permute-done((bf16[9,32,128]{2,1,0:T(8,128)(2,1)S(1)}, bf16[9,32,128]{2,1,0:T(8,128)(2,1)S(1)}, u32[]{:S(2)}, u32[]{:S(2)}) %collective-permute-start.21) | collective-permute-done | bytes 73760 | tf_op jit(solution)/shard_map/ppermute | solution.py:539
  83.3 0.0 collective-permute-done.20.refs_4_
  83.3 0.0 copy-done.1
  83.3 1.6 %shard_map.59 = (bf16[256,1152]{1,0:T(8,128)(2,1)S(1)}, bf16[1152,1152]{1,0:T(8,128)(2,1)S(1)}) custom-call(bf16[256,1152]{1,0:T(8,128)(2,1)S(1)} %shard_map.56.refs_0_, bf16[288,3456]{1,0:T(8,128)(2,1)S(1)} %copy-done, bf16[288,1152]{1,0:T(8,128)(2,1)S(1)} %copy-done.1, bf16[12,64,1152]{2,1,0:T(8,128)(2,1)S(1)} %constant_dynamic-update-slice_fusion.5.refs_3_, ...), custom_call_target="tpu_custom_call" | custom-call | flops 679477248 | bytes 5308416 | tf_op jit(solution)/shard_map/pallas_call | solution.py:164
  84.9 2.3 %shard_map.61 = bf16[256,1152]{1,0:T(8,128)(2,1)} custom-call(bf16[256,1152]{1,0:T(8,128)(2,1)S(1)} %get-tuple-element.58.queries_ref, bf16[1152,1152]{1,0:T(8,128)(2,1)S(1)} %get-tuple-element.59.weight_ref, f32[9,32,128]{2,1,0:T(8,128)S(1)} %convert_add_fusion.state_ref, f32[256,1152]{1,0:T(8,128)S(1)} %bitcast.5, f32[1,1152]{1,0:T(1,128)S(1)} %broadcast_in_dim.7.gain_ref), custom_call_target="tpu_custom_call" | custom-call | flops 679477248 | bytes 2654208 | tf_op jit(solution)/shard_map/pallas_call | solution.py:164
  (17 shorter events, 0.4 us)
Async XLA Ops:
  0.0 7.1 %copy-start.3 = (bf16[1,4,64,1152]{3,2,1,0:T(8,128)(2,1)S(1)}, bf16[1,4,64,1152]{3,2,1,0:T(8,128)(2,1)}, u32[]{:S(2)}) copy-start(bf16[1,4,64,1152]{3,2,1,0:T(8,128)(2,1)} %param.5) | copy-start | bytes 1769476
  2.0 10.8 %collective-permute-start = (bf16[1,80,1152]{2,1,0:T(8,128)(2,1)}, bf16[1,80,1152]{2,1,0:T(8,128)(2,1)S(1)}, u32[]{:S(2)}, u32[]{:S(2)}) collective-permute-start(bf16[1,80,1152]{2,1,0:T(8,128)(2,1)} %bitcast.8), channel_id=1, source_target_pairs={{0,1},{1,2},{2,3},{3,0},{4,5},{5,6},{6,7},{7,4},{8,9},{9,10},{10,1... | collective-permute-start | bytes 552968 | tf_op jit(solution)/shard_map/ppermute | solution.py:104
  5.0 10.3 %collective-permute-start.1 = (bf16[1,80,1152]{2,1,0:T(8,128)(2,1)}, bf16[1,80,1152]{2,1,0:T(8,128)(2,1)S(1)}, u32[]{:S(2)}, u32[]{:S(2)}) collective-permute-start(bf16[1,80,1152]{2,1,0:T(8,128)(2,1)} %bitcast.9), channel_id=1, source_target_pairs={{0,3},{1,0},{2,1},{3,2},{4,7},{5,4},{6,5},{7,6},{8,11},{9,8},{10,9... | collective-permute-start | bytes 552968 | tf_op jit(solution)/shard_map/ppermute | solution.py:104
  8.3 17.6 %copy-start.5 = (bf16[2,64,1152]{2,1,0:T(8,128)(2,1)S(1)}, bf16[2,64,1152]{2,1,0:T(8,128)(2,1)}, u32[]{:S(2)}) copy-start(bf16[2,64,1152]{2,1,0:T(8,128)(2,1)} %get-tuple-element.41) | copy-start | bytes 884740
  8.3 35.4 %copy-start = (bf16[288,3456]{1,0:T(8,128)(2,1)S(1)}, bf16[288,3456]{1,0:T(8,128)(2,1)}, u32[]{:S(2)}) copy-start(bf16[288,3456]{1,0:T(8,128)(2,1)} %refs_1_.1) | copy-start | bytes 5971972
  8.3 16.1 %collective-permute-start.4 = (bf16[256,1152]{1,0:T(8,128)(2,1)S(1)}, bf16[256,1152]{1,0:T(8,128)(2,1)S(1)}, u32[]{:S(2)}, u32[]{:S(2)}) collective-permute-start(bf16[256,1152]{1,0:T(8,128)(2,1)S(1)} %shard_map.56.refs_0_), channel_id=1, source_target_pairs={{0,4},{4,0},{8,12},{12,8},{16,20},{20,16},{24,28},{28,24},{1,5},{5... | collective-permute-start | bytes 1769480 | tf_op jit(solution)/shard_map/ppermute | solution.py:108
  15.3 9.0 %collective-permute-start.2 = (bf16[2,80,1152]{2,1,0:T(8,128)(2,1)S(1)}, bf16[2,80,1152]{2,1,0:T(8,128)(2,1)S(1)}, u32[]{:S(2)}, u32[]{:S(2)}) collective-permute-start(bf16[2,80,1152]{2,1,0:T(8,128)(2,1)S(1)} %constant_dynamic-update-slice_fusion), channel_id=1, source_target_pairs={{0,8},{4,20},{8,0},{12,28},{16,24},{20,4},{24,16},{28,12},{1,9},{5... | collective-permute-start | bytes 1105928 | tf_op jit(solution)/shard_map/ppermute | solution.py:108
  16.9 7.5 %collective-permute-start.3 = (bf16[1,80,1152]{2,1,0:T(8,128)(2,1)S(1)}, bf16[1,80,1152]{2,1,0:T(8,128)(2,1)S(1)}, u32[]{:S(2)}, u32[]{:S(2)}) collective-permute-start(bf16[1,80,1152]{2,1,0:T(8,128)(2,1)S(1)} %collective-permute-done), channel_id=1, source_target_pairs={{0,1},{1,2},{2,3},{3,0},{4,5},{5,6},{6,7},{7,4},{8,9},{9,10},{10,1... | collective-permute-start | bytes 552968 | tf_op jit(solution)/shard_map/ppermute | solution.py:104
  24.5 19.2 %collective-permute-start.12 = (bf16[5,80,1152]{2,1,0:T(8,128)(2,1)S(1)}, bf16[5,80,1152]{2,1,0:T(8,128)(2,1)S(1)}, u32[]{:S(2)}, u32[]{:S(2)}) collective-permute-start(bf16[5,80,1152]{2,1,0:T(8,128)(2,1)S(1)} %constant_dynamic-update-slice_fusion.2.refs_3_), channel_id=1, source_target_pairs={{0,16},{4,12},{8,24},{12,4},{16,0},{20,28},{24,8},{28,20},{1,17},{... | collective-permute-start | bytes 2764808 | tf_op jit(solution)/shard_map/ppermute | solution.py:108
  25.9 11.7 %collective-permute-start.5 = (bf16[2,64,1152]{2,1,0:T(8,128)(2,1)S(1)}, bf16[2,64,1152]{2,1,0:T(8,128)(2,1)S(1)}, u32[]{:S(2)}, u32[]{:S(2)}) collective-permute-start(bf16[2,64,1152]{2,1,0:T(8,128)(2,1)S(1)} %copy-done.5), channel_id=1, source_target_pairs={{0,1},{1,2},{2,3},{3,0},{4,5},{5,6},{6,7},{7,4},{8,9},{9,10},{10,1... | collective-permute-start | bytes 884744 | tf_op jit(solution)/shard_map/ppermute | solution.py:104
  25.9 7.6 %collective-permute-start.6 = (bf16[1,80,1152]{2,1,0:T(8,128)(2,1)S(1)}, bf16[1,80,1152]{2,1,0:T(8,128)(2,1)S(1)}, u32[]{:S(2)}, u32[]{:S(2)}) collective-permute-start(bf16[1,80,1152]{2,1,0:T(8,128)(2,1)S(1)} %collective-permute-done.3), channel_id=1, source_target_pairs={{0,8},{4,20},{8,0},{12,28},{16,24},{20,4},{24,16},{28,12},{1,9},{5... | collective-permute-start | bytes 552968 | tf_op jit(solution)/shard_map/ppermute | solution.py:108
  27.2 10.3 %collective-permute-start.7 = (bf16[1,80,1152]{2,1,0:T(8,128)(2,1)S(1)}, bf16[1,80,1152]{2,1,0:T(8,128)(2,1)S(1)}, u32[]{:S(2)}, u32[]{:S(2)}) collective-permute-start(bf16[1,80,1152]{2,1,0:T(8,128)(2,1)S(1)} %collective-permute-done.3), channel_id=1, source_target_pairs={{0,24},{4,28},{8,16},{12,20},{16,8},{20,12},{24,0},{28,4},{1,25},{... | collective-permute-start | bytes 552968 | tf_op jit(solution)/shard_map/ppermute | solution.py:108
  28.1 13.7 %collective-permute-start.9 = (bf16[2,64,1152]{2,1,0:T(8,128)(2,1)S(1)}, bf16[2,64,1152]{2,1,0:T(8,128)(2,1)S(1)}, u32[]{:S(2)}, u32[]{:S(2)}) collective-permute-start(bf16[2,64,1152]{2,1,0:T(8,128)(2,1)S(1)} %copy-done.5), channel_id=1, source_target_pairs={{0,3},{1,0},{2,1},{3,2},{4,7},{5,4},{6,5},{7,6},{8,11},{9,8},{10,9... | collective-permute-start | bytes 884744 | tf_op jit(solution)/shard_map/ppermute | solution.py:104
  37.7 8.9 %collective-permute-start.8 = (bf16[2,64,1152]{2,1,0:T(8,128)(2,1)S(1)}, bf16[2,64,1152]{2,1,0:T(8,128)(2,1)S(1)}, u32[]{:S(2)}, u32[]{:S(2)}) collective-permute-start(bf16[2,64,1152]{2,1,0:T(8,128)(2,1)S(1)} %collective-permute-done.5), channel_id=1, source_target_pairs={{0,1},{1,2},{2,3},{3,0},{4,5},{5,6},{6,7},{7,4},{8,9},{9,10},{10,1... | collective-permute-start | bytes 884744 | tf_op jit(solution)/shard_map/ppermute | solution.py:104
  46.6 6.0 %collective-permute-start.13 = (bf16[608,1152]{1,0:T(8,128)(2,1)S(1)}, bf16[608,1152]{1,0:T(8,128)(2,1)S(1)}, u32[]{:S(2)}, u32[]{:S(2)}) collective-permute-start(bf16[608,1152]{1,0:T(8,128)(2,1)S(1)} %shard_map.57.mine_ref.refs_5_), channel_id=1, source_target_pairs={{0,4},{4,0},{8,12},{12,8},{16,20},{20,16},{24,28},{28,24},{1,5},{5... | collective-permute-start | bytes 4202504 | tf_op jit(solution)/shard_map/ppermute | solution.py:108
  49.3 14.9 %collective-permute-start.10 = (bf16[3,64,1152]{2,1,0:T(8,128)(2,1)S(1)}, bf16[3,64,1152]{2,1,0:T(8,128)(2,1)S(1)}, u32[]{:S(2)}, u32[]{:S(2)}) collective-permute-start(bf16[3,64,1152]{2,1,0:T(8,128)(2,1)S(1)} %pad_maximum_fusion), channel_id=1, source_target_pairs={{0,8},{4,20},{8,0},{12,28},{16,24},{20,4},{24,16},{28,12},{1,9},{5... | collective-permute-start | bytes 1327112 | tf_op jit(solution)/shard_map/ppermute | solution.py:108
  50.8 13.4 %collective-permute-start.11 = (bf16[3,64,1152]{2,1,0:T(8,128)(2,1)S(1)}, bf16[3,64,1152]{2,1,0:T(8,128)(2,1)S(1)}, u32[]{:S(2)}, u32[]{:S(2)}) collective-permute-start(bf16[3,64,1152]{2,1,0:T(8,128)(2,1)S(1)} %pad_maximum_fusion), channel_id=1, source_target_pairs={{0,16},{4,12},{8,24},{12,4},{16,0},{20,28},{24,8},{28,20},{1,17},{... | collective-permute-start | bytes 1327112 | tf_op jit(solution)/shard_map/ppermute | solution.py:108
  53.4 9.2 %collective-permute-start.16 = (bf16[9,32,128]{2,1,0:T(8,128)(2,1)S(1)}, bf16[9,32,128]{2,1,0:T(8,128)(2,1)S(1)}, u32[]{:S(2)}, u32[]{:S(2)}) collective-permute-start(bf16[9,32,128]{2,1,0:T(8,128)(2,1)S(1)} %get-tuple-element.46), channel_id=1, source_target_pairs={{0,24},{4,28},{8,16},{12,20},{1,25},{5,29},{9,17},{13,21},{2,26},{... | collective-permute-start | bytes 221192 | tf_op jit(solution)/shard_map/ppermute | solution.py:526
  57.4 6.3 %collective-permute-start.15 = (bf16[9,32,128]{2,1,0:T(8,128)(2,1)S(1)}, bf16[9,32,128]{2,1,0:T(8,128)(2,1)S(1)}, u32[]{:S(2)}, u32[]{:S(2)}) collective-permute-start(bf16[9,32,128]{2,1,0:T(8,128)(2,1)S(1)} %get-tuple-element.46), channel_id=1, source_target_pairs={{0,16},{4,20},{8,24},{12,28},{1,17},{5,21},{9,25},{13,29},{2,18},{... | collective-permute-start | bytes 221192 | tf_op jit(solution)/shard_map/ppermute | solution.py:526
  58.7 5.5 %collective-permute-start.14 = (bf16[9,32,128]{2,1,0:T(8,128)(2,1)S(1)}, bf16[9,32,128]{2,1,0:T(8,128)(2,1)S(1)}, u32[]{:S(2)}, u32[]{:S(2)}) collective-permute-start(bf16[9,32,128]{2,1,0:T(8,128)(2,1)S(1)} %get-tuple-element.46), channel_id=1, source_target_pairs={{0,8},{4,12},{16,24},{20,28},{1,9},{5,13},{17,25},{21,29},{2,10},{... | collective-permute-start | bytes 221192 | tf_op jit(solution)/shard_map/ppermute | solution.py:526
  64.2 5.3 %collective-permute-start.17 = (bf16[9,32,128]{2,1,0:T(8,128)(2,1)S(1)}, bf16[9,32,128]{2,1,0:T(8,128)(2,1)S(1)}, u32[]{:S(2)}, u32[]{:S(2)}) collective-permute-start(bf16[9,32,128]{2,1,0:T(8,128)(2,1)S(1)} %convert_add_fusion.1), channel_id=1, source_target_pairs={{0,1},{1,0},{2,3},{3,2},{4,5},{5,4},{6,7},{7,6},{8,9},{9,8},{10,11... | collective-permute-start | bytes 221192 | tf_op jit(solution)/shard_map/ppermute | solution.py:539
  64.3 7.4 %collective-permute-start.18 = (bf16[1,64,1152]{2,1,0:T(8,128)(2,1)S(1)}, bf16[1,64,1152]{2,1,0:T(8,128)(2,1)S(1)}, u32[]{:S(2)}, u32[]{:S(2)}) collective-permute-start(bf16[1,64,1152]{2,1,0:T(8,128)(2,1)S(1)} %get-tuple-element.50), channel_id=1, source_target_pairs={{0,1},{1,2},{2,3},{4,5},{5,6},{6,7},{8,9},{9,10},{10,11},{12,13},{... | collective-permute-start | bytes 442376 | tf_op jit(solution)/shard_map/ppermute | solution.py:531
  68.2 7.6 %collective-permute-start.19 = (bf16[1,64,1152]{2,1,0:T(8,128)(2,1)S(1)}, bf16[1,64,1152]{2,1,0:T(8,128)(2,1)S(1)}, u32[]{:S(2)}, u32[]{:S(2)}) collective-permute-start(bf16[1,64,1152]{2,1,0:T(8,128)(2,1)S(1)} %get-tuple-element.51), channel_id=1, source_target_pairs={{1,0},{2,1},{3,2},{5,4},{6,5},{7,6},{9,8},{10,9},{11,10},{13,12},{... | collective-permute-start | bytes 442376 | tf_op jit(solution)/shard_map/ppermute | solution.py:532
  69.6 6.8 %copy-start.4 = (f32[1152]{0:T(1024)S(1)}, f32[1152]{0:T(1024)}, u32[]{:S(2)}) copy-start(f32[1152]{0:T(1024)} %param.9) | copy-start | bytes 13828
  69.6 6.8 %copy-start.2 = (f32[3,3,1152]{2,1,0:T(4,128)S(1)}, f32[3,3,1152]{2,1,0:T(4,128)}, u32[]{:S(2)}) copy-start(f32[3,3,1152]{2,1,0:T(4,128)} %conv_ref.1) | copy-start | bytes 124420
  76.0 7.3 %copy-start.1 = (bf16[288,1152]{1,0:T(8,128)(2,1)S(1)}, bf16[288,1152]{1,0:T(8,128)(2,1)}, u32[]{:S(2)}) copy-start(bf16[288,1152]{1,0:T(8,128)(2,1)} %refs_2_.3) | copy-start | bytes 1990660
  76.1 7.3 %collective-permute-start.20 = (bf16[12,64,1152]{2,1,0:T(8,128)(2,1)S(1)}, bf16[12,64,1152]{2,1,0:T(8,128)(2,1)S(1)}, u32[]{:S(2)}, u32[]{:S(2)}) collective-permute-start(bf16[12,64,1152]{2,1,0:T(8,128)(2,1)S(1)} %constant_dynamic-update-slice_fusion.5.refs_3_), channel_id=1, source_target_pairs={{0,4},{4,0},{8,12},{12,8},{16,20},{20,16},{24,28},{28,24},{1,5},{5... | collective-permute-start | bytes 5308424 | tf_op jit(solution)/shard_map/ppermute | solution.py:108
  76.1 7.2 %collective-permute-start.21 = (bf16[9,32,128]{2,1,0:T(8,128)(2,1)S(1)}, bf16[9,32,128]{2,1,0:T(8,128)(2,1)S(1)}, u32[]{:S(2)}, u32[]{:S(2)}) collective-permute-start(bf16[9,32,128]{2,1,0:T(8,128)(2,1)S(1)} %add_convert_fusion), channel_id=1, source_target_pairs={{0,2},{1,3},{2,0},{3,1},{4,6},{5,7},{6,4},{7,5},{8,10},{9,11},{10,... | collective-permute-start | bytes 221192 | tf_op jit(solution)/shard_map/ppermute | solution.py:539

commit v3 on v2

--- a/solution.py
+++ b/solution.py
@@ -259,10 +259,10 @@
 def first_kernel(*refs):
     tokens_ref, other_ref, qkv_ref, near_ref, away_ref, first_ref, far_ref, mine_ref = refs
     slots = (
-        ((near_ref, 0), (near_ref, 4), (near_ref, 1)),
-        ((near_ref, 2), (first_ref, 0), (near_ref, 3)),
-        ((away_ref, 0), (away_ref, 4), (away_ref, 1)),
-        ((away_ref, 2), (far_ref, 0), (away_ref, 3)),
+        ((near_ref, 0), (first_ref, 0), (near_ref, 1)),
+        ((near_ref, 2), (first_ref, 1), (near_ref, 3)),
+        ((away_ref, 0), (far_ref, 0), (away_ref, 1)),
+        ((away_ref, 2), (far_ref, 1), (away_ref, 3)),
     )
     _, x, core = coordinates()
     count, depth = tokens_ref.shape
@@ -396,8 +396,7 @@
 
 
 def query_kernel(*refs):
-    tokens_ref, qkv_ref, out_ref, mine_ref, theirs_ref, ours_ref, other_ref, *results = refs
-    query_ref, weight_ref = results
+    tokens_ref, qkv_ref, out_ref, *packs, ours_ref, other_ref, query_ref, weight_ref = refs
     y, x, core = coordinates()
     depth = tokens_ref.shape[1]
     rows = qkv_ref.shape[0]
@@ -406,8 +405,11 @@
     places = chip_places(y, x)
     width = 3 * LANES
 
-    def block(of_core, k, lanes):
+    def block(of_core, index, lanes):
+        pack, k = index
+        mine_ref, theirs_ref = packs[2 * pack], packs[2 * pack + 1]
         return jnp.where(core == of_core, mine_ref[k, :, lanes], theirs_ref[k, :, lanes])
+
 
     def rest(of_core, lanes):
         return jnp.where(core == of_core, ours_ref[rest_at:, lanes], other_ref[rest_at:, lanes])
@@ -417,8 +419,8 @@
 
     for at in range(0, depth, width):
         lanes = slice(at, at + width)
-        order = [2 * k for k in range(steps)] + [2 * steps + k for k in range(2 * steps)]
-        order += [2 * k + 1 for k in range(steps)]
+        order = [(0, 2 * k) for k in range(steps)] + [(1, k) for k in range(2 * steps)]
+        order += [(0, 2 * k + 1) for k in range(steps)]
         columns = [qkv_ref[:, lanes]] + [block(0, k, lanes) for k in order] + [rest(0, lanes)]
         queries = jnp.dot(
             tokens_ref[...], jnp.concatenate(columns, axis=0), preferred_element_type=jnp.float32
@@ -429,7 +431,7 @@
         tiles = rest(1, lanes)
         for k, step in enumerate(STEPS):
             base = source_plane(step) * rows
-            held = (2 * k, 3 * steps + k, 2 * steps + k, 2 * k + 1)
+            held = ((0, 2 * k), (1, steps + k), (1, k), (0, 2 * k + 1))
             for place, index in zip(places, held):
                 put(base + place * MAIN, block(1, index, lanes), lanes)
             for run, tile in enumerate((y, 1 - y)):
@@ -437,9 +439,9 @@
                 put(base + 4 * MAIN + tile * REST, tiles[start : start + REST], lanes)
 
 
-def query_call(tokens, qkv_weight, out_weight, mine, theirs, ours, other):
+def query_call(tokens, qkv_weight, out_weight, *landed):
     depth = tokens.shape[1]
-    inputs = (tokens, qkv_weight, out_weight, mine, theirs, ours, other)
+    inputs = (tokens, qkv_weight, out_weight) + landed
     return kernel_call(
         query_kernel,
         [
@@ -503,19 +505,22 @@
     pair = jnp.concatenate([one, three])
     two = shifted(one, 1)
     pair_first = flipped(pair, (2, 4))
-    near = jnp.concatenate(after((pair, pair_first, two), other_tokens))
+    near = jnp.concatenate(after((pair, pair_first), other_tokens))
     away = flipped(near, (4, 2))
-    two_first = flipped(two, (2, 4))
-    two_far = flipped(two, (6, 6))
-
-    second_ready = after(second_piece, near)
+    two_near = jnp.concatenate([two, flipped(two, (2, 4))])
+    two_away = flipped(two_near, (4, 2))
+
+    second_ready = after(second_piece, one, three)
     second_one = shifted(second_ready, 1)
     second_three = shifted(second_ready, -1)
-    second_two = shifted(after(second_one, two_first, two_far), 1)
-
-    mine = first_call(after(tokens, second_one, second_three), other_tokens, qkv_weight, near, away, two_first, two_far)
+    second_two = shifted(after(second_one, two_near), 1)
+
+    mine = first_call(after(tokens, second_one, second_three), other_tokens, qkv_weight, near, away, two_near, two_away)
     other = flipped(after(mine, second_two), (1, 1))
+    straight = jnp.concatenate([second_one, second_two, second_three])
+    swapped_straight = flipped(straight, (1, 1))
     values, top, bottom, upto, total = state_call(mine, other, tokens.shape[0], col_count)
+    total = after(total, swapped_straight)
 
     second_own = jnp.stack([second_one[0], second_two[0], second_three[0]])
     second_first = flipped(second_own, (2, 4))
@@ -525,25 +530,33 @@
         pairs = [(t, t ^ bit) for t in range(8) if not t & guard]
         upto = upto + lax.ppermute(total, "tm", pairs).astype(jnp.float32)
     count = lax.axis_size("space")
-    top, bottom = after((top, bottom), upto)
     forward = [(i, i + 1) for i in range(count - 1)]
     backward = [(target, source) for source, target in forward]
-    above = lax.ppermute(bottom, "space", forward)
-    below = lax.ppermute(top, "space", backward)
     state = after(upto, second_first, second_second)
     for bit in (1, 2):
         share = state.astype(jnp.bfloat16)
         if bit == 2:
-            share = after(share, above, below)
+            top, bottom = after((top, bottom), share)
         pairs = [(i, i ^ bit) for i in range(count)]
         state = share.astype(jnp.float32) + lax.ppermute(share, "space", pairs).astype(jnp.float32)
+    above = lax.ppermute(bottom, "space", forward)
+    below = lax.ppermute(top, "space", backward)
     grid = values.reshape(row_count, col_count, depth)
     local_term = local_call(grid, above, below, conv_weight).reshape(-1, depth)
 
-    parts = (second_one, second_two, second_three, second_first, second_second)
-    held = jnp.concatenate(after(parts, share))
-    swapped = flipped(held, (1, 1))
-    queries, weight = query_call(tokens, qkv_weight, out_weight, held, swapped, mine, other)
+    turned = jnp.concatenate([second_first, second_second])
+    swapped_turned = flipped(after(turned, share), (1, 1))
+    queries, weight = query_call(
+        tokens,
+        qkv_weight,
+        out_weight,
+        straight,
+        swapped_straight,
+        turned,
+        swapped_turned,
+        mine,
+        other,
+    )
     result = finish_call(queries, weight, state, local_term, norm_gain[None])
     return result.reshape(1, row_count, col_count, depth)
 

time: 87.5 us -> 82.8 us (0.946)
  starting transfers between devices: 34.7 us -> 26.5 us
  waiting for transfers between devices: 40.7 us -> 44.2 us
    ppermute x6, waiting for transfers between devices: 17.9 us -> 22.3 us  [shifted(): lax.ppermute(value, 'space', [(i, (i + step) % count) for i in range(coun...]
    ppermute x9 -> x10, starting transfers between devices: 11.1 us -> 7.06 us  [flipped(): lax.ppermute(value, 'tm', [(t, t ^ bit_on_core[t % 2]) for t in range(8)])]
    ppermute x3, waiting for transfers between devices: 3 us -> 0.39 us  [plane_form(): upto = upto + lax.ppermute(total, 'tm', pairs).astype(jnp.float32)]
    ppermute x1, waiting for transfers between devices: 2.1 us -> 0.01 us  [plane_form(): above = lax.ppermute(bottom, 'space', forward)]
    ppermute x1, starting transfers between devices: 3.91 us -> 1.92 us  [plane_form(): above = lax.ppermute(bottom, 'space', forward)]
    ppermute x9 -> x10, waiting for transfers between devices: 7.6 us -> 9.41 us  [flipped(): lax.ppermute(value, 'tm', [(t, t ^ bit_on_core[t % 2]) for t in range(8)])]
    ppermute x2, waiting for transfers between devices: 5.94 us -> 7.55 us  [plane_form(): lax.ppermute(share, 'space', pairs).astype(jnp.float32)]
    ppermute x6, starting transfers between devices: 10.4 us -> 9.05 us  [shifted(): lax.ppermute(value, 'space', [(i, (i + step) % count) for i in range(coun...]
  transfers between devices with their start and end apart: 22 -> 23, of which waited for: 15 -> 13; matrix products, arithmetic and copies ran while one was open for 0% -> 1% of each run, Pallas kernels for 6% -> 6%
where the time goes in v3:
time: 82.8 us; the launch traced here: 82.6 us
  waiting for transfers between devices  44.2 us (53%)
  starting transfers between devices  26.5 us (32%)
  Pallas kernels  11 us (13%)
    ppermute x6, waiting for transfers between devices, shifted(): lax.ppermute(value, 'space', [(i, (i + step) % count) for i in range(coun...  22.3 us
    pallas_call x7, Pallas kernels, kernel_call(): pl.pallas_call(body, out_shape=outputs, in_specs=in_specs, out_specs=jax....  11 us
    ppermute x10, waiting for transfers between devices, flipped(): lax.ppermute(value, 'tm', [(t, t ^ bit_on_core[t % 2]) for t in range(8)])  9.41 us
    ppermute x6, starting transfers between devices, shifted(): lax.ppermute(value, 'space', [(i, (i + step) % count) for i in range(coun...  9.05 us
    ppermute x2, waiting for transfers between devices, plane_form(): lax.ppermute(share, 'space', pairs).astype(jnp.float32)  7.55 us
    ppermute x3, starting transfers between devices, plane_form(): upto = upto + lax.ppermute(total, 'tm', pairs).astype(jnp.float32)  7.06 us
    ppermute x10, starting transfers between devices, flipped(): lax.ppermute(value, 'tm', [(t, t ^ bit_on_core[t % 2]) for t in range(8)])  7.06 us
    ppermute x1, waiting for transfers between devices, plane_form(): below = lax.ppermute(top, 'space', backward)  4.63 us
  transfers between devices with their start and end apart: 23, of which 13 were waited for; matrix products, arithmetic and copies ran while one was open for 1% of the time, Pallas kernels for 6%

profile of v3, /device:TPU:0, one launch (start us, length us, event | category | flops | bytes accessed | tf_op | source)
XLA Modules:
  0.0 82.6 jit_solution(9020179731425559123)
XLA Ops:
  0.0 1.9 %shard_map.55 = (bf16[80,1152]{1,0:T(8,128)(2,1)}, bf16[2,64,1152]{2,1,0:T(8,128)(2,1)}) custom-call(bf16[288,3456]{1,0:T(8,128)(2,1)} %refs_1_.1, bf16[288,1152]{1,0:T(8,128)(2,1)} %refs_2_.3), custom_call_target="tpu_custom_call" | custom-call | bytes 958464 | tf_op jit(solution)/shard_map/pallas_call | solution.py:164
  2.0 3.1 %collective-permute-start = (bf16[1,80,1152]{2,1,0:T(8,128)(2,1)}, bf16[1,80,1152]{2,1,0:T(8,128)(2,1)S(1)}, u32[]{:S(2)}, u32[]{:S(2)}) collective-permute-start(bf16[1,80,1152]{2,1,0:T(8,128)(2,1)} %bitcast.8), channel_id=1, source_target_pairs={{0,1},{1,2},{2,3},{3,0},{4,5},{5,6},{6,7},{7,4},{8,9},{9,10},{10,1... | collective-permute-start | bytes 552968 | tf_op jit(solution)/shard_map/ppermute | solution.py:104
  5.0 2.1 %collective-permute-start.1 = (bf16[1,80,1152]{2,1,0:T(8,128)(2,1)}, bf16[1,80,1152]{2,1,0:T(8,128)(2,1)S(1)}, u32[]{:S(2)}, u32[]{:S(2)}) collective-permute-start(bf16[1,80,1152]{2,1,0:T(8,128)(2,1)} %bitcast.9), channel_id=1, source_target_pairs={{0,3},{1,0},{2,1},{3,2},{4,7},{5,4},{6,5},{7,6},{8,11},{9,8},{10,9... | collective-permute-start | bytes 552968 | tf_op jit(solution)/shard_map/ppermute | solution.py:104
  7.1 0.0 copy-done.3
  7.1 1.2 %shard_map.56.refs_0_ = bf16[256,1152]{1,0:T(8,128)(2,1)S(1)} custom-call(bf16[256,1152]{1,0:T(8,128)(2,1)S(1)} %bitcast.7), custom_call_target="tpu_custom_call" | custom-call | flops 679477248 | bytes 589824 | tf_op jit(solution)/shard_map/pallas_call | solution.py:164
  8.3 0.0 copy-start
  8.3 0.1 collective-permute-start.10
  8.4 4.4 %collective-permute-done = bf16[1,80,1152]{2,1,0:T(8,128)(2,1)S(1)} collective-permute-done((bf16[1,80,1152]{2,1,0:T(8,128)(2,1)}, bf16[1,80,1152]{2,1,0:T(8,128)(2,1)S(1)}, u32[]{:S(2)}, u32[]{:S(2)}) %collective-permute-start) | collective-permute-done | bytes 184352 | tf_op jit(solution)/shard_map/ppermute | solution.py:104
  12.8 2.5 %collective-permute-done.1 = bf16[1,80,1152]{2,1,0:T(8,128)(2,1)S(1)} collective-permute-done((bf16[1,80,1152]{2,1,0:T(8,128)(2,1)}, bf16[1,80,1152]{2,1,0:T(8,128)(2,1)S(1)}, u32[]{:S(2)}, u32[]{:S(2)}) %collective-permute-start.1) | collective-permute-done | bytes 184352 | tf_op jit(solution)/shard_map/ppermute | solution.py:104
  15.3 1.6 %collective-permute-start.11 = (bf16[2,80,1152]{2,1,0:T(8,128)(2,1)S(1)}, bf16[2,80,1152]{2,1,0:T(8,128)(2,1)S(1)}, u32[]{:S(2)}, u32[]{:S(2)}) collective-permute-start(bf16[2,80,1152]{2,1,0:T(8,128)(2,1)S(1)} %constant_dynamic-update-slice_fusion.7), channel_id=1, source_target_pairs={{0,8},{4,20},{8,0},{12,28},{16,24},{20,4},{24,16},{28,12},{1,9},{5... | collective-permute-start | bytes 1105928 | tf_op jit(solution)/shard_map/ppermute | solution.py:108
  16.9 1.1 %collective-permute-start.3 = (bf16[1,80,1152]{2,1,0:T(8,128)(2,1)S(1)}, bf16[1,80,1152]{2,1,0:T(8,128)(2,1)S(1)}, u32[]{:S(2)}, u32[]{:S(2)}) collective-permute-start(bf16[1,80,1152]{2,1,0:T(8,128)(2,1)S(1)} %collective-permute-done), channel_id=1, source_target_pairs={{0,1},{1,2},{2,3},{3,0},{4,5},{5,6},{6,7},{7,4},{8,9},{9,10},{10,1... | collective-permute-start | bytes 552968 | tf_op jit(solution)/shard_map/ppermute | solution.py:104
  18.0 0.0 copy-done.5
  18.0 0.7 collective-permute-start.2
  18.8 7.5 %collective-permute-done.3 = bf16[1,80,1152]{2,1,0:T(8,128)(2,1)S(1)} collective-permute-done((bf16[1,80,1152]{2,1,0:T(8,128)(2,1)S(1)}, bf16[1,80,1152]{2,1,0:T(8,128)(2,1)S(1)}, u32[]{:S(2)}, u32[]{:S(2)}) %collective-permute-start.3) | collective-permute-done | bytes 184352 | tf_op jit(solution)/shard_map/ppermute | solution.py:104
  26.3 0.4 collective-permute-start.4
  26.7 0.0 collective-permute-done.11
  26.7 0.0 collective-permute-done.10.refs_1_
  26.8 1.7 %collective-permute-start.12 = (bf16[4,80,1152]{2,1,0:T(8,128)(2,1)S(1)}, bf16[4,80,1152]{2,1,0:T(8,128)(2,1)S(1)}, u32[]{:S(2)}, u32[]{:S(2)}) collective-permute-start(bf16[4,80,1152]{2,1,0:T(8,128)(2,1)S(1)} %constant_dynamic-update-slice_fusion.9.refs_3_), channel_id=1, source_target_pairs={{0,16},{4,12},{8,24},{12,4},{16,0},{20,28},{24,8},{28,20},{1,17},{... | collective-permute-start | bytes 2211848 | tf_op jit(solution)/shard_map/ppermute | solution.py:108
  28.5 5.3 %collective-permute-done.4 = bf16[1,80,1152]{2,1,0:T(8,128)(2,1)S(1)} collective-permute-done((bf16[1,80,1152]{2,1,0:T(8,128)(2,1)S(1)}, bf16[1,80,1152]{2,1,0:T(8,128)(2,1)S(1)}, u32[]{:S(2)}, u32[]{:S(2)}) %collective-permute-start.4) | collective-permute-done | bytes 184352 | tf_op jit(solution)/shard_map/ppermute | solution.py:108
  33.9 1.6 %collective-permute-start.13 = (bf16[2,80,1152]{2,1,0:T(8,128)(2,1)S(1)}, bf16[2,80,1152]{2,1,0:T(8,128)(2,1)S(1)}, u32[]{:S(2)}, u32[]{:S(2)}) collective-permute-start(bf16[2,80,1152]{2,1,0:T(8,128)(2,1)S(1)} %constant_dynamic-update-slice_fusion.refs_5_), channel_id=1, source_target_pairs={{0,16},{4,12},{8,24},{12,4},{16,0},{20,28},{24,8},{28,20},{1,17},{... | collective-permute-start | bytes 1105928 | tf_op jit(solution)/shard_map/ppermute | solution.py:108
  35.4 0.1 collective-permute-start.6
  35.6 0.0 collective-permute-done.2
  35.6 1.9 %collective-permute-start.5 = (bf16[2,64,1152]{2,1,0:T(8,128)(2,1)S(1)}, bf16[2,64,1152]{2,1,0:T(8,128)(2,1)S(1)}, u32[]{:S(2)}, u32[]{:S(2)}) collective-permute-start(bf16[2,64,1152]{2,1,0:T(8,128)(2,1)S(1)} %collective-permute-done.2), channel_id=1, source_target_pairs={{0,1},{1,2},{2,3},{3,0},{4,5},{5,6},{6,7},{7,4},{8,9},{9,10},{10,1... | collective-permute-start | bytes 884744 | tf_op jit(solution)/shard_map/ppermute | solution.py:104
  37.5 7.9 %collective-permute-done.6 = bf16[2,64,1152]{2,1,0:T(8,128)(2,1)S(1)} collective-permute-done((bf16[2,64,1152]{2,1,0:T(8,128)(2,1)S(1)}, bf16[2,64,1152]{2,1,0:T(8,128)(2,1)S(1)}, u32[]{:S(2)}, u32[]{:S(2)}) %collective-permute-start.6) | collective-permute-done | bytes 294944 | tf_op jit(solution)/shard_map/ppermute | solution.py:104
  45.3 0.0 collective-permute-done.13.refs_6_
  45.3 0.0 collective-permute-done.12.refs_4_
  45.3 0.0 copy-done
  45.3 2.1 %shard_map.57.mine_ref.refs_7_ = bf16[608,1152]{1,0:T(8,128)(2,1)S(1)} custom-call(bf16[256,1152]{1,0:T(8,128)(2,1)S(1)} %shard_map.56.refs_0_, bf16[256,1152]{1,0:T(8,128)(2,1)S(1)} %collective-permute-done.10.refs_1_, bf16[288,3456]{1,0:T(8,128)(2,1)S(1)} %copy-done, bf16[4,80,1152]{2,1,0:T(8,128)(2,1)S(1)} %constant_dynamic-update-slice_fusion.9.refs_3_, ...), custom_call_target="tpu_custom_call" | custom-call | flops 1358954496 | bytes 2654208 | tf_op jit(solution)/shard_map/pallas_call | solution.py:164
  47.5 0.0 collective-permute-done.5
  47.5 0.1 collective-permute-start.14
  47.7 0.6 collective-permute-start.7
  48.3 0.1 pad_maximum_fusion
  48.4 0.6 collective-permute-start.8
  49.0 0.4 collective-permute-start.9
  49.4 1.3 %collective-permute-done.14.other_ref.refs_8_ = bf16[608,1152]{1,0:T(8,128)(2,1)S(1)} collective-permute-done((bf16[608,1152]{1,0:T(8,128)(2,1)S(1)}, bf16[608,1152]{1,0:T(8,128)(2,1)S(1)}, u32[]{:S(2)}, u32[]{:S(2)}) %collective-permute-start.14) | collective-permute-done | bytes 1400864 | tf_op jit(solution)/shard_map/ppermute | solution.py:108
  50.7 0.9 %shard_map.58 = (bf16[256,1152]{1,0:T(8,128)(2,1)S(1)}, bf16[1,64,1152]{2,1,0:T(8,128)(2,1)S(1)}, bf16[1,64,1152]{2,1,0:T(8,128)(2,1)S(1)}, f32[9,32,128]{2,1,0:T(8,128)S(1)}, bf16[9,32,128]{2,1,0:T(8,128)(2,1)S(1)}) custom-call(bf16[608,1152]{1,0:T(8,128)(2,1)S(1)} %shard_map.57.mine_ref.refs_7_, bf16[608,1152]{1,0:T(8,128)(2,1)S(1)} %collective-permute-done.14.other_ref.refs_8_), custom_call_target="tpu_custom_call" | custom-call | flops 150994944 | bytes 2359296 | tf_op jit(solution)/shard_map/pallas_call | solution.py:164
  51.6 0.0 copy-start.4
  51.6 0.0 copy-start.2
  51.6 0.4 collective-permute-done.7.refs_4_
  52.0 2.8 %collective-permute-start.17 = (bf16[9,32,128]{2,1,0:T(8,128)(2,1)S(1)}, bf16[9,32,128]{2,1,0:T(8,128)(2,1)S(1)}, u32[]{:S(2)}, u32[]{:S(2)}) collective-permute-start(bf16[9,32,128]{2,1,0:T(8,128)(2,1)S(1)} %get-tuple-element.41), channel_id=1, source_target_pairs={{0,24},{4,28},{8,16},{12,20},{1,25},{5,29},{9,17},{13,21},{2,26},{... | collective-permute-start | bytes 221192 | tf_op jit(solution)/shard_map/ppermute | solution.py:531
  54.8 1.3 %collective-permute-start.16 = (bf16[9,32,128]{2,1,0:T(8,128)(2,1)S(1)}, bf16[9,32,128]{2,1,0:T(8,128)(2,1)S(1)}, u32[]{:S(2)}, u32[]{:S(2)}) collective-permute-start(bf16[9,32,128]{2,1,0:T(8,128)(2,1)S(1)} %get-tuple-element.41), channel_id=1, source_target_pairs={{0,16},{4,20},{8,24},{12,28},{1,17},{5,21},{9,25},{13,29},{2,18},{... | collective-permute-start | bytes 221192 | tf_op jit(solution)/shard_map/ppermute | solution.py:531
  56.1 3.0 %collective-permute-start.15 = (bf16[9,32,128]{2,1,0:T(8,128)(2,1)S(1)}, bf16[9,32,128]{2,1,0:T(8,128)(2,1)S(1)}, u32[]{:S(2)}, u32[]{:S(2)}) collective-permute-start(bf16[9,32,128]{2,1,0:T(8,128)(2,1)S(1)} %get-tuple-element.41), channel_id=1, source_target_pairs={{0,8},{4,12},{16,24},{20,28},{1,9},{5,13},{17,25},{21,29},{2,10},{... | collective-permute-start | bytes 221192 | tf_op jit(solution)/shard_map/ppermute | solution.py:531
  59.1 2.4 %collective-permute-done.8 = bf16[3,64,1152]{2,1,0:T(8,128)(2,1)S(1)} collective-permute-done((bf16[3,64,1152]{2,1,0:T(8,128)(2,1)S(1)}, bf16[3,64,1152]{2,1,0:T(8,128)(2,1)S(1)}, u32[]{:S(2)}, u32[]{:S(2)}) %collective-permute-start.8) | collective-permute-done | bytes 442400 | tf_op jit(solution)/shard_map/ppermute | solution.py:108
  61.5 0.0 collective-permute-done.17
  61.5 0.3 collective-permute-done.16
  61.7 0.1 collective-permute-done.15
  61.9 0.0 collective-permute-done.9
  61.9 0.1 collective-permute-start.18
  62.1 0.0 copy-start.1
  62.1 4.3 %collective-permute-done.18 = bf16[9,32,128]{2,1,0:T(8,128)(2,1)S(1)} collective-permute-done((bf16[9,32,128]{2,1,0:T(8,128)(2,1)S(1)}, bf16[9,32,128]{2,1,0:T(8,128)(2,1)S(1)}, u32[]{:S(2)}, u32[]{:S(2)}) %collective-permute-start.18) | collective-permute-done | bytes 73760 | tf_op jit(solution)/shard_map/ppermute | solution.py:541
  66.4 0.1 collective-permute-start.19
  66.5 0.1 collective-permute-start.20
  66.5 0.0 copy-done.4
  66.6 1.9 %collective-permute-start.21 = (bf16[1,64,1152]{2,1,0:T(8,128)(2,1)S(1)}, bf16[1,64,1152]{2,1,0:T(8,128)(2,1)S(1)}, u32[]{:S(2)}, u32[]{:S(2)}) collective-permute-start(bf16[1,64,1152]{2,1,0:T(8,128)(2,1)S(1)} %get-tuple-element.49), channel_id=1, source_target_pairs={{0,1},{1,2},{2,3},{4,5},{5,6},{6,7},{8,9},{9,10},{10,11},{12,13},{... | collective-permute-start | bytes 442376 | tf_op jit(solution)/shard_map/ppermute | solution.py:542
  68.5 1.3 %collective-permute-start.22 = (bf16[1,64,1152]{2,1,0:T(8,128)(2,1)S(1)}, bf16[1,64,1152]{2,1,0:T(8,128)(2,1)S(1)}, u32[]{:S(2)}, u32[]{:S(2)}) collective-permute-start(bf16[1,64,1152]{2,1,0:T(8,128)(2,1)S(1)} %get-tuple-element.50), channel_id=1, source_target_pairs={{1,0},{2,1},{3,2},{5,4},{6,5},{7,6},{9,8},{10,9},{11,10},{13,12},{... | collective-permute-start | bytes 442376 | tf_op jit(solution)/shard_map/ppermute | solution.py:543
  69.8 3.3 %collective-permute-done.20 = bf16[9,32,128]{2,1,0:T(8,128)(2,1)S(1)} collective-permute-done((bf16[9,32,128]{2,1,0:T(8,128)(2,1)S(1)}, bf16[9,32,128]{2,1,0:T(8,128)(2,1)S(1)}, u32[]{:S(2)}, u32[]{:S(2)}) %collective-permute-start.20) | collective-permute-done | bytes 73760 | tf_op jit(solution)/shard_map/ppermute | solution.py:541
  73.1 0.0 collective-permute-done.21.above_ref
  73.1 4.6 %collective-permute-done.22.below_ref = bf16[1,64,1152]{2,1,0:T(8,128)(2,1)S(1)} collective-permute-done((bf16[1,64,1152]{2,1,0:T(8,128)(2,1)S(1)}, bf16[1,64,1152]{2,1,0:T(8,128)(2,1)S(1)}, u32[]{:S(2)}, u32[]{:S(2)}) %collective-permute-start.22) | collective-permute-done | bytes 147488 | tf_op jit(solution)/shard_map/ppermute | solution.py:543
  77.7 0.0 copy-done.2
  77.7 0.9 %shard_map.60 = f32[4,64,1152]{2,1,0:T(8,128)S(1)} custom-call(bf16[4,64,1152]{2,1,0:T(8,128)(2,1)S(1)} %bitcast.6, bf16[1,64,1152]{2,1,0:T(8,128)(2,1)S(1)} %collective-permute-done.21.above_ref, bf16[1,64,1152]{2,1,0:T(8,128)(2,1)S(1)} %collective-permute-done.22.below_ref, f32[3,3,1152]{2,1,0:T(4,128)S(1)} %copy-done.2), custom_call_target="tpu_custom_call" | custom-call | flops 5308416 | bytes 1769472 | tf_op jit(solution)/shard_map/pallas_call | solution.py:164
  78.7 0.0 collective-permute-done.19.refs_6_
  78.7 0.0 copy-done.1
  78.7 1.6 %shard_map.59 = (bf16[256,1152]{1,0:T(8,128)(2,1)S(1)}, bf16[1152,1152]{1,0:T(8,128)(2,1)S(1)}) custom-call(bf16[256,1152]{1,0:T(8,128)(2,1)S(1)} %shard_map.56.refs_0_, bf16[288,3456]{1,0:T(8,128)(2,1)S(1)} %copy-done, bf16[288,1152]{1,0:T(8,128)(2,1)S(1)} %copy-done.1, bf16[6,64,1152]{2,1,0:T(8,128)(2,1)S(1)} %constant_dynamic-update-slice_fusion.2.refs_3_, ...), custom_call_target="tpu_custom_call" | custom-call | flops 679477248 | bytes 5308416 | tf_op jit(solution)/shard_map/pallas_call | solution.py:164
  80.2 2.4 %shard_map.61 = bf16[256,1152]{1,0:T(8,128)(2,1)} custom-call(bf16[256,1152]{1,0:T(8,128)(2,1)S(1)} %get-tuple-element.44.queries_ref, bf16[1152,1152]{1,0:T(8,128)(2,1)S(1)} %get-tuple-element.45.weight_ref, f32[9,32,128]{2,1,0:T(8,128)S(1)} %convert_add_fusion.state_ref, f32[256,1152]{1,0:T(8,128)S(1)} %bitcast.5, f32[1,1152]{1,0:T(1,128)S(1)} %broadcast_in_dim.7.gain_ref), custom_call_target="tpu_custom_call" | custom-call | flops 679477248 | bytes 2654208 | tf_op jit(solution)/shard_map/pallas_call | solution.py:164
  (20 shorter events, 0.4 us)
Async XLA Ops:
  0.0 7.1 %copy-start.3 = (bf16[1,4,64,1152]{3,2,1,0:T(8,128)(2,1)S(1)}, bf16[1,4,64,1152]{3,2,1,0:T(8,128)(2,1)}, u32[]{:S(2)}) copy-start(bf16[1,4,64,1152]{3,2,1,0:T(8,128)(2,1)} %param.5) | copy-start | bytes 1769476
  2.0 10.8 %collective-permute-start = (bf16[1,80,1152]{2,1,0:T(8,128)(2,1)}, bf16[1,80,1152]{2,1,0:T(8,128)(2,1)S(1)}, u32[]{:S(2)}, u32[]{:S(2)}) collective-permute-start(bf16[1,80,1152]{2,1,0:T(8,128)(2,1)} %bitcast.8), channel_id=1, source_target_pairs={{0,1},{1,2},{2,3},{3,0},{4,5},{5,6},{6,7},{7,4},{8,9},{9,10},{10,1... | collective-permute-start | bytes 552968 | tf_op jit(solution)/shard_map/ppermute | solution.py:104
  5.0 10.3 %collective-permute-start.1 = (bf16[1,80,1152]{2,1,0:T(8,128)(2,1)}, bf16[1,80,1152]{2,1,0:T(8,128)(2,1)S(1)}, u32[]{:S(2)}, u32[]{:S(2)}) collective-permute-start(bf16[1,80,1152]{2,1,0:T(8,128)(2,1)} %bitcast.9), channel_id=1, source_target_pairs={{0,3},{1,0},{2,1},{3,2},{4,7},{5,4},{6,5},{7,6},{8,11},{9,8},{10,9... | collective-permute-start | bytes 552968 | tf_op jit(solution)/shard_map/ppermute | solution.py:104
  7.1 10.9 %copy-start.5 = (bf16[2,64,1152]{2,1,0:T(8,128)(2,1)S(1)}, bf16[2,64,1152]{2,1,0:T(8,128)(2,1)}, u32[]{:S(2)}) copy-start(bf16[2,64,1152]{2,1,0:T(8,128)(2,1)} %get-tuple-element.33) | copy-start | bytes 884740
  8.3 37.0 %copy-start = (bf16[288,3456]{1,0:T(8,128)(2,1)S(1)}, bf16[288,3456]{1,0:T(8,128)(2,1)}, u32[]{:S(2)}) copy-start(bf16[288,3456]{1,0:T(8,128)(2,1)} %refs_1_.1) | copy-start | bytes 5971972
  8.3 18.4 %collective-permute-start.10 = (bf16[256,1152]{1,0:T(8,128)(2,1)S(1)}, bf16[256,1152]{1,0:T(8,128)(2,1)S(1)}, u32[]{:S(2)}, u32[]{:S(2)}) collective-permute-start(bf16[256,1152]{1,0:T(8,128)(2,1)S(1)} %shard_map.56.refs_0_), channel_id=1, source_target_pairs={{0,4},{4,0},{8,12},{12,8},{16,20},{20,16},{24,28},{28,24},{1,5},{5... | collective-permute-start | bytes 1769480 | tf_op jit(solution)/shard_map/ppermute | solution.py:108
  15.3 11.4 %collective-permute-start.11 = (bf16[2,80,1152]{2,1,0:T(8,128)(2,1)S(1)}, bf16[2,80,1152]{2,1,0:T(8,128)(2,1)S(1)}, u32[]{:S(2)}, u32[]{:S(2)}) collective-permute-start(bf16[2,80,1152]{2,1,0:T(8,128)(2,1)S(1)} %constant_dynamic-update-slice_fusion.7), channel_id=1, source_target_pairs={{0,8},{4,20},{8,0},{12,28},{16,24},{20,4},{24,16},{28,12},{1,9},{5... | collective-permute-start | bytes 1105928 | tf_op jit(solution)/shard_map/ppermute | solution.py:108
  16.9 9.4 %collective-permute-start.3 = (bf16[1,80,1152]{2,1,0:T(8,128)(2,1)S(1)}, bf16[1,80,1152]{2,1,0:T(8,128)(2,1)S(1)}, u32[]{:S(2)}, u32[]{:S(2)}) collective-permute-start(bf16[1,80,1152]{2,1,0:T(8,128)(2,1)S(1)} %collective-permute-done), channel_id=1, source_target_pairs={{0,1},{1,2},{2,3},{3,0},{4,5},{5,6},{6,7},{7,4},{8,9},{9,10},{10,1... | collective-permute-start | bytes 552968 | tf_op jit(solution)/shard_map/ppermute | solution.py:104
  18.0 17.6 %collective-permute-start.2 = (bf16[2,64,1152]{2,1,0:T(8,128)(2,1)S(1)}, bf16[2,64,1152]{2,1,0:T(8,128)(2,1)S(1)}, u32[]{:S(2)}, u32[]{:S(2)}) collective-permute-start(bf16[2,64,1152]{2,1,0:T(8,128)(2,1)S(1)} %copy-done.5), channel_id=1, source_target_pairs={{0,1},{1,2},{2,3},{3,0},{4,5},{5,6},{6,7},{7,4},{8,9},{9,10},{10,1... | collective-permute-start | bytes 884744 | tf_op jit(solution)/shard_map/ppermute | solution.py:104
  26.3 7.6 %collective-permute-start.4 = (bf16[1,80,1152]{2,1,0:T(8,128)(2,1)S(1)}, bf16[1,80,1152]{2,1,0:T(8,128)(2,1)S(1)}, u32[]{:S(2)}, u32[]{:S(2)}) collective-permute-start(bf16[1,80,1152]{2,1,0:T(8,128)(2,1)S(1)} %collective-permute-done.3), channel_id=1, source_target_pairs={{0,8},{4,20},{8,0},{12,28},{16,24},{20,4},{24,16},{28,12},{1,9},{5... | collective-permute-start | bytes 552968 | tf_op jit(solution)/shard_map/ppermute | solution.py:108
  26.8 18.5 %collective-permute-start.12 = (bf16[4,80,1152]{2,1,0:T(8,128)(2,1)S(1)}, bf16[4,80,1152]{2,1,0:T(8,128)(2,1)S(1)}, u32[]{:S(2)}, u32[]{:S(2)}) collective-permute-start(bf16[4,80,1152]{2,1,0:T(8,128)(2,1)S(1)} %constant_dynamic-update-slice_fusion.9.refs_3_), channel_id=1, source_target_pairs={{0,16},{4,12},{8,24},{12,4},{16,0},{20,28},{24,8},{28,20},{1,17},{... | collective-permute-start | bytes 2211848 | tf_op jit(solution)/shard_map/ppermute | solution.py:108
  33.9 11.5 %collective-permute-start.13 = (bf16[2,80,1152]{2,1,0:T(8,128)(2,1)S(1)}, bf16[2,80,1152]{2,1,0:T(8,128)(2,1)S(1)}, u32[]{:S(2)}, u32[]{:S(2)}) collective-permute-start(bf16[2,80,1152]{2,1,0:T(8,128)(2,1)S(1)} %constant_dynamic-update-slice_fusion.refs_5_), channel_id=1, source_target_pairs={{0,16},{4,12},{8,24},{12,4},{16,0},{20,28},{24,8},{28,20},{1,17},{... | collective-permute-start | bytes 1105928 | tf_op jit(solution)/shard_map/ppermute | solution.py:108
  35.4 9.9 %collective-permute-start.6 = (bf16[2,64,1152]{2,1,0:T(8,128)(2,1)S(1)}, bf16[2,64,1152]{2,1,0:T(8,128)(2,1)S(1)}, u32[]{:S(2)}, u32[]{:S(2)}) collective-permute-start(bf16[2,64,1152]{2,1,0:T(8,128)(2,1)S(1)} %copy-done.5), channel_id=1, source_target_pairs={{0,3},{1,0},{2,1},{3,2},{4,7},{5,4},{6,5},{7,6},{8,11},{9,8},{10,9... | collective-permute-start | bytes 884744 | tf_op jit(solution)/shard_map/ppermute | solution.py:104
  35.6 11.9 %collective-permute-start.5 = (bf16[2,64,1152]{2,1,0:T(8,128)(2,1)S(1)}, bf16[2,64,1152]{2,1,0:T(8,128)(2,1)S(1)}, u32[]{:S(2)}, u32[]{:S(2)}) collective-permute-start(bf16[2,64,1152]{2,1,0:T(8,128)(2,1)S(1)} %collective-permute-done.2), channel_id=1, source_target_pairs={{0,1},{1,2},{2,3},{3,0},{4,5},{5,6},{6,7},{7,4},{8,9},{9,10},{10,1... | collective-permute-start | bytes 884744 | tf_op jit(solution)/shard_map/ppermute | solution.py:104
  47.5 3.2 %collective-permute-start.14 = (bf16[608,1152]{1,0:T(8,128)(2,1)S(1)}, bf16[608,1152]{1,0:T(8,128)(2,1)S(1)}, u32[]{:S(2)}, u32[]{:S(2)}) collective-permute-start(bf16[608,1152]{1,0:T(8,128)(2,1)S(1)} %shard_map.57.mine_ref.refs_7_), channel_id=1, source_target_pairs={{0,4},{4,0},{8,12},{12,8},{16,20},{20,16},{24,28},{28,24},{1,5},{5... | collective-permute-start | bytes 4202504 | tf_op jit(solution)/shard_map/ppermute | solution.py:108
  47.7 4.3 %collective-permute-start.7 = (bf16[6,64,1152]{2,1,0:T(8,128)(2,1)S(1)}, bf16[6,64,1152]{2,1,0:T(8,128)(2,1)S(1)}, u32[]{:S(2)}, u32[]{:S(2)}) collective-permute-start(bf16[6,64,1152]{2,1,0:T(8,128)(2,1)S(1)} %constant_dynamic-update-slice_fusion.2.refs_3_), channel_id=1, source_target_pairs={{0,4},{4,0},{8,12},{12,8},{16,20},{20,16},{24,28},{28,24},{1,5},{5... | collective-permute-start | bytes 2654216 | tf_op jit(solution)/shard_map/ppermute | solution.py:108
  48.4 13.1 %collective-permute-start.8 = (bf16[3,64,1152]{2,1,0:T(8,128)(2,1)S(1)}, bf16[3,64,1152]{2,1,0:T(8,128)(2,1)S(1)}, u32[]{:S(2)}, u32[]{:S(2)}) collective-permute-start(bf16[3,64,1152]{2,1,0:T(8,128)(2,1)S(1)} %pad_maximum_fusion), channel_id=1, source_target_pairs={{0,8},{4,20},{8,0},{12,28},{16,24},{20,4},{24,16},{28,12},{1,9},{5... | collective-permute-start | bytes 1327112 | tf_op jit(solution)/shard_map/ppermute | solution.py:108
  49.0 13.0 %collective-permute-start.9 = (bf16[3,64,1152]{2,1,0:T(8,128)(2,1)S(1)}, bf16[3,64,1152]{2,1,0:T(8,128)(2,1)S(1)}, u32[]{:S(2)}, u32[]{:S(2)}) collective-permute-start(bf16[3,64,1152]{2,1,0:T(8,128)(2,1)S(1)} %pad_maximum_fusion), channel_id=1, source_target_pairs={{0,16},{4,12},{8,24},{12,4},{16,0},{20,28},{24,8},{28,20},{1,17},{... | collective-permute-start | bytes 1327112 | tf_op jit(solution)/shard_map/ppermute | solution.py:108
  51.6 14.9 %copy-start.4 = (f32[1152]{0:T(1024)S(1)}, f32[1152]{0:T(1024)}, u32[]{:S(2)}) copy-start(f32[1152]{0:T(1024)} %param.9) | copy-start | bytes 13828
  51.6 26.1 %copy-start.2 = (f32[3,3,1152]{2,1,0:T(4,128)S(1)}, f32[3,3,1152]{2,1,0:T(4,128)}, u32[]{:S(2)}) copy-start(f32[3,3,1152]{2,1,0:T(4,128)} %conv_ref.1) | copy-start | bytes 124420
  52.0 9.5 %collective-permute-start.17 = (bf16[9,32,128]{2,1,0:T(8,128)(2,1)S(1)}, bf16[9,32,128]{2,1,0:T(8,128)(2,1)S(1)}, u32[]{:S(2)}, u32[]{:S(2)}) collective-permute-start(bf16[9,32,128]{2,1,0:T(8,128)(2,1)S(1)} %get-tuple-element.41), channel_id=1, source_target_pairs={{0,24},{4,28},{8,16},{12,20},{1,25},{5,29},{9,17},{13,21},{2,26},{... | collective-permute-start | bytes 221192 | tf_op jit(solution)/shard_map/ppermute | solution.py:531
  54.8 7.0 %collective-permute-start.16 = (bf16[9,32,128]{2,1,0:T(8,128)(2,1)S(1)}, bf16[9,32,128]{2,1,0:T(8,128)(2,1)S(1)}, u32[]{:S(2)}, u32[]{:S(2)}) collective-permute-start(bf16[9,32,128]{2,1,0:T(8,128)(2,1)S(1)} %get-tuple-element.41), channel_id=1, source_target_pairs={{0,16},{4,20},{8,24},{12,28},{1,17},{5,21},{9,25},{13,29},{2,18},{... | collective-permute-start | bytes 221192 | tf_op jit(solution)/shard_map/ppermute | solution.py:531
  56.1 5.8 %collective-permute-start.15 = (bf16[9,32,128]{2,1,0:T(8,128)(2,1)S(1)}, bf16[9,32,128]{2,1,0:T(8,128)(2,1)S(1)}, u32[]{:S(2)}, u32[]{:S(2)}) collective-permute-start(bf16[9,32,128]{2,1,0:T(8,128)(2,1)S(1)} %get-tuple-element.41), channel_id=1, source_target_pairs={{0,8},{4,12},{16,24},{20,28},{1,9},{5,13},{17,25},{21,29},{2,10},{... | collective-permute-start | bytes 221192 | tf_op jit(solution)/shard_map/ppermute | solution.py:531
  61.9 4.4 %collective-permute-start.18 = (bf16[9,32,128]{2,1,0:T(8,128)(2,1)S(1)}, bf16[9,32,128]{2,1,0:T(8,128)(2,1)S(1)}, u32[]{:S(2)}, u32[]{:S(2)}) collective-permute-start(bf16[9,32,128]{2,1,0:T(8,128)(2,1)S(1)} %convert_add_fusion.1), channel_id=1, source_target_pairs={{0,1},{1,0},{2,3},{3,2},{4,5},{5,4},{6,7},{7,6},{8,9},{9,8},{10,11... | collective-permute-start | bytes 221192 | tf_op jit(solution)/shard_map/ppermute | solution.py:541
  62.1 16.6 %copy-start.1 = (bf16[288,1152]{1,0:T(8,128)(2,1)S(1)}, bf16[288,1152]{1,0:T(8,128)(2,1)}, u32[]{:S(2)}) copy-start(bf16[288,1152]{1,0:T(8,128)(2,1)} %refs_2_.3) | copy-start | bytes 1990660
  66.4 12.3 %collective-permute-start.19 = (bf16[6,64,1152]{2,1,0:T(8,128)(2,1)S(1)}, bf16[6,64,1152]{2,1,0:T(8,128)(2,1)S(1)}, u32[]{:S(2)}, u32[]{:S(2)}) collective-permute-start(bf16[6,64,1152]{2,1,0:T(8,128)(2,1)S(1)} %constant_dynamic-update-slice_fusion.5.refs_5_), channel_id=1, source_target_pairs={{0,4},{4,0},{8,12},{12,8},{16,20},{20,16},{24,28},{28,24},{1,5},{5... | collective-permute-start | bytes 2654216 | tf_op jit(solution)/shard_map/ppermute | solution.py:108
  66.5 6.6 %collective-permute-start.20 = (bf16[9,32,128]{2,1,0:T(8,128)(2,1)S(1)}, bf16[9,32,128]{2,1,0:T(8,128)(2,1)S(1)}, u32[]{:S(2)}, u32[]{:S(2)}) collective-permute-start(bf16[9,32,128]{2,1,0:T(8,128)(2,1)S(1)} %add_convert_fusion), channel_id=1, source_target_pairs={{0,2},{1,3},{2,0},{3,1},{4,6},{5,7},{6,4},{7,5},{8,10},{9,11},{10,... | collective-permute-start | bytes 221192 | tf_op jit(solution)/shard_map/ppermute | solution.py:541
  66.6 6.5 %collective-permute-start.21 = (bf16[1,64,1152]{2,1,0:T(8,128)(2,1)S(1)}, bf16[1,64,1152]{2,1,0:T(8,128)(2,1)S(1)}, u32[]{:S(2)}, u32[]{:S(2)}) collective-permute-start(bf16[1,64,1152]{2,1,0:T(8,128)(2,1)S(1)} %get-tuple-element.49), channel_id=1, source_target_pairs={{0,1},{1,2},{2,3},{4,5},{5,6},{6,7},{8,9},{9,10},{10,11},{12,13},{... | collective-permute-start | bytes 442376 | tf_op jit(solution)/shard_map/ppermute | solution.py:542
  68.5 9.2 %collective-permute-start.22 = (bf16[1,64,1152]{2,1,0:T(8,128)(2,1)S(1)}, bf16[1,64,1152]{2,1,0:T(8,128)(2,1)S(1)}, u32[]{:S(2)}, u32[]{:S(2)}) collective-permute-start(bf16[1,64,1152]{2,1,0:T(8,128)(2,1)S(1)} %get-tuple-element.50), channel_id=1, source_target_pairs={{1,0},{2,1},{3,2},{5,4},{6,5},{7,6},{9,8},{10,9},{11,10},{13,12},{... | collective-permute-start | bytes 442376 | tf_op jit(solution)/shard_map/ppermute | solution.py:543

commit v4 on v3

--- a/solution.py
+++ b/solution.py
@@ -532,17 +532,13 @@
     count = lax.axis_size("space")
     forward = [(i, i + 1) for i in range(count - 1)]
     backward = [(target, source) for source, target in forward]
-    state = after(upto, second_first, second_second)
-    for bit in (1, 2):
-        share = state.astype(jnp.bfloat16)
-        if bit == 2:
-            top, bottom = after((top, bottom), share)
-        pairs = [(i, i ^ bit) for i in range(count)]
-        state = share.astype(jnp.float32) + lax.ppermute(share, "space", pairs).astype(jnp.float32)
-    above = lax.ppermute(bottom, "space", forward)
-    below = lax.ppermute(top, "space", backward)
-    grid = values.reshape(row_count, col_count, depth)
-    local_term = local_call(grid, above, below, conv_weight).reshape(-1, depth)
+    above = lax.ppermute(after(bottom, upto), "space", forward)
+    share = after(upto, second_first, second_second).astype(jnp.bfloat16)
+    arrived = lax.ppermute(share, "space", [(i, i ^ 1) for i in range(count)])
+    share = (share.astype(jnp.float32) + arrived.astype(jnp.float32)).astype(jnp.bfloat16)
+    share = after(share, above)
+    arrived = lax.ppermute(share, "space", [(i, i ^ 2) for i in range(count)])
+    below = lax.ppermute(after(top, share), "space", backward)
 
     turned = jnp.concatenate([second_first, second_second])
     swapped_turned = flipped(after(turned, share), (1, 1))
@@ -557,6 +553,10 @@
         mine,
         other,
     )
+    grid = values.reshape(row_count, col_count, depth)
+    local_term = local_call(grid, above, after(below, queries), conv_weight).reshape(-1, depth)
+    arrived = after(arrived, local_term)
+    state = share.astype(jnp.float32) + arrived.astype(jnp.float32)
     result = finish_call(queries, weight, state, local_term, norm_gain[None])
     return result.reshape(1, row_count, col_count, depth)
 

time: 82.8 us -> 84.4 us (1.019)
  starting transfers between devices: 26.5 us -> 32.6 us
  waiting for transfers between devices: 44.2 us -> 39.9 us
    ppermute x4, starting transfers between devices: 3.35 us -> 9.88 us  [the longest x1 4.61 us: plane_form(): arrived = lax.ppermute(share, 'space', [(i, i ^ 2) for i in range(count)])]
    ppermute x4, waiting for transfers between devices: 12.2 us -> 7.39 us  [the longest x1 3.38 us: plane_form(): arrived = lax.ppermute(share, 'space', [(i, i ^ 2) for i in range(count)])]
  transfers between devices with their start and end apart: 23 -> 23, of which waited for: 13 -> 14; matrix products, arithmetic and copies ran while one was open for 1% -> 1% of each run, Pallas kernels for 6% -> 8%
where the time goes in v4:
time: 84.4 us; the launch traced here: 84.2 us
  waiting for transfers between devices  39.9 us (47%)
  starting transfers between devices  32.6 us (39%)
  Pallas kernels  11 us (13%)
    ppermute x6, waiting for transfers between devices, shifted(): lax.ppermute(value, 'space', [(i, (i + step) % count) for i in range(coun...  22.3 us
    pallas_call x7, Pallas kernels, kernel_call(): pl.pallas_call(body, out_shape=outputs, in_specs=in_specs, out_specs=jax....  11 us
    ppermute x10, waiting for transfers between devices, flipped(): lax.ppermute(value, 'tm', [(t, t ^ bit_on_core[t % 2]) for t in range(8)])  9.82 us
    ppermute x6, starting transfers between devices, shifted(): lax.ppermute(value, 'space', [(i, (i + step) % count) for i in range(coun...  9.05 us
    ppermute x10, starting transfers between devices, flipped(): lax.ppermute(value, 'tm', [(t, t ^ bit_on_core[t % 2]) for t in range(8)])  6.99 us
    ppermute x3, starting transfers between devices, plane_form(): upto = upto + lax.ppermute(total, 'tm', pairs).astype(jnp.float32)  6.66 us
    ppermute x1, starting transfers between devices, plane_form(): arrived = lax.ppermute(share, 'space', [(i, i ^ 2) for i in range(count)])  4.61 us
    ppermute x1, starting transfers between devices, plane_form(): above = lax.ppermute(after(bottom, upto), 'space', forward)  3.92 us
  transfers between devices with their start and end apart: 23, of which 14 were waited for; matrix products, arithmetic and copies ran while one was open for 1% of the time, Pallas kernels for 8%

profile of v4, /device:TPU:0, one launch (start us, length us, event | category | flops | bytes accessed | tf_op | source)
XLA Modules:
  0.0 84.2 jit_solution(18191539343148791413)
XLA Ops:
  0.0 0.0 copy-start.3
  0.0 1.9 %shard_map.55 = (bf16[80,1152]{1,0:T(8,128)(2,1)}, bf16[2,64,1152]{2,1,0:T(8,128)(2,1)}) custom-call(bf16[288,3456]{1,0:T(8,128)(2,1)} %refs_1_.1, bf16[288,1152]{1,0:T(8,128)(2,1)} %refs_2_.3), custom_call_target="tpu_custom_call" | custom-call | bytes 958464 | tf_op jit(solution)/shard_map/pallas_call | solution.py:164
  2.0 3.1 %collective-permute-start = (bf16[1,80,1152]{2,1,0:T(8,128)(2,1)}, bf16[1,80,1152]{2,1,0:T(8,128)(2,1)S(1)}, u32[]{:S(2)}, u32[]{:S(2)}) collective-permute-start(bf16[1,80,1152]{2,1,0:T(8,128)(2,1)} %bitcast.8), channel_id=1, source_target_pairs={{0,1},{1,2},{2,3},{3,0},{4,5},{5,6},{6,7},{7,4},{8,9},{9,10},{10,1... | collective-permute-start | bytes 552968 | tf_op jit(solution)/shard_map/ppermute | solution.py:104
  5.0 2.1 %collective-permute-start.1 = (bf16[1,80,1152]{2,1,0:T(8,128)(2,1)}, bf16[1,80,1152]{2,1,0:T(8,128)(2,1)S(1)}, u32[]{:S(2)}, u32[]{:S(2)}) collective-permute-start(bf16[1,80,1152]{2,1,0:T(8,128)(2,1)} %bitcast.9), channel_id=1, source_target_pairs={{0,3},{1,0},{2,1},{3,2},{4,7},{5,4},{6,5},{7,6},{8,11},{9,8},{10,9... | collective-permute-start | bytes 552968 | tf_op jit(solution)/shard_map/ppermute | solution.py:104
  7.1 0.0 copy-done.3
  7.1 1.2 %shard_map.56.refs_0_ = bf16[256,1152]{1,0:T(8,128)(2,1)S(1)} custom-call(bf16[256,1152]{1,0:T(8,128)(2,1)S(1)} %bitcast.7), custom_call_target="tpu_custom_call" | custom-call | flops 679477248 | bytes 589824 | tf_op jit(solution)/shard_map/pallas_call | solution.py:164
  8.3 0.0 copy-start
  8.3 0.1 collective-permute-start.10
  8.4 4.4 %collective-permute-done = bf16[1,80,1152]{2,1,0:T(8,128)(2,1)S(1)} collective-permute-done((bf16[1,80,1152]{2,1,0:T(8,128)(2,1)}, bf16[1,80,1152]{2,1,0:T(8,128)(2,1)S(1)}, u32[]{:S(2)}, u32[]{:S(2)}) %collective-permute-start) | collective-permute-done | bytes 184352 | tf_op jit(solution)/shard_map/ppermute | solution.py:104
  12.8 2.5 %collective-permute-done.1 = bf16[1,80,1152]{2,1,0:T(8,128)(2,1)S(1)} collective-permute-done((bf16[1,80,1152]{2,1,0:T(8,128)(2,1)}, bf16[1,80,1152]{2,1,0:T(8,128)(2,1)S(1)}, u32[]{:S(2)}, u32[]{:S(2)}) %collective-permute-start.1) | collective-permute-done | bytes 184352 | tf_op jit(solution)/shard_map/ppermute | solution.py:104
  15.3 1.6 %collective-permute-start.11 = (bf16[2,80,1152]{2,1,0:T(8,128)(2,1)S(1)}, bf16[2,80,1152]{2,1,0:T(8,128)(2,1)S(1)}, u32[]{:S(2)}, u32[]{:S(2)}) collective-permute-start(bf16[2,80,1152]{2,1,0:T(8,128)(2,1)S(1)} %constant_dynamic-update-slice_fusion.7), channel_id=1, source_target_pairs={{0,8},{4,20},{8,0},{12,28},{16,24},{20,4},{24,16},{28,12},{1,9},{5... | collective-permute-start | bytes 1105928 | tf_op jit(solution)/shard_map/ppermute | solution.py:108
  16.9 1.1 %collective-permute-start.3 = (bf16[1,80,1152]{2,1,0:T(8,128)(2,1)S(1)}, bf16[1,80,1152]{2,1,0:T(8,128)(2,1)S(1)}, u32[]{:S(2)}, u32[]{:S(2)}) collective-permute-start(bf16[1,80,1152]{2,1,0:T(8,128)(2,1)S(1)} %collective-permute-done), channel_id=1, source_target_pairs={{0,1},{1,2},{2,3},{3,0},{4,5},{5,6},{6,7},{7,4},{8,9},{9,10},{10,1... | collective-permute-start | bytes 552968 | tf_op jit(solution)/shard_map/ppermute | solution.py:104
  18.0 0.0 copy-done.5
  18.0 0.7 collective-permute-start.2
  18.8 7.5 %collective-permute-done.3 = bf16[1,80,1152]{2,1,0:T(8,128)(2,1)S(1)} collective-permute-done((bf16[1,80,1152]{2,1,0:T(8,128)(2,1)S(1)}, bf16[1,80,1152]{2,1,0:T(8,128)(2,1)S(1)}, u32[]{:S(2)}, u32[]{:S(2)}) %collective-permute-start.3) | collective-permute-done | bytes 184352 | tf_op jit(solution)/shard_map/ppermute | solution.py:104
  26.3 0.4 collective-permute-start.4
  26.7 0.0 collective-permute-done.11
  26.7 0.0 collective-permute-done.10.refs_1_
  26.8 1.7 %collective-permute-start.12 = (bf16[4,80,1152]{2,1,0:T(8,128)(2,1)S(1)}, bf16[4,80,1152]{2,1,0:T(8,128)(2,1)S(1)}, u32[]{:S(2)}, u32[]{:S(2)}) collective-permute-start(bf16[4,80,1152]{2,1,0:T(8,128)(2,1)S(1)} %constant_dynamic-update-slice_fusion.9.refs_3_), channel_id=1, source_target_pairs={{0,16},{4,12},{8,24},{12,4},{16,0},{20,28},{24,8},{28,20},{1,17},{... | collective-permute-start | bytes 2211848 | tf_op jit(solution)/shard_map/ppermute | solution.py:108
  28.5 5.3 %collective-permute-done.4 = bf16[1,80,1152]{2,1,0:T(8,128)(2,1)S(1)} collective-permute-done((bf16[1,80,1152]{2,1,0:T(8,128)(2,1)S(1)}, bf16[1,80,1152]{2,1,0:T(8,128)(2,1)S(1)}, u32[]{:S(2)}, u32[]{:S(2)}) %collective-permute-start.4) | collective-permute-done | bytes 184352 | tf_op jit(solution)/shard_map/ppermute | solution.py:108
  33.9 1.6 %collective-permute-start.13 = (bf16[2,80,1152]{2,1,0:T(8,128)(2,1)S(1)}, bf16[2,80,1152]{2,1,0:T(8,128)(2,1)S(1)}, u32[]{:S(2)}, u32[]{:S(2)}) collective-permute-start(bf16[2,80,1152]{2,1,0:T(8,128)(2,1)S(1)} %constant_dynamic-update-slice_fusion.refs_5_), channel_id=1, source_target_pairs={{0,16},{4,12},{8,24},{12,4},{16,0},{20,28},{24,8},{28,20},{1,17},{... | collective-permute-start | bytes 1105928 | tf_op jit(solution)/shard_map/ppermute | solution.py:108
  35.4 0.1 collective-permute-start.6
  35.6 0.0 collective-permute-done.2
  35.6 1.9 %collective-permute-start.5 = (bf16[2,64,1152]{2,1,0:T(8,128)(2,1)S(1)}, bf16[2,64,1152]{2,1,0:T(8,128)(2,1)S(1)}, u32[]{:S(2)}, u32[]{:S(2)}) collective-permute-start(bf16[2,64,1152]{2,1,0:T(8,128)(2,1)S(1)} %collective-permute-done.2), channel_id=1, source_target_pairs={{0,1},{1,2},{2,3},{3,0},{4,5},{5,6},{6,7},{7,4},{8,9},{9,10},{10,1... | collective-permute-start | bytes 884744 | tf_op jit(solution)/shard_map/ppermute | solution.py:104
  37.5 7.9 %collective-permute-done.6 = bf16[2,64,1152]{2,1,0:T(8,128)(2,1)S(1)} collective-permute-done((bf16[2,64,1152]{2,1,0:T(8,128)(2,1)S(1)}, bf16[2,64,1152]{2,1,0:T(8,128)(2,1)S(1)}, u32[]{:S(2)}, u32[]{:S(2)}) %collective-permute-start.6) | collective-permute-done | bytes 294944 | tf_op jit(solution)/shard_map/ppermute | solution.py:104
  45.3 0.0 collective-permute-done.13.refs_6_
  45.3 0.0 collective-permute-done.12.refs_4_
  45.3 0.0 copy-done
  45.3 2.1 %shard_map.57.mine_ref.refs_7_ = bf16[608,1152]{1,0:T(8,128)(2,1)S(1)} custom-call(bf16[256,1152]{1,0:T(8,128)(2,1)S(1)} %shard_map.56.refs_0_, bf16[256,1152]{1,0:T(8,128)(2,1)S(1)} %collective-permute-done.10.refs_1_, bf16[288,3456]{1,0:T(8,128)(2,1)S(1)} %copy-done, bf16[4,80,1152]{2,1,0:T(8,128)(2,1)S(1)} %constant_dynamic-update-slice_fusion.9.refs_3_, ...), custom_call_target="tpu_custom_call" | custom-call | flops 1358954496 | bytes 2654208 | tf_op jit(solution)/shard_map/pallas_call | solution.py:164
  47.5 0.0 collective-permute-done.5
  47.5 0.1 collective-permute-start.14
  47.7 0.6 collective-permute-start.7
  48.3 0.1 pad_maximum_fusion
  48.4 0.6 collective-permute-start.8
  49.0 0.4 collective-permute-start.9
  49.4 1.3 %collective-permute-done.14.other_ref.refs_8_ = bf16[608,1152]{1,0:T(8,128)(2,1)S(1)} collective-permute-done((bf16[608,1152]{1,0:T(8,128)(2,1)S(1)}, bf16[608,1152]{1,0:T(8,128)(2,1)S(1)}, u32[]{:S(2)}, u32[]{:S(2)}) %collective-permute-start.14) | collective-permute-done | bytes 1400864 | tf_op jit(solution)/shard_map/ppermute | solution.py:108
  50.7 0.9 %shard_map.58 = (bf16[256,1152]{1,0:T(8,128)(2,1)S(1)}, bf16[1,64,1152]{2,1,0:T(8,128)(2,1)S(1)}, bf16[1,64,1152]{2,1,0:T(8,128)(2,1)S(1)}, f32[9,32,128]{2,1,0:T(8,128)S(1)}, bf16[9,32,128]{2,1,0:T(8,128)(2,1)S(1)}) custom-call(bf16[608,1152]{1,0:T(8,128)(2,1)S(1)} %shard_map.57.mine_ref.refs_7_, bf16[608,1152]{1,0:T(8,128)(2,1)S(1)} %collective-permute-done.14.other_ref.refs_8_), custom_call_target="tpu_custom_call" | custom-call | flops 150994944 | bytes 2359296 | tf_op jit(solution)/shard_map/pallas_call | solution.py:164
  51.6 0.0 copy-start.4
  51.6 0.0 copy-start.1
  51.6 0.4 collective-permute-done.7.refs_4_
  52.0 2.4 %collective-permute-start.15 = (bf16[9,32,128]{2,1,0:T(8,128)(2,1)S(1)}, bf16[9,32,128]{2,1,0:T(8,128)(2,1)S(1)}, u32[]{:S(2)}, u32[]{:S(2)}) collective-permute-start(bf16[9,32,128]{2,1,0:T(8,128)(2,1)S(1)} %get-tuple-element.44), channel_id=1, source_target_pairs={{0,8},{4,12},{16,24},{20,28},{1,9},{5,13},{17,25},{21,29},{2,10},{... | collective-permute-start | bytes 221192 | tf_op jit(solution)/shard_map/ppermute | solution.py:531
  54.4 2.9 %collective-permute-start.16 = (bf16[9,32,128]{2,1,0:T(8,128)(2,1)S(1)}, bf16[9,32,128]{2,1,0:T(8,128)(2,1)S(1)}, u32[]{:S(2)}, u32[]{:S(2)}) collective-permute-start(bf16[9,32,128]{2,1,0:T(8,128)(2,1)S(1)} %get-tuple-element.44), channel_id=1, source_target_pairs={{0,16},{4,20},{8,24},{12,28},{1,17},{5,21},{9,25},{13,29},{2,18},{... | collective-permute-start | bytes 221192 | tf_op jit(solution)/shard_map/ppermute | solution.py:531
  57.4 1.3 %collective-permute-start.17 = (bf16[9,32,128]{2,1,0:T(8,128)(2,1)S(1)}, bf16[9,32,128]{2,1,0:T(8,128)(2,1)S(1)}, u32[]{:S(2)}, u32[]{:S(2)}) collective-permute-start(bf16[9,32,128]{2,1,0:T(8,128)(2,1)S(1)} %get-tuple-element.44), channel_id=1, source_target_pairs={{0,24},{4,28},{8,16},{12,20},{1,25},{5,29},{9,17},{13,21},{2,26},{... | collective-permute-start | bytes 221192 | tf_op jit(solution)/shard_map/ppermute | solution.py:531
  58.7 2.8 %collective-permute-done.8 = bf16[3,64,1152]{2,1,0:T(8,128)(2,1)S(1)} collective-permute-done((bf16[3,64,1152]{2,1,0:T(8,128)(2,1)S(1)}, bf16[3,64,1152]{2,1,0:T(8,128)(2,1)S(1)}, u32[]{:S(2)}, u32[]{:S(2)}) %collective-permute-start.8) | collective-permute-done | bytes 442400 | tf_op jit(solution)/shard_map/ppermute | solution.py:108
  61.5 0.0 collective-permute-done.15
  61.5 0.3 collective-permute-done.16
  61.7 0.1 collective-permute-done.17
  61.9 0.0 collective-permute-done.9
  61.9 0.1 collective-permute-start.18
  62.1 3.9 %collective-permute-start.19 = (bf16[1,64,1152]{2,1,0:T(8,128)(2,1)S(1)}, bf16[1,64,1152]{2,1,0:T(8,128)(2,1)S(1)}, u32[]{:S(2)}, u32[]{:S(2)}) collective-permute-start(bf16[1,64,1152]{2,1,0:T(8,128)(2,1)S(1)} %get-tuple-element.47), channel_id=1, source_target_pairs={{0,1},{1,2},{2,3},{4,5},{5,6},{6,7},{8,9},{9,10},{10,11},{12,13},{... | collective-permute-start | bytes 442376 | tf_op jit(solution)/shard_map/ppermute | solution.py:535
  66.0 0.4 collective-permute-done.18
  66.4 2.3 %collective-permute-done.19.above_ref = bf16[1,64,1152]{2,1,0:T(8,128)(2,1)S(1)} collective-permute-done((bf16[1,64,1152]{2,1,0:T(8,128)(2,1)S(1)}, bf16[1,64,1152]{2,1,0:T(8,128)(2,1)S(1)}, u32[]{:S(2)}, u32[]{:S(2)}) %collective-permute-start.19) | collective-permute-done | bytes 147488 | tf_op jit(solution)/shard_map/ppermute | solution.py:535
  68.6 0.0 collective-permute-start.20
  68.6 1.3 %collective-permute-start.22 = (bf16[1,64,1152]{2,1,0:T(8,128)(2,1)S(1)}, bf16[1,64,1152]{2,1,0:T(8,128)(2,1)S(1)}, u32[]{:S(2)}, u32[]{:S(2)}) collective-permute-start(bf16[1,64,1152]{2,1,0:T(8,128)(2,1)S(1)} %get-tuple-element.54), channel_id=1, source_target_pairs={{1,0},{2,1},{3,2},{5,4},{6,5},{7,6},{9,8},{10,9},{11,10},{13,12},{... | collective-permute-start | bytes 442376 | tf_op jit(solution)/shard_map/ppermute | solution.py:541
  69.9 4.6 %collective-permute-start.21 = (bf16[9,32,128]{2,1,0:T(8,128)(2,1)S(1)}, bf16[9,32,128]{2,1,0:T(8,128)(2,1)S(1)}, u32[]{:S(2)}, u32[]{:S(2)}) collective-permute-start(bf16[9,32,128]{2,1,0:T(8,128)(2,1)S(1)} %add_convert_fusion), channel_id=1, source_target_pairs={{0,2},{1,3},{2,0},{3,1},{4,6},{5,7},{6,4},{7,5},{8,10},{9,11},{10,... | collective-permute-start | bytes 221192 | tf_op jit(solution)/shard_map/ppermute | solution.py:540
  74.5 0.0 copy-done.4
  74.6 0.0 collective-permute-done.20.refs_6_
  74.6 0.0 copy-done.1
  74.6 1.5 %shard_map.59 = (bf16[256,1152]{1,0:T(8,128)(2,1)S(1)}, bf16[1152,1152]{1,0:T(8,128)(2,1)S(1)}) custom-call(bf16[256,1152]{1,0:T(8,128)(2,1)S(1)} %shard_map.56.refs_0_, bf16[288,3456]{1,0:T(8,128)(2,1)S(1)} %copy-done, bf16[288,1152]{1,0:T(8,128)(2,1)S(1)} %copy-done.1, bf16[6,64,1152]{2,1,0:T(8,128)(2,1)S(1)} %constant_dynamic-update-slice_fusion.2.refs_3_, ...), custom_call_target="tpu_custom_call" | custom-call | flops 679477248 | bytes 5308416 | tf_op jit(solution)/shard_map/pallas_call | solution.py:164
  76.1 1.4 %collective-permute-done.22.below_ref = bf16[1,64,1152]{2,1,0:T(8,128)(2,1)S(1)} collective-permute-done((bf16[1,64,1152]{2,1,0:T(8,128)(2,1)S(1)}, bf16[1,64,1152]{2,1,0:T(8,128)(2,1)S(1)}, u32[]{:S(2)}, u32[]{:S(2)}) %collective-permute-start.22) | collective-permute-done | bytes 147488 | tf_op jit(solution)/shard_map/ppermute | solution.py:541
  77.5 0.0 copy-done.2
  77.5 0.9 %shard_map.60 = f32[4,64,1152]{2,1,0:T(8,128)S(1)} custom-call(bf16[4,64,1152]{2,1,0:T(8,128)(2,1)S(1)} %bitcast.6, bf16[1,64,1152]{2,1,0:T(8,128)(2,1)S(1)} %collective-permute-done.19.above_ref, bf16[1,64,1152]{2,1,0:T(8,128)(2,1)S(1)} %collective-permute-done.22.below_ref, f32[3,3,1152]{2,1,0:T(4,128)S(1)} %copy-done.2), custom_call_target="tpu_custom_call" | custom-call | flops 5308416 | bytes 1769472 | tf_op jit(solution)/shard_map/pallas_call | solution.py:164
  78.5 3.4 %collective-permute-done.21 = bf16[9,32,128]{2,1,0:T(8,128)(2,1)S(1)} collective-permute-done((bf16[9,32,128]{2,1,0:T(8,128)(2,1)S(1)}, bf16[9,32,128]{2,1,0:T(8,128)(2,1)S(1)}, u32[]{:S(2)}, u32[]{:S(2)}) %collective-permute-start.21) | collective-permute-done | bytes 73760 | tf_op jit(solution)/shard_map/ppermute | solution.py:540
  81.9 2.3 %shard_map.61 = bf16[256,1152]{1,0:T(8,128)(2,1)} custom-call(bf16[256,1152]{1,0:T(8,128)(2,1)S(1)} %get-tuple-element.50.queries_ref, bf16[1152,1152]{1,0:T(8,128)(2,1)S(1)} %get-tuple-element.51.weight_ref, f32[9,32,128]{2,1,0:T(8,128)S(1)} %convert_add_fusion.state_ref, f32[256,1152]{1,0:T(8,128)S(1)} %bitcast.5, f32[1,1152]{1,0:T(1,128)S(1)} %broadcast_in_dim.7.gain_ref), custom_call_target="tpu_custom_call" | custom-call | flops 679477248 | bytes 2654208 | tf_op jit(solution)/shard_map/pallas_call | solution.py:164
  (20 shorter events, 0.4 us)
Async XLA Ops:
  0.0 7.1 %copy-start.3 = (bf16[1,4,64,1152]{3,2,1,0:T(8,128)(2,1)S(1)}, bf16[1,4,64,1152]{3,2,1,0:T(8,128)(2,1)}, u32[]{:S(2)}) copy-start(bf16[1,4,64,1152]{3,2,1,0:T(8,128)(2,1)} %param.5) | copy-start | bytes 1769476
  2.0 10.8 %collective-permute-start = (bf16[1,80,1152]{2,1,0:T(8,128)(2,1)}, bf16[1,80,1152]{2,1,0:T(8,128)(2,1)S(1)}, u32[]{:S(2)}, u32[]{:S(2)}) collective-permute-start(bf16[1,80,1152]{2,1,0:T(8,128)(2,1)} %bitcast.8), channel_id=1, source_target_pairs={{0,1},{1,2},{2,3},{3,0},{4,5},{5,6},{6,7},{7,4},{8,9},{9,10},{10,1... | collective-permute-start | bytes 552968 | tf_op jit(solution)/shard_map/ppermute | solution.py:104
  5.0 10.3 %collective-permute-start.1 = (bf16[1,80,1152]{2,1,0:T(8,128)(2,1)}, bf16[1,80,1152]{2,1,0:T(8,128)(2,1)S(1)}, u32[]{:S(2)}, u32[]{:S(2)}) collective-permute-start(bf16[1,80,1152]{2,1,0:T(8,128)(2,1)} %bitcast.9), channel_id=1, source_target_pairs={{0,3},{1,0},{2,1},{3,2},{4,7},{5,4},{6,5},{7,6},{8,11},{9,8},{10,9... | collective-permute-start | bytes 552968 | tf_op jit(solution)/shard_map/ppermute | solution.py:104
  7.1 10.9 %copy-start.5 = (bf16[2,64,1152]{2,1,0:T(8,128)(2,1)S(1)}, bf16[2,64,1152]{2,1,0:T(8,128)(2,1)}, u32[]{:S(2)}) copy-start(bf16[2,64,1152]{2,1,0:T(8,128)(2,1)} %get-tuple-element.36) | copy-start | bytes 884740
  8.3 37.0 %copy-start = (bf16[288,3456]{1,0:T(8,128)(2,1)S(1)}, bf16[288,3456]{1,0:T(8,128)(2,1)}, u32[]{:S(2)}) copy-start(bf16[288,3456]{1,0:T(8,128)(2,1)} %refs_1_.1) | copy-start | bytes 5971972
  8.3 18.4 %collective-permute-start.10 = (bf16[256,1152]{1,0:T(8,128)(2,1)S(1)}, bf16[256,1152]{1,0:T(8,128)(2,1)S(1)}, u32[]{:S(2)}, u32[]{:S(2)}) collective-permute-start(bf16[256,1152]{1,0:T(8,128)(2,1)S(1)} %shard_map.56.refs_0_), channel_id=1, source_target_pairs={{0,4},{4,0},{8,12},{12,8},{16,20},{20,16},{24,28},{28,24},{1,5},{5... | collective-permute-start | bytes 1769480 | tf_op jit(solution)/shard_map/ppermute | solution.py:108
  15.3 11.4 %collective-permute-start.11 = (bf16[2,80,1152]{2,1,0:T(8,128)(2,1)S(1)}, bf16[2,80,1152]{2,1,0:T(8,128)(2,1)S(1)}, u32[]{:S(2)}, u32[]{:S(2)}) collective-permute-start(bf16[2,80,1152]{2,1,0:T(8,128)(2,1)S(1)} %constant_dynamic-update-slice_fusion.7), channel_id=1, source_target_pairs={{0,8},{4,20},{8,0},{12,28},{16,24},{20,4},{24,16},{28,12},{1,9},{5... | collective-permute-start | bytes 1105928 | tf_op jit(solution)/shard_map/ppermute | solution.py:108
  16.9 9.4 %collective-permute-start.3 = (bf16[1,80,1152]{2,1,0:T(8,128)(2,1)S(1)}, bf16[1,80,1152]{2,1,0:T(8,128)(2,1)S(1)}, u32[]{:S(2)}, u32[]{:S(2)}) collective-permute-start(bf16[1,80,1152]{2,1,0:T(8,128)(2,1)S(1)} %collective-permute-done), channel_id=1, source_target_pairs={{0,1},{1,2},{2,3},{3,0},{4,5},{5,6},{6,7},{7,4},{8,9},{9,10},{10,1... | collective-permute-start | bytes 552968 | tf_op jit(solution)/shard_map/ppermute | solution.py:104
  18.0 17.6 %collective-permute-start.2 = (bf16[2,64,1152]{2,1,0:T(8,128)(2,1)S(1)}, bf16[2,64,1152]{2,1,0:T(8,128)(2,1)S(1)}, u32[]{:S(2)}, u32[]{:S(2)}) collective-permute-start(bf16[2,64,1152]{2,1,0:T(8,128)(2,1)S(1)} %copy-done.5), channel_id=1, source_target_pairs={{0,1},{1,2},{2,3},{3,0},{4,5},{5,6},{6,7},{7,4},{8,9},{9,10},{10,1... | collective-permute-start | bytes 884744 | tf_op jit(solution)/shard_map/ppermute | solution.py:104
  26.3 7.6 %collective-permute-start.4 = (bf16[1,80,1152]{2,1,0:T(8,128)(2,1)S(1)}, bf16[1,80,1152]{2,1,0:T(8,128)(2,1)S(1)}, u32[]{:S(2)}, u32[]{:S(2)}) collective-permute-start(bf16[1,80,1152]{2,1,0:T(8,128)(2,1)S(1)} %collective-permute-done.3), channel_id=1, source_target_pairs={{0,8},{4,20},{8,0},{12,28},{16,24},{20,4},{24,16},{28,12},{1,9},{5... | collective-permute-start | bytes 552968 | tf_op jit(solution)/shard_map/ppermute | solution.py:108
  26.8 18.5 %collective-permute-start.12 = (bf16[4,80,1152]{2,1,0:T(8,128)(2,1)S(1)}, bf16[4,80,1152]{2,1,0:T(8,128)(2,1)S(1)}, u32[]{:S(2)}, u32[]{:S(2)}) collective-permute-start(bf16[4,80,1152]{2,1,0:T(8,128)(2,1)S(1)} %constant_dynamic-update-slice_fusion.9.refs_3_), channel_id=1, source_target_pairs={{0,16},{4,12},{8,24},{12,4},{16,0},{20,28},{24,8},{28,20},{1,17},{... | collective-permute-start | bytes 2211848 | tf_op jit(solution)/shard_map/ppermute | solution.py:108
  33.9 11.5 %collective-permute-start.13 = (bf16[2,80,1152]{2,1,0:T(8,128)(2,1)S(1)}, bf16[2,80,1152]{2,1,0:T(8,128)(2,1)S(1)}, u32[]{:S(2)}, u32[]{:S(2)}) collective-permute-start(bf16[2,80,1152]{2,1,0:T(8,128)(2,1)S(1)} %constant_dynamic-update-slice_fusion.refs_5_), channel_id=1, source_target_pairs={{0,16},{4,12},{8,24},{12,4},{16,0},{20,28},{24,8},{28,20},{1,17},{... | collective-permute-start | bytes 1105928 | tf_op jit(solution)/shard_map/ppermute | solution.py:108
  35.4 9.9 %collective-permute-start.6 = (bf16[2,64,1152]{2,1,0:T(8,128)(2,1)S(1)}, bf16[2,64,1152]{2,1,0:T(8,128)(2,1)S(1)}, u32[]{:S(2)}, u32[]{:S(2)}) collective-permute-start(bf16[2,64,1152]{2,1,0:T(8,128)(2,1)S(1)} %copy-done.5), channel_id=1, source_target_pairs={{0,3},{1,0},{2,1},{3,2},{4,7},{5,4},{6,5},{7,6},{8,11},{9,8},{10,9... | collective-permute-start | bytes 884744 | tf_op jit(solution)/shard_map/ppermute | solution.py:104
  35.6 11.9 %collective-permute-start.5 = (bf16[2,64,1152]{2,1,0:T(8,128)(2,1)S(1)}, bf16[2,64,1152]{2,1,0:T(8,128)(2,1)S(1)}, u32[]{:S(2)}, u32[]{:S(2)}) collective-permute-start(bf16[2,64,1152]{2,1,0:T(8,128)(2,1)S(1)} %collective-permute-done.2), channel_id=1, source_target_pairs={{0,1},{1,2},{2,3},{3,0},{4,5},{5,6},{6,7},{7,4},{8,9},{9,10},{10,1... | collective-permute-start | bytes 884744 | tf_op jit(solution)/shard_map/ppermute | solution.py:104
  47.5 3.2 %collective-permute-start.14 = (bf16[608,1152]{1,0:T(8,128)(2,1)S(1)}, bf16[608,1152]{1,0:T(8,128)(2,1)S(1)}, u32[]{:S(2)}, u32[]{:S(2)}) collective-permute-start(bf16[608,1152]{1,0:T(8,128)(2,1)S(1)} %shard_map.57.mine_ref.refs_7_), channel_id=1, source_target_pairs={{0,4},{4,0},{8,12},{12,8},{16,20},{20,16},{24,28},{28,24},{1,5},{5... | collective-permute-start | bytes 4202504 | tf_op jit(solution)/shard_map/ppermute | solution.py:108
  47.7 4.3 %collective-permute-start.7 = (bf16[6,64,1152]{2,1,0:T(8,128)(2,1)S(1)}, bf16[6,64,1152]{2,1,0:T(8,128)(2,1)S(1)}, u32[]{:S(2)}, u32[]{:S(2)}) collective-permute-start(bf16[6,64,1152]{2,1,0:T(8,128)(2,1)S(1)} %constant_dynamic-update-slice_fusion.2.refs_3_), channel_id=1, source_target_pairs={{0,4},{4,0},{8,12},{12,8},{16,20},{20,16},{24,28},{28,24},{1,5},{5... | collective-permute-start | bytes 2654216 | tf_op jit(solution)/shard_map/ppermute | solution.py:108
  48.4 13.1 %collective-permute-start.8 = (bf16[3,64,1152]{2,1,0:T(8,128)(2,1)S(1)}, bf16[3,64,1152]{2,1,0:T(8,128)(2,1)S(1)}, u32[]{:S(2)}, u32[]{:S(2)}) collective-permute-start(bf16[3,64,1152]{2,1,0:T(8,128)(2,1)S(1)} %pad_maximum_fusion), channel_id=1, source_target_pairs={{0,8},{4,20},{8,0},{12,28},{16,24},{20,4},{24,16},{28,12},{1,9},{5... | collective-permute-start | bytes 1327112 | tf_op jit(solution)/shard_map/ppermute | solution.py:108
  49.0 13.0 %collective-permute-start.9 = (bf16[3,64,1152]{2,1,0:T(8,128)(2,1)S(1)}, bf16[3,64,1152]{2,1,0:T(8,128)(2,1)S(1)}, u32[]{:S(2)}, u32[]{:S(2)}) collective-permute-start(bf16[3,64,1152]{2,1,0:T(8,128)(2,1)S(1)} %pad_maximum_fusion), channel_id=1, source_target_pairs={{0,16},{4,12},{8,24},{12,4},{16,0},{20,28},{24,8},{28,20},{1,17},{... | collective-permute-start | bytes 1327112 | tf_op jit(solution)/shard_map/ppermute | solution.py:108
  51.6 22.9 %copy-start.4 = (f32[1152]{0:T(1024)S(1)}, f32[1152]{0:T(1024)}, u32[]{:S(2)}) copy-start(f32[1152]{0:T(1024)} %param.9) | copy-start | bytes 13828
  51.6 23.0 %copy-start.1 = (bf16[288,1152]{1,0:T(8,128)(2,1)S(1)}, bf16[288,1152]{1,0:T(8,128)(2,1)}, u32[]{:S(2)}) copy-start(bf16[288,1152]{1,0:T(8,128)(2,1)} %refs_2_.3) | copy-start | bytes 1990660
  52.0 9.5 %collective-permute-start.15 = (bf16[9,32,128]{2,1,0:T(8,128)(2,1)S(1)}, bf16[9,32,128]{2,1,0:T(8,128)(2,1)S(1)}, u32[]{:S(2)}, u32[]{:S(2)}) collective-permute-start(bf16[9,32,128]{2,1,0:T(8,128)(2,1)S(1)} %get-tuple-element.44), channel_id=1, source_target_pairs={{0,8},{4,12},{16,24},{20,28},{1,9},{5,13},{17,25},{21,29},{2,10},{... | collective-permute-start | bytes 221192 | tf_op jit(solution)/shard_map/ppermute | solution.py:531
  54.4 7.3 %collective-permute-start.16 = (bf16[9,32,128]{2,1,0:T(8,128)(2,1)S(1)}, bf16[9,32,128]{2,1,0:T(8,128)(2,1)S(1)}, u32[]{:S(2)}, u32[]{:S(2)}) collective-permute-start(bf16[9,32,128]{2,1,0:T(8,128)(2,1)S(1)} %get-tuple-element.44), channel_id=1, source_target_pairs={{0,16},{4,20},{8,24},{12,28},{1,17},{5,21},{9,25},{13,29},{2,18},{... | collective-permute-start | bytes 221192 | tf_op jit(solution)/shard_map/ppermute | solution.py:531
  57.4 4.5 %collective-permute-start.17 = (bf16[9,32,128]{2,1,0:T(8,128)(2,1)S(1)}, bf16[9,32,128]{2,1,0:T(8,128)(2,1)S(1)}, u32[]{:S(2)}, u32[]{:S(2)}) collective-permute-start(bf16[9,32,128]{2,1,0:T(8,128)(2,1)S(1)} %get-tuple-element.44), channel_id=1, source_target_pairs={{0,24},{4,28},{8,16},{12,20},{1,25},{5,29},{9,17},{13,21},{2,26},{... | collective-permute-start | bytes 221192 | tf_op jit(solution)/shard_map/ppermute | solution.py:531
  61.9 4.4 %collective-permute-start.18 = (bf16[9,32,128]{2,1,0:T(8,128)(2,1)S(1)}, bf16[9,32,128]{2,1,0:T(8,128)(2,1)S(1)}, u32[]{:S(2)}, u32[]{:S(2)}) collective-permute-start(bf16[9,32,128]{2,1,0:T(8,128)(2,1)S(1)} %convert_add_fusion.1), channel_id=1, source_target_pairs={{0,1},{1,0},{2,3},{3,2},{4,5},{5,4},{6,7},{7,6},{8,9},{9,8},{10,11... | collective-permute-start | bytes 221192 | tf_op jit(solution)/shard_map/ppermute | solution.py:537
  62.1 6.6 %collective-permute-start.19 = (bf16[1,64,1152]{2,1,0:T(8,128)(2,1)S(1)}, bf16[1,64,1152]{2,1,0:T(8,128)(2,1)S(1)}, u32[]{:S(2)}, u32[]{:S(2)}) collective-permute-start(bf16[1,64,1152]{2,1,0:T(8,128)(2,1)S(1)} %get-tuple-element.47), channel_id=1, source_target_pairs={{0,1},{1,2},{2,3},{4,5},{5,6},{6,7},{8,9},{9,10},{10,11},{12,13},{... | collective-permute-start | bytes 442376 | tf_op jit(solution)/shard_map/ppermute | solution.py:535
  68.6 5.9 %collective-permute-start.20 = (bf16[6,64,1152]{2,1,0:T(8,128)(2,1)S(1)}, bf16[6,64,1152]{2,1,0:T(8,128)(2,1)S(1)}, u32[]{:S(2)}, u32[]{:S(2)}) collective-permute-start(bf16[6,64,1152]{2,1,0:T(8,128)(2,1)S(1)} %constant_dynamic-update-slice_fusion.5.refs_5_), channel_id=1, source_target_pairs={{0,4},{4,0},{8,12},{12,8},{16,20},{20,16},{24,28},{28,24},{1,5},{5... | collective-permute-start | bytes 2654216 | tf_op jit(solution)/shard_map/ppermute | solution.py:108
  68.6 8.9 %collective-permute-start.22 = (bf16[1,64,1152]{2,1,0:T(8,128)(2,1)S(1)}, bf16[1,64,1152]{2,1,0:T(8,128)(2,1)S(1)}, u32[]{:S(2)}, u32[]{:S(2)}) collective-permute-start(bf16[1,64,1152]{2,1,0:T(8,128)(2,1)S(1)} %get-tuple-element.54), channel_id=1, source_target_pairs={{1,0},{2,1},{3,2},{5,4},{6,5},{7,6},{9,8},{10,9},{11,10},{13,12},{... | collective-permute-start | bytes 442376 | tf_op jit(solution)/shard_map/ppermute | solution.py:541
  69.9 11.9 %collective-permute-start.21 = (bf16[9,32,128]{2,1,0:T(8,128)(2,1)S(1)}, bf16[9,32,128]{2,1,0:T(8,128)(2,1)S(1)}, u32[]{:S(2)}, u32[]{:S(2)}) collective-permute-start(bf16[9,32,128]{2,1,0:T(8,128)(2,1)S(1)} %add_convert_fusion), channel_id=1, source_target_pairs={{0,2},{1,3},{2,0},{3,1},{4,6},{5,7},{6,4},{7,5},{8,10},{9,11},{10,... | collective-permute-start | bytes 221192 | tf_op jit(solution)/shard_map/ppermute | solution.py:540
  74.5 3.0 %copy-start.2 = (f32[3,3,1152]{2,1,0:T(4,128)S(1)}, f32[3,3,1152]{2,1,0:T(4,128)}, u32[]{:S(2)}) copy-start(f32[3,3,1152]{2,1,0:T(4,128)} %conv_ref.1) | copy-start | bytes 124420

commit v5 on v4

--- a/solution.py
+++ b/solution.py
@@ -13,6 +13,7 @@
 MAIN = 64
 REST = 16
 STEPS = (1, 2, 3)
+FRAME_ROWS = 4
 VMEM_LIMIT = 24 * 1024 * 1024
 WHOLE_VMEM = 63 * 1024 * 1024
 
@@ -257,7 +258,7 @@
 
 
 def first_kernel(*refs):
-    tokens_ref, other_ref, qkv_ref, near_ref, away_ref, first_ref, far_ref, mine_ref = refs
+    tokens_ref, other_ref, qkv_ref, near_ref, away_ref, first_ref, far_ref, *results = refs
     slots = (
         ((near_ref, 0), (first_ref, 0), (near_ref, 1)),
         ((near_ref, 2), (first_ref, 1), (near_ref, 3)),
@@ -265,7 +266,7 @@
         ((away_ref, 2), (far_ref, 1), (away_ref, 3)),
     )
     _, x, core = coordinates()
-    count, depth = tokens_ref.shape
+    depth = tokens_ref.shape[1]
     floor = jnp.where(core == 0, 0.0, -jnp.inf).astype(jnp.float32)
     width = 3 * LANES
 
@@ -286,22 +287,27 @@
         rest = by_place(MAIN, MAIN + REST)
         even = jnp.concatenate([rest[0], rest[2]], axis=0)
         odd = jnp.concatenate([rest[1], rest[3]], axis=0)
-        mine_ref[2 * count :, lanes] = jnp.where(x == 1, even, odd)
+        for ref in results:
+            ref[-even.shape[0] :, lanes] = jnp.where(x == 1, even, odd)
         columns = jnp.concatenate(
             (own,) + by_place(0, MAIN) + (jnp.where(x == 0, even, odd),), axis=0
         )
         for k, ref in enumerate((tokens_ref, other_ref)):
             product = jnp.dot(ref[...], columns, preferred_element_type=jnp.float32)
             product = jnp.maximum(product, floor).astype(jnp.bfloat16)
-            mine_ref[k * count : (k + 1) * count, lanes] = product
+            count = FRAME_ROWS * product.shape[0] // (FRAME_ROWS + 2)
+            for result in results:
+                result[k * count : (k + 1) * count, lanes] = product[:count]
+            results[k][2 * count : count + product.shape[0], lanes] = product[count:]
 
 
 def first_call(tokens, other, qkv_weight, *landed):
     count, depth = tokens.shape
+    rows = 2 * (FRAME_ROWS + 1) * count // (FRAME_ROWS + 2) + 2 * len(STEPS) * REST
     inputs = (tokens, other, qkv_weight) + landed
     return kernel_call(
         first_kernel,
-        jax.ShapeDtypeStruct((2 * count + 2 * len(STEPS) * REST, depth), jnp.bfloat16),
+        [jax.ShapeDtypeStruct((rows, depth), jnp.bfloat16)] * 2,
         inputs,
         [whole_vmem()] * len(inputs),
         flops=4 * tokens.size * depth,
@@ -315,10 +321,9 @@
     return rows == columns
 
 
-def state_kernel(mine_ref, other_ref, values_ref, top_ref, bottom_ref, upto_ref, total_ref):
+def state_kernel(mine_ref, other_ref, values_ref, upto_ref, total_ref):
     _, _, core = coordinates()
     mask = diagonal_mask()
-    columns = top_ref.shape[1]
     count = values_ref.shape[0]
     later = jnp.where(core == 1, 1.0, 0.0).astype(jnp.float32)
     for group in range(mine_ref.shape[1] // LANES):
@@ -340,22 +345,17 @@
         here, values = state(mine_ref[low, at], other_ref[high, at])
         there, _ = state(mine_ref[high, at], other_ref[low, at])
         values_ref[:, at] = values
-        top_ref[0, :, at] = values[:columns]
-        bottom_ref[0, :, at] = values[-columns:]
         upto_ref[group] = here + later * there
         total_ref[group] = (here + there).astype(jnp.bfloat16)
 
 
-def state_call(mine, other, count, columns):
+def state_call(mine, other, count):
     depth = mine.shape[1]
     compact = (depth // LANES, HEAD_DIM, LANES)
-    edge = jax.ShapeDtypeStruct((1, columns, depth), jnp.bfloat16)
     return kernel_call(
         state_kernel,
         [
             jax.ShapeDtypeStruct((count, depth), jnp.bfloat16),
-            edge,
-            edge,
             jax.ShapeDtypeStruct(compact, jnp.float32),
             jax.ShapeDtypeStruct(compact, jnp.bfloat16),
         ],
@@ -366,14 +366,17 @@
     )
 
 
-def local_kernel(values_ref, above_ref, below_ref, conv_ref, local_ref):
+def local_kernel(values_ref, mine_ref, other_ref, conv_ref, local_ref):
     rows, columns, depth = values_ref.shape
+    _, _, core = coordinates()
+    at_halo = 2 * rows * columns
     for at in range(0, depth, LANES):
         lanes = slice(at, at + LANES)
         taps = conv_ref[:, :, lanes]
-        sheet = jnp.concatenate(
-            [above_ref[:, :, lanes], values_ref[:, :, lanes], below_ref[:, :, lanes]], axis=0
-        ).astype(jnp.float32)
+        halos = [ref[at_halo : at_halo + 2 * columns, lanes] for ref in (mine_ref, other_ref)]
+        halo = jnp.where(core == 1, *halos).reshape(2, columns, LANES)
+        sheet = jnp.concatenate([halo[:1], values_ref[:, :, lanes], halo[1:]], axis=0)
+        sheet = sheet.astype(jnp.float32)
         edge = jnp.zeros((rows + 2, 1, LANES), jnp.float32)
         before = jnp.concatenate([edge, sheet[:, :-1]], axis=1)
         behind = jnp.concatenate([sheet[:, 1:], edge], axis=1)
@@ -384,11 +387,11 @@
         local_ref[:, :, lanes] = total
 
 
-def local_call(values, above, below, conv_weight):
+def local_call(values, mine, other, conv_weight):
     return kernel_call(
         local_kernel,
         jax.ShapeDtypeStruct(values.shape, jnp.float32),
-        (values, above, below, conv_weight),
+        (values, mine, other, conv_weight),
         [whole_vmem()] * 4,
         flops=18 * values.size,
         bytes_accessed=6 * values.size,
@@ -423,7 +426,9 @@
         order += [(0, 2 * k + 1) for k in range(steps)]
         columns = [qkv_ref[:, lanes]] + [block(0, k, lanes) for k in order] + [rest(0, lanes)]
         queries = jnp.dot(
-            tokens_ref[...], jnp.concatenate(columns, axis=0), preferred_element_type=jnp.float32
+            tokens_ref[: query_ref.shape[0]],
+            jnp.concatenate(columns, axis=0),
+            preferred_element_type=jnp.float32,
         )
         query_ref[:, lanes] = jnp.maximum(queries, 0.0).astype(jnp.bfloat16)
 
@@ -439,13 +444,13 @@
                 put(base + 4 * MAIN + tile * REST, tiles[start : start + REST], lanes)
 
 
-def query_call(tokens, qkv_weight, out_weight, *landed):
+def query_call(count, tokens, qkv_weight, out_weight, *landed):
     depth = tokens.shape[1]
     inputs = (tokens, qkv_weight, out_weight) + landed
     return kernel_call(
         query_kernel,
         [
-            jax.ShapeDtypeStruct(tokens.shape, jnp.bfloat16),
+            jax.ShapeDtypeStruct((count, depth), jnp.bfloat16),
             jax.ShapeDtypeStruct((depth, depth), jnp.bfloat16),
         ],
         inputs,
@@ -496,16 +501,22 @@
 
     first_piece, second_piece = pieces_call(qkv_weight, out_weight)
     first_piece = first_piece[None]
+    planes = lax.axis_size("space")
+    forward = [(i, i + 1) for i in range(planes - 1)]
+    backward = [(target, source) for source, target in forward]
+    above = lax.ppermute(tokens[-col_count:], "space", forward)
+    below = lax.ppermute(tokens[:col_count], "space", backward)
     one = shifted(first_piece, 1)
     three = shifted(first_piece, -1)
-    tokens = reorder_call(after(tokens, second_piece), qkv_weight.shape[0])
-    other_tokens = flipped(tokens, (1, 1))
-    one, three = after((one, three), tokens)
+    landed = jnp.concatenate([tokens, above, below])
+    landed = reorder_call(after(landed, second_piece), qkv_weight.shape[0])
+    other_landed = flipped(landed, (1, 1))
+    one, three = after((one, three), landed)
 
     pair = jnp.concatenate([one, three])
     two = shifted(one, 1)
     pair_first = flipped(pair, (2, 4))
-    near = jnp.concatenate(after((pair, pair_first), other_tokens))
+    near = jnp.concatenate(after((pair, pair_first), other_landed))
     away = flipped(near, (4, 2))
     two_near = jnp.concatenate([two, flipped(two, (2, 4))])
     two_away = flipped(two_near, (4, 2))
@@ -515,12 +526,22 @@
     second_three = shifted(second_ready, -1)
     second_two = shifted(after(second_one, two_near), 1)
 
-    mine = first_call(after(tokens, second_one, second_three), other_tokens, qkv_weight, near, away, two_near, two_away)
-    other = flipped(after(mine, second_two), (1, 1))
+    mine, sent = first_call(
+        after(landed, second_one, second_three),
+        other_landed,
+        qkv_weight,
+        near,
+        away,
+        two_near,
+        two_away,
+    )
+    other = flipped(after(sent, second_two), (1, 1))
     straight = jnp.concatenate([second_one, second_two, second_three])
     swapped_straight = flipped(straight, (1, 1))
-    values, top, bottom, upto, total = state_call(mine, other, tokens.shape[0], col_count)
+    values, upto, total = state_call(mine, other, tokens.shape[0])
     total = after(total, swapped_straight)
+    grid = values.reshape(row_count, col_count, depth)
+    local_term = local_call(grid, mine, other, conv_weight).reshape(-1, depth)
 
     second_own = jnp.stack([second_one[0], second_two[0], second_three[0]])
     second_first = flipped(second_own, (2, 4))
@@ -529,21 +550,11 @@
     for bit, guard in ((2, 2), (4, 4), (6, 4)):
         pairs = [(t, t ^ bit) for t in range(8) if not t & guard]
         upto = upto + lax.ppermute(total, "tm", pairs).astype(jnp.float32)
-    count = lax.axis_size("space")
-    forward = [(i, i + 1) for i in range(count - 1)]
-    backward = [(target, source) for source, target in forward]
-    above = lax.ppermute(after(bottom, upto), "space", forward)
-    share = after(upto, second_first, second_second).astype(jnp.bfloat16)
-    arrived = lax.ppermute(share, "space", [(i, i ^ 1) for i in range(count)])
-    share = (share.astype(jnp.float32) + arrived.astype(jnp.float32)).astype(jnp.bfloat16)
-    share = after(share, above)
-    arrived = lax.ppermute(share, "space", [(i, i ^ 2) for i in range(count)])
-    below = lax.ppermute(after(top, share), "space", backward)
-
-    turned = jnp.concatenate([second_first, second_second])
-    swapped_turned = flipped(after(turned, share), (1, 1))
+    turned = jnp.concatenate(after((second_first, second_second), upto))
+    swapped_turned = flipped(after(turned, upto), (1, 1))
     queries, weight = query_call(
-        tokens,
+        tokens.shape[0],
+        landed,
         qkv_weight,
         out_weight,
         straight,
@@ -553,9 +564,11 @@
         mine,
         other,
     )
-    grid = values.reshape(row_count, col_count, depth)
-    local_term = local_call(grid, above, after(below, queries), conv_weight).reshape(-1, depth)
-    arrived = after(arrived, local_term)
+    share = after(upto, turned).astype(jnp.bfloat16)
+    arrived = lax.ppermute(share, "space", [(i, i ^ 1) for i in range(planes)])
+    share = (share.astype(jnp.float32) + arrived.astype(jnp.float32)).astype(jnp.bfloat16)
+    arrived = lax.ppermute(share, "space", [(i, i ^ 2) for i in range(planes)])
+    arrived = after(arrived, queries, weight, local_term)
     state = share.astype(jnp.float32) + arrived.astype(jnp.float32)
     result = finish_call(queries, weight, state, local_term, norm_gain[None])
     return result.reshape(1, row_count, col_count, depth)

time: 84.4 us -> 83.8 us (level)
  starting transfers between devices: 32.6 us -> 29 us
  local copies, waits for them, and re-layouts: 0.38 us -> 2.18 us
  Pallas kernels: 11 us -> 12.4 us
    ppermute x4, starting transfers between devices: 9.88 us -> 7.07 us  [the longest x1 5.56 us: plane_form(): above = lax.ppermute(tokens[-col_count:], 'space', forward)]
    ppermute x10, waiting for transfers between devices: 9.82 us -> 7.47 us  [flipped(): lax.ppermute(value, 'tm', [(t, t ^ bit_on_core[t % 2]) for t in range(8)])]
    ppermute x3, waiting for transfers between devices: 0.4 us -> 2.38 us  [plane_form(): upto = upto + lax.ppermute(total, 'tm', pairs).astype(jnp.float32)]
    slice x0 -> x1, local copies, waits for them, and re-layouts: none -> 1.79 us  [plane_form(): above = lax.ppermute(tokens[-col_count:], 'space', forward)]
    pallas_call x7, Pallas kernels: 11 us -> 12.4 us  [kernel_call(): pl.pallas_call(body, out_shape=outputs, in_specs=in_specs, out_specs=jax....]
    ppermute x6, starting transfers between devices: 9.05 us -> 7.77 us  [shifted(): lax.ppermute(value, 'space', [(i, (i + step) % count) for i in range(coun...]
  transfers between devices with their start and end apart: 23 -> 23, of which waited for: 14 -> 12; matrix products, arithmetic and copies ran while one was open for 1% -> 1% of each run, Pallas kernels for 8% -> 12%
where the time goes in v5:
time: 83.8 us; the launch traced here: 83.5 us
  waiting for transfers between devices  39.4 us (47%)
  starting transfers between devices  29 us (35%)
  Pallas kernels  12.4 us (15%)
  local copies, waits for them, and re-layouts  2.18 us (3%)
    ppermute x6, waiting for transfers between devices, shifted(): lax.ppermute(value, 'space', [(i, (i + step) % count) for i in range(coun...  21.4 us
    pallas_call x7, Pallas kernels, kernel_call(): pl.pallas_call(body, out_shape=outputs, in_specs=in_specs, out_specs=jax....  12.4 us
    ppermute x6, starting transfers between devices, shifted(): lax.ppermute(value, 'space', [(i, (i + step) % count) for i in range(coun...  7.77 us
    ppermute x10, waiting for transfers between devices, flipped(): lax.ppermute(value, 'tm', [(t, t ^ bit_on_core[t % 2]) for t in range(8)])  7.47 us
    ppermute x3, starting transfers between devices, plane_form(): upto = upto + lax.ppermute(total, 'tm', pairs).astype(jnp.float32)  7.07 us
    ppermute x10, starting transfers between devices, flipped(): lax.ppermute(value, 'tm', [(t, t ^ bit_on_core[t % 2]) for t in range(8)])  7.06 us
    ppermute x1, starting transfers between devices, plane_form(): above = lax.ppermute(tokens[-col_count:], 'space', forward)  5.56 us
    ppermute x1, waiting for transfers between devices, plane_form(): arrived = lax.ppermute(share, 'space', [(i, i ^ 2) for i in range(planes)])  4.57 us
  transfers between devices with their start and end apart: 23, of which 12 were waited for; matrix products, arithmetic and copies ran while one was open for 1% of the time, Pallas kernels for 12%

profile of v5, /device:TPU:0, one launch (start us, length us, event | category | flops | bytes accessed | tf_op | source)
XLA Modules:
  0.0 83.5 jit_solution(7898856705368396505)
XLA Ops:
  0.0 1.8 %slice_bitcast_fusion.1 = (bf16[64,1152]{1,0:T(8,128)(2,1)}, bf16[64,1152]{1,0:T(8,128)(2,1)}) fusion(bf16[1,4,64,1152]{3,2,1,0:T(8,128)(2,1)} %param.5), kind=kLoop, calls=%fused_computation.6 | loop fusion | bytes 589824 | tf_op jit(solution)/shard_map/slice | solution.py:507
  1.8 1.3 %collective-permute-start.1 = (bf16[64,1152]{1,0:T(8,128)(2,1)}, bf16[64,1152]{1,0:T(8,128)(2,1)S(1)}, u32[]{:S(2)}, u32[]{:S(2)}) collective-permute-start(bf16[64,1152]{1,0:T(8,128)(2,1)} %get-tuple-element.54), channel_id=1, source_target_pairs={{1,0},{2,1},{3,2},{5,4},{6,5},{7,6},{9,8},{10,9},{11,10},{13,12},{... | collective-permute-start | bytes 442376 | tf_op jit(solution)/shard_map/ppermute | solution.py:508
  3.1 5.6 %collective-permute-start = (bf16[64,1152]{1,0:T(8,128)(2,1)}, bf16[64,1152]{1,0:T(8,128)(2,1)S(1)}, u32[]{:S(2)}, u32[]{:S(2)}) collective-permute-start(bf16[64,1152]{1,0:T(8,128)(2,1)} %get-tuple-element.53), channel_id=1, source_target_pairs={{0,1},{1,2},{2,3},{4,5},{5,6},{6,7},{8,9},{9,10},{10,11},{12,13},{... | collective-permute-start | bytes 442376 | tf_op jit(solution)/shard_map/ppermute | solution.py:507
  8.7 1.9 %shard_map.55 = (bf16[80,1152]{1,0:T(8,128)(2,1)}, bf16[2,64,1152]{2,1,0:T(8,128)(2,1)}) custom-call(bf16[288,3456]{1,0:T(8,128)(2,1)} %refs_1_.1, bf16[288,1152]{1,0:T(8,128)(2,1)} %refs_2_.3), custom_call_target="tpu_custom_call" | custom-call | bytes 958464 | tf_op jit(solution)/shard_map/pallas_call | solution.py:165
  10.6 2.1 %collective-permute-start.2 = (bf16[1,80,1152]{2,1,0:T(8,128)(2,1)}, bf16[1,80,1152]{2,1,0:T(8,128)(2,1)S(1)}, u32[]{:S(2)}, u32[]{:S(2)}) collective-permute-start(bf16[1,80,1152]{2,1,0:T(8,128)(2,1)} %bitcast.12), channel_id=1, source_target_pairs={{0,1},{1,2},{2,3},{3,0},{4,5},{5,6},{6,7},{7,4},{8,9},{9,10},{10,1... | collective-permute-start | bytes 552968 | tf_op jit(solution)/shard_map/ppermute | solution.py:105
  12.6 1.8 %collective-permute-start.3 = (bf16[1,80,1152]{2,1,0:T(8,128)(2,1)}, bf16[1,80,1152]{2,1,0:T(8,128)(2,1)S(1)}, u32[]{:S(2)}, u32[]{:S(2)}) collective-permute-start(bf16[1,80,1152]{2,1,0:T(8,128)(2,1)} %bitcast.13), channel_id=1, source_target_pairs={{0,3},{1,0},{2,1},{3,2},{4,7},{5,4},{6,5},{7,6},{8,11},{9,8},{10,9... | collective-permute-start | bytes 552968 | tf_op jit(solution)/shard_map/ppermute | solution.py:105
  14.4 0.0 collective-permute-done.1
  14.5 0.0 collective-permute-done
  14.5 0.0 copy-done.3
  14.5 0.1 pad_maximum_fusion.tokens_ref
  14.5 0.0 copy-start.5
  14.5 1.6 %shard_map.56.refs_0_ = bf16[384,1152]{1,0:T(8,128)(2,1)S(1)} custom-call(bf16[384,1152]{1,0:T(8,128)(2,1)S(1)} %pad_maximum_fusion.tokens_ref), custom_call_target="tpu_custom_call" | custom-call | flops 1019215872 | bytes 884736 | tf_op jit(solution)/shard_map/pallas_call | solution.py:165
  16.2 0.0 copy-start
  16.2 0.1 collective-permute-start.12
  16.3 4.0 %collective-permute-done.2 = bf16[1,80,1152]{2,1,0:T(8,128)(2,1)S(1)} collective-permute-done((bf16[1,80,1152]{2,1,0:T(8,128)(2,1)}, bf16[1,80,1152]{2,1,0:T(8,128)(2,1)S(1)}, u32[]{:S(2)}, u32[]{:S(2)}) %collective-permute-start.2) | collective-permute-done | bytes 184352 | tf_op jit(solution)/shard_map/ppermute | solution.py:105
  20.2 2.1 %collective-permute-done.3 = bf16[1,80,1152]{2,1,0:T(8,128)(2,1)S(1)} collective-permute-done((bf16[1,80,1152]{2,1,0:T(8,128)(2,1)}, bf16[1,80,1152]{2,1,0:T(8,128)(2,1)S(1)}, u32[]{:S(2)}, u32[]{:S(2)}) %collective-permute-start.3) | collective-permute-done | bytes 184352 | tf_op jit(solution)/shard_map/ppermute | solution.py:105
  22.4 1.6 %collective-permute-start.13 = (bf16[2,80,1152]{2,1,0:T(8,128)(2,1)S(1)}, bf16[2,80,1152]{2,1,0:T(8,128)(2,1)S(1)}, u32[]{:S(2)}, u32[]{:S(2)}) collective-permute-start(bf16[2,80,1152]{2,1,0:T(8,128)(2,1)S(1)} %constant_dynamic-update-slice_fusion.5), channel_id=1, source_target_pairs={{0,8},{4,20},{8,0},{12,28},{16,24},{20,4},{24,16},{28,12},{1,9},{5... | collective-permute-start | bytes 1105928 | tf_op jit(solution)/shard_map/ppermute | solution.py:109
  23.9 1.1 %collective-permute-start.5 = (bf16[1,80,1152]{2,1,0:T(8,128)(2,1)S(1)}, bf16[1,80,1152]{2,1,0:T(8,128)(2,1)S(1)}, u32[]{:S(2)}, u32[]{:S(2)}) collective-permute-start(bf16[1,80,1152]{2,1,0:T(8,128)(2,1)S(1)} %collective-permute-done.2), channel_id=1, source_target_pairs={{0,1},{1,2},{2,3},{3,0},{4,5},{5,6},{6,7},{7,4},{8,9},{9,10},{10,1... | collective-permute-start | bytes 552968 | tf_op jit(solution)/shard_map/ppermute | solution.py:105
  25.0 0.0 copy-done.5
  25.0 0.8 collective-permute-start.4
  25.8 7.5 %collective-permute-done.5 = bf16[1,80,1152]{2,1,0:T(8,128)(2,1)S(1)} collective-permute-done((bf16[1,80,1152]{2,1,0:T(8,128)(2,1)S(1)}, bf16[1,80,1152]{2,1,0:T(8,128)(2,1)S(1)}, u32[]{:S(2)}, u32[]{:S(2)}) %collective-permute-start.5) | collective-permute-done | bytes 184352 | tf_op jit(solution)/shard_map/ppermute | solution.py:105
  33.3 0.4 collective-permute-start.6
  33.8 0.0 collective-permute-done.13
  33.8 0.0 collective-permute-done.12.refs_1_
  33.8 1.7 %collective-permute-start.14 = (bf16[4,80,1152]{2,1,0:T(8,128)(2,1)S(1)}, bf16[4,80,1152]{2,1,0:T(8,128)(2,1)S(1)}, u32[]{:S(2)}, u32[]{:S(2)}) collective-permute-start(bf16[4,80,1152]{2,1,0:T(8,128)(2,1)S(1)} %constant_dynamic-update-slice_fusion.7.refs_3_), channel_id=1, source_target_pairs={{0,16},{4,12},{8,24},{12,4},{16,0},{20,28},{24,8},{28,20},{1,17},{... | collective-permute-start | bytes 2211848 | tf_op jit(solution)/shard_map/ppermute | solution.py:109
  35.5 5.3 %collective-permute-done.6 = bf16[1,80,1152]{2,1,0:T(8,128)(2,1)S(1)} collective-permute-done((bf16[1,80,1152]{2,1,0:T(8,128)(2,1)S(1)}, bf16[1,80,1152]{2,1,0:T(8,128)(2,1)S(1)}, u32[]{:S(2)}, u32[]{:S(2)}) %collective-permute-start.6) | collective-permute-done | bytes 184352 | tf_op jit(solution)/shard_map/ppermute | solution.py:109
  40.9 1.6 %collective-permute-start.15 = (bf16[2,80,1152]{2,1,0:T(8,128)(2,1)S(1)}, bf16[2,80,1152]{2,1,0:T(8,128)(2,1)S(1)}, u32[]{:S(2)}, u32[]{:S(2)}) collective-permute-start(bf16[2,80,1152]{2,1,0:T(8,128)(2,1)S(1)} %constant_dynamic-update-slice_fusion.refs_5_), channel_id=1, source_target_pairs={{0,16},{4,12},{8,24},{12,4},{16,0},{20,28},{24,8},{28,20},{1,17},{... | collective-permute-start | bytes 1105928 | tf_op jit(solution)/shard_map/ppermute | solution.py:109
  42.5 0.2 collective-permute-start.8
  42.7 0.0 collective-permute-done.4
  42.7 1.8 %collective-permute-start.7 = (bf16[2,64,1152]{2,1,0:T(8,128)(2,1)S(1)}, bf16[2,64,1152]{2,1,0:T(8,128)(2,1)S(1)}, u32[]{:S(2)}, u32[]{:S(2)}) collective-permute-start(bf16[2,64,1152]{2,1,0:T(8,128)(2,1)S(1)} %collective-permute-done.4), channel_id=1, source_target_pairs={{0,1},{1,2},{2,3},{3,0},{4,5},{5,6},{6,7},{7,4},{8,9},{9,10},{10,1... | collective-permute-start | bytes 884744 | tf_op jit(solution)/shard_map/ppermute | solution.py:105
  44.5 7.9 %collective-permute-done.8 = bf16[2,64,1152]{2,1,0:T(8,128)(2,1)S(1)} collective-permute-done((bf16[2,64,1152]{2,1,0:T(8,128)(2,1)S(1)}, bf16[2,64,1152]{2,1,0:T(8,128)(2,1)S(1)}, u32[]{:S(2)}, u32[]{:S(2)}) %collective-permute-start.8) | collective-permute-done | bytes 294944 | tf_op jit(solution)/shard_map/ppermute | solution.py:105
  52.4 0.0 collective-permute-done.15.refs_6_
  52.4 0.0 collective-permute-done.14.refs_4_
  52.4 3.1 %shard_map.57 = (bf16[736,1152]{1,0:T(8,128)(2,1)S(1)}, bf16[736,1152]{1,0:T(8,128)(2,1)S(1)}) custom-call(bf16[384,1152]{1,0:T(8,128)(2,1)S(1)} %shard_map.56.refs_0_, bf16[384,1152]{1,0:T(8,128)(2,1)S(1)} %collective-permute-done.12.refs_1_, bf16[288,3456]{1,0:T(8,128)(2,1)S(1)} %copy-done, ...), custom_call_target="tpu_custom_call" | custom-call | flops 2038431744 | bytes 2654208 | tf_op jit(solution)/shard_map/pallas_call | solution.py:165
  55.5 0.0 collective-permute-done.7
  55.5 0.1 collective-permute-start.16
  55.7 0.6 collective-permute-start.9
  56.3 0.1 pad_maximum_fusion.1
  56.4 0.6 collective-permute-start.10
  57.0 0.4 collective-permute-start.11
  57.4 1.8 %collective-permute-done.16.other_ref.refs_8_ = bf16[736,1152]{1,0:T(8,128)(2,1)S(1)} collective-permute-done((bf16[736,1152]{1,0:T(8,128)(2,1)S(1)}, bf16[736,1152]{1,0:T(8,128)(2,1)S(1)}, u32[]{:S(2)}, u32[]{:S(2)}) %collective-permute-start.16) | collective-permute-done | bytes 1695776 | tf_op jit(solution)/shard_map/ppermute | solution.py:109
  59.2 0.9 %shard_map.58 = (bf16[256,1152]{1,0:T(8,128)(2,1)S(1)}, f32[9,32,128]{2,1,0:T(8,128)S(1)}, bf16[9,32,128]{2,1,0:T(8,128)(2,1)S(1)}) custom-call(bf16[736,1152]{1,0:T(8,128)(2,1)S(1)} %get-tuple-element.39.mine_ref.refs_7_, bf16[736,1152]{1,0:T(8,128)(2,1)S(1)} %collective-permute-done.16.other_ref.refs_8_), custom_call_target="tpu_custom_call" | custom-call | flops 150994944 | bytes 2359296 | tf_op jit(solution)/shard_map/pallas_call | solution.py:165
  60.1 0.0 copy-start.4
  60.1 0.0 copy-start.2
  60.1 0.4 collective-permute-done.9.refs_4_
  60.5 2.3 %collective-permute-start.19 = (bf16[9,32,128]{2,1,0:T(8,128)(2,1)S(1)}, bf16[9,32,128]{2,1,0:T(8,128)(2,1)S(1)}, u32[]{:S(2)}, u32[]{:S(2)}) collective-permute-start(bf16[9,32,128]{2,1,0:T(8,128)(2,1)S(1)} %get-tuple-element.44), channel_id=1, source_target_pairs={{0,24},{4,28},{8,16},{12,20},{1,25},{5,29},{9,17},{13,21},{2,26},{... | collective-permute-start | bytes 221192 | tf_op jit(solution)/shard_map/ppermute | solution.py:552
  62.8 1.3 %collective-permute-start.18 = (bf16[9,32,128]{2,1,0:T(8,128)(2,1)S(1)}, bf16[9,32,128]{2,1,0:T(8,128)(2,1)S(1)}, u32[]{:S(2)}, u32[]{:S(2)}) collective-permute-start(bf16[9,32,128]{2,1,0:T(8,128)(2,1)S(1)} %get-tuple-element.44), channel_id=1, source_target_pairs={{0,16},{4,20},{8,24},{12,28},{1,17},{5,21},{9,25},{13,29},{2,18},{... | collective-permute-start | bytes 221192 | tf_op jit(solution)/shard_map/ppermute | solution.py:552
  64.2 3.4 %collective-permute-start.17 = (bf16[9,32,128]{2,1,0:T(8,128)(2,1)S(1)}, bf16[9,32,128]{2,1,0:T(8,128)(2,1)S(1)}, u32[]{:S(2)}, u32[]{:S(2)}) collective-permute-start(bf16[9,32,128]{2,1,0:T(8,128)(2,1)S(1)} %get-tuple-element.44), channel_id=1, source_target_pairs={{0,8},{4,12},{16,24},{20,28},{1,9},{5,13},{17,25},{21,29},{2,10},{... | collective-permute-start | bytes 221192 | tf_op jit(solution)/shard_map/ppermute | solution.py:552
  67.6 1.6 %collective-permute-done.19 = bf16[9,32,128]{2,1,0:T(8,128)(2,1)S(1)} collective-permute-done((bf16[9,32,128]{2,1,0:T(8,128)(2,1)S(1)}, bf16[9,32,128]{2,1,0:T(8,128)(2,1)S(1)}, u32[]{:S(2)}, u32[]{:S(2)}) %collective-permute-start.19) | collective-permute-done | bytes 73760 | tf_op jit(solution)/shard_map/ppermute | solution.py:552
  69.1 0.7 collective-permute-done.18
  69.8 0.1 collective-permute-done.17
  70.0 0.0 collective-permute-done.10
  70.0 0.0 collective-permute-done.11
  70.1 0.1 collective-permute-start.20
  70.2 0.2 collective-permute-start.21
  70.3 0.0 copy-start.1
  70.4 1.0 %shard_map.60 = f32[4,64,1152]{2,1,0:T(8,128)S(1)} custom-call(bf16[4,64,1152]{2,1,0:T(8,128)(2,1)S(1)} %bitcast.10, bf16[736,1152]{1,0:T(8,128)(2,1)S(1)} %get-tuple-element.39.mine_ref.refs_7_, bf16[736,1152]{1,0:T(8,128)(2,1)S(1)} %collective-permute-done.16.other_ref.refs_8_, f32[3,3,1152]{2,1,0:T(4,128)S(1)} %copy-done.2), custom_call_target="tpu_custom_call" | custom-call | flops 5308416 | bytes 1769472 | tf_op jit(solution)/shard_map/pallas_call | solution.py:165
  71.3 3.5 %collective-permute-done.21 = bf16[9,32,128]{2,1,0:T(8,128)(2,1)S(1)} collective-permute-done((bf16[9,32,128]{2,1,0:T(8,128)(2,1)S(1)}, bf16[9,32,128]{2,1,0:T(8,128)(2,1)S(1)}, u32[]{:S(2)}, u32[]{:S(2)}) %collective-permute-start.21) | collective-permute-done | bytes 73760 | tf_op jit(solution)/shard_map/ppermute | solution.py:568
  74.9 0.1 collective-permute-start.22
  75.0 0.0 collective-permute-done.20.refs_6_
  75.0 0.0 copy-done.1
  75.0 1.5 %shard_map.59 = (bf16[256,1152]{1,0:T(8,128)(2,1)S(1)}, bf16[1152,1152]{1,0:T(8,128)(2,1)S(1)}) custom-call(bf16[384,1152]{1,0:T(8,128)(2,1)S(1)} %shard_map.56.refs_0_, bf16[288,3456]{1,0:T(8,128)(2,1)S(1)} %copy-done, bf16[288,1152]{1,0:T(8,128)(2,1)S(1)} %copy-done.1, bf16[6,64,1152]{2,1,0:T(8,128)(2,1)S(1)} %constant_dynamic-update-slice_fusion.2.refs_3_, ...), custom_call_target="tpu_custom_call" | custom-call | flops 1019215872 | bytes 5308416 | tf_op jit(solution)/shard_map/pallas_call | solution.py:165
  76.5 4.6 %collective-permute-done.22 = bf16[9,32,128]{2,1,0:T(8,128)(2,1)S(1)} collective-permute-done((bf16[9,32,128]{2,1,0:T(8,128)(2,1)S(1)}, bf16[9,32,128]{2,1,0:T(8,128)(2,1)S(1)}, u32[]{:S(2)}, u32[]{:S(2)}) %collective-permute-start.22) | collective-permute-done | bytes 73760 | tf_op jit(solution)/shard_map/ppermute | solution.py:570
  81.1 2.4 %shard_map.61 = bf16[256,1152]{1,0:T(8,128)(2,1)} custom-call(bf16[256,1152]{1,0:T(8,128)(2,1)S(1)} %get-tuple-element.48.queries_ref, bf16[1152,1152]{1,0:T(8,128)(2,1)S(1)} %get-tuple-element.49.weight_ref, f32[9,32,128]{2,1,0:T(8,128)S(1)} %convert_add_fusion.state_ref, f32[256,1152]{1,0:T(8,128)S(1)} %bitcast.9, f32[1,1152]{1,0:T(1,128)S(1)} %broadcast_in_dim.7.gain_ref), custom_call_target="tpu_custom_call" | custom-call | flops 679477248 | bytes 2654208 | tf_op jit(solution)/shard_map/pallas_call | solution.py:165
  (22 shorter events, 0.4 us)
Async XLA Ops:
  0.0 14.5 %copy-start.3 = (bf16[1,4,64,1152]{3,2,1,0:T(8,128)(2,1)S(1)}, bf16[1,4,64,1152]{3,2,1,0:T(8,128)(2,1)}, u32[]{:S(2)}) copy-start(bf16[1,4,64,1152]{3,2,1,0:T(8,128)(2,1)} %param.5) | copy-start | bytes 1769476
  1.8 12.7 %collective-permute-start.1 = (bf16[64,1152]{1,0:T(8,128)(2,1)}, bf16[64,1152]{1,0:T(8,128)(2,1)S(1)}, u32[]{:S(2)}, u32[]{:S(2)}) collective-permute-start(bf16[64,1152]{1,0:T(8,128)(2,1)} %get-tuple-element.54), channel_id=1, source_target_pairs={{1,0},{2,1},{3,2},{5,4},{6,5},{7,6},{9,8},{10,9},{11,10},{13,12},{... | collective-permute-start | bytes 442376 | tf_op jit(solution)/shard_map/ppermute | solution.py:508
  3.1 11.4 %collective-permute-start = (bf16[64,1152]{1,0:T(8,128)(2,1)}, bf16[64,1152]{1,0:T(8,128)(2,1)S(1)}, u32[]{:S(2)}, u32[]{:S(2)}) collective-permute-start(bf16[64,1152]{1,0:T(8,128)(2,1)} %get-tuple-element.53), channel_id=1, source_target_pairs={{0,1},{1,2},{2,3},{4,5},{5,6},{6,7},{8,9},{9,10},{10,11},{12,13},{... | collective-permute-start | bytes 442376 | tf_op jit(solution)/shard_map/ppermute | solution.py:507
  10.6 9.7 %collective-permute-start.2 = (bf16[1,80,1152]{2,1,0:T(8,128)(2,1)}, bf16[1,80,1152]{2,1,0:T(8,128)(2,1)S(1)}, u32[]{:S(2)}, u32[]{:S(2)}) collective-permute-start(bf16[1,80,1152]{2,1,0:T(8,128)(2,1)} %bitcast.12), channel_id=1, source_target_pairs={{0,1},{1,2},{2,3},{3,0},{4,5},{5,6},{6,7},{7,4},{8,9},{9,10},{10,1... | collective-permute-start | bytes 552968 | tf_op jit(solution)/shard_map/ppermute | solution.py:105
  12.6 9.7 %collective-permute-start.3 = (bf16[1,80,1152]{2,1,0:T(8,128)(2,1)}, bf16[1,80,1152]{2,1,0:T(8,128)(2,1)S(1)}, u32[]{:S(2)}, u32[]{:S(2)}) collective-permute-start(bf16[1,80,1152]{2,1,0:T(8,128)(2,1)} %bitcast.13), channel_id=1, source_target_pairs={{0,3},{1,0},{2,1},{3,2},{4,7},{5,4},{6,5},{7,6},{8,11},{9,8},{10,9... | collective-permute-start | bytes 552968 | tf_op jit(solution)/shard_map/ppermute | solution.py:105
  14.5 10.5 %copy-start.5 = (bf16[2,64,1152]{2,1,0:T(8,128)(2,1)S(1)}, bf16[2,64,1152]{2,1,0:T(8,128)(2,1)}, u32[]{:S(2)}) copy-start(bf16[2,64,1152]{2,1,0:T(8,128)(2,1)} %get-tuple-element.34) | copy-start | bytes 884740
  16.2 36.2 %copy-start = (bf16[288,3456]{1,0:T(8,128)(2,1)S(1)}, bf16[288,3456]{1,0:T(8,128)(2,1)}, u32[]{:S(2)}) copy-start(bf16[288,3456]{1,0:T(8,128)(2,1)} %refs_1_.1) | copy-start | bytes 5971972
  16.2 17.6 %collective-permute-start.12 = (bf16[384,1152]{1,0:T(8,128)(2,1)S(1)}, bf16[384,1152]{1,0:T(8,128)(2,1)S(1)}, u32[]{:S(2)}, u32[]{:S(2)}) collective-permute-start(bf16[384,1152]{1,0:T(8,128)(2,1)S(1)} %shard_map.56.refs_0_), channel_id=1, source_target_pairs={{0,4},{4,0},{8,12},{12,8},{16,20},{20,16},{24,28},{28,24},{1,5},{5... | collective-permute-start | bytes 2654216 | tf_op jit(solution)/shard_map/ppermute | solution.py:109
  22.4 11.4 %collective-permute-start.13 = (bf16[2,80,1152]{2,1,0:T(8,128)(2,1)S(1)}, bf16[2,80,1152]{2,1,0:T(8,128)(2,1)S(1)}, u32[]{:S(2)}, u32[]{:S(2)}) collective-permute-start(bf16[2,80,1152]{2,1,0:T(8,128)(2,1)S(1)} %constant_dynamic-update-slice_fusion.5), channel_id=1, source_target_pairs={{0,8},{4,20},{8,0},{12,28},{16,24},{20,4},{24,16},{28,12},{1,9},{5... | collective-permute-start | bytes 1105928 | tf_op jit(solution)/shard_map/ppermute | solution.py:109
  23.9 9.4 %collective-permute-start.5 = (bf16[1,80,1152]{2,1,0:T(8,128)(2,1)S(1)}, bf16[1,80,1152]{2,1,0:T(8,128)(2,1)S(1)}, u32[]{:S(2)}, u32[]{:S(2)}) collective-permute-start(bf16[1,80,1152]{2,1,0:T(8,128)(2,1)S(1)} %collective-permute-done.2), channel_id=1, source_target_pairs={{0,1},{1,2},{2,3},{3,0},{4,5},{5,6},{6,7},{7,4},{8,9},{9,10},{10,1... | collective-permute-start | bytes 552968 | tf_op jit(solution)/shard_map/ppermute | solution.py:105
  25.0 17.7 %collective-permute-start.4 = (bf16[2,64,1152]{2,1,0:T(8,128)(2,1)S(1)}, bf16[2,64,1152]{2,1,0:T(8,128)(2,1)S(1)}, u32[]{:S(2)}, u32[]{:S(2)}) collective-permute-start(bf16[2,64,1152]{2,1,0:T(8,128)(2,1)S(1)} %copy-done.5), channel_id=1, source_target_pairs={{0,1},{1,2},{2,3},{3,0},{4,5},{5,6},{6,7},{7,4},{8,9},{9,10},{10,1... | collective-permute-start | bytes 884744 | tf_op jit(solution)/shard_map/ppermute | solution.py:105
  33.3 7.6 %collective-permute-start.6 = (bf16[1,80,1152]{2,1,0:T(8,128)(2,1)S(1)}, bf16[1,80,1152]{2,1,0:T(8,128)(2,1)S(1)}, u32[]{:S(2)}, u32[]{:S(2)}) collective-permute-start(bf16[1,80,1152]{2,1,0:T(8,128)(2,1)S(1)} %collective-permute-done.5), channel_id=1, source_target_pairs={{0,8},{4,20},{8,0},{12,28},{16,24},{20,4},{24,16},{28,12},{1,9},{5... | collective-permute-start | bytes 552968 | tf_op jit(solution)/shard_map/ppermute | solution.py:109
  33.8 18.5 %collective-permute-start.14 = (bf16[4,80,1152]{2,1,0:T(8,128)(2,1)S(1)}, bf16[4,80,1152]{2,1,0:T(8,128)(2,1)S(1)}, u32[]{:S(2)}, u32[]{:S(2)}) collective-permute-start(bf16[4,80,1152]{2,1,0:T(8,128)(2,1)S(1)} %constant_dynamic-update-slice_fusion.7.refs_3_), channel_id=1, source_target_pairs={{0,16},{4,12},{8,24},{12,4},{16,0},{20,28},{24,8},{28,20},{1,17},{... | collective-permute-start | bytes 2211848 | tf_op jit(solution)/shard_map/ppermute | solution.py:109
  40.9 11.5 %collective-permute-start.15 = (bf16[2,80,1152]{2,1,0:T(8,128)(2,1)S(1)}, bf16[2,80,1152]{2,1,0:T(8,128)(2,1)S(1)}, u32[]{:S(2)}, u32[]{:S(2)}) collective-permute-start(bf16[2,80,1152]{2,1,0:T(8,128)(2,1)S(1)} %constant_dynamic-update-slice_fusion.refs_5_), channel_id=1, source_target_pairs={{0,16},{4,12},{8,24},{12,4},{16,0},{20,28},{24,8},{28,20},{1,17},{... | collective-permute-start | bytes 1105928 | tf_op jit(solution)/shard_map/ppermute | solution.py:109
  42.5 9.9 %collective-permute-start.8 = (bf16[2,64,1152]{2,1,0:T(8,128)(2,1)S(1)}, bf16[2,64,1152]{2,1,0:T(8,128)(2,1)S(1)}, u32[]{:S(2)}, u32[]{:S(2)}) collective-permute-start(bf16[2,64,1152]{2,1,0:T(8,128)(2,1)S(1)} %copy-done.5), channel_id=1, source_target_pairs={{0,3},{1,0},{2,1},{3,2},{4,7},{5,4},{6,5},{7,6},{8,11},{9,8},{10,9... | collective-permute-start | bytes 884744 | tf_op jit(solution)/shard_map/ppermute | solution.py:105
  42.7 12.9 %collective-permute-start.7 = (bf16[2,64,1152]{2,1,0:T(8,128)(2,1)S(1)}, bf16[2,64,1152]{2,1,0:T(8,128)(2,1)S(1)}, u32[]{:S(2)}, u32[]{:S(2)}) collective-permute-start(bf16[2,64,1152]{2,1,0:T(8,128)(2,1)S(1)} %collective-permute-done.4), channel_id=1, source_target_pairs={{0,1},{1,2},{2,3},{3,0},{4,5},{5,6},{6,7},{7,4},{8,9},{9,10},{10,1... | collective-permute-start | bytes 884744 | tf_op jit(solution)/shard_map/ppermute | solution.py:105
  55.5 3.7 %collective-permute-start.16 = (bf16[736,1152]{1,0:T(8,128)(2,1)S(1)}, bf16[736,1152]{1,0:T(8,128)(2,1)S(1)}, u32[]{:S(2)}, u32[]{:S(2)}) collective-permute-start(bf16[736,1152]{1,0:T(8,128)(2,1)S(1)} %get-tuple-element.41), channel_id=1, source_target_pairs={{0,4},{4,0},{8,12},{12,8},{16,20},{20,16},{24,28},{28,24},{1,5},{5... | collective-permute-start | bytes 5087240 | tf_op jit(solution)/shard_map/ppermute | solution.py:109
  55.7 4.7 %collective-permute-start.9 = (bf16[6,64,1152]{2,1,0:T(8,128)(2,1)S(1)}, bf16[6,64,1152]{2,1,0:T(8,128)(2,1)S(1)}, u32[]{:S(2)}, u32[]{:S(2)}) collective-permute-start(bf16[6,64,1152]{2,1,0:T(8,128)(2,1)S(1)} %constant_dynamic-update-slice_fusion.2.refs_3_), channel_id=1, source_target_pairs={{0,4},{4,0},{8,12},{12,8},{16,20},{20,16},{24,28},{28,24},{1,5},{5... | collective-permute-start | bytes 2654216 | tf_op jit(solution)/shard_map/ppermute | solution.py:109
  56.4 13.6 %collective-permute-start.10 = (bf16[3,64,1152]{2,1,0:T(8,128)(2,1)S(1)}, bf16[3,64,1152]{2,1,0:T(8,128)(2,1)S(1)}, u32[]{:S(2)}, u32[]{:S(2)}) collective-permute-start(bf16[3,64,1152]{2,1,0:T(8,128)(2,1)S(1)} %pad_maximum_fusion.1), channel_id=1, source_target_pairs={{0,8},{4,20},{8,0},{12,28},{16,24},{20,4},{24,16},{28,12},{1,9},{5... | collective-permute-start | bytes 1327112 | tf_op jit(solution)/shard_map/ppermute | solution.py:109
  57.0 13.0 %collective-permute-start.11 = (bf16[3,64,1152]{2,1,0:T(8,128)(2,1)S(1)}, bf16[3,64,1152]{2,1,0:T(8,128)(2,1)S(1)}, u32[]{:S(2)}, u32[]{:S(2)}) collective-permute-start(bf16[3,64,1152]{2,1,0:T(8,128)(2,1)S(1)} %pad_maximum_fusion.1), channel_id=1, source_target_pairs={{0,16},{4,12},{8,24},{12,4},{16,0},{20,28},{24,8},{28,20},{1,17},{... | collective-permute-start | bytes 1327112 | tf_op jit(solution)/shard_map/ppermute | solution.py:109
  60.1 10.2 %copy-start.4 = (f32[1152]{0:T(1024)S(1)}, f32[1152]{0:T(1024)}, u32[]{:S(2)}) copy-start(f32[1152]{0:T(1024)} %param.9) | copy-start | bytes 13828
  60.1 10.2 %copy-start.2 = (f32[3,3,1152]{2,1,0:T(4,128)S(1)}, f32[3,3,1152]{2,1,0:T(4,128)}, u32[]{:S(2)}) copy-start(f32[3,3,1152]{2,1,0:T(4,128)} %conv_ref.1) | copy-start | bytes 124420
  60.5 8.7 %collective-permute-start.19 = (bf16[9,32,128]{2,1,0:T(8,128)(2,1)S(1)}, bf16[9,32,128]{2,1,0:T(8,128)(2,1)S(1)}, u32[]{:S(2)}, u32[]{:S(2)}) collective-permute-start(bf16[9,32,128]{2,1,0:T(8,128)(2,1)S(1)} %get-tuple-element.44), channel_id=1, source_target_pairs={{0,24},{4,28},{8,16},{12,20},{1,25},{5,29},{9,17},{13,21},{2,26},{... | collective-permute-start | bytes 221192 | tf_op jit(solution)/shard_map/ppermute | solution.py:552
  62.8 7.0 %collective-permute-start.18 = (bf16[9,32,128]{2,1,0:T(8,128)(2,1)S(1)}, bf16[9,32,128]{2,1,0:T(8,128)(2,1)S(1)}, u32[]{:S(2)}, u32[]{:S(2)}) collective-permute-start(bf16[9,32,128]{2,1,0:T(8,128)(2,1)S(1)} %get-tuple-element.44), channel_id=1, source_target_pairs={{0,16},{4,20},{8,24},{12,28},{1,17},{5,21},{9,25},{13,29},{2,18},{... | collective-permute-start | bytes 221192 | tf_op jit(solution)/shard_map/ppermute | solution.py:552
  64.2 5.8 %collective-permute-start.17 = (bf16[9,32,128]{2,1,0:T(8,128)(2,1)S(1)}, bf16[9,32,128]{2,1,0:T(8,128)(2,1)S(1)}, u32[]{:S(2)}, u32[]{:S(2)}) collective-permute-start(bf16[9,32,128]{2,1,0:T(8,128)(2,1)S(1)} %get-tuple-element.44), channel_id=1, source_target_pairs={{0,8},{4,12},{16,24},{20,28},{1,9},{5,13},{17,25},{21,29},{2,10},{... | collective-permute-start | bytes 221192 | tf_op jit(solution)/shard_map/ppermute | solution.py:552
  70.1 4.9 %collective-permute-start.20 = (bf16[6,64,1152]{2,1,0:T(8,128)(2,1)S(1)}, bf16[6,64,1152]{2,1,0:T(8,128)(2,1)S(1)}, u32[]{:S(2)}, u32[]{:S(2)}) collective-permute-start(bf16[6,64,1152]{2,1,0:T(8,128)(2,1)S(1)} %constant_dynamic-update-slice_fusion.9.refs_5_), channel_id=1, source_target_pairs={{0,4},{4,0},{8,12},{12,8},{16,20},{20,16},{24,28},{28,24},{1,5},{5... | collective-permute-start | bytes 2654216 | tf_op jit(solution)/shard_map/ppermute | solution.py:109
  70.2 4.7 %collective-permute-start.21 = (bf16[9,32,128]{2,1,0:T(8,128)(2,1)S(1)}, bf16[9,32,128]{2,1,0:T(8,128)(2,1)S(1)}, u32[]{:S(2)}, u32[]{:S(2)}) collective-permute-start(bf16[9,32,128]{2,1,0:T(8,128)(2,1)S(1)} %convert_add_fusion.1), channel_id=1, source_target_pairs={{0,1},{1,0},{2,3},{3,2},{4,5},{5,4},{6,7},{7,6},{8,9},{9,8},{10,11... | collective-permute-start | bytes 221192 | tf_op jit(solution)/shard_map/ppermute | solution.py:568
  70.3 4.6 %copy-start.1 = (bf16[288,1152]{1,0:T(8,128)(2,1)S(1)}, bf16[288,1152]{1,0:T(8,128)(2,1)}, u32[]{:S(2)}) copy-start(bf16[288,1152]{1,0:T(8,128)(2,1)} %refs_2_.3) | copy-start | bytes 1990660
  74.9 6.2 %collective-permute-start.22 = (bf16[9,32,128]{2,1,0:T(8,128)(2,1)S(1)}, bf16[9,32,128]{2,1,0:T(8,128)(2,1)S(1)}, u32[]{:S(2)}, u32[]{:S(2)}) collective-permute-start(bf16[9,32,128]{2,1,0:T(8,128)(2,1)S(1)} %add_convert_fusion), channel_id=1, source_target_pairs={{0,2},{1,3},{2,0},{3,1},{4,6},{5,7},{6,4},{7,5},{8,10},{9,11},{10,... | collective-permute-start | bytes 221192 | tf_op jit(solution)/shard_map/ppermute | solution.py:570

commit v6 on v4

--- a/solution.py
+++ b/solution.py
@@ -366,30 +366,32 @@
     )
 
 
-def local_kernel(values_ref, above_ref, below_ref, conv_ref, local_ref):
-    rows, columns, depth = values_ref.shape
+def column_taps(sheet, taps):
+    edge = jnp.zeros_like(sheet[:, :1])
+    before = jnp.concatenate([edge, sheet[:, :-1]], axis=1)
+    behind = jnp.concatenate([sheet[:, 1:], edge], axis=1)
+    return taps[0] * before + taps[1] * sheet + taps[2] * behind
+
+
+def local_kernel(values_ref, conv_ref, local_ref):
+    rows, _, depth = values_ref.shape
     for at in range(0, depth, LANES):
         lanes = slice(at, at + LANES)
         taps = conv_ref[:, :, lanes]
-        sheet = jnp.concatenate(
-            [above_ref[:, :, lanes], values_ref[:, :, lanes], below_ref[:, :, lanes]], axis=0
-        ).astype(jnp.float32)
-        edge = jnp.zeros((rows + 2, 1, LANES), jnp.float32)
-        before = jnp.concatenate([edge, sheet[:, :-1]], axis=1)
-        behind = jnp.concatenate([sheet[:, 1:], edge], axis=1)
-        total = jnp.zeros((rows, columns, LANES), jnp.float32)
-        for col_shift, moved in enumerate((before, sheet, behind)):
-            for row_shift in range(3):
-                total = total + taps[row_shift, col_shift] * moved[row_shift : row_shift + rows]
-        local_ref[:, :, lanes] = total
-
-
-def local_call(values, above, below, conv_weight):
+        sheet = values_ref[:, :, lanes].astype(jnp.float32)
+        local_ref[:, :, lanes] = column_taps(sheet, taps[1])
+        local_ref[1:, :, lanes] = local_ref[1:, :, lanes] + column_taps(sheet[:-1], taps[0])
+        local_ref[: rows - 1, :, lanes] = (
+            local_ref[: rows - 1, :, lanes] + column_taps(sheet[1:], taps[2])
+        )
+
+
+def local_call(values, conv_weight):
     return kernel_call(
         local_kernel,
         jax.ShapeDtypeStruct(values.shape, jnp.float32),
-        (values, above, below, conv_weight),
-        [whole_vmem()] * 4,
+        (values, conv_weight),
+        [whole_vmem()] * 2,
         flops=18 * values.size,
         bytes_accessed=6 * values.size,
     )
@@ -455,8 +457,11 @@
     )
 
 
-def finish_kernel(queries_ref, weight_ref, state_ref, local_ref, gain_ref, result_ref, read_ref):
+def finish_kernel(*refs):
+    queries_ref, weight_ref, state_ref, local_ref, above_ref, below_ref, *refs = refs
+    conv_ref, gain_ref, result_ref, read_ref, mixture_ref = refs
     count, depth = queries_ref.shape
+    columns = above_ref.shape[1]
     mask = diagonal_mask()
     square = jnp.zeros((count, LANES), jnp.float32)
     for group in range(depth // LANES):
@@ -467,25 +472,35 @@
         read_ref[:, lanes] = read
         square = square + read * read
     scale = lax.rsqrt(jnp.sum(square, axis=1, keepdims=True) / depth + 1e-06)
-    mixture = read_ref[...] * scale * gain_ref[...] + local_ref[...]
-    mixture = mixture.astype(jnp.bfloat16)
+    for at in range(0, depth, LANES):
+        lanes = slice(at, at + LANES)
+        taps = conv_ref[:, :, lanes]
+        mixture = read_ref[:, lanes] * scale * gain_ref[:, lanes] + local_ref[:, lanes]
+        above = column_taps(above_ref[:, :, lanes].astype(jnp.float32), taps[0])[0]
+        below = column_taps(below_ref[:, :, lanes].astype(jnp.float32), taps[2])[0]
+        middle = mixture[columns : count - columns]
+        mixture = jnp.concatenate(
+            [mixture[:columns] + above, middle, mixture[count - columns :] + below], axis=0
+        )
+        mixture_ref[:, lanes] = mixture.astype(jnp.bfloat16)
     width = 3 * LANES
     for at in range(0, depth, width):
         lanes = slice(at, at + width)
-        product = jnp.dot(mixture, weight_ref[:, lanes], preferred_element_type=jnp.float32)
+        product = jnp.dot(
+            mixture_ref[...], weight_ref[:, lanes], preferred_element_type=jnp.float32
+        )
         result_ref[:, lanes] = product.astype(jnp.bfloat16)
 
 
-def finish_call(queries, weight, state, local_term, gain):
-    inputs = (queries, weight, state, local_term, gain)
+def finish_call(queries, *inputs):
     return kernel_call(
         finish_kernel,
         jax.ShapeDtypeStruct(queries.shape, jnp.bfloat16),
-        inputs,
-        [whole_vmem()] * len(inputs),
-        [pltpu.VMEM(queries.shape, jnp.float32)],
+        (queries,) + inputs,
+        [whole_vmem()] * (1 + len(inputs)),
+        [pltpu.VMEM(queries.shape, jnp.float32), pltpu.VMEM(queries.shape, jnp.bfloat16)],
         flops=2 * queries.size * queries.shape[1],
-        bytes_accessed=2 * weight.size,
+        bytes_accessed=2 * queries.shape[1] ** 2,
     )
 
 
@@ -532,13 +547,17 @@
     count = lax.axis_size("space")
     forward = [(i, i + 1) for i in range(count - 1)]
     backward = [(target, source) for source, target in forward]
-    above = lax.ppermute(after(bottom, upto), "space", forward)
-    share = after(upto, second_first, second_second).astype(jnp.bfloat16)
+    state = after(upto, second_first, second_second)
+    share = state.astype(jnp.bfloat16)
+    grid = values.reshape(row_count, col_count, depth)
+    local_term = local_call(grid, conv_weight).reshape(-1, depth)
     arrived = lax.ppermute(share, "space", [(i, i ^ 1) for i in range(count)])
+    arrived = after(arrived, local_term)
     share = (share.astype(jnp.float32) + arrived.astype(jnp.float32)).astype(jnp.bfloat16)
-    share = after(share, above)
     arrived = lax.ppermute(share, "space", [(i, i ^ 2) for i in range(count)])
-    below = lax.ppermute(after(top, share), "space", backward)
+    top, bottom = after((top, bottom), share)
+    above = lax.ppermute(bottom, "space", forward)
+    below = lax.ppermute(top, "space", backward)
 
     turned = jnp.concatenate([second_first, second_second])
     swapped_turned = flipped(after(turned, share), (1, 1))
@@ -553,11 +572,18 @@
         mine,
         other,
     )
-    grid = values.reshape(row_count, col_count, depth)
-    local_term = local_call(grid, above, after(below, queries), conv_weight).reshape(-1, depth)
-    arrived = after(arrived, local_term)
     state = share.astype(jnp.float32) + arrived.astype(jnp.float32)
-    result = finish_call(queries, weight, state, local_term, norm_gain[None])
+    above, below = after((above, below), queries, weight)
+    result = finish_call(
+        queries,
+        weight,
+        state,
+        local_term,
+        above,
+        below,
+        conv_weight,
+        norm_gain[None],
+    )
     return result.reshape(1, row_count, col_count, depth)
 
 

time: 84.4 us -> 80.5 us (0.954)
  starting transfers between devices: 32.6 us -> 26 us
  waiting for transfers between devices: 39.9 us -> 42.4 us
    ppermute x1, starting transfers between devices: 4.61 us -> 0.07 us  [plane_form(): arrived = lax.ppermute(share, 'space', [(i, i ^ 2) for i in range(count)])]
    ppermute x1, waiting for transfers between devices: 0.36 us -> 3.4 us  [plane_form(): arrived = lax.ppermute(share, 'space', [(i, i ^ 1) for i in range(count)])]
    ppermute x2, starting transfers between devices: 5.2 us -> 3.21 us  [the longest x1 1.92 us: plane_form(): above = lax.ppermute(bottom, 'space', forward)]
  transfers between devices with their start and end apart: 23 -> 23, of which waited for: 14 -> 13; matrix products, arithmetic and copies ran while one was open for 1% -> 1% of each run, Pallas kernels for 8% -> 8%
where the time goes in v6:
time: 80.5 us; the launch traced here: 80.2 us
  waiting for transfers between devices  42.4 us (53%)
  starting transfers between devices  26 us (32%)
  Pallas kernels  11 us (14%)
    ppermute x6, waiting for transfers between devices, shifted(): lax.ppermute(value, 'space', [(i, (i + step) % count) for i in range(coun...  22.3 us
    pallas_call x7, Pallas kernels, kernel_call(): pl.pallas_call(body, out_shape=outputs, in_specs=in_specs, out_specs=jax....  11 us
    ppermute x10, waiting for transfers between devices, flipped(): lax.ppermute(value, 'tm', [(t, t ^ bit_on_core[t % 2]) for t in range(8)])  9.97 us
    ppermute x6, starting transfers between devices, shifted(): lax.ppermute(value, 'space', [(i, (i + step) % count) for i in range(coun...  9.05 us
    ppermute x10, starting transfers between devices, flipped(): lax.ppermute(value, 'tm', [(t, t ^ bit_on_core[t % 2]) for t in range(8)])  7.06 us
    ppermute x3, starting transfers between devices, plane_form(): upto = upto + lax.ppermute(total, 'tm', pairs).astype(jnp.float32)  6.51 us
    ppermute x1, waiting for transfers between devices, plane_form(): arrived = lax.ppermute(share, 'space', [(i, i ^ 1) for i in range(count)])  3.4 us
    ppermute x1, waiting for transfers between devices, plane_form(): arrived = lax.ppermute(share, 'space', [(i, i ^ 2) for i in range(count)])  3.28 us
  transfers between devices with their start and end apart: 23, of which 13 were waited for; matrix products, arithmetic and copies ran while one was open for 1% of the time, Pallas kernels for 8%

profile of v6, /device:TPU:0, one launch (start us, length us, event | category | flops | bytes accessed | tf_op | source)
XLA Modules:
  0.0 80.2 jit_solution(12667242806749234119)
XLA Ops:
  0.0 1.9 %shard_map.55 = (bf16[80,1152]{1,0:T(8,128)(2,1)}, bf16[2,64,1152]{2,1,0:T(8,128)(2,1)}) custom-call(bf16[288,3456]{1,0:T(8,128)(2,1)} %refs_1_.1, bf16[288,1152]{1,0:T(8,128)(2,1)} %refs_2_.3), custom_call_target="tpu_custom_call" | custom-call | bytes 958464 | tf_op jit(solution)/shard_map/pallas_call | solution.py:164
  2.0 3.1 %collective-permute-start = (bf16[1,80,1152]{2,1,0:T(8,128)(2,1)}, bf16[1,80,1152]{2,1,0:T(8,128)(2,1)S(1)}, u32[]{:S(2)}, u32[]{:S(2)}) collective-permute-start(bf16[1,80,1152]{2,1,0:T(8,128)(2,1)} %bitcast.8), channel_id=1, source_target_pairs={{0,1},{1,2},{2,3},{3,0},{4,5},{5,6},{6,7},{7,4},{8,9},{9,10},{10,1... | collective-permute-start | bytes 552968 | tf_op jit(solution)/shard_map/ppermute | solution.py:104
  5.0 2.1 %collective-permute-start.1 = (bf16[1,80,1152]{2,1,0:T(8,128)(2,1)}, bf16[1,80,1152]{2,1,0:T(8,128)(2,1)S(1)}, u32[]{:S(2)}, u32[]{:S(2)}) collective-permute-start(bf16[1,80,1152]{2,1,0:T(8,128)(2,1)} %bitcast.9), channel_id=1, source_target_pairs={{0,3},{1,0},{2,1},{3,2},{4,7},{5,4},{6,5},{7,6},{8,11},{9,8},{10,9... | collective-permute-start | bytes 552968 | tf_op jit(solution)/shard_map/ppermute | solution.py:104
  7.1 0.0 copy-done.3
  7.1 1.2 %shard_map.56.refs_0_ = bf16[256,1152]{1,0:T(8,128)(2,1)S(1)} custom-call(bf16[256,1152]{1,0:T(8,128)(2,1)S(1)} %bitcast.7), custom_call_target="tpu_custom_call" | custom-call | flops 679477248 | bytes 589824 | tf_op jit(solution)/shard_map/pallas_call | solution.py:164
  8.3 0.0 copy-start
  8.3 0.1 collective-permute-start.10
  8.4 4.4 %collective-permute-done = bf16[1,80,1152]{2,1,0:T(8,128)(2,1)S(1)} collective-permute-done((bf16[1,80,1152]{2,1,0:T(8,128)(2,1)}, bf16[1,80,1152]{2,1,0:T(8,128)(2,1)S(1)}, u32[]{:S(2)}, u32[]{:S(2)}) %collective-permute-start) | collective-permute-done | bytes 184352 | tf_op jit(solution)/shard_map/ppermute | solution.py:104
  12.8 2.5 %collective-permute-done.1 = bf16[1,80,1152]{2,1,0:T(8,128)(2,1)S(1)} collective-permute-done((bf16[1,80,1152]{2,1,0:T(8,128)(2,1)}, bf16[1,80,1152]{2,1,0:T(8,128)(2,1)S(1)}, u32[]{:S(2)}, u32[]{:S(2)}) %collective-permute-start.1) | collective-permute-done | bytes 184352 | tf_op jit(solution)/shard_map/ppermute | solution.py:104
  15.3 1.6 %collective-permute-start.11 = (bf16[2,80,1152]{2,1,0:T(8,128)(2,1)S(1)}, bf16[2,80,1152]{2,1,0:T(8,128)(2,1)S(1)}, u32[]{:S(2)}, u32[]{:S(2)}) collective-permute-start(bf16[2,80,1152]{2,1,0:T(8,128)(2,1)S(1)} %constant_dynamic-update-slice_fusion.7), channel_id=1, source_target_pairs={{0,8},{4,20},{8,0},{12,28},{16,24},{20,4},{24,16},{28,12},{1,9},{5... | collective-permute-start | bytes 1105928 | tf_op jit(solution)/shard_map/ppermute | solution.py:108
  16.9 1.1 %collective-permute-start.3 = (bf16[1,80,1152]{2,1,0:T(8,128)(2,1)S(1)}, bf16[1,80,1152]{2,1,0:T(8,128)(2,1)S(1)}, u32[]{:S(2)}, u32[]{:S(2)}) collective-permute-start(bf16[1,80,1152]{2,1,0:T(8,128)(2,1)S(1)} %collective-permute-done), channel_id=1, source_target_pairs={{0,1},{1,2},{2,3},{3,0},{4,5},{5,6},{6,7},{7,4},{8,9},{9,10},{10,1... | collective-permute-start | bytes 552968 | tf_op jit(solution)/shard_map/ppermute | solution.py:104
  18.0 0.0 copy-done.5
  18.0 0.7 collective-permute-start.2
  18.8 7.5 %collective-permute-done.3 = bf16[1,80,1152]{2,1,0:T(8,128)(2,1)S(1)} collective-permute-done((bf16[1,80,1152]{2,1,0:T(8,128)(2,1)S(1)}, bf16[1,80,1152]{2,1,0:T(8,128)(2,1)S(1)}, u32[]{:S(2)}, u32[]{:S(2)}) %collective-permute-start.3) | collective-permute-done | bytes 184352 | tf_op jit(solution)/shard_map/ppermute | solution.py:104
  26.3 0.4 collective-permute-start.4
  26.7 0.0 collective-permute-done.11
  26.7 0.0 collective-permute-done.10.refs_1_
  26.8 1.7 %collective-permute-start.12 = (bf16[4,80,1152]{2,1,0:T(8,128)(2,1)S(1)}, bf16[4,80,1152]{2,1,0:T(8,128)(2,1)S(1)}, u32[]{:S(2)}, u32[]{:S(2)}) collective-permute-start(bf16[4,80,1152]{2,1,0:T(8,128)(2,1)S(1)} %constant_dynamic-update-slice_fusion.9.refs_3_), channel_id=1, source_target_pairs={{0,16},{4,12},{8,24},{12,4},{16,0},{20,28},{24,8},{28,20},{1,17},{... | collective-permute-start | bytes 2211848 | tf_op jit(solution)/shard_map/ppermute | solution.py:108
  28.5 5.3 %collective-permute-done.4 = bf16[1,80,1152]{2,1,0:T(8,128)(2,1)S(1)} collective-permute-done((bf16[1,80,1152]{2,1,0:T(8,128)(2,1)S(1)}, bf16[1,80,1152]{2,1,0:T(8,128)(2,1)S(1)}, u32[]{:S(2)}, u32[]{:S(2)}) %collective-permute-start.4) | collective-permute-done | bytes 184352 | tf_op jit(solution)/shard_map/ppermute | solution.py:108
  33.9 1.6 %collective-permute-start.13 = (bf16[2,80,1152]{2,1,0:T(8,128)(2,1)S(1)}, bf16[2,80,1152]{2,1,0:T(8,128)(2,1)S(1)}, u32[]{:S(2)}, u32[]{:S(2)}) collective-permute-start(bf16[2,80,1152]{2,1,0:T(8,128)(2,1)S(1)} %constant_dynamic-update-slice_fusion.refs_5_), channel_id=1, source_target_pairs={{0,16},{4,12},{8,24},{12,4},{16,0},{20,28},{24,8},{28,20},{1,17},{... | collective-permute-start | bytes 1105928 | tf_op jit(solution)/shard_map/ppermute | solution.py:108
  35.4 0.1 collective-permute-start.6
  35.6 0.0 collective-permute-done.2
  35.6 1.9 %collective-permute-start.5 = (bf16[2,64,1152]{2,1,0:T(8,128)(2,1)S(1)}, bf16[2,64,1152]{2,1,0:T(8,128)(2,1)S(1)}, u32[]{:S(2)}, u32[]{:S(2)}) collective-permute-start(bf16[2,64,1152]{2,1,0:T(8,128)(2,1)S(1)} %collective-permute-done.2), channel_id=1, source_target_pairs={{0,1},{1,2},{2,3},{3,0},{4,5},{5,6},{6,7},{7,4},{8,9},{9,10},{10,1... | collective-permute-start | bytes 884744 | tf_op jit(solution)/shard_map/ppermute | solution.py:104
  37.5 7.9 %collective-permute-done.6 = bf16[2,64,1152]{2,1,0:T(8,128)(2,1)S(1)} collective-permute-done((bf16[2,64,1152]{2,1,0:T(8,128)(2,1)S(1)}, bf16[2,64,1152]{2,1,0:T(8,128)(2,1)S(1)}, u32[]{:S(2)}, u32[]{:S(2)}) %collective-permute-start.6) | collective-permute-done | bytes 294944 | tf_op jit(solution)/shard_map/ppermute | solution.py:104
  45.3 0.0 collective-permute-done.13.refs_6_
  45.3 0.0 collective-permute-done.12.refs_4_
  45.3 0.0 copy-done
  45.3 2.1 %shard_map.57.mine_ref.refs_7_ = bf16[608,1152]{1,0:T(8,128)(2,1)S(1)} custom-call(bf16[256,1152]{1,0:T(8,128)(2,1)S(1)} %shard_map.56.refs_0_, bf16[256,1152]{1,0:T(8,128)(2,1)S(1)} %collective-permute-done.10.refs_1_, bf16[288,3456]{1,0:T(8,128)(2,1)S(1)} %copy-done, bf16[4,80,1152]{2,1,0:T(8,128)(2,1)S(1)} %constant_dynamic-update-slice_fusion.9.refs_3_, ...), custom_call_target="tpu_custom_call" | custom-call | flops 1358954496 | bytes 2654208 | tf_op jit(solution)/shard_map/pallas_call | solution.py:164
  47.5 0.0 collective-permute-done.5
  47.5 0.1 collective-permute-start.14
  47.7 0.6 collective-permute-start.7
  48.3 0.1 pad_maximum_fusion
  48.4 0.6 collective-permute-start.8
  49.0 0.4 collective-permute-start.9
  49.4 1.3 %collective-permute-done.14.other_ref.refs_8_ = bf16[608,1152]{1,0:T(8,128)(2,1)S(1)} collective-permute-done((bf16[608,1152]{1,0:T(8,128)(2,1)S(1)}, bf16[608,1152]{1,0:T(8,128)(2,1)S(1)}, u32[]{:S(2)}, u32[]{:S(2)}) %collective-permute-start.14) | collective-permute-done | bytes 1400864 | tf_op jit(solution)/shard_map/ppermute | solution.py:108
  50.7 0.9 %shard_map.58 = (bf16[256,1152]{1,0:T(8,128)(2,1)S(1)}, bf16[1,64,1152]{2,1,0:T(8,128)(2,1)S(1)}, bf16[1,64,1152]{2,1,0:T(8,128)(2,1)S(1)}, f32[9,32,128]{2,1,0:T(8,128)S(1)}, bf16[9,32,128]{2,1,0:T(8,128)(2,1)S(1)}) custom-call(bf16[608,1152]{1,0:T(8,128)(2,1)S(1)} %shard_map.57.mine_ref.refs_7_, bf16[608,1152]{1,0:T(8,128)(2,1)S(1)} %collective-permute-done.14.other_ref.refs_8_), custom_call_target="tpu_custom_call" | custom-call | flops 150994944 | bytes 2359296 | tf_op jit(solution)/shard_map/pallas_call | solution.py:164
  51.6 0.0 copy-start.2
  51.6 0.4 collective-permute-done.7.refs_4_
  52.0 2.4 %collective-permute-start.15 = (bf16[9,32,128]{2,1,0:T(8,128)(2,1)S(1)}, bf16[9,32,128]{2,1,0:T(8,128)(2,1)S(1)}, u32[]{:S(2)}, u32[]{:S(2)}) collective-permute-start(bf16[9,32,128]{2,1,0:T(8,128)(2,1)S(1)} %get-tuple-element.44), channel_id=1, source_target_pairs={{0,8},{4,12},{16,24},{20,28},{1,9},{5,13},{17,25},{21,29},{2,10},{... | collective-permute-start | bytes 221192 | tf_op jit(solution)/shard_map/ppermute | solution.py:546
  54.4 2.8 %collective-permute-start.16 = (bf16[9,32,128]{2,1,0:T(8,128)(2,1)S(1)}, bf16[9,32,128]{2,1,0:T(8,128)(2,1)S(1)}, u32[]{:S(2)}, u32[]{:S(2)}) collective-permute-start(bf16[9,32,128]{2,1,0:T(8,128)(2,1)S(1)} %get-tuple-element.44), channel_id=1, source_target_pairs={{0,16},{4,20},{8,24},{12,28},{1,17},{5,21},{9,25},{13,29},{2,18},{... | collective-permute-start | bytes 221192 | tf_op jit(solution)/shard_map/ppermute | solution.py:546
  57.2 1.3 %collective-permute-start.17 = (bf16[9,32,128]{2,1,0:T(8,128)(2,1)S(1)}, bf16[9,32,128]{2,1,0:T(8,128)(2,1)S(1)}, u32[]{:S(2)}, u32[]{:S(2)}) collective-permute-start(bf16[9,32,128]{2,1,0:T(8,128)(2,1)S(1)} %get-tuple-element.44), channel_id=1, source_target_pairs={{0,24},{4,28},{8,16},{12,20},{1,25},{5,29},{9,17},{13,21},{2,26},{... | collective-permute-start | bytes 221192 | tf_op jit(solution)/shard_map/ppermute | solution.py:546
  58.5 2.9 %collective-permute-done.8 = bf16[3,64,1152]{2,1,0:T(8,128)(2,1)S(1)} collective-permute-done((bf16[3,64,1152]{2,1,0:T(8,128)(2,1)S(1)}, bf16[3,64,1152]{2,1,0:T(8,128)(2,1)S(1)}, u32[]{:S(2)}, u32[]{:S(2)}) %collective-permute-start.8) | collective-permute-done | bytes 442400 | tf_op jit(solution)/shard_map/ppermute | solution.py:108
  61.5 0.0 collective-permute-done.15
  61.5 0.3 collective-permute-done.16
  61.7 0.1 collective-permute-done.17
  61.9 0.0 copy-start.4
  61.9 0.0 collective-permute-done.9
  61.9 0.1 collective-permute-start.18
  62.1 0.0 copy-start.1
  62.1 0.0 copy-done.2
  62.1 0.9 %shard_map.59 = f32[4,64,1152]{2,1,0:T(8,128)S(1)} custom-call(bf16[4,64,1152]{2,1,0:T(8,128)(2,1)S(1)} %bitcast.6, f32[3,3,1152]{2,1,0:T(4,128)S(1)} %copy-done.2), custom_call_target="tpu_custom_call" | custom-call | flops 5308416 | bytes 1769472 | tf_op jit(solution)/shard_map/pallas_call | solution.py:164
  63.0 3.4 %collective-permute-done.18 = bf16[9,32,128]{2,1,0:T(8,128)(2,1)S(1)} collective-permute-done((bf16[9,32,128]{2,1,0:T(8,128)(2,1)S(1)}, bf16[9,32,128]{2,1,0:T(8,128)(2,1)S(1)}, u32[]{:S(2)}, u32[]{:S(2)}) %collective-permute-start.18) | collective-permute-done | bytes 73760 | tf_op jit(solution)/shard_map/ppermute | solution.py:554
  66.4 0.1 collective-permute-start.19
  66.5 0.1 collective-permute-start.20
  66.5 0.0 copy-done.4
  66.6 1.9 %collective-permute-start.21 = (bf16[1,64,1152]{2,1,0:T(8,128)(2,1)S(1)}, bf16[1,64,1152]{2,1,0:T(8,128)(2,1)S(1)}, u32[]{:S(2)}, u32[]{:S(2)}) collective-permute-start(bf16[1,64,1152]{2,1,0:T(8,128)(2,1)S(1)} %get-tuple-element.53), channel_id=1, source_target_pairs={{0,1},{1,2},{2,3},{4,5},{5,6},{6,7},{8,9},{9,10},{10,11},{12,13},{... | collective-permute-start | bytes 442376 | tf_op jit(solution)/shard_map/ppermute | solution.py:559
  68.5 1.3 %collective-permute-start.22 = (bf16[1,64,1152]{2,1,0:T(8,128)(2,1)S(1)}, bf16[1,64,1152]{2,1,0:T(8,128)(2,1)S(1)}, u32[]{:S(2)}, u32[]{:S(2)}) collective-permute-start(bf16[1,64,1152]{2,1,0:T(8,128)(2,1)S(1)} %get-tuple-element.54), channel_id=1, source_target_pairs={{1,0},{2,1},{3,2},{5,4},{6,5},{7,6},{9,8},{10,9},{11,10},{13,12},{... | collective-permute-start | bytes 442376 | tf_op jit(solution)/shard_map/ppermute | solution.py:560
  69.8 3.3 %collective-permute-done.20 = bf16[9,32,128]{2,1,0:T(8,128)(2,1)S(1)} collective-permute-done((bf16[9,32,128]{2,1,0:T(8,128)(2,1)S(1)}, bf16[9,32,128]{2,1,0:T(8,128)(2,1)S(1)}, u32[]{:S(2)}, u32[]{:S(2)}) %collective-permute-start.20) | collective-permute-done | bytes 73760 | tf_op jit(solution)/shard_map/ppermute | solution.py:557
  73.1 0.0 collective-permute-done.19.refs_6_
  73.1 0.0 copy-done.1
  73.1 1.5 %shard_map.60 = (bf16[256,1152]{1,0:T(8,128)(2,1)S(1)}, bf16[1152,1152]{1,0:T(8,128)(2,1)S(1)}) custom-call(bf16[256,1152]{1,0:T(8,128)(2,1)S(1)} %shard_map.56.refs_0_, bf16[288,3456]{1,0:T(8,128)(2,1)S(1)} %copy-done, bf16[288,1152]{1,0:T(8,128)(2,1)S(1)} %copy-done.1, bf16[6,64,1152]{2,1,0:T(8,128)(2,1)S(1)} %constant_dynamic-update-slice_fusion.2.refs_3_, ...), custom_call_target="tpu_custom_call" | custom-call | flops 679477248 | bytes 5308416 | tf_op jit(solution)/shard_map/pallas_call | solution.py:164
  74.6 0.0 collective-permute-done.21.refs_4_
  74.7 3.1 %collective-permute-done.22.refs_5_ = bf16[1,64,1152]{2,1,0:T(8,128)(2,1)S(1)} collective-permute-done((bf16[1,64,1152]{2,1,0:T(8,128)(2,1)S(1)}, bf16[1,64,1152]{2,1,0:T(8,128)(2,1)S(1)}, u32[]{:S(2)}, u32[]{:S(2)}) %collective-permute-start.22) | collective-permute-done | bytes 147488 | tf_op jit(solution)/shard_map/ppermute | solution.py:560
  77.7 2.5 %shard_map.61 = bf16[256,1152]{1,0:T(8,128)(2,1)} custom-call(bf16[256,1152]{1,0:T(8,128)(2,1)S(1)} %get-tuple-element.49.refs_0_, bf16[1152,1152]{1,0:T(8,128)(2,1)S(1)} %get-tuple-element.50.refs_1_, f32[9,32,128]{2,1,0:T(8,128)S(1)} %convert_add_fusion.refs_2_, f32[256,1152]{1,0:T(8,128)S(1)} %bitcast.5, ...), custom_call_target="tpu_custom_call" | custom-call | flops 679477248 | bytes 2654208 | tf_op jit(solution)/shard_map/pallas_call | solution.py:164
  (20 shorter events, 0.4 us)
Async XLA Ops:
  0.0 7.1 %copy-start.3 = (bf16[1,4,64,1152]{3,2,1,0:T(8,128)(2,1)S(1)}, bf16[1,4,64,1152]{3,2,1,0:T(8,128)(2,1)}, u32[]{:S(2)}) copy-start(bf16[1,4,64,1152]{3,2,1,0:T(8,128)(2,1)} %param.5) | copy-start | bytes 1769476
  2.0 10.8 %collective-permute-start = (bf16[1,80,1152]{2,1,0:T(8,128)(2,1)}, bf16[1,80,1152]{2,1,0:T(8,128)(2,1)S(1)}, u32[]{:S(2)}, u32[]{:S(2)}) collective-permute-start(bf16[1,80,1152]{2,1,0:T(8,128)(2,1)} %bitcast.8), channel_id=1, source_target_pairs={{0,1},{1,2},{2,3},{3,0},{4,5},{5,6},{6,7},{7,4},{8,9},{9,10},{10,1... | collective-permute-start | bytes 552968 | tf_op jit(solution)/shard_map/ppermute | solution.py:104
  5.0 10.3 %collective-permute-start.1 = (bf16[1,80,1152]{2,1,0:T(8,128)(2,1)}, bf16[1,80,1152]{2,1,0:T(8,128)(2,1)S(1)}, u32[]{:S(2)}, u32[]{:S(2)}) collective-permute-start(bf16[1,80,1152]{2,1,0:T(8,128)(2,1)} %bitcast.9), channel_id=1, source_target_pairs={{0,3},{1,0},{2,1},{3,2},{4,7},{5,4},{6,5},{7,6},{8,11},{9,8},{10,9... | collective-permute-start | bytes 552968 | tf_op jit(solution)/shard_map/ppermute | solution.py:104
  7.1 10.9 %copy-start.5 = (bf16[2,64,1152]{2,1,0:T(8,128)(2,1)S(1)}, bf16[2,64,1152]{2,1,0:T(8,128)(2,1)}, u32[]{:S(2)}) copy-start(bf16[2,64,1152]{2,1,0:T(8,128)(2,1)} %get-tuple-element.36) | copy-start | bytes 884740
  8.3 37.0 %copy-start = (bf16[288,3456]{1,0:T(8,128)(2,1)S(1)}, bf16[288,3456]{1,0:T(8,128)(2,1)}, u32[]{:S(2)}) copy-start(bf16[288,3456]{1,0:T(8,128)(2,1)} %refs_1_.1) | copy-start | bytes 5971972
  8.3 18.4 %collective-permute-start.10 = (bf16[256,1152]{1,0:T(8,128)(2,1)S(1)}, bf16[256,1152]{1,0:T(8,128)(2,1)S(1)}, u32[]{:S(2)}, u32[]{:S(2)}) collective-permute-start(bf16[256,1152]{1,0:T(8,128)(2,1)S(1)} %shard_map.56.refs_0_), channel_id=1, source_target_pairs={{0,4},{4,0},{8,12},{12,8},{16,20},{20,16},{24,28},{28,24},{1,5},{5... | collective-permute-start | bytes 1769480 | tf_op jit(solution)/shard_map/ppermute | solution.py:108
  15.3 11.4 %collective-permute-start.11 = (bf16[2,80,1152]{2,1,0:T(8,128)(2,1)S(1)}, bf16[2,80,1152]{2,1,0:T(8,128)(2,1)S(1)}, u32[]{:S(2)}, u32[]{:S(2)}) collective-permute-start(bf16[2,80,1152]{2,1,0:T(8,128)(2,1)S(1)} %constant_dynamic-update-slice_fusion.7), channel_id=1, source_target_pairs={{0,8},{4,20},{8,0},{12,28},{16,24},{20,4},{24,16},{28,12},{1,9},{5... | collective-permute-start | bytes 1105928 | tf_op jit(solution)/shard_map/ppermute | solution.py:108
  16.9 9.4 %collective-permute-start.3 = (bf16[1,80,1152]{2,1,0:T(8,128)(2,1)S(1)}, bf16[1,80,1152]{2,1,0:T(8,128)(2,1)S(1)}, u32[]{:S(2)}, u32[]{:S(2)}) collective-permute-start(bf16[1,80,1152]{2,1,0:T(8,128)(2,1)S(1)} %collective-permute-done), channel_id=1, source_target_pairs={{0,1},{1,2},{2,3},{3,0},{4,5},{5,6},{6,7},{7,4},{8,9},{9,10},{10,1... | collective-permute-start | bytes 552968 | tf_op jit(solution)/shard_map/ppermute | solution.py:104
  18.0 17.6 %collective-permute-start.2 = (bf16[2,64,1152]{2,1,0:T(8,128)(2,1)S(1)}, bf16[2,64,1152]{2,1,0:T(8,128)(2,1)S(1)}, u32[]{:S(2)}, u32[]{:S(2)}) collective-permute-start(bf16[2,64,1152]{2,1,0:T(8,128)(2,1)S(1)} %copy-done.5), channel_id=1, source_target_pairs={{0,1},{1,2},{2,3},{3,0},{4,5},{5,6},{6,7},{7,4},{8,9},{9,10},{10,1... | collective-permute-start | bytes 884744 | tf_op jit(solution)/shard_map/ppermute | solution.py:104
  26.3 7.6 %collective-permute-start.4 = (bf16[1,80,1152]{2,1,0:T(8,128)(2,1)S(1)}, bf16[1,80,1152]{2,1,0:T(8,128)(2,1)S(1)}, u32[]{:S(2)}, u32[]{:S(2)}) collective-permute-start(bf16[1,80,1152]{2,1,0:T(8,128)(2,1)S(1)} %collective-permute-done.3), channel_id=1, source_target_pairs={{0,8},{4,20},{8,0},{12,28},{16,24},{20,4},{24,16},{28,12},{1,9},{5... | collective-permute-start | bytes 552968 | tf_op jit(solution)/shard_map/ppermute | solution.py:108
  26.8 18.5 %collective-permute-start.12 = (bf16[4,80,1152]{2,1,0:T(8,128)(2,1)S(1)}, bf16[4,80,1152]{2,1,0:T(8,128)(2,1)S(1)}, u32[]{:S(2)}, u32[]{:S(2)}) collective-permute-start(bf16[4,80,1152]{2,1,0:T(8,128)(2,1)S(1)} %constant_dynamic-update-slice_fusion.9.refs_3_), channel_id=1, source_target_pairs={{0,16},{4,12},{8,24},{12,4},{16,0},{20,28},{24,8},{28,20},{1,17},{... | collective-permute-start | bytes 2211848 | tf_op jit(solution)/shard_map/ppermute | solution.py:108
  33.9 11.5 %collective-permute-start.13 = (bf16[2,80,1152]{2,1,0:T(8,128)(2,1)S(1)}, bf16[2,80,1152]{2,1,0:T(8,128)(2,1)S(1)}, u32[]{:S(2)}, u32[]{:S(2)}) collective-permute-start(bf16[2,80,1152]{2,1,0:T(8,128)(2,1)S(1)} %constant_dynamic-update-slice_fusion.refs_5_), channel_id=1, source_target_pairs={{0,16},{4,12},{8,24},{12,4},{16,0},{20,28},{24,8},{28,20},{1,17},{... | collective-permute-start | bytes 1105928 | tf_op jit(solution)/shard_map/ppermute | solution.py:108
  35.4 9.9 %collective-permute-start.6 = (bf16[2,64,1152]{2,1,0:T(8,128)(2,1)S(1)}, bf16[2,64,1152]{2,1,0:T(8,128)(2,1)S(1)}, u32[]{:S(2)}, u32[]{:S(2)}) collective-permute-start(bf16[2,64,1152]{2,1,0:T(8,128)(2,1)S(1)} %copy-done.5), channel_id=1, source_target_pairs={{0,3},{1,0},{2,1},{3,2},{4,7},{5,4},{6,5},{7,6},{8,11},{9,8},{10,9... | collective-permute-start | bytes 884744 | tf_op jit(solution)/shard_map/ppermute | solution.py:104
  35.6 11.9 %collective-permute-start.5 = (bf16[2,64,1152]{2,1,0:T(8,128)(2,1)S(1)}, bf16[2,64,1152]{2,1,0:T(8,128)(2,1)S(1)}, u32[]{:S(2)}, u32[]{:S(2)}) collective-permute-start(bf16[2,64,1152]{2,1,0:T(8,128)(2,1)S(1)} %collective-permute-done.2), channel_id=1, source_target_pairs={{0,1},{1,2},{2,3},{3,0},{4,5},{5,6},{6,7},{7,4},{8,9},{9,10},{10,1... | collective-permute-start | bytes 884744 | tf_op jit(solution)/shard_map/ppermute | solution.py:104
  47.5 3.2 %collective-permute-start.14 = (bf16[608,1152]{1,0:T(8,128)(2,1)S(1)}, bf16[608,1152]{1,0:T(8,128)(2,1)S(1)}, u32[]{:S(2)}, u32[]{:S(2)}) collective-permute-start(bf16[608,1152]{1,0:T(8,128)(2,1)S(1)} %shard_map.57.mine_ref.refs_7_), channel_id=1, source_target_pairs={{0,4},{4,0},{8,12},{12,8},{16,20},{20,16},{24,28},{28,24},{1,5},{5... | collective-permute-start | bytes 4202504 | tf_op jit(solution)/shard_map/ppermute | solution.py:108
  47.7 4.3 %collective-permute-start.7 = (bf16[6,64,1152]{2,1,0:T(8,128)(2,1)S(1)}, bf16[6,64,1152]{2,1,0:T(8,128)(2,1)S(1)}, u32[]{:S(2)}, u32[]{:S(2)}) collective-permute-start(bf16[6,64,1152]{2,1,0:T(8,128)(2,1)S(1)} %constant_dynamic-update-slice_fusion.2.refs_3_), channel_id=1, source_target_pairs={{0,4},{4,0},{8,12},{12,8},{16,20},{20,16},{24,28},{28,24},{1,5},{5... | collective-permute-start | bytes 2654216 | tf_op jit(solution)/shard_map/ppermute | solution.py:108
  48.4 13.1 %collective-permute-start.8 = (bf16[3,64,1152]{2,1,0:T(8,128)(2,1)S(1)}, bf16[3,64,1152]{2,1,0:T(8,128)(2,1)S(1)}, u32[]{:S(2)}, u32[]{:S(2)}) collective-permute-start(bf16[3,64,1152]{2,1,0:T(8,128)(2,1)S(1)} %pad_maximum_fusion), channel_id=1, source_target_pairs={{0,8},{4,20},{8,0},{12,28},{16,24},{20,4},{24,16},{28,12},{1,9},{5... | collective-permute-start | bytes 1327112 | tf_op jit(solution)/shard_map/ppermute | solution.py:108
  49.0 13.0 %collective-permute-start.9 = (bf16[3,64,1152]{2,1,0:T(8,128)(2,1)S(1)}, bf16[3,64,1152]{2,1,0:T(8,128)(2,1)S(1)}, u32[]{:S(2)}, u32[]{:S(2)}) collective-permute-start(bf16[3,64,1152]{2,1,0:T(8,128)(2,1)S(1)} %pad_maximum_fusion), channel_id=1, source_target_pairs={{0,16},{4,12},{8,24},{12,4},{16,0},{20,28},{24,8},{28,20},{1,17},{... | collective-permute-start | bytes 1327112 | tf_op jit(solution)/shard_map/ppermute | solution.py:108
  51.6 10.5 %copy-start.2 = (f32[3,3,1152]{2,1,0:T(4,128)S(1)}, f32[3,3,1152]{2,1,0:T(4,128)}, u32[]{:S(2)}) copy-start(f32[3,3,1152]{2,1,0:T(4,128)} %refs_6_.1) | copy-start | bytes 124420
  52.0 9.5 %collective-permute-start.15 = (bf16[9,32,128]{2,1,0:T(8,128)(2,1)S(1)}, bf16[9,32,128]{2,1,0:T(8,128)(2,1)S(1)}, u32[]{:S(2)}, u32[]{:S(2)}) collective-permute-start(bf16[9,32,128]{2,1,0:T(8,128)(2,1)S(1)} %get-tuple-element.44), channel_id=1, source_target_pairs={{0,8},{4,12},{16,24},{20,28},{1,9},{5,13},{17,25},{21,29},{2,10},{... | collective-permute-start | bytes 221192 | tf_op jit(solution)/shard_map/ppermute | solution.py:546
  54.4 7.3 %collective-permute-start.16 = (bf16[9,32,128]{2,1,0:T(8,128)(2,1)S(1)}, bf16[9,32,128]{2,1,0:T(8,128)(2,1)S(1)}, u32[]{:S(2)}, u32[]{:S(2)}) collective-permute-start(bf16[9,32,128]{2,1,0:T(8,128)(2,1)S(1)} %get-tuple-element.44), channel_id=1, source_target_pairs={{0,16},{4,20},{8,24},{12,28},{1,17},{5,21},{9,25},{13,29},{2,18},{... | collective-permute-start | bytes 221192 | tf_op jit(solution)/shard_map/ppermute | solution.py:546
  57.2 4.7 %collective-permute-start.17 = (bf16[9,32,128]{2,1,0:T(8,128)(2,1)S(1)}, bf16[9,32,128]{2,1,0:T(8,128)(2,1)S(1)}, u32[]{:S(2)}, u32[]{:S(2)}) collective-permute-start(bf16[9,32,128]{2,1,0:T(8,128)(2,1)S(1)} %get-tuple-element.44), channel_id=1, source_target_pairs={{0,24},{4,28},{8,16},{12,20},{1,25},{5,29},{9,17},{13,21},{2,26},{... | collective-permute-start | bytes 221192 | tf_op jit(solution)/shard_map/ppermute | solution.py:546
  61.9 4.6 %copy-start.4 = (f32[1152]{0:T(1024)S(1)}, f32[1152]{0:T(1024)}, u32[]{:S(2)}) copy-start(f32[1152]{0:T(1024)} %param.9) | copy-start | bytes 13828
  61.9 4.4 %collective-permute-start.18 = (bf16[9,32,128]{2,1,0:T(8,128)(2,1)S(1)}, bf16[9,32,128]{2,1,0:T(8,128)(2,1)S(1)}, u32[]{:S(2)}, u32[]{:S(2)}) collective-permute-start(bf16[9,32,128]{2,1,0:T(8,128)(2,1)S(1)} %convert_add_fusion.1), channel_id=1, source_target_pairs={{0,1},{1,0},{2,3},{3,2},{4,5},{5,4},{6,7},{7,6},{8,9},{9,8},{10,11... | collective-permute-start | bytes 221192 | tf_op jit(solution)/shard_map/ppermute | solution.py:554
  62.1 11.0 %copy-start.1 = (bf16[288,1152]{1,0:T(8,128)(2,1)S(1)}, bf16[288,1152]{1,0:T(8,128)(2,1)}, u32[]{:S(2)}) copy-start(bf16[288,1152]{1,0:T(8,128)(2,1)} %refs_2_.3) | copy-start | bytes 1990660
  66.4 6.7 %collective-permute-start.19 = (bf16[6,64,1152]{2,1,0:T(8,128)(2,1)S(1)}, bf16[6,64,1152]{2,1,0:T(8,128)(2,1)S(1)}, u32[]{:S(2)}, u32[]{:S(2)}) collective-permute-start(bf16[6,64,1152]{2,1,0:T(8,128)(2,1)S(1)} %constant_dynamic-update-slice_fusion.5.refs_5_), channel_id=1, source_target_pairs={{0,4},{4,0},{8,12},{12,8},{16,20},{20,16},{24,28},{28,24},{1,5},{5... | collective-permute-start | bytes 2654216 | tf_op jit(solution)/shard_map/ppermute | solution.py:108
  66.5 6.6 %collective-permute-start.20 = (bf16[9,32,128]{2,1,0:T(8,128)(2,1)S(1)}, bf16[9,32,128]{2,1,0:T(8,128)(2,1)S(1)}, u32[]{:S(2)}, u32[]{:S(2)}) collective-permute-start(bf16[9,32,128]{2,1,0:T(8,128)(2,1)S(1)} %add_convert_fusion), channel_id=1, source_target_pairs={{0,2},{1,3},{2,0},{3,1},{4,6},{5,7},{6,4},{7,5},{8,10},{9,11},{10,... | collective-permute-start | bytes 221192 | tf_op jit(solution)/shard_map/ppermute | solution.py:557
  66.6 8.1 %collective-permute-start.21 = (bf16[1,64,1152]{2,1,0:T(8,128)(2,1)S(1)}, bf16[1,64,1152]{2,1,0:T(8,128)(2,1)S(1)}, u32[]{:S(2)}, u32[]{:S(2)}) collective-permute-start(bf16[1,64,1152]{2,1,0:T(8,128)(2,1)S(1)} %get-tuple-element.53), channel_id=1, source_target_pairs={{0,1},{1,2},{2,3},{4,5},{5,6},{6,7},{8,9},{9,10},{10,11},{12,13},{... | collective-permute-start | bytes 442376 | tf_op jit(solution)/shard_map/ppermute | solution.py:559
  68.5 9.2 %collective-permute-start.22 = (bf16[1,64,1152]{2,1,0:T(8,128)(2,1)S(1)}, bf16[1,64,1152]{2,1,0:T(8,128)(2,1)S(1)}, u32[]{:S(2)}, u32[]{:S(2)}) collective-permute-start(bf16[1,64,1152]{2,1,0:T(8,128)(2,1)S(1)} %get-tuple-element.54), channel_id=1, source_target_pairs={{1,0},{2,1},{3,2},{5,4},{6,5},{7,6},{9,8},{10,9},{11,10},{13,12},{... | collective-permute-start | bytes 442376 | tf_op jit(solution)/shard_map/ppermute | solution.py:560

commit v7 on v6

--- a/solution.py
+++ b/solution.py
@@ -552,12 +552,11 @@
     grid = values.reshape(row_count, col_count, depth)
     local_term = local_call(grid, conv_weight).reshape(-1, depth)
     arrived = lax.ppermute(share, "space", [(i, i ^ 1) for i in range(count)])
-    arrived = after(arrived, local_term)
+    above = lax.ppermute(after(bottom, share), "space", forward)
+    arrived = after(arrived, local_term, above)
     share = (share.astype(jnp.float32) + arrived.astype(jnp.float32)).astype(jnp.bfloat16)
     arrived = lax.ppermute(share, "space", [(i, i ^ 2) for i in range(count)])
-    top, bottom = after((top, bottom), share)
-    above = lax.ppermute(bottom, "space", forward)
-    below = lax.ppermute(top, "space", backward)
+    below = lax.ppermute(after(top, share), "space", backward)
 
     turned = jnp.concatenate([second_first, second_second])
     swapped_turned = flipped(after(turned, share), (1, 1))

time: 80.5 us -> 81.4 us (1.011)
  starting transfers between devices: 26 us -> 30 us
  waiting for transfers between devices: 42.4 us -> 39.3 us
    ppermute x1, waiting for transfers between devices: 3.4 us -> 0.01 us  [plane_form(): arrived = lax.ppermute(share, 'space', [(i, i ^ 1) for i in range(count)])]
    ppermute x2, starting transfers between devices: 3.21 us -> 5.32 us  [the longest x1 4.03 us: plane_form(): above = lax.ppermute(after(bottom, share), 'space', forward)]
    ppermute x1, starting transfers between devices: 0.07 us -> 1.98 us  [plane_form(): arrived = lax.ppermute(share, 'space', [(i, i ^ 2) for i in range(count)])]
    ppermute x2, waiting for transfers between devices: 3.08 us -> 4.33 us  [the longest x1 2.64 us: plane_form(): below = lax.ppermute(after(top, share), 'space', backward)]
    ppermute x1, waiting for transfers between devices: 3.28 us -> 2.31 us  [plane_form(): arrived = lax.ppermute(share, 'space', [(i, i ^ 2) for i in range(count)])]
where the time goes in v7:
time: 81.4 us; the launch traced here: 81.1 us
  waiting for transfers between devices  39.3 us (48%)
  starting transfers between devices  30 us (37%)
  Pallas kernels  11 us (14%)
    ppermute x6, waiting for transfers between devices, shifted(): lax.ppermute(value, 'space', [(i, (i + step) % count) for i in range(coun...  22.3 us
    pallas_call x7, Pallas kernels, kernel_call(): pl.pallas_call(body, out_shape=outputs, in_specs=in_specs, out_specs=jax....  11 us
    ppermute x10, waiting for transfers between devices, flipped(): lax.ppermute(value, 'tm', [(t, t ^ bit_on_core[t % 2]) for t in range(8)])  9.97 us
    ppermute x6, starting transfers between devices, shifted(): lax.ppermute(value, 'space', [(i, (i + step) % count) for i in range(coun...  9.05 us
    ppermute x10, starting transfers between devices, flipped(): lax.ppermute(value, 'tm', [(t, t ^ bit_on_core[t % 2]) for t in range(8)])  7.06 us
    ppermute x3, starting transfers between devices, plane_form(): upto = upto + lax.ppermute(total, 'tm', pairs).astype(jnp.float32)  6.51 us
    ppermute x1, starting transfers between devices, plane_form(): above = lax.ppermute(after(bottom, share), 'space', forward)  4.03 us
    ppermute x1, waiting for transfers between devices, plane_form(): below = lax.ppermute(after(top, share), 'space', backward)  2.64 us
  transfers between devices with their start and end apart: 23, of which 13 were waited for; matrix products, arithmetic and copies ran while one was open for 1% of the time, Pallas kernels for 8%

profile of v7, /device:TPU:0, one launch (start us, length us, event | category | flops | bytes accessed | tf_op | source)
XLA Modules:
  0.0 81.1 jit_solution(15344487756879807572)
XLA Ops:
  0.0 1.9 %shard_map.55 = (bf16[80,1152]{1,0:T(8,128)(2,1)}, bf16[2,64,1152]{2,1,0:T(8,128)(2,1)}) custom-call(bf16[288,3456]{1,0:T(8,128)(2,1)} %refs_1_.1, bf16[288,1152]{1,0:T(8,128)(2,1)} %refs_2_.3), custom_call_target="tpu_custom_call" | custom-call | bytes 958464 | tf_op jit(solution)/shard_map/pallas_call | solution.py:164
  2.0 3.1 %collective-permute-start = (bf16[1,80,1152]{2,1,0:T(8,128)(2,1)}, bf16[1,80,1152]{2,1,0:T(8,128)(2,1)S(1)}, u32[]{:S(2)}, u32[]{:S(2)}) collective-permute-start(bf16[1,80,1152]{2,1,0:T(8,128)(2,1)} %bitcast.8), channel_id=1, source_target_pairs={{0,1},{1,2},{2,3},{3,0},{4,5},{5,6},{6,7},{7,4},{8,9},{9,10},{10,1... | collective-permute-start | bytes 552968 | tf_op jit(solution)/shard_map/ppermute | solution.py:104
  5.0 2.1 %collective-permute-start.1 = (bf16[1,80,1152]{2,1,0:T(8,128)(2,1)}, bf16[1,80,1152]{2,1,0:T(8,128)(2,1)S(1)}, u32[]{:S(2)}, u32[]{:S(2)}) collective-permute-start(bf16[1,80,1152]{2,1,0:T(8,128)(2,1)} %bitcast.9), channel_id=1, source_target_pairs={{0,3},{1,0},{2,1},{3,2},{4,7},{5,4},{6,5},{7,6},{8,11},{9,8},{10,9... | collective-permute-start | bytes 552968 | tf_op jit(solution)/shard_map/ppermute | solution.py:104
  7.1 0.0 copy-done.3
  7.1 1.2 %shard_map.56.refs_0_ = bf16[256,1152]{1,0:T(8,128)(2,1)S(1)} custom-call(bf16[256,1152]{1,0:T(8,128)(2,1)S(1)} %bitcast.7), custom_call_target="tpu_custom_call" | custom-call | flops 679477248 | bytes 589824 | tf_op jit(solution)/shard_map/pallas_call | solution.py:164
  8.3 0.0 copy-start
  8.3 0.1 collective-permute-start.10
  8.4 4.4 %collective-permute-done = bf16[1,80,1152]{2,1,0:T(8,128)(2,1)S(1)} collective-permute-done((bf16[1,80,1152]{2,1,0:T(8,128)(2,1)}, bf16[1,80,1152]{2,1,0:T(8,128)(2,1)S(1)}, u32[]{:S(2)}, u32[]{:S(2)}) %collective-permute-start) | collective-permute-done | bytes 184352 | tf_op jit(solution)/shard_map/ppermute | solution.py:104
  12.8 2.5 %collective-permute-done.1 = bf16[1,80,1152]{2,1,0:T(8,128)(2,1)S(1)} collective-permute-done((bf16[1,80,1152]{2,1,0:T(8,128)(2,1)}, bf16[1,80,1152]{2,1,0:T(8,128)(2,1)S(1)}, u32[]{:S(2)}, u32[]{:S(2)}) %collective-permute-start.1) | collective-permute-done | bytes 184352 | tf_op jit(solution)/shard_map/ppermute | solution.py:104
  15.3 1.6 %collective-permute-start.11 = (bf16[2,80,1152]{2,1,0:T(8,128)(2,1)S(1)}, bf16[2,80,1152]{2,1,0:T(8,128)(2,1)S(1)}, u32[]{:S(2)}, u32[]{:S(2)}) collective-permute-start(bf16[2,80,1152]{2,1,0:T(8,128)(2,1)S(1)} %constant_dynamic-update-slice_fusion.7), channel_id=1, source_target_pairs={{0,8},{4,20},{8,0},{12,28},{16,24},{20,4},{24,16},{28,12},{1,9},{5... | collective-permute-start | bytes 1105928 | tf_op jit(solution)/shard_map/ppermute | solution.py:108
  16.9 1.1 %collective-permute-start.3 = (bf16[1,80,1152]{2,1,0:T(8,128)(2,1)S(1)}, bf16[1,80,1152]{2,1,0:T(8,128)(2,1)S(1)}, u32[]{:S(2)}, u32[]{:S(2)}) collective-permute-start(bf16[1,80,1152]{2,1,0:T(8,128)(2,1)S(1)} %collective-permute-done), channel_id=1, source_target_pairs={{0,1},{1,2},{2,3},{3,0},{4,5},{5,6},{6,7},{7,4},{8,9},{9,10},{10,1... | collective-permute-start | bytes 552968 | tf_op jit(solution)/shard_map/ppermute | solution.py:104
  18.0 0.0 copy-done.5
  18.0 0.7 collective-permute-start.2
  18.8 7.5 %collective-permute-done.3 = bf16[1,80,1152]{2,1,0:T(8,128)(2,1)S(1)} collective-permute-done((bf16[1,80,1152]{2,1,0:T(8,128)(2,1)S(1)}, bf16[1,80,1152]{2,1,0:T(8,128)(2,1)S(1)}, u32[]{:S(2)}, u32[]{:S(2)}) %collective-permute-start.3) | collective-permute-done | bytes 184352 | tf_op jit(solution)/shard_map/ppermute | solution.py:104
  26.3 0.4 collective-permute-start.4
  26.7 0.0 collective-permute-done.11
  26.7 0.0 collective-permute-done.10.refs_1_
  26.8 1.7 %collective-permute-start.12 = (bf16[4,80,1152]{2,1,0:T(8,128)(2,1)S(1)}, bf16[4,80,1152]{2,1,0:T(8,128)(2,1)S(1)}, u32[]{:S(2)}, u32[]{:S(2)}) collective-permute-start(bf16[4,80,1152]{2,1,0:T(8,128)(2,1)S(1)} %constant_dynamic-update-slice_fusion.9.refs_3_), channel_id=1, source_target_pairs={{0,16},{4,12},{8,24},{12,4},{16,0},{20,28},{24,8},{28,20},{1,17},{... | collective-permute-start | bytes 2211848 | tf_op jit(solution)/shard_map/ppermute | solution.py:108
  28.5 5.3 %collective-permute-done.4 = bf16[1,80,1152]{2,1,0:T(8,128)(2,1)S(1)} collective-permute-done((bf16[1,80,1152]{2,1,0:T(8,128)(2,1)S(1)}, bf16[1,80,1152]{2,1,0:T(8,128)(2,1)S(1)}, u32[]{:S(2)}, u32[]{:S(2)}) %collective-permute-start.4) | collective-permute-done | bytes 184352 | tf_op jit(solution)/shard_map/ppermute | solution.py:108
  33.9 1.6 %collective-permute-start.13 = (bf16[2,80,1152]{2,1,0:T(8,128)(2,1)S(1)}, bf16[2,80,1152]{2,1,0:T(8,128)(2,1)S(1)}, u32[]{:S(2)}, u32[]{:S(2)}) collective-permute-start(bf16[2,80,1152]{2,1,0:T(8,128)(2,1)S(1)} %constant_dynamic-update-slice_fusion.refs_5_), channel_id=1, source_target_pairs={{0,16},{4,12},{8,24},{12,4},{16,0},{20,28},{24,8},{28,20},{1,17},{... | collective-permute-start | bytes 1105928 | tf_op jit(solution)/shard_map/ppermute | solution.py:108
  35.4 0.1 collective-permute-start.6
  35.6 0.0 collective-permute-done.2
  35.6 1.9 %collective-permute-start.5 = (bf16[2,64,1152]{2,1,0:T(8,128)(2,1)S(1)}, bf16[2,64,1152]{2,1,0:T(8,128)(2,1)S(1)}, u32[]{:S(2)}, u32[]{:S(2)}) collective-permute-start(bf16[2,64,1152]{2,1,0:T(8,128)(2,1)S(1)} %collective-permute-done.2), channel_id=1, source_target_pairs={{0,1},{1,2},{2,3},{3,0},{4,5},{5,6},{6,7},{7,4},{8,9},{9,10},{10,1... | collective-permute-start | bytes 884744 | tf_op jit(solution)/shard_map/ppermute | solution.py:104
  37.5 7.9 %collective-permute-done.6 = bf16[2,64,1152]{2,1,0:T(8,128)(2,1)S(1)} collective-permute-done((bf16[2,64,1152]{2,1,0:T(8,128)(2,1)S(1)}, bf16[2,64,1152]{2,1,0:T(8,128)(2,1)S(1)}, u32[]{:S(2)}, u32[]{:S(2)}) %collective-permute-start.6) | collective-permute-done | bytes 294944 | tf_op jit(solution)/shard_map/ppermute | solution.py:104
  45.3 0.0 collective-permute-done.13.refs_6_
  45.3 0.0 collective-permute-done.12.refs_4_
  45.3 0.0 copy-done
  45.3 2.1 %shard_map.57.mine_ref.refs_7_ = bf16[608,1152]{1,0:T(8,128)(2,1)S(1)} custom-call(bf16[256,1152]{1,0:T(8,128)(2,1)S(1)} %shard_map.56.refs_0_, bf16[256,1152]{1,0:T(8,128)(2,1)S(1)} %collective-permute-done.10.refs_1_, bf16[288,3456]{1,0:T(8,128)(2,1)S(1)} %copy-done, bf16[4,80,1152]{2,1,0:T(8,128)(2,1)S(1)} %constant_dynamic-update-slice_fusion.9.refs_3_, ...), custom_call_target="tpu_custom_call" | custom-call | flops 1358954496 | bytes 2654208 | tf_op jit(solution)/shard_map/pallas_call | solution.py:164
  47.5 0.0 collective-permute-done.5
  47.5 0.1 collective-permute-start.14
  47.7 0.6 collective-permute-start.7
  48.3 0.1 pad_maximum_fusion
  48.4 0.6 collective-permute-start.8
  49.0 0.4 collective-permute-start.9
  49.4 1.3 %collective-permute-done.14.other_ref.refs_8_ = bf16[608,1152]{1,0:T(8,128)(2,1)S(1)} collective-permute-done((bf16[608,1152]{1,0:T(8,128)(2,1)S(1)}, bf16[608,1152]{1,0:T(8,128)(2,1)S(1)}, u32[]{:S(2)}, u32[]{:S(2)}) %collective-permute-start.14) | collective-permute-done | bytes 1400864 | tf_op jit(solution)/shard_map/ppermute | solution.py:108
  50.7 0.9 %shard_map.58 = (bf16[256,1152]{1,0:T(8,128)(2,1)S(1)}, bf16[1,64,1152]{2,1,0:T(8,128)(2,1)S(1)}, bf16[1,64,1152]{2,1,0:T(8,128)(2,1)S(1)}, f32[9,32,128]{2,1,0:T(8,128)S(1)}, bf16[9,32,128]{2,1,0:T(8,128)(2,1)S(1)}) custom-call(bf16[608,1152]{1,0:T(8,128)(2,1)S(1)} %shard_map.57.mine_ref.refs_7_, bf16[608,1152]{1,0:T(8,128)(2,1)S(1)} %collective-permute-done.14.other_ref.refs_8_), custom_call_target="tpu_custom_call" | custom-call | flops 150994944 | bytes 2359296 | tf_op jit(solution)/shard_map/pallas_call | solution.py:164
  51.6 0.0 copy-start.2
  51.6 0.4 collective-permute-done.7.refs_4_
  52.0 2.4 %collective-permute-start.15 = (bf16[9,32,128]{2,1,0:T(8,128)(2,1)S(1)}, bf16[9,32,128]{2,1,0:T(8,128)(2,1)S(1)}, u32[]{:S(2)}, u32[]{:S(2)}) collective-permute-start(bf16[9,32,128]{2,1,0:T(8,128)(2,1)S(1)} %get-tuple-element.44), channel_id=1, source_target_pairs={{0,8},{4,12},{16,24},{20,28},{1,9},{5,13},{17,25},{21,29},{2,10},{... | collective-permute-start | bytes 221192 | tf_op jit(solution)/shard_map/ppermute | solution.py:546
  54.4 2.8 %collective-permute-start.16 = (bf16[9,32,128]{2,1,0:T(8,128)(2,1)S(1)}, bf16[9,32,128]{2,1,0:T(8,128)(2,1)S(1)}, u32[]{:S(2)}, u32[]{:S(2)}) collective-permute-start(bf16[9,32,128]{2,1,0:T(8,128)(2,1)S(1)} %get-tuple-element.44), channel_id=1, source_target_pairs={{0,16},{4,20},{8,24},{12,28},{1,17},{5,21},{9,25},{13,29},{2,18},{... | collective-permute-start | bytes 221192 | tf_op jit(solution)/shard_map/ppermute | solution.py:546
  57.2 1.3 %collective-permute-start.17 = (bf16[9,32,128]{2,1,0:T(8,128)(2,1)S(1)}, bf16[9,32,128]{2,1,0:T(8,128)(2,1)S(1)}, u32[]{:S(2)}, u32[]{:S(2)}) collective-permute-start(bf16[9,32,128]{2,1,0:T(8,128)(2,1)S(1)} %get-tuple-element.44), channel_id=1, source_target_pairs={{0,24},{4,28},{8,16},{12,20},{1,25},{5,29},{9,17},{13,21},{2,26},{... | collective-permute-start | bytes 221192 | tf_op jit(solution)/shard_map/ppermute | solution.py:546
  58.5 2.9 %collective-permute-done.8 = bf16[3,64,1152]{2,1,0:T(8,128)(2,1)S(1)} collective-permute-done((bf16[3,64,1152]{2,1,0:T(8,128)(2,1)S(1)}, bf16[3,64,1152]{2,1,0:T(8,128)(2,1)S(1)}, u32[]{:S(2)}, u32[]{:S(2)}) %collective-permute-start.8) | collective-permute-done | bytes 442400 | tf_op jit(solution)/shard_map/ppermute | solution.py:108
  61.5 0.0 collective-permute-done.15
  61.5 0.3 collective-permute-done.16
  61.7 0.1 collective-permute-done.17
  61.9 0.0 collective-permute-done.9
  61.9 0.1 collective-permute-start.18
  62.0 0.0 copy-start.4
  62.0 4.0 %collective-permute-start.19 = (bf16[1,64,1152]{2,1,0:T(8,128)(2,1)S(1)}, bf16[1,64,1152]{2,1,0:T(8,128)(2,1)S(1)}, u32[]{:S(2)}, u32[]{:S(2)}) collective-permute-start(bf16[1,64,1152]{2,1,0:T(8,128)(2,1)S(1)} %get-tuple-element.48), channel_id=1, source_target_pairs={{0,1},{1,2},{2,3},{4,5},{5,6},{6,7},{8,9},{9,10},{10,11},{12,13},{... | collective-permute-start | bytes 442376 | tf_op jit(solution)/shard_map/ppermute | solution.py:555
  66.1 0.0 copy-start.1
  66.1 0.0 copy-done.2
  66.1 0.9 %shard_map.59 = f32[4,64,1152]{2,1,0:T(8,128)S(1)} custom-call(bf16[4,64,1152]{2,1,0:T(8,128)(2,1)S(1)} %bitcast.6, f32[3,3,1152]{2,1,0:T(4,128)S(1)} %copy-done.2), custom_call_target="tpu_custom_call" | custom-call | flops 5308416 | bytes 1769472 | tf_op jit(solution)/shard_map/pallas_call | solution.py:164
  67.0 0.0 collective-permute-done.18
  67.0 1.7 %collective-permute-done.19.refs_4_ = bf16[1,64,1152]{2,1,0:T(8,128)(2,1)S(1)} collective-permute-done((bf16[1,64,1152]{2,1,0:T(8,128)(2,1)S(1)}, bf16[1,64,1152]{2,1,0:T(8,128)(2,1)S(1)}, u32[]{:S(2)}, u32[]{:S(2)}) %collective-permute-start.19) | collective-permute-done | bytes 147488 | tf_op jit(solution)/shard_map/ppermute | solution.py:555
  68.7 0.1 collective-permute-start.20
  68.8 2.0 %collective-permute-start.21 = (bf16[9,32,128]{2,1,0:T(8,128)(2,1)S(1)}, bf16[9,32,128]{2,1,0:T(8,128)(2,1)S(1)}, u32[]{:S(2)}, u32[]{:S(2)}) collective-permute-start(bf16[9,32,128]{2,1,0:T(8,128)(2,1)S(1)} %add_convert_fusion), channel_id=1, source_target_pairs={{0,2},{1,3},{2,0},{3,1},{4,6},{5,7},{6,4},{7,5},{8,10},{9,11},{10,... | collective-permute-start | bytes 221192 | tf_op jit(solution)/shard_map/ppermute | solution.py:558
  70.8 0.0 copy-done.4
  70.8 1.3 %collective-permute-start.22 = (bf16[1,64,1152]{2,1,0:T(8,128)(2,1)S(1)}, bf16[1,64,1152]{2,1,0:T(8,128)(2,1)S(1)}, u32[]{:S(2)}, u32[]{:S(2)}) collective-permute-start(bf16[1,64,1152]{2,1,0:T(8,128)(2,1)S(1)} %get-tuple-element.54), channel_id=1, source_target_pairs={{1,0},{2,1},{3,2},{5,4},{6,5},{7,6},{9,8},{10,9},{11,10},{13,12},{... | collective-permute-start | bytes 442376 | tf_op jit(solution)/shard_map/ppermute | solution.py:559
  72.1 2.3 %collective-permute-done.21 = bf16[9,32,128]{2,1,0:T(8,128)(2,1)S(1)} collective-permute-done((bf16[9,32,128]{2,1,0:T(8,128)(2,1)S(1)}, bf16[9,32,128]{2,1,0:T(8,128)(2,1)S(1)}, u32[]{:S(2)}, u32[]{:S(2)}) %collective-permute-start.21) | collective-permute-done | bytes 73760 | tf_op jit(solution)/shard_map/ppermute | solution.py:558
  74.4 0.0 collective-permute-done.20.refs_6_
  74.4 0.0 copy-done.1
  74.4 1.5 %shard_map.60 = (bf16[256,1152]{1,0:T(8,128)(2,1)S(1)}, bf16[1152,1152]{1,0:T(8,128)(2,1)S(1)}) custom-call(bf16[256,1152]{1,0:T(8,128)(2,1)S(1)} %shard_map.56.refs_0_, bf16[288,3456]{1,0:T(8,128)(2,1)S(1)} %copy-done, bf16[288,1152]{1,0:T(8,128)(2,1)S(1)} %copy-done.1, bf16[6,64,1152]{2,1,0:T(8,128)(2,1)S(1)} %constant_dynamic-update-slice_fusion.2.refs_3_, ...), custom_call_target="tpu_custom_call" | custom-call | flops 679477248 | bytes 5308416 | tf_op jit(solution)/shard_map/pallas_call | solution.py:164
  76.0 2.6 %collective-permute-done.22.refs_5_ = bf16[1,64,1152]{2,1,0:T(8,128)(2,1)S(1)} collective-permute-done((bf16[1,64,1152]{2,1,0:T(8,128)(2,1)S(1)}, bf16[1,64,1152]{2,1,0:T(8,128)(2,1)S(1)}, u32[]{:S(2)}, u32[]{:S(2)}) %collective-permute-start.22) | collective-permute-done | bytes 147488 | tf_op jit(solution)/shard_map/ppermute | solution.py:559
  78.6 2.5 %shard_map.61 = bf16[256,1152]{1,0:T(8,128)(2,1)} custom-call(bf16[256,1152]{1,0:T(8,128)(2,1)S(1)} %get-tuple-element.51.refs_0_, bf16[1152,1152]{1,0:T(8,128)(2,1)S(1)} %get-tuple-element.52.refs_1_, f32[9,32,128]{2,1,0:T(8,128)S(1)} %convert_add_fusion.refs_2_, f32[256,1152]{1,0:T(8,128)S(1)} %bitcast.5, ...), custom_call_target="tpu_custom_call" | custom-call | flops 679477248 | bytes 2654208 | tf_op jit(solution)/shard_map/pallas_call | solution.py:164
  (20 shorter events, 0.4 us)
Async XLA Ops:
  0.0 7.1 %copy-start.3 = (bf16[1,4,64,1152]{3,2,1,0:T(8,128)(2,1)S(1)}, bf16[1,4,64,1152]{3,2,1,0:T(8,128)(2,1)}, u32[]{:S(2)}) copy-start(bf16[1,4,64,1152]{3,2,1,0:T(8,128)(2,1)} %param.5) | copy-start | bytes 1769476
  2.0 10.8 %collective-permute-start = (bf16[1,80,1152]{2,1,0:T(8,128)(2,1)}, bf16[1,80,1152]{2,1,0:T(8,128)(2,1)S(1)}, u32[]{:S(2)}, u32[]{:S(2)}) collective-permute-start(bf16[1,80,1152]{2,1,0:T(8,128)(2,1)} %bitcast.8), channel_id=1, source_target_pairs={{0,1},{1,2},{2,3},{3,0},{4,5},{5,6},{6,7},{7,4},{8,9},{9,10},{10,1... | collective-permute-start | bytes 552968 | tf_op jit(solution)/shard_map/ppermute | solution.py:104
  5.0 10.3 %collective-permute-start.1 = (bf16[1,80,1152]{2,1,0:T(8,128)(2,1)}, bf16[1,80,1152]{2,1,0:T(8,128)(2,1)S(1)}, u32[]{:S(2)}, u32[]{:S(2)}) collective-permute-start(bf16[1,80,1152]{2,1,0:T(8,128)(2,1)} %bitcast.9), channel_id=1, source_target_pairs={{0,3},{1,0},{2,1},{3,2},{4,7},{5,4},{6,5},{7,6},{8,11},{9,8},{10,9... | collective-permute-start | bytes 552968 | tf_op jit(solution)/shard_map/ppermute | solution.py:104
  7.1 10.9 %copy-start.5 = (bf16[2,64,1152]{2,1,0:T(8,128)(2,1)S(1)}, bf16[2,64,1152]{2,1,0:T(8,128)(2,1)}, u32[]{:S(2)}) copy-start(bf16[2,64,1152]{2,1,0:T(8,128)(2,1)} %get-tuple-element.36) | copy-start | bytes 884740
  8.3 37.0 %copy-start = (bf16[288,3456]{1,0:T(8,128)(2,1)S(1)}, bf16[288,3456]{1,0:T(8,128)(2,1)}, u32[]{:S(2)}) copy-start(bf16[288,3456]{1,0:T(8,128)(2,1)} %refs_1_.1) | copy-start | bytes 5971972
  8.3 18.4 %collective-permute-start.10 = (bf16[256,1152]{1,0:T(8,128)(2,1)S(1)}, bf16[256,1152]{1,0:T(8,128)(2,1)S(1)}, u32[]{:S(2)}, u32[]{:S(2)}) collective-permute-start(bf16[256,1152]{1,0:T(8,128)(2,1)S(1)} %shard_map.56.refs_0_), channel_id=1, source_target_pairs={{0,4},{4,0},{8,12},{12,8},{16,20},{20,16},{24,28},{28,24},{1,5},{5... | collective-permute-start | bytes 1769480 | tf_op jit(solution)/shard_map/ppermute | solution.py:108
  15.3 11.4 %collective-permute-start.11 = (bf16[2,80,1152]{2,1,0:T(8,128)(2,1)S(1)}, bf16[2,80,1152]{2,1,0:T(8,128)(2,1)S(1)}, u32[]{:S(2)}, u32[]{:S(2)}) collective-permute-start(bf16[2,80,1152]{2,1,0:T(8,128)(2,1)S(1)} %constant_dynamic-update-slice_fusion.7), channel_id=1, source_target_pairs={{0,8},{4,20},{8,0},{12,28},{16,24},{20,4},{24,16},{28,12},{1,9},{5... | collective-permute-start | bytes 1105928 | tf_op jit(solution)/shard_map/ppermute | solution.py:108
  16.9 9.4 %collective-permute-start.3 = (bf16[1,80,1152]{2,1,0:T(8,128)(2,1)S(1)}, bf16[1,80,1152]{2,1,0:T(8,128)(2,1)S(1)}, u32[]{:S(2)}, u32[]{:S(2)}) collective-permute-start(bf16[1,80,1152]{2,1,0:T(8,128)(2,1)S(1)} %collective-permute-done), channel_id=1, source_target_pairs={{0,1},{1,2},{2,3},{3,0},{4,5},{5,6},{6,7},{7,4},{8,9},{9,10},{10,1... | collective-permute-start | bytes 552968 | tf_op jit(solution)/shard_map/ppermute | solution.py:104
  18.0 17.6 %collective-permute-start.2 = (bf16[2,64,1152]{2,1,0:T(8,128)(2,1)S(1)}, bf16[2,64,1152]{2,1,0:T(8,128)(2,1)S(1)}, u32[]{:S(2)}, u32[]{:S(2)}) collective-permute-start(bf16[2,64,1152]{2,1,0:T(8,128)(2,1)S(1)} %copy-done.5), channel_id=1, source_target_pairs={{0,1},{1,2},{2,3},{3,0},{4,5},{5,6},{6,7},{7,4},{8,9},{9,10},{10,1... | collective-permute-start | bytes 884744 | tf_op jit(solution)/shard_map/ppermute | solution.py:104
  26.3 7.6 %collective-permute-start.4 = (bf16[1,80,1152]{2,1,0:T(8,128)(2,1)S(1)}, bf16[1,80,1152]{2,1,0:T(8,128)(2,1)S(1)}, u32[]{:S(2)}, u32[]{:S(2)}) collective-permute-start(bf16[1,80,1152]{2,1,0:T(8,128)(2,1)S(1)} %collective-permute-done.3), channel_id=1, source_target_pairs={{0,8},{4,20},{8,0},{12,28},{16,24},{20,4},{24,16},{28,12},{1,9},{5... | collective-permute-start | bytes 552968 | tf_op jit(solution)/shard_map/ppermute | solution.py:108
  26.8 18.5 %collective-permute-start.12 = (bf16[4,80,1152]{2,1,0:T(8,128)(2,1)S(1)}, bf16[4,80,1152]{2,1,0:T(8,128)(2,1)S(1)}, u32[]{:S(2)}, u32[]{:S(2)}) collective-permute-start(bf16[4,80,1152]{2,1,0:T(8,128)(2,1)S(1)} %constant_dynamic-update-slice_fusion.9.refs_3_), channel_id=1, source_target_pairs={{0,16},{4,12},{8,24},{12,4},{16,0},{20,28},{24,8},{28,20},{1,17},{... | collective-permute-start | bytes 2211848 | tf_op jit(solution)/shard_map/ppermute | solution.py:108
  33.9 11.5 %collective-permute-start.13 = (bf16[2,80,1152]{2,1,0:T(8,128)(2,1)S(1)}, bf16[2,80,1152]{2,1,0:T(8,128)(2,1)S(1)}, u32[]{:S(2)}, u32[]{:S(2)}) collective-permute-start(bf16[2,80,1152]{2,1,0:T(8,128)(2,1)S(1)} %constant_dynamic-update-slice_fusion.refs_5_), channel_id=1, source_target_pairs={{0,16},{4,12},{8,24},{12,4},{16,0},{20,28},{24,8},{28,20},{1,17},{... | collective-permute-start | bytes 1105928 | tf_op jit(solution)/shard_map/ppermute | solution.py:108
  35.4 9.9 %collective-permute-start.6 = (bf16[2,64,1152]{2,1,0:T(8,128)(2,1)S(1)}, bf16[2,64,1152]{2,1,0:T(8,128)(2,1)S(1)}, u32[]{:S(2)}, u32[]{:S(2)}) collective-permute-start(bf16[2,64,1152]{2,1,0:T(8,128)(2,1)S(1)} %copy-done.5), channel_id=1, source_target_pairs={{0,3},{1,0},{2,1},{3,2},{4,7},{5,4},{6,5},{7,6},{8,11},{9,8},{10,9... | collective-permute-start | bytes 884744 | tf_op jit(solution)/shard_map/ppermute | solution.py:104
  35.6 11.9 %collective-permute-start.5 = (bf16[2,64,1152]{2,1,0:T(8,128)(2,1)S(1)}, bf16[2,64,1152]{2,1,0:T(8,128)(2,1)S(1)}, u32[]{:S(2)}, u32[]{:S(2)}) collective-permute-start(bf16[2,64,1152]{2,1,0:T(8,128)(2,1)S(1)} %collective-permute-done.2), channel_id=1, source_target_pairs={{0,1},{1,2},{2,3},{3,0},{4,5},{5,6},{6,7},{7,4},{8,9},{9,10},{10,1... | collective-permute-start | bytes 884744 | tf_op jit(solution)/shard_map/ppermute | solution.py:104
  47.5 3.2 %collective-permute-start.14 = (bf16[608,1152]{1,0:T(8,128)(2,1)S(1)}, bf16[608,1152]{1,0:T(8,128)(2,1)S(1)}, u32[]{:S(2)}, u32[]{:S(2)}) collective-permute-start(bf16[608,1152]{1,0:T(8,128)(2,1)S(1)} %shard_map.57.mine_ref.refs_7_), channel_id=1, source_target_pairs={{0,4},{4,0},{8,12},{12,8},{16,20},{20,16},{24,28},{28,24},{1,5},{5... | collective-permute-start | bytes 4202504 | tf_op jit(solution)/shard_map/ppermute | solution.py:108
  47.7 4.3 %collective-permute-start.7 = (bf16[6,64,1152]{2,1,0:T(8,128)(2,1)S(1)}, bf16[6,64,1152]{2,1,0:T(8,128)(2,1)S(1)}, u32[]{:S(2)}, u32[]{:S(2)}) collective-permute-start(bf16[6,64,1152]{2,1,0:T(8,128)(2,1)S(1)} %constant_dynamic-update-slice_fusion.2.refs_3_), channel_id=1, source_target_pairs={{0,4},{4,0},{8,12},{12,8},{16,20},{20,16},{24,28},{28,24},{1,5},{5... | collective-permute-start | bytes 2654216 | tf_op jit(solution)/shard_map/ppermute | solution.py:108
  48.4 13.1 %collective-permute-start.8 = (bf16[3,64,1152]{2,1,0:T(8,128)(2,1)S(1)}, bf16[3,64,1152]{2,1,0:T(8,128)(2,1)S(1)}, u32[]{:S(2)}, u32[]{:S(2)}) collective-permute-start(bf16[3,64,1152]{2,1,0:T(8,128)(2,1)S(1)} %pad_maximum_fusion), channel_id=1, source_target_pairs={{0,8},{4,20},{8,0},{12,28},{16,24},{20,4},{24,16},{28,12},{1,9},{5... | collective-permute-start | bytes 1327112 | tf_op jit(solution)/shard_map/ppermute | solution.py:108
  49.0 13.0 %collective-permute-start.9 = (bf16[3,64,1152]{2,1,0:T(8,128)(2,1)S(1)}, bf16[3,64,1152]{2,1,0:T(8,128)(2,1)S(1)}, u32[]{:S(2)}, u32[]{:S(2)}) collective-permute-start(bf16[3,64,1152]{2,1,0:T(8,128)(2,1)S(1)} %pad_maximum_fusion), channel_id=1, source_target_pairs={{0,16},{4,12},{8,24},{12,4},{16,0},{20,28},{24,8},{28,20},{1,17},{... | collective-permute-start | bytes 1327112 | tf_op jit(solution)/shard_map/ppermute | solution.py:108
  51.6 14.5 %copy-start.2 = (f32[3,3,1152]{2,1,0:T(4,128)S(1)}, f32[3,3,1152]{2,1,0:T(4,128)}, u32[]{:S(2)}) copy-start(f32[3,3,1152]{2,1,0:T(4,128)} %refs_6_.1) | copy-start | bytes 124420
  52.0 9.5 %collective-permute-start.15 = (bf16[9,32,128]{2,1,0:T(8,128)(2,1)S(1)}, bf16[9,32,128]{2,1,0:T(8,128)(2,1)S(1)}, u32[]{:S(2)}, u32[]{:S(2)}) collective-permute-start(bf16[9,32,128]{2,1,0:T(8,128)(2,1)S(1)} %get-tuple-element.44), channel_id=1, source_target_pairs={{0,8},{4,12},{16,24},{20,28},{1,9},{5,13},{17,25},{21,29},{2,10},{... | collective-permute-start | bytes 221192 | tf_op jit(solution)/shard_map/ppermute | solution.py:546
  54.4 7.3 %collective-permute-start.16 = (bf16[9,32,128]{2,1,0:T(8,128)(2,1)S(1)}, bf16[9,32,128]{2,1,0:T(8,128)(2,1)S(1)}, u32[]{:S(2)}, u32[]{:S(2)}) collective-permute-start(bf16[9,32,128]{2,1,0:T(8,128)(2,1)S(1)} %get-tuple-element.44), channel_id=1, source_target_pairs={{0,16},{4,20},{8,24},{12,28},{1,17},{5,21},{9,25},{13,29},{2,18},{... | collective-permute-start | bytes 221192 | tf_op jit(solution)/shard_map/ppermute | solution.py:546
  57.2 4.7 %collective-permute-start.17 = (bf16[9,32,128]{2,1,0:T(8,128)(2,1)S(1)}, bf16[9,32,128]{2,1,0:T(8,128)(2,1)S(1)}, u32[]{:S(2)}, u32[]{:S(2)}) collective-permute-start(bf16[9,32,128]{2,1,0:T(8,128)(2,1)S(1)} %get-tuple-element.44), channel_id=1, source_target_pairs={{0,24},{4,28},{8,16},{12,20},{1,25},{5,29},{9,17},{13,21},{2,26},{... | collective-permute-start | bytes 221192 | tf_op jit(solution)/shard_map/ppermute | solution.py:546
  61.9 5.1 %collective-permute-start.18 = (bf16[9,32,128]{2,1,0:T(8,128)(2,1)S(1)}, bf16[9,32,128]{2,1,0:T(8,128)(2,1)S(1)}, u32[]{:S(2)}, u32[]{:S(2)}) collective-permute-start(bf16[9,32,128]{2,1,0:T(8,128)(2,1)S(1)} %convert_add_fusion.1), channel_id=1, source_target_pairs={{0,1},{1,0},{2,3},{3,2},{4,5},{5,4},{6,7},{7,6},{8,9},{9,8},{10,11... | collective-permute-start | bytes 221192 | tf_op jit(solution)/shard_map/ppermute | solution.py:554
  62.0 8.8 %copy-start.4 = (f32[1152]{0:T(1024)S(1)}, f32[1152]{0:T(1024)}, u32[]{:S(2)}) copy-start(f32[1152]{0:T(1024)} %param.9) | copy-start | bytes 13828
  62.0 6.7 %collective-permute-start.19 = (bf16[1,64,1152]{2,1,0:T(8,128)(2,1)S(1)}, bf16[1,64,1152]{2,1,0:T(8,128)(2,1)S(1)}, u32[]{:S(2)}, u32[]{:S(2)}) collective-permute-start(bf16[1,64,1152]{2,1,0:T(8,128)(2,1)S(1)} %get-tuple-element.48), channel_id=1, source_target_pairs={{0,1},{1,2},{2,3},{4,5},{5,6},{6,7},{8,9},{9,10},{10,11},{12,13},{... | collective-permute-start | bytes 442376 | tf_op jit(solution)/shard_map/ppermute | solution.py:555
  66.1 8.3 %copy-start.1 = (bf16[288,1152]{1,0:T(8,128)(2,1)S(1)}, bf16[288,1152]{1,0:T(8,128)(2,1)}, u32[]{:S(2)}) copy-start(bf16[288,1152]{1,0:T(8,128)(2,1)} %refs_2_.3) | copy-start | bytes 1990660
  68.7 5.7 %collective-permute-start.20 = (bf16[6,64,1152]{2,1,0:T(8,128)(2,1)S(1)}, bf16[6,64,1152]{2,1,0:T(8,128)(2,1)S(1)}, u32[]{:S(2)}, u32[]{:S(2)}) collective-permute-start(bf16[6,64,1152]{2,1,0:T(8,128)(2,1)S(1)} %constant_dynamic-update-slice_fusion.5.refs_5_), channel_id=1, source_target_pairs={{0,4},{4,0},{8,12},{12,8},{16,20},{20,16},{24,28},{28,24},{1,5},{5... | collective-permute-start | bytes 2654216 | tf_op jit(solution)/shard_map/ppermute | solution.py:108
  68.8 5.6 %collective-permute-start.21 = (bf16[9,32,128]{2,1,0:T(8,128)(2,1)S(1)}, bf16[9,32,128]{2,1,0:T(8,128)(2,1)S(1)}, u32[]{:S(2)}, u32[]{:S(2)}) collective-permute-start(bf16[9,32,128]{2,1,0:T(8,128)(2,1)S(1)} %add_convert_fusion), channel_id=1, source_target_pairs={{0,2},{1,3},{2,0},{3,1},{4,6},{5,7},{6,4},{7,5},{8,10},{9,11},{10,... | collective-permute-start | bytes 221192 | tf_op jit(solution)/shard_map/ppermute | solution.py:558
  70.8 7.8 %collective-permute-start.22 = (bf16[1,64,1152]{2,1,0:T(8,128)(2,1)S(1)}, bf16[1,64,1152]{2,1,0:T(8,128)(2,1)S(1)}, u32[]{:S(2)}, u32[]{:S(2)}) collective-permute-start(bf16[1,64,1152]{2,1,0:T(8,128)(2,1)S(1)} %get-tuple-element.54), channel_id=1, source_target_pairs={{1,0},{2,1},{3,2},{5,4},{6,5},{7,6},{9,8},{10,9},{11,10},{13,12},{... | collective-permute-start | bytes 442376 | tf_op jit(solution)/shard_map/ppermute | solution.py:559

commit v8 on v6

--- a/solution.py
+++ b/solution.py
@@ -159,13 +159,21 @@
 
 
 def kernel_call(
-    body, outputs, inputs, in_specs, scratch=(), flops=0, bytes_accessed=0, limit=VMEM_LIMIT
+    body,
+    outputs,
+    inputs,
+    in_specs,
+    scratch=(),
+    flops=0,
+    bytes_accessed=0,
+    limit=VMEM_LIMIT,
+    out_spec=whole_vmem,
 ):
     return pl.pallas_call(
         body,
         out_shape=outputs,
         in_specs=in_specs,
-        out_specs=jax.tree.map(lambda _: whole_vmem(), outputs),
+        out_specs=jax.tree.map(lambda _: out_spec(), outputs),
         scratch_shapes=list(scratch),
         compiler_params=pltpu.CompilerParams(vmem_limit_bytes=limit),
         cost_estimate=pl.CostEstimate(
@@ -230,6 +238,7 @@
         [pltpu.SemaphoreType.DMA((4,))],
         bytes_accessed=4 * (3 * MAIN + REST) * depth,
         limit=WHOLE_VMEM,
+        out_spec=anywhere,
     )
 
 
@@ -539,7 +548,7 @@
 
     second_own = jnp.stack([second_one[0], second_two[0], second_three[0]])
     second_first = flipped(second_own, (2, 4))
-    second_second = flipped(second_own, (4, 2))
+    second_second = flipped(after(second_own, total), (4, 2))
 
     for bit, guard in ((2, 2), (4, 4), (6, 4)):
         pairs = [(t, t ^ bit) for t in range(8) if not t & guard]
@@ -547,7 +556,7 @@
     count = lax.axis_size("space")
     forward = [(i, i + 1) for i in range(count - 1)]
     backward = [(target, source) for source, target in forward]
-    state = after(upto, second_first, second_second)
+    state = after(upto, second_first)
     share = state.astype(jnp.bfloat16)
     grid = values.reshape(row_count, col_count, depth)
     local_term = local_call(grid, conv_weight).reshape(-1, depth)

time: 80.5 us -> 94.2 us (1.17)
  Pallas kernels: 11 us -> 24.7 us
  waiting for transfers between devices: 42.4 us -> 43.4 us
    pallas_call x7, Pallas kernels: 11 us -> 24.7 us  [kernel_call(): pl.pallas_call(body, out_shape=outputs, in_specs=in_specs, out_specs=jax....]
    ppermute x3, waiting for transfers between devices: 0.39 us -> 2.39 us  [plane_form(): upto = upto + lax.ppermute(total, 'tm', pairs).astype(jnp.float32)]
    ppermute x10, waiting for transfers between devices: 9.97 us -> 8.88 us  [flipped(): lax.ppermute(value, 'tm', [(t, t ^ bit_on_core[t % 2]) for t in range(8)])]
  transfers between devices with their start and end apart: 23 -> 23, of which waited for: 13 -> 13; matrix products, arithmetic and copies ran while one was open for 1% -> 0% of each run, Pallas kernels for 8% -> 7%
where the time goes in v8:
time: 94.2 us; the launch traced here: 94 us
  waiting for transfers between devices  43.4 us (46%)
  starting transfers between devices  25.1 us (27%)
  Pallas kernels  24.7 us (26%)
    pallas_call x7, Pallas kernels, kernel_call(): pl.pallas_call(body, out_shape=outputs, in_specs=in_specs, out_specs=jax....  24.7 us
    ppermute x6, waiting for transfers between devices, shifted(): lax.ppermute(value, 'space', [(i, (i + step) % count) for i in range(coun...  22.3 us
    ppermute x6, starting transfers between devices, shifted(): lax.ppermute(value, 'space', [(i, (i + step) % count) for i in range(coun...  9.05 us
    ppermute x10, waiting for transfers between devices, flipped(): lax.ppermute(value, 'tm', [(t, t ^ bit_on_core[t % 2]) for t in range(8)])  8.88 us
    ppermute x10, starting transfers between devices, flipped(): lax.ppermute(value, 'tm', [(t, t ^ bit_on_core[t % 2]) for t in range(8)])  6.7 us
    ppermute x3, starting transfers between devices, plane_form(): upto = upto + lax.ppermute(total, 'tm', pairs).astype(jnp.float32)  6.05 us
    ppermute x1, waiting for transfers between devices, plane_form(): arrived = lax.ppermute(share, 'space', [(i, i ^ 1) for i in range(count)])  3.4 us
    ppermute x1, waiting for transfers between devices, plane_form(): arrived = lax.ppermute(share, 'space', [(i, i ^ 2) for i in range(count)])  3.28 us
  transfers between devices with their start and end apart: 23, of which 13 were waited for; matrix products, arithmetic and copies ran while one was open for 0% of the time, Pallas kernels for 7%

profile of v8, /device:TPU:0, one launch (start us, length us, event | category | flops | bytes accessed | tf_op | source)
XLA Modules:
  0.0 94.0 jit_solution(6469004208931456066)
XLA Ops:
  0.0 15.7 %shard_map.55 = (bf16[80,1152]{1,0:T(8,128)(2,1)}, bf16[2,64,1152]{2,1,0:T(8,128)(2,1)}) custom-call(bf16[288,3456]{1,0:T(8,128)(2,1)} %refs_1_.1, bf16[288,1152]{1,0:T(8,128)(2,1)} %refs_2_.3), custom_call_target="tpu_custom_call" | custom-call | bytes 958464 | tf_op jit(solution)/shard_map/pallas_call | solution.py:172
  15.7 3.1 %collective-permute-start = (bf16[1,80,1152]{2,1,0:T(8,128)(2,1)}, bf16[1,80,1152]{2,1,0:T(8,128)(2,1)S(1)}, u32[]{:S(2)}, u32[]{:S(2)}) collective-permute-start(bf16[1,80,1152]{2,1,0:T(8,128)(2,1)} %bitcast.8), channel_id=1, source_target_pairs={{0,1},{1,2},{2,3},{3,0},{4,5},{5,6},{6,7},{7,4},{8,9},{9,10},{10,1... | collective-permute-start | bytes 552968 | tf_op jit(solution)/shard_map/ppermute | solution.py:104
  18.7 2.1 %collective-permute-start.1 = (bf16[1,80,1152]{2,1,0:T(8,128)(2,1)}, bf16[1,80,1152]{2,1,0:T(8,128)(2,1)S(1)}, u32[]{:S(2)}, u32[]{:S(2)}) collective-permute-start(bf16[1,80,1152]{2,1,0:T(8,128)(2,1)} %bitcast.9), channel_id=1, source_target_pairs={{0,3},{1,0},{2,1},{3,2},{4,7},{5,4},{6,5},{7,6},{8,11},{9,8},{10,9... | collective-permute-start | bytes 552968 | tf_op jit(solution)/shard_map/ppermute | solution.py:104
  20.8 0.0 copy-done.3
  20.8 1.2 %shard_map.56.refs_0_ = bf16[256,1152]{1,0:T(8,128)(2,1)S(1)} custom-call(bf16[256,1152]{1,0:T(8,128)(2,1)S(1)} %bitcast.7), custom_call_target="tpu_custom_call" | custom-call | flops 679477248 | bytes 589824 | tf_op jit(solution)/shard_map/pallas_call | solution.py:172
  22.0 0.0 copy-start
  22.0 0.1 collective-permute-start.9
  22.1 4.4 %collective-permute-done = bf16[1,80,1152]{2,1,0:T(8,128)(2,1)S(1)} collective-permute-done((bf16[1,80,1152]{2,1,0:T(8,128)(2,1)}, bf16[1,80,1152]{2,1,0:T(8,128)(2,1)S(1)}, u32[]{:S(2)}, u32[]{:S(2)}) %collective-permute-start) | collective-permute-done | bytes 184352 | tf_op jit(solution)/shard_map/ppermute | solution.py:104
  26.5 2.5 %collective-permute-done.1 = bf16[1,80,1152]{2,1,0:T(8,128)(2,1)S(1)} collective-permute-done((bf16[1,80,1152]{2,1,0:T(8,128)(2,1)}, bf16[1,80,1152]{2,1,0:T(8,128)(2,1)S(1)}, u32[]{:S(2)}, u32[]{:S(2)}) %collective-permute-start.1) | collective-permute-done | bytes 184352 | tf_op jit(solution)/shard_map/ppermute | solution.py:104
  29.0 1.6 %collective-permute-start.10 = (bf16[2,80,1152]{2,1,0:T(8,128)(2,1)S(1)}, bf16[2,80,1152]{2,1,0:T(8,128)(2,1)S(1)}, u32[]{:S(2)}, u32[]{:S(2)}) collective-permute-start(bf16[2,80,1152]{2,1,0:T(8,128)(2,1)S(1)} %constant_dynamic-update-slice_fusion.5), channel_id=1, source_target_pairs={{0,8},{4,20},{8,0},{12,28},{16,24},{20,4},{24,16},{28,12},{1,9},{5... | collective-permute-start | bytes 1105928 | tf_op jit(solution)/shard_map/ppermute | solution.py:108
  30.6 1.1 %collective-permute-start.3 = (bf16[1,80,1152]{2,1,0:T(8,128)(2,1)S(1)}, bf16[1,80,1152]{2,1,0:T(8,128)(2,1)S(1)}, u32[]{:S(2)}, u32[]{:S(2)}) collective-permute-start(bf16[1,80,1152]{2,1,0:T(8,128)(2,1)S(1)} %collective-permute-done), channel_id=1, source_target_pairs={{0,1},{1,2},{2,3},{3,0},{4,5},{5,6},{6,7},{7,4},{8,9},{9,10},{10,1... | collective-permute-start | bytes 552968 | tf_op jit(solution)/shard_map/ppermute | solution.py:104
  31.7 0.0 copy-done.5
  31.7 0.7 collective-permute-start.2
  32.5 7.5 %collective-permute-done.3 = bf16[1,80,1152]{2,1,0:T(8,128)(2,1)S(1)} collective-permute-done((bf16[1,80,1152]{2,1,0:T(8,128)(2,1)S(1)}, bf16[1,80,1152]{2,1,0:T(8,128)(2,1)S(1)}, u32[]{:S(2)}, u32[]{:S(2)}) %collective-permute-start.3) | collective-permute-done | bytes 184352 | tf_op jit(solution)/shard_map/ppermute | solution.py:104
  40.0 0.4 collective-permute-start.4
  40.4 0.0 collective-permute-done.10
  40.4 0.0 collective-permute-done.9.refs_1_
  40.5 1.7 %collective-permute-start.11 = (bf16[4,80,1152]{2,1,0:T(8,128)(2,1)S(1)}, bf16[4,80,1152]{2,1,0:T(8,128)(2,1)S(1)}, u32[]{:S(2)}, u32[]{:S(2)}) collective-permute-start(bf16[4,80,1152]{2,1,0:T(8,128)(2,1)S(1)} %constant_dynamic-update-slice_fusion.7.refs_3_), channel_id=1, source_target_pairs={{0,16},{4,12},{8,24},{12,4},{16,0},{20,28},{24,8},{28,20},{1,17},{... | collective-permute-start | bytes 2211848 | tf_op jit(solution)/shard_map/ppermute | solution.py:108
  42.2 5.4 %collective-permute-done.4 = bf16[1,80,1152]{2,1,0:T(8,128)(2,1)S(1)} collective-permute-done((bf16[1,80,1152]{2,1,0:T(8,128)(2,1)S(1)}, bf16[1,80,1152]{2,1,0:T(8,128)(2,1)S(1)}, u32[]{:S(2)}, u32[]{:S(2)}) %collective-permute-start.4) | collective-permute-done | bytes 184352 | tf_op jit(solution)/shard_map/ppermute | solution.py:108
  47.6 1.6 %collective-permute-start.12 = (bf16[2,80,1152]{2,1,0:T(8,128)(2,1)S(1)}, bf16[2,80,1152]{2,1,0:T(8,128)(2,1)S(1)}, u32[]{:S(2)}, u32[]{:S(2)}) collective-permute-start(bf16[2,80,1152]{2,1,0:T(8,128)(2,1)S(1)} %constant_dynamic-update-slice_fusion.refs_5_), channel_id=1, source_target_pairs={{0,16},{4,12},{8,24},{12,4},{16,0},{20,28},{24,8},{28,20},{1,17},{... | collective-permute-start | bytes 1105928 | tf_op jit(solution)/shard_map/ppermute | solution.py:108
  49.2 0.1 collective-permute-start.6
  49.3 0.0 collective-permute-done.2
  49.3 1.9 %collective-permute-start.5 = (bf16[2,64,1152]{2,1,0:T(8,128)(2,1)S(1)}, bf16[2,64,1152]{2,1,0:T(8,128)(2,1)S(1)}, u32[]{:S(2)}, u32[]{:S(2)}) collective-permute-start(bf16[2,64,1152]{2,1,0:T(8,128)(2,1)S(1)} %collective-permute-done.2), channel_id=1, source_target_pairs={{0,1},{1,2},{2,3},{3,0},{4,5},{5,6},{6,7},{7,4},{8,9},{9,10},{10,1... | collective-permute-start | bytes 884744 | tf_op jit(solution)/shard_map/ppermute | solution.py:104
  51.2 7.9 %collective-permute-done.6 = bf16[2,64,1152]{2,1,0:T(8,128)(2,1)S(1)} collective-permute-done((bf16[2,64,1152]{2,1,0:T(8,128)(2,1)S(1)}, bf16[2,64,1152]{2,1,0:T(8,128)(2,1)S(1)}, u32[]{:S(2)}, u32[]{:S(2)}) %collective-permute-start.6) | collective-permute-done | bytes 294944 | tf_op jit(solution)/shard_map/ppermute | solution.py:104
  59.0 0.0 collective-permute-done.12.refs_6_
  59.0 0.0 collective-permute-done.11.refs_4_
  59.1 0.0 copy-done
  59.1 2.1 %shard_map.57.mine_ref.refs_7_ = bf16[608,1152]{1,0:T(8,128)(2,1)S(1)} custom-call(bf16[256,1152]{1,0:T(8,128)(2,1)S(1)} %shard_map.56.refs_0_, bf16[256,1152]{1,0:T(8,128)(2,1)S(1)} %collective-permute-done.9.refs_1_, bf16[288,3456]{1,0:T(8,128)(2,1)S(1)} %copy-done, bf16[4,80,1152]{2,1,0:T(8,128)(2,1)S(1)} %constant_dynamic-update-slice_fusion.7.refs_3_, ...), custom_call_target="tpu_custom_call" | custom-call | flops 1358954496 | bytes 2654208 | tf_op jit(solution)/shard_map/pallas_call | solution.py:172
  61.2 0.0 collective-permute-done.5
  61.2 0.1 collective-permute-start.13
  61.4 0.6 collective-permute-start.7
  62.0 0.1 pad_maximum_fusion
  62.1 0.0 copy-start.2
  62.1 0.6 collective-permute-start.8
  62.7 1.7 %collective-permute-done.13.other_ref.refs_8_ = bf16[608,1152]{1,0:T(8,128)(2,1)S(1)} collective-permute-done((bf16[608,1152]{1,0:T(8,128)(2,1)S(1)}, bf16[608,1152]{1,0:T(8,128)(2,1)S(1)}, u32[]{:S(2)}, u32[]{:S(2)}) %collective-permute-start.13) | collective-permute-done | bytes 1400864 | tf_op jit(solution)/shard_map/ppermute | solution.py:108
  64.4 0.9 shard_map.58
  65.3 0.4 collective-permute-done.7.refs_4_
  65.7 2.4 %collective-permute-start.15 = (bf16[9,32,128]{2,1,0:T(8,128)(2,1)S(1)}, bf16[9,32,128]{2,1,0:T(8,128)(2,1)S(1)}, u32[]{:S(2)}, u32[]{:S(2)}) collective-permute-start(bf16[9,32,128]{2,1,0:T(8,128)(2,1)S(1)} %get-tuple-element.44), channel_id=1, source_target_pairs={{0,8},{4,12},{16,24},{20,28},{1,9},{5,13},{17,25},{21,29},{2,10},{... | collective-permute-start | bytes 221192 | tf_op jit(solution)/shard_map/ppermute | solution.py:555
  68.1 2.3 %collective-permute-start.16 = (bf16[9,32,128]{2,1,0:T(8,128)(2,1)S(1)}, bf16[9,32,128]{2,1,0:T(8,128)(2,1)S(1)}, u32[]{:S(2)}, u32[]{:S(2)}) collective-permute-start(bf16[9,32,128]{2,1,0:T(8,128)(2,1)S(1)} %get-tuple-element.44), channel_id=1, source_target_pairs={{0,16},{4,20},{8,24},{12,28},{1,17},{5,21},{9,25},{13,29},{2,18},{... | collective-permute-start | bytes 221192 | tf_op jit(solution)/shard_map/ppermute | solution.py:555
  70.5 1.3 %collective-permute-start.17 = (bf16[9,32,128]{2,1,0:T(8,128)(2,1)S(1)}, bf16[9,32,128]{2,1,0:T(8,128)(2,1)S(1)}, u32[]{:S(2)}, u32[]{:S(2)}) collective-permute-start(bf16[9,32,128]{2,1,0:T(8,128)(2,1)S(1)} %get-tuple-element.44), channel_id=1, source_target_pairs={{0,24},{4,28},{8,16},{12,20},{1,25},{5,29},{9,17},{13,21},{2,26},{... | collective-permute-start | bytes 221192 | tf_op jit(solution)/shard_map/ppermute | solution.py:555
  71.8 0.1 collective-permute-start.14
  71.8 0.0 collective-permute-done.15
  71.9 0.6 collective-permute-done.16
  72.4 1.8 %collective-permute-done.17 = bf16[9,32,128]{2,1,0:T(8,128)(2,1)S(1)} collective-permute-done((bf16[9,32,128]{2,1,0:T(8,128)(2,1)S(1)}, bf16[9,32,128]{2,1,0:T(8,128)(2,1)S(1)}, u32[]{:S(2)}, u32[]{:S(2)}) %collective-permute-start.17) | collective-permute-done | bytes 73760 | tf_op jit(solution)/shard_map/ppermute | solution.py:555
  74.3 0.0 collective-permute-done.8
  74.3 0.1 collective-permute-start.18
  74.4 0.0 copy-done.2
  74.4 0.0 copy-start.4
  74.5 0.0 copy-start.1
  74.5 0.9 shard_map.59
  75.3 3.4 %collective-permute-done.18 = bf16[9,32,128]{2,1,0:T(8,128)(2,1)S(1)} collective-permute-done((bf16[9,32,128]{2,1,0:T(8,128)(2,1)S(1)}, bf16[9,32,128]{2,1,0:T(8,128)(2,1)S(1)}, u32[]{:S(2)}, u32[]{:S(2)}) %collective-permute-start.18) | collective-permute-done | bytes 73760 | tf_op jit(solution)/shard_map/ppermute | solution.py:563
  78.8 1.4 %collective-permute-done.14 = bf16[3,64,1152]{2,1,0:T(8,128)(2,1)S(1)} collective-permute-done((bf16[3,64,1152]{2,1,0:T(8,128)(2,1)S(1)}, bf16[3,64,1152]{2,1,0:T(8,128)(2,1)S(1)}, u32[]{:S(2)}, u32[]{:S(2)}) %collective-permute-start.14) | collective-permute-done | bytes 442400 | tf_op jit(solution)/shard_map/ppermute | solution.py:108
  80.2 0.1 collective-permute-start.19
  80.3 0.1 collective-permute-start.20
  80.3 0.0 copy-done.4
  80.4 1.8 %collective-permute-start.21 = (bf16[1,64,1152]{2,1,0:T(8,128)(2,1)S(1)}, bf16[1,64,1152]{2,1,0:T(8,128)(2,1)S(1)}, u32[]{:S(2)}, u32[]{:S(2)}) collective-permute-start(bf16[1,64,1152]{2,1,0:T(8,128)(2,1)S(1)} %get-tuple-element.55), channel_id=1, source_target_pairs={{0,1},{1,2},{2,3},{4,5},{5,6},{6,7},{8,9},{9,10},{10,11},{12,13},{... | collective-permute-start | bytes 442376 | tf_op jit(solution)/shard_map/ppermute | solution.py:568
  82.2 1.3 %collective-permute-start.22 = (bf16[1,64,1152]{2,1,0:T(8,128)(2,1)S(1)}, bf16[1,64,1152]{2,1,0:T(8,128)(2,1)S(1)}, u32[]{:S(2)}, u32[]{:S(2)}) collective-permute-start(bf16[1,64,1152]{2,1,0:T(8,128)(2,1)S(1)} %get-tuple-element.56), channel_id=1, source_target_pairs={{1,0},{2,1},{3,2},{5,4},{6,5},{7,6},{9,8},{10,9},{11,10},{13,12},{... | collective-permute-start | bytes 442376 | tf_op jit(solution)/shard_map/ppermute | solution.py:569
  83.5 3.3 %collective-permute-done.20 = bf16[9,32,128]{2,1,0:T(8,128)(2,1)S(1)} collective-permute-done((bf16[9,32,128]{2,1,0:T(8,128)(2,1)S(1)}, bf16[9,32,128]{2,1,0:T(8,128)(2,1)S(1)}, u32[]{:S(2)}, u32[]{:S(2)}) %collective-permute-start.20) | collective-permute-done | bytes 73760 | tf_op jit(solution)/shard_map/ppermute | solution.py:566
  86.8 0.0 collective-permute-done.19.refs_6_
  86.8 0.0 copy-done.1
  86.8 1.5 %shard_map.60 = (bf16[256,1152]{1,0:T(8,128)(2,1)S(1)}, bf16[1152,1152]{1,0:T(8,128)(2,1)S(1)}) custom-call(bf16[256,1152]{1,0:T(8,128)(2,1)S(1)} %shard_map.56.refs_0_, bf16[288,3456]{1,0:T(8,128)(2,1)S(1)} %copy-done, bf16[288,1152]{1,0:T(8,128)(2,1)S(1)} %copy-done.1, bf16[6,64,1152]{2,1,0:T(8,128)(2,1)S(1)} %constant_dynamic-update-slice_fusion.2.refs_3_, ...), custom_call_target="tpu_custom_call" | custom-call | flops 679477248 | bytes 5308416 | tf_op jit(solution)/shard_map/pallas_call | solution.py:172
  88.4 0.0 collective-permute-done.21.refs_4_
  88.4 3.2 %collective-permute-done.22.refs_5_ = bf16[1,64,1152]{2,1,0:T(8,128)(2,1)S(1)} collective-permute-done((bf16[1,64,1152]{2,1,0:T(8,128)(2,1)S(1)}, bf16[1,64,1152]{2,1,0:T(8,128)(2,1)S(1)}, u32[]{:S(2)}, u32[]{:S(2)}) %collective-permute-start.22) | collective-permute-done | bytes 147488 | tf_op jit(solution)/shard_map/ppermute | solution.py:569
  91.5 2.5 %shard_map.61 = bf16[256,1152]{1,0:T(8,128)(2,1)} custom-call(bf16[256,1152]{1,0:T(8,128)(2,1)S(1)} %get-tuple-element.51.refs_0_, bf16[1152,1152]{1,0:T(8,128)(2,1)S(1)} %get-tuple-element.52.refs_1_, f32[9,32,128]{2,1,0:T(8,128)S(1)} %convert_add_fusion.refs_2_, f32[256,1152]{1,0:T(8,128)S(1)} %bitcast.5, ...), custom_call_target="tpu_custom_call" | custom-call | flops 679477248 | bytes 2654208 | tf_op jit(solution)/shard_map/pallas_call | solution.py:172
  (20 shorter events, 0.4 us)
Async XLA Ops:
  0.0 20.8 %copy-start.3 = (bf16[1,4,64,1152]{3,2,1,0:T(8,128)(2,1)S(1)}, bf16[1,4,64,1152]{3,2,1,0:T(8,128)(2,1)}, u32[]{:S(2)}) copy-start(bf16[1,4,64,1152]{3,2,1,0:T(8,128)(2,1)} %param.5) | copy-start | bytes 1769476
  15.7 10.8 %collective-permute-start = (bf16[1,80,1152]{2,1,0:T(8,128)(2,1)}, bf16[1,80,1152]{2,1,0:T(8,128)(2,1)S(1)}, u32[]{:S(2)}, u32[]{:S(2)}) collective-permute-start(bf16[1,80,1152]{2,1,0:T(8,128)(2,1)} %bitcast.8), channel_id=1, source_target_pairs={{0,1},{1,2},{2,3},{3,0},{4,5},{5,6},{6,7},{7,4},{8,9},{9,10},{10,1... | collective-permute-start | bytes 552968 | tf_op jit(solution)/shard_map/ppermute | solution.py:104
  18.7 10.3 %collective-permute-start.1 = (bf16[1,80,1152]{2,1,0:T(8,128)(2,1)}, bf16[1,80,1152]{2,1,0:T(8,128)(2,1)S(1)}, u32[]{:S(2)}, u32[]{:S(2)}) collective-permute-start(bf16[1,80,1152]{2,1,0:T(8,128)(2,1)} %bitcast.9), channel_id=1, source_target_pairs={{0,3},{1,0},{2,1},{3,2},{4,7},{5,4},{6,5},{7,6},{8,11},{9,8},{10,9... | collective-permute-start | bytes 552968 | tf_op jit(solution)/shard_map/ppermute | solution.py:104
  20.8 10.9 %copy-start.5 = (bf16[2,64,1152]{2,1,0:T(8,128)(2,1)S(1)}, bf16[2,64,1152]{2,1,0:T(8,128)(2,1)}, u32[]{:S(2)}) copy-start(bf16[2,64,1152]{2,1,0:T(8,128)(2,1)} %get-tuple-element.37) | copy-start | bytes 884740
  22.0 37.0 %copy-start = (bf16[288,3456]{1,0:T(8,128)(2,1)S(1)}, bf16[288,3456]{1,0:T(8,128)(2,1)}, u32[]{:S(2)}) copy-start(bf16[288,3456]{1,0:T(8,128)(2,1)} %refs_1_.1) | copy-start | bytes 5971972
  22.0 18.4 %collective-permute-start.9 = (bf16[256,1152]{1,0:T(8,128)(2,1)S(1)}, bf16[256,1152]{1,0:T(8,128)(2,1)S(1)}, u32[]{:S(2)}, u32[]{:S(2)}) collective-permute-start(bf16[256,1152]{1,0:T(8,128)(2,1)S(1)} %shard_map.56.refs_0_), channel_id=1, source_target_pairs={{0,4},{4,0},{8,12},{12,8},{16,20},{20,16},{24,28},{28,24},{1,5},{5... | collective-permute-start | bytes 1769480 | tf_op jit(solution)/shard_map/ppermute | solution.py:108
  29.0 11.4 %collective-permute-start.10 = (bf16[2,80,1152]{2,1,0:T(8,128)(2,1)S(1)}, bf16[2,80,1152]{2,1,0:T(8,128)(2,1)S(1)}, u32[]{:S(2)}, u32[]{:S(2)}) collective-permute-start(bf16[2,80,1152]{2,1,0:T(8,128)(2,1)S(1)} %constant_dynamic-update-slice_fusion.5), channel_id=1, source_target_pairs={{0,8},{4,20},{8,0},{12,28},{16,24},{20,4},{24,16},{28,12},{1,9},{5... | collective-permute-start | bytes 1105928 | tf_op jit(solution)/shard_map/ppermute | solution.py:108
  30.6 9.4 %collective-permute-start.3 = (bf16[1,80,1152]{2,1,0:T(8,128)(2,1)S(1)}, bf16[1,80,1152]{2,1,0:T(8,128)(2,1)S(1)}, u32[]{:S(2)}, u32[]{:S(2)}) collective-permute-start(bf16[1,80,1152]{2,1,0:T(8,128)(2,1)S(1)} %collective-permute-done), channel_id=1, source_target_pairs={{0,1},{1,2},{2,3},{3,0},{4,5},{5,6},{6,7},{7,4},{8,9},{9,10},{10,1... | collective-permute-start | bytes 552968 | tf_op jit(solution)/shard_map/ppermute | solution.py:104
  31.7 17.6 %collective-permute-start.2 = (bf16[2,64,1152]{2,1,0:T(8,128)(2,1)S(1)}, bf16[2,64,1152]{2,1,0:T(8,128)(2,1)S(1)}, u32[]{:S(2)}, u32[]{:S(2)}) collective-permute-start(bf16[2,64,1152]{2,1,0:T(8,128)(2,1)S(1)} %copy-done.5), channel_id=1, source_target_pairs={{0,1},{1,2},{2,3},{3,0},{4,5},{5,6},{6,7},{7,4},{8,9},{9,10},{10,1... | collective-permute-start | bytes 884744 | tf_op jit(solution)/shard_map/ppermute | solution.py:104
  40.0 7.6 %collective-permute-start.4 = (bf16[1,80,1152]{2,1,0:T(8,128)(2,1)S(1)}, bf16[1,80,1152]{2,1,0:T(8,128)(2,1)S(1)}, u32[]{:S(2)}, u32[]{:S(2)}) collective-permute-start(bf16[1,80,1152]{2,1,0:T(8,128)(2,1)S(1)} %collective-permute-done.3), channel_id=1, source_target_pairs={{0,8},{4,20},{8,0},{12,28},{16,24},{20,4},{24,16},{28,12},{1,9},{5... | collective-permute-start | bytes 552968 | tf_op jit(solution)/shard_map/ppermute | solution.py:108
  40.5 18.5 %collective-permute-start.11 = (bf16[4,80,1152]{2,1,0:T(8,128)(2,1)S(1)}, bf16[4,80,1152]{2,1,0:T(8,128)(2,1)S(1)}, u32[]{:S(2)}, u32[]{:S(2)}) collective-permute-start(bf16[4,80,1152]{2,1,0:T(8,128)(2,1)S(1)} %constant_dynamic-update-slice_fusion.7.refs_3_), channel_id=1, source_target_pairs={{0,16},{4,12},{8,24},{12,4},{16,0},{20,28},{24,8},{28,20},{1,17},{... | collective-permute-start | bytes 2211848 | tf_op jit(solution)/shard_map/ppermute | solution.py:108
  47.6 11.5 %collective-permute-start.12 = (bf16[2,80,1152]{2,1,0:T(8,128)(2,1)S(1)}, bf16[2,80,1152]{2,1,0:T(8,128)(2,1)S(1)}, u32[]{:S(2)}, u32[]{:S(2)}) collective-permute-start(bf16[2,80,1152]{2,1,0:T(8,128)(2,1)S(1)} %constant_dynamic-update-slice_fusion.refs_5_), channel_id=1, source_target_pairs={{0,16},{4,12},{8,24},{12,4},{16,0},{20,28},{24,8},{28,20},{1,17},{... | collective-permute-start | bytes 1105928 | tf_op jit(solution)/shard_map/ppermute | solution.py:108
  49.2 9.9 %collective-permute-start.6 = (bf16[2,64,1152]{2,1,0:T(8,128)(2,1)S(1)}, bf16[2,64,1152]{2,1,0:T(8,128)(2,1)S(1)}, u32[]{:S(2)}, u32[]{:S(2)}) collective-permute-start(bf16[2,64,1152]{2,1,0:T(8,128)(2,1)S(1)} %copy-done.5), channel_id=1, source_target_pairs={{0,3},{1,0},{2,1},{3,2},{4,7},{5,4},{6,5},{7,6},{8,11},{9,8},{10,9... | collective-permute-start | bytes 884744 | tf_op jit(solution)/shard_map/ppermute | solution.py:104
  49.3 11.9 %collective-permute-start.5 = (bf16[2,64,1152]{2,1,0:T(8,128)(2,1)S(1)}, bf16[2,64,1152]{2,1,0:T(8,128)(2,1)S(1)}, u32[]{:S(2)}, u32[]{:S(2)}) collective-permute-start(bf16[2,64,1152]{2,1,0:T(8,128)(2,1)S(1)} %collective-permute-done.2), channel_id=1, source_target_pairs={{0,1},{1,2},{2,3},{3,0},{4,5},{5,6},{6,7},{7,4},{8,9},{9,10},{10,1... | collective-permute-start | bytes 884744 | tf_op jit(solution)/shard_map/ppermute | solution.py:104
  61.2 3.2 %collective-permute-start.13 = (bf16[608,1152]{1,0:T(8,128)(2,1)S(1)}, bf16[608,1152]{1,0:T(8,128)(2,1)S(1)}, u32[]{:S(2)}, u32[]{:S(2)}) collective-permute-start(bf16[608,1152]{1,0:T(8,128)(2,1)S(1)} %shard_map.57.mine_ref.refs_7_), channel_id=1, source_target_pairs={{0,4},{4,0},{8,12},{12,8},{16,20},{20,16},{24,28},{28,24},{1,5},{5... | collective-permute-start | bytes 4202504 | tf_op jit(solution)/shard_map/ppermute | solution.py:108
  61.4 4.3 %collective-permute-start.7 = (bf16[6,64,1152]{2,1,0:T(8,128)(2,1)S(1)}, bf16[6,64,1152]{2,1,0:T(8,128)(2,1)S(1)}, u32[]{:S(2)}, u32[]{:S(2)}) collective-permute-start(bf16[6,64,1152]{2,1,0:T(8,128)(2,1)S(1)} %constant_dynamic-update-slice_fusion.2.refs_3_), channel_id=1, source_target_pairs={{0,4},{4,0},{8,12},{12,8},{16,20},{20,16},{24,28},{28,24},{1,5},{5... | collective-permute-start | bytes 2654216 | tf_op jit(solution)/shard_map/ppermute | solution.py:108
  62.1 12.4 %copy-start.2 = (f32[3,3,1152]{2,1,0:T(4,128)S(1)}, f32[3,3,1152]{2,1,0:T(4,128)}, u32[]{:S(2)}) copy-start(f32[3,3,1152]{2,1,0:T(4,128)} %refs_6_.1) | copy-start | bytes 124420
  62.1 12.2 %collective-permute-start.8 = (bf16[3,64,1152]{2,1,0:T(8,128)(2,1)S(1)}, bf16[3,64,1152]{2,1,0:T(8,128)(2,1)S(1)}, u32[]{:S(2)}, u32[]{:S(2)}) collective-permute-start(bf16[3,64,1152]{2,1,0:T(8,128)(2,1)S(1)} %pad_maximum_fusion), channel_id=1, source_target_pairs={{0,8},{4,20},{8,0},{12,28},{16,24},{20,4},{24,16},{28,12},{1,9},{5... | collective-permute-start | bytes 1327112 | tf_op jit(solution)/shard_map/ppermute | solution.py:108
  65.7 6.2 %collective-permute-start.15 = (bf16[9,32,128]{2,1,0:T(8,128)(2,1)S(1)}, bf16[9,32,128]{2,1,0:T(8,128)(2,1)S(1)}, u32[]{:S(2)}, u32[]{:S(2)}) collective-permute-start(bf16[9,32,128]{2,1,0:T(8,128)(2,1)S(1)} %get-tuple-element.44), channel_id=1, source_target_pairs={{0,8},{4,12},{16,24},{20,28},{1,9},{5,13},{17,25},{21,29},{2,10},{... | collective-permute-start | bytes 221192 | tf_op jit(solution)/shard_map/ppermute | solution.py:555
  68.1 4.3 %collective-permute-start.16 = (bf16[9,32,128]{2,1,0:T(8,128)(2,1)S(1)}, bf16[9,32,128]{2,1,0:T(8,128)(2,1)S(1)}, u32[]{:S(2)}, u32[]{:S(2)}) collective-permute-start(bf16[9,32,128]{2,1,0:T(8,128)(2,1)S(1)} %get-tuple-element.44), channel_id=1, source_target_pairs={{0,16},{4,20},{8,24},{12,28},{1,17},{5,21},{9,25},{13,29},{2,18},{... | collective-permute-start | bytes 221192 | tf_op jit(solution)/shard_map/ppermute | solution.py:555
  70.5 3.8 %collective-permute-start.17 = (bf16[9,32,128]{2,1,0:T(8,128)(2,1)S(1)}, bf16[9,32,128]{2,1,0:T(8,128)(2,1)S(1)}, u32[]{:S(2)}, u32[]{:S(2)}) collective-permute-start(bf16[9,32,128]{2,1,0:T(8,128)(2,1)S(1)} %get-tuple-element.44), channel_id=1, source_target_pairs={{0,24},{4,28},{8,16},{12,20},{1,25},{5,29},{9,17},{13,21},{2,26},{... | collective-permute-start | bytes 221192 | tf_op jit(solution)/shard_map/ppermute | solution.py:555
  71.8 8.4 %collective-permute-start.14 = (bf16[3,64,1152]{2,1,0:T(8,128)(2,1)S(1)}, bf16[3,64,1152]{2,1,0:T(8,128)(2,1)S(1)}, u32[]{:S(2)}, u32[]{:S(2)}) collective-permute-start(bf16[3,64,1152]{2,1,0:T(8,128)(2,1)S(1)} %pad_maximum_fusion), channel_id=1, source_target_pairs={{0,16},{4,12},{8,24},{12,4},{16,0},{20,28},{24,8},{28,20},{1,17},{... | collective-permute-start | bytes 1327112 | tf_op jit(solution)/shard_map/ppermute | solution.py:108
  74.3 4.4 %collective-permute-start.18 = (bf16[9,32,128]{2,1,0:T(8,128)(2,1)S(1)}, bf16[9,32,128]{2,1,0:T(8,128)(2,1)S(1)}, u32[]{:S(2)}, u32[]{:S(2)}) collective-permute-start(bf16[9,32,128]{2,1,0:T(8,128)(2,1)S(1)} %convert_add_fusion.1), channel_id=1, source_target_pairs={{0,1},{1,0},{2,3},{3,2},{4,5},{5,4},{6,7},{7,6},{8,9},{9,8},{10,11... | collective-permute-start | bytes 221192 | tf_op jit(solution)/shard_map/ppermute | solution.py:563
  74.4 5.9 %copy-start.4 = (f32[1152]{0:T(1024)S(1)}, f32[1152]{0:T(1024)}, u32[]{:S(2)}) copy-start(f32[1152]{0:T(1024)} %param.9) | copy-start | bytes 13828
  74.5 12.4 %copy-start.1 = (bf16[288,1152]{1,0:T(8,128)(2,1)S(1)}, bf16[288,1152]{1,0:T(8,128)(2,1)}, u32[]{:S(2)}) copy-start(bf16[288,1152]{1,0:T(8,128)(2,1)} %refs_2_.3) | copy-start | bytes 1990660
  80.2 6.6 %collective-permute-start.19 = (bf16[6,64,1152]{2,1,0:T(8,128)(2,1)S(1)}, bf16[6,64,1152]{2,1,0:T(8,128)(2,1)S(1)}, u32[]{:S(2)}, u32[]{:S(2)}) collective-permute-start(bf16[6,64,1152]{2,1,0:T(8,128)(2,1)S(1)} %constant_dynamic-update-slice_fusion.9.refs_5_), channel_id=1, source_target_pairs={{0,4},{4,0},{8,12},{12,8},{16,20},{20,16},{24,28},{28,24},{1,5},{5... | collective-permute-start | bytes 2654216 | tf_op jit(solution)/shard_map/ppermute | solution.py:108
  80.3 6.5 %collective-permute-start.20 = (bf16[9,32,128]{2,1,0:T(8,128)(2,1)S(1)}, bf16[9,32,128]{2,1,0:T(8,128)(2,1)S(1)}, u32[]{:S(2)}, u32[]{:S(2)}) collective-permute-start(bf16[9,32,128]{2,1,0:T(8,128)(2,1)S(1)} %add_convert_fusion), channel_id=1, source_target_pairs={{0,2},{1,3},{2,0},{3,1},{4,6},{5,7},{6,4},{7,5},{8,10},{9,11},{10,... | collective-permute-start | bytes 221192 | tf_op jit(solution)/shard_map/ppermute | solution.py:566
  80.4 8.0 %collective-permute-start.21 = (bf16[1,64,1152]{2,1,0:T(8,128)(2,1)S(1)}, bf16[1,64,1152]{2,1,0:T(8,128)(2,1)S(1)}, u32[]{:S(2)}, u32[]{:S(2)}) collective-permute-start(bf16[1,64,1152]{2,1,0:T(8,128)(2,1)S(1)} %get-tuple-element.55), channel_id=1, source_target_pairs={{0,1},{1,2},{2,3},{4,5},{5,6},{6,7},{8,9},{9,10},{10,11},{12,13},{... | collective-permute-start | bytes 442376 | tf_op jit(solution)/shard_map/ppermute | solution.py:568
  82.2 9.3 %collective-permute-start.22 = (bf16[1,64,1152]{2,1,0:T(8,128)(2,1)S(1)}, bf16[1,64,1152]{2,1,0:T(8,128)(2,1)S(1)}, u32[]{:S(2)}, u32[]{:S(2)}) collective-permute-start(bf16[1,64,1152]{2,1,0:T(8,128)(2,1)S(1)} %get-tuple-element.56), channel_id=1, source_target_pairs={{1,0},{2,1},{3,2},{5,4},{6,5},{7,6},{9,8},{10,9},{11,10},{13,12},{... | collective-permute-start | bytes 442376 | tf_op jit(solution)/shard_map/ppermute | solution.py:569

commit v9 on v6

--- a/solution.py
+++ b/solution.py
@@ -559,8 +559,8 @@
     above = lax.ppermute(bottom, "space", forward)
     below = lax.ppermute(top, "space", backward)
 
-    turned = jnp.concatenate([second_first, second_second])
-    swapped_turned = flipped(after(turned, share), (1, 1))
+    turned = jnp.concatenate(after((second_first, second_second), total))
+    swapped_turned = flipped(after(turned, upto), (1, 1))
     queries, weight = query_call(
         tokens,
         qkv_weight,

time: 80.5 us -> 80.7 us (level)
    ppermute x6, waiting for transfers between devices: 22.3 us -> 23.3 us  [shifted(): lax.ppermute(value, 'space', [(i, (i + step) % count) for i in range(coun...]
where the time goes in v9:
time: 80.7 us; the launch traced here: 80.4 us
  waiting for transfers between devices  42.1 us (52%)
  starting transfers between devices  26.5 us (33%)
  Pallas kernels  11 us (14%)
    ppermute x6, waiting for transfers between devices, shifted(): lax.ppermute(value, 'space', [(i, (i + step) % count) for i in range(coun...  23.3 us
    pallas_call x7, Pallas kernels, kernel_call(): pl.pallas_call(body, out_shape=outputs, in_specs=in_specs, out_specs=jax....  11 us
    ppermute x10, waiting for transfers between devices, flipped(): lax.ppermute(value, 'tm', [(t, t ^ bit_on_core[t % 2]) for t in range(8)])  9.29 us
    ppermute x6, starting transfers between devices, shifted(): lax.ppermute(value, 'space', [(i, (i + step) % count) for i in range(coun...  8.78 us
    ppermute x3, starting transfers between devices, plane_form(): upto = upto + lax.ppermute(total, 'tm', pairs).astype(jnp.float32)  7.07 us
    ppermute x10, starting transfers between devices, flipped(): lax.ppermute(value, 'tm', [(t, t ^ bit_on_core[t % 2]) for t in range(8)])  7.06 us
    ppermute x1, waiting for transfers between devices, plane_form(): arrived = lax.ppermute(share, 'space', [(i, i ^ 1) for i in range(count)])  3.73 us
    ppermute x1, waiting for transfers between devices, plane_form(): arrived = lax.ppermute(share, 'space', [(i, i ^ 2) for i in range(count)])  2.68 us
  transfers between devices with their start and end apart: 23, of which 13 were waited for; matrix products, arithmetic and copies ran while one was open for 1% of the time, Pallas kernels for 8%

profile of v9, /device:TPU:0, one launch (start us, length us, event | category | flops | bytes accessed | tf_op | source)
XLA Modules:
  0.0 80.4 jit_solution(14997809767545546621)
XLA Ops:
  0.0 1.9 %shard_map.55 = (bf16[80,1152]{1,0:T(8,128)(2,1)}, bf16[2,64,1152]{2,1,0:T(8,128)(2,1)}) custom-call(bf16[288,3456]{1,0:T(8,128)(2,1)} %refs_1_.1, bf16[288,1152]{1,0:T(8,128)(2,1)} %refs_2_.3), custom_call_target="tpu_custom_call" | custom-call | bytes 958464 | tf_op jit(solution)/shard_map/pallas_call | solution.py:164
  2.0 5.1 %collective-permute-start.1 = (bf16[1,80,1152]{2,1,0:T(8,128)(2,1)}, bf16[1,80,1152]{2,1,0:T(8,128)(2,1)S(1)}, u32[]{:S(2)}, u32[]{:S(2)}) collective-permute-start(bf16[1,80,1152]{2,1,0:T(8,128)(2,1)} %bitcast.8), channel_id=1, source_target_pairs={{0,3},{1,0},{2,1},{3,2},{4,7},{5,4},{6,5},{7,6},{8,11},{9,8},{10,9... | collective-permute-start | bytes 552968 | tf_op jit(solution)/shard_map/ppermute | solution.py:104
  7.1 0.0 collective-permute-start
  7.1 0.0 copy-done.3
  7.1 0.0 copy-start.5
  7.1 1.2 %shard_map.56.refs_0_ = bf16[256,1152]{1,0:T(8,128)(2,1)S(1)} custom-call(bf16[256,1152]{1,0:T(8,128)(2,1)S(1)} %bitcast.7), custom_call_target="tpu_custom_call" | custom-call | flops 679477248 | bytes 589824 | tf_op jit(solution)/shard_map/pallas_call | solution.py:164
  8.2 0.0 copy-start
  8.3 0.1 collective-permute-start.10
  8.3 4.1 %collective-permute-done.1 = bf16[1,80,1152]{2,1,0:T(8,128)(2,1)S(1)} collective-permute-done((bf16[1,80,1152]{2,1,0:T(8,128)(2,1)}, bf16[1,80,1152]{2,1,0:T(8,128)(2,1)S(1)}, u32[]{:S(2)}, u32[]{:S(2)}) %collective-permute-start.1) | collective-permute-done | bytes 184352 | tf_op jit(solution)/shard_map/ppermute | solution.py:104
  12.4 3.6 %collective-permute-done = bf16[1,80,1152]{2,1,0:T(8,128)(2,1)S(1)} collective-permute-done((bf16[1,80,1152]{2,1,0:T(8,128)(2,1)}, bf16[1,80,1152]{2,1,0:T(8,128)(2,1)S(1)}, u32[]{:S(2)}, u32[]{:S(2)}) %collective-permute-start) | collective-permute-done | bytes 184352 | tf_op jit(solution)/shard_map/ppermute | solution.py:104
  16.1 1.6 %collective-permute-start.11 = (bf16[2,80,1152]{2,1,0:T(8,128)(2,1)S(1)}, bf16[2,80,1152]{2,1,0:T(8,128)(2,1)S(1)}, u32[]{:S(2)}, u32[]{:S(2)}) collective-permute-start(bf16[2,80,1152]{2,1,0:T(8,128)(2,1)S(1)} %constant_dynamic-update-slice_fusion.5), channel_id=1, source_target_pairs={{0,8},{4,20},{8,0},{12,28},{16,24},{20,4},{24,16},{28,12},{1,9},{5... | collective-permute-start | bytes 1105928 | tf_op jit(solution)/shard_map/ppermute | solution.py:108
  17.6 1.6 %collective-permute-start.3 = (bf16[1,80,1152]{2,1,0:T(8,128)(2,1)S(1)}, bf16[1,80,1152]{2,1,0:T(8,128)(2,1)S(1)}, u32[]{:S(2)}, u32[]{:S(2)}) collective-permute-start(bf16[1,80,1152]{2,1,0:T(8,128)(2,1)S(1)} %collective-permute-done), channel_id=1, source_target_pairs={{0,1},{1,2},{2,3},{3,0},{4,5},{5,6},{6,7},{7,4},{8,9},{9,10},{10,1... | collective-permute-start | bytes 552968 | tf_op jit(solution)/shard_map/ppermute | solution.py:104
  19.2 0.0 copy-done.5
  19.2 0.0 collective-permute-start.2
  19.3 7.7 %collective-permute-done.3 = bf16[1,80,1152]{2,1,0:T(8,128)(2,1)S(1)} collective-permute-done((bf16[1,80,1152]{2,1,0:T(8,128)(2,1)S(1)}, bf16[1,80,1152]{2,1,0:T(8,128)(2,1)S(1)}, u32[]{:S(2)}, u32[]{:S(2)}) %collective-permute-start.3) | collective-permute-done | bytes 184352 | tf_op jit(solution)/shard_map/ppermute | solution.py:104
  27.0 0.5 collective-permute-start.4
  27.5 0.0 collective-permute-done.11
  27.5 0.0 collective-permute-done.10.refs_1_
  27.5 1.7 %collective-permute-start.12 = (bf16[4,80,1152]{2,1,0:T(8,128)(2,1)S(1)}, bf16[4,80,1152]{2,1,0:T(8,128)(2,1)S(1)}, u32[]{:S(2)}, u32[]{:S(2)}) collective-permute-start(bf16[4,80,1152]{2,1,0:T(8,128)(2,1)S(1)} %constant_dynamic-update-slice_fusion.7.refs_3_), channel_id=1, source_target_pairs={{0,16},{4,12},{8,24},{12,4},{16,0},{20,28},{24,8},{28,20},{1,17},{... | collective-permute-start | bytes 2211848 | tf_op jit(solution)/shard_map/ppermute | solution.py:108
  29.2 5.4 %collective-permute-done.4 = bf16[1,80,1152]{2,1,0:T(8,128)(2,1)S(1)} collective-permute-done((bf16[1,80,1152]{2,1,0:T(8,128)(2,1)S(1)}, bf16[1,80,1152]{2,1,0:T(8,128)(2,1)S(1)}, u32[]{:S(2)}, u32[]{:S(2)}) %collective-permute-start.4) | collective-permute-done | bytes 184352 | tf_op jit(solution)/shard_map/ppermute | solution.py:108
  34.6 1.6 %collective-permute-start.13 = (bf16[2,80,1152]{2,1,0:T(8,128)(2,1)S(1)}, bf16[2,80,1152]{2,1,0:T(8,128)(2,1)S(1)}, u32[]{:S(2)}, u32[]{:S(2)}) collective-permute-start(bf16[2,80,1152]{2,1,0:T(8,128)(2,1)S(1)} %constant_dynamic-update-slice_fusion.refs_5_), channel_id=1, source_target_pairs={{0,16},{4,12},{8,24},{12,4},{16,0},{20,28},{24,8},{28,20},{1,17},{... | collective-permute-start | bytes 1105928 | tf_op jit(solution)/shard_map/ppermute | solution.py:108
  36.2 0.0 collective-permute-start.6
  36.2 0.0 collective-permute-done.2
  36.2 2.0 %collective-permute-start.5 = (bf16[2,64,1152]{2,1,0:T(8,128)(2,1)S(1)}, bf16[2,64,1152]{2,1,0:T(8,128)(2,1)S(1)}, u32[]{:S(2)}, u32[]{:S(2)}) collective-permute-start(bf16[2,64,1152]{2,1,0:T(8,128)(2,1)S(1)} %collective-permute-done.2), channel_id=1, source_target_pairs={{0,1},{1,2},{2,3},{3,0},{4,5},{5,6},{6,7},{7,4},{8,9},{9,10},{10,1... | collective-permute-start | bytes 884744 | tf_op jit(solution)/shard_map/ppermute | solution.py:104
  38.2 7.9 %collective-permute-done.6 = bf16[2,64,1152]{2,1,0:T(8,128)(2,1)S(1)} collective-permute-done((bf16[2,64,1152]{2,1,0:T(8,128)(2,1)S(1)}, bf16[2,64,1152]{2,1,0:T(8,128)(2,1)S(1)}, u32[]{:S(2)}, u32[]{:S(2)}) %collective-permute-start.6) | collective-permute-done | bytes 294944 | tf_op jit(solution)/shard_map/ppermute | solution.py:104
  46.1 0.0 collective-permute-done.13.refs_6_
  46.1 0.0 collective-permute-done.12.refs_4_
  46.1 0.0 copy-done
  46.1 2.1 %shard_map.57.mine_ref.refs_7_ = bf16[608,1152]{1,0:T(8,128)(2,1)S(1)} custom-call(bf16[256,1152]{1,0:T(8,128)(2,1)S(1)} %shard_map.56.refs_0_, bf16[256,1152]{1,0:T(8,128)(2,1)S(1)} %collective-permute-done.10.refs_1_, bf16[288,3456]{1,0:T(8,128)(2,1)S(1)} %copy-done, bf16[4,80,1152]{2,1,0:T(8,128)(2,1)S(1)} %constant_dynamic-update-slice_fusion.7.refs_3_, ...), custom_call_target="tpu_custom_call" | custom-call | flops 1358954496 | bytes 2654208 | tf_op jit(solution)/shard_map/pallas_call | solution.py:164
  48.2 0.0 collective-permute-done.5
  48.2 0.1 collective-permute-start.14
  48.4 0.6 collective-permute-start.7
  49.0 0.1 pad_maximum_fusion
  49.1 0.6 collective-permute-start.9
  49.7 0.5 collective-permute-start.8
  50.1 1.3 %collective-permute-done.14.other_ref.refs_8_ = bf16[608,1152]{1,0:T(8,128)(2,1)S(1)} collective-permute-done((bf16[608,1152]{1,0:T(8,128)(2,1)S(1)}, bf16[608,1152]{1,0:T(8,128)(2,1)S(1)}, u32[]{:S(2)}, u32[]{:S(2)}) %collective-permute-start.14) | collective-permute-done | bytes 1400864 | tf_op jit(solution)/shard_map/ppermute | solution.py:108
  51.4 0.9 %shard_map.58 = (bf16[256,1152]{1,0:T(8,128)(2,1)S(1)}, bf16[1,64,1152]{2,1,0:T(8,128)(2,1)S(1)}, bf16[1,64,1152]{2,1,0:T(8,128)(2,1)S(1)}, f32[9,32,128]{2,1,0:T(8,128)S(1)}, bf16[9,32,128]{2,1,0:T(8,128)(2,1)S(1)}) custom-call(bf16[608,1152]{1,0:T(8,128)(2,1)S(1)} %shard_map.57.mine_ref.refs_7_, bf16[608,1152]{1,0:T(8,128)(2,1)S(1)} %collective-permute-done.14.other_ref.refs_8_), custom_call_target="tpu_custom_call" | custom-call | flops 150994944 | bytes 2359296 | tf_op jit(solution)/shard_map/pallas_call | solution.py:164
  52.3 0.0 copy-start.2
  52.3 0.4 collective-permute-done.7.refs_4_
  52.7 2.8 %collective-permute-start.17 = (bf16[9,32,128]{2,1,0:T(8,128)(2,1)S(1)}, bf16[9,32,128]{2,1,0:T(8,128)(2,1)S(1)}, u32[]{:S(2)}, u32[]{:S(2)}) collective-permute-start(bf16[9,32,128]{2,1,0:T(8,128)(2,1)S(1)} %get-tuple-element.45), channel_id=1, source_target_pairs={{0,24},{4,28},{8,16},{12,20},{1,25},{5,29},{9,17},{13,21},{2,26},{... | collective-permute-start | bytes 221192 | tf_op jit(solution)/shard_map/ppermute | solution.py:546
  55.5 1.3 %collective-permute-start.16 = (bf16[9,32,128]{2,1,0:T(8,128)(2,1)S(1)}, bf16[9,32,128]{2,1,0:T(8,128)(2,1)S(1)}, u32[]{:S(2)}, u32[]{:S(2)}) collective-permute-start(bf16[9,32,128]{2,1,0:T(8,128)(2,1)S(1)} %get-tuple-element.45), channel_id=1, source_target_pairs={{0,16},{4,20},{8,24},{12,28},{1,17},{5,21},{9,25},{13,29},{2,18},{... | collective-permute-start | bytes 221192 | tf_op jit(solution)/shard_map/ppermute | solution.py:546
  56.8 3.0 %collective-permute-start.15 = (bf16[9,32,128]{2,1,0:T(8,128)(2,1)S(1)}, bf16[9,32,128]{2,1,0:T(8,128)(2,1)S(1)}, u32[]{:S(2)}, u32[]{:S(2)}) collective-permute-start(bf16[9,32,128]{2,1,0:T(8,128)(2,1)S(1)} %get-tuple-element.45), channel_id=1, source_target_pairs={{0,8},{4,12},{16,24},{20,28},{1,9},{5,13},{17,25},{21,29},{2,10},{... | collective-permute-start | bytes 221192 | tf_op jit(solution)/shard_map/ppermute | solution.py:546
  59.8 1.7 %collective-permute-done.9 = bf16[3,64,1152]{2,1,0:T(8,128)(2,1)S(1)} collective-permute-done((bf16[3,64,1152]{2,1,0:T(8,128)(2,1)S(1)}, bf16[3,64,1152]{2,1,0:T(8,128)(2,1)S(1)}, u32[]{:S(2)}, u32[]{:S(2)}) %collective-permute-start.9) | collective-permute-done | bytes 442400 | tf_op jit(solution)/shard_map/ppermute | solution.py:108
  61.5 0.5 collective-permute-done.8
  62.1 0.0 copy-start.4
  62.1 0.0 collective-permute-done.17
  62.2 0.5 collective-permute-done.16
  62.6 0.0 collective-permute-done.15
  62.7 0.1 collective-permute-start.18
  62.7 0.1 collective-permute-start.19
  62.8 0.0 copy-done.2
  62.8 0.9 %shard_map.60 = f32[4,64,1152]{2,1,0:T(8,128)S(1)} custom-call(bf16[4,64,1152]{2,1,0:T(8,128)(2,1)S(1)} %bitcast.6, f32[3,3,1152]{2,1,0:T(4,128)S(1)} %copy-done.2), custom_call_target="tpu_custom_call" | custom-call | flops 5308416 | bytes 1769472 | tf_op jit(solution)/shard_map/pallas_call | solution.py:164
  63.7 3.7 %collective-permute-done.19 = bf16[9,32,128]{2,1,0:T(8,128)(2,1)S(1)} collective-permute-done((bf16[9,32,128]{2,1,0:T(8,128)(2,1)S(1)}, bf16[9,32,128]{2,1,0:T(8,128)(2,1)S(1)}, u32[]{:S(2)}, u32[]{:S(2)}) %collective-permute-start.19) | collective-permute-done | bytes 73760 | tf_op jit(solution)/shard_map/ppermute | solution.py:554
  67.5 0.1 collective-permute-start.20
  67.5 0.0 copy-done.4
  67.6 2.2 %collective-permute-start.21 = (bf16[1,64,1152]{2,1,0:T(8,128)(2,1)S(1)}, bf16[1,64,1152]{2,1,0:T(8,128)(2,1)S(1)}, u32[]{:S(2)}, u32[]{:S(2)}) collective-permute-start(bf16[1,64,1152]{2,1,0:T(8,128)(2,1)S(1)} %get-tuple-element.57), channel_id=1, source_target_pairs={{0,1},{1,2},{2,3},{4,5},{5,6},{6,7},{8,9},{9,10},{10,11},{12,13},{... | collective-permute-start | bytes 442376 | tf_op jit(solution)/shard_map/ppermute | solution.py:559
  69.7 1.3 %collective-permute-start.22 = (bf16[1,64,1152]{2,1,0:T(8,128)(2,1)S(1)}, bf16[1,64,1152]{2,1,0:T(8,128)(2,1)S(1)}, u32[]{:S(2)}, u32[]{:S(2)}) collective-permute-start(bf16[1,64,1152]{2,1,0:T(8,128)(2,1)S(1)} %get-tuple-element.58), channel_id=1, source_target_pairs={{1,0},{2,1},{3,2},{5,4},{6,5},{7,6},{9,8},{10,9},{11,10},{13,12},{... | collective-permute-start | bytes 442376 | tf_op jit(solution)/shard_map/ppermute | solution.py:560
  71.0 2.7 %collective-permute-done.20 = bf16[9,32,128]{2,1,0:T(8,128)(2,1)S(1)} collective-permute-done((bf16[9,32,128]{2,1,0:T(8,128)(2,1)S(1)}, bf16[9,32,128]{2,1,0:T(8,128)(2,1)S(1)}, u32[]{:S(2)}, u32[]{:S(2)}) %collective-permute-start.20) | collective-permute-done | bytes 73760 | tf_op jit(solution)/shard_map/ppermute | solution.py:557
  73.7 0.0 collective-permute-done.18.refs_6_
  73.8 0.0 copy-done.1
  73.8 1.5 %shard_map.59 = (bf16[256,1152]{1,0:T(8,128)(2,1)S(1)}, bf16[1152,1152]{1,0:T(8,128)(2,1)S(1)}) custom-call(bf16[256,1152]{1,0:T(8,128)(2,1)S(1)} %shard_map.56.refs_0_, bf16[288,3456]{1,0:T(8,128)(2,1)S(1)} %copy-done, bf16[288,1152]{1,0:T(8,128)(2,1)S(1)} %copy-done.1, bf16[6,64,1152]{2,1,0:T(8,128)(2,1)S(1)} %constant_dynamic-update-slice_fusion.2.refs_3_, ...), custom_call_target="tpu_custom_call" | custom-call | flops 679477248 | bytes 5308416 | tf_op jit(solution)/shard_map/pallas_call | solution.py:164
  75.3 0.0 collective-permute-done.21.refs_4_
  75.3 2.6 %collective-permute-done.22.refs_5_ = bf16[1,64,1152]{2,1,0:T(8,128)(2,1)S(1)} collective-permute-done((bf16[1,64,1152]{2,1,0:T(8,128)(2,1)S(1)}, bf16[1,64,1152]{2,1,0:T(8,128)(2,1)S(1)}, u32[]{:S(2)}, u32[]{:S(2)}) %collective-permute-start.22) | collective-permute-done | bytes 147488 | tf_op jit(solution)/shard_map/ppermute | solution.py:560
  77.9 2.5 %shard_map.61 = bf16[256,1152]{1,0:T(8,128)(2,1)} custom-call(bf16[256,1152]{1,0:T(8,128)(2,1)S(1)} %get-tuple-element.50.refs_0_, bf16[1152,1152]{1,0:T(8,128)(2,1)S(1)} %get-tuple-element.51.refs_1_, f32[9,32,128]{2,1,0:T(8,128)S(1)} %convert_add_fusion.refs_2_, f32[256,1152]{1,0:T(8,128)S(1)} %bitcast.5, ...), custom_call_target="tpu_custom_call" | custom-call | flops 679477248 | bytes 2654208 | tf_op jit(solution)/shard_map/pallas_call | solution.py:164
  (20 shorter events, 0.4 us)
Async XLA Ops:
  0.0 7.1 %copy-start.3 = (bf16[1,4,64,1152]{3,2,1,0:T(8,128)(2,1)S(1)}, bf16[1,4,64,1152]{3,2,1,0:T(8,128)(2,1)}, u32[]{:S(2)}) copy-start(bf16[1,4,64,1152]{3,2,1,0:T(8,128)(2,1)} %param.5) | copy-start | bytes 1769476
  2.0 10.5 %collective-permute-start.1 = (bf16[1,80,1152]{2,1,0:T(8,128)(2,1)}, bf16[1,80,1152]{2,1,0:T(8,128)(2,1)S(1)}, u32[]{:S(2)}, u32[]{:S(2)}) collective-permute-start(bf16[1,80,1152]{2,1,0:T(8,128)(2,1)} %bitcast.8), channel_id=1, source_target_pairs={{0,3},{1,0},{2,1},{3,2},{4,7},{5,4},{6,5},{7,6},{8,11},{9,8},{10,9... | collective-permute-start | bytes 552968 | tf_op jit(solution)/shard_map/ppermute | solution.py:104
  7.1 9.0 %collective-permute-start = (bf16[1,80,1152]{2,1,0:T(8,128)(2,1)}, bf16[1,80,1152]{2,1,0:T(8,128)(2,1)S(1)}, u32[]{:S(2)}, u32[]{:S(2)}) collective-permute-start(bf16[1,80,1152]{2,1,0:T(8,128)(2,1)} %bitcast.9), channel_id=1, source_target_pairs={{0,1},{1,2},{2,3},{3,0},{4,5},{5,6},{6,7},{7,4},{8,9},{9,10},{10,1... | collective-permute-start | bytes 552968 | tf_op jit(solution)/shard_map/ppermute | solution.py:104
  7.1 12.2 %copy-start.5 = (bf16[2,64,1152]{2,1,0:T(8,128)(2,1)S(1)}, bf16[2,64,1152]{2,1,0:T(8,128)(2,1)}, u32[]{:S(2)}) copy-start(bf16[2,64,1152]{2,1,0:T(8,128)(2,1)} %get-tuple-element.38) | copy-start | bytes 884740
  8.2 37.8 %copy-start = (bf16[288,3456]{1,0:T(8,128)(2,1)S(1)}, bf16[288,3456]{1,0:T(8,128)(2,1)}, u32[]{:S(2)}) copy-start(bf16[288,3456]{1,0:T(8,128)(2,1)} %refs_1_.1) | copy-start | bytes 5971972
  8.3 19.2 %collective-permute-start.10 = (bf16[256,1152]{1,0:T(8,128)(2,1)S(1)}, bf16[256,1152]{1,0:T(8,128)(2,1)S(1)}, u32[]{:S(2)}, u32[]{:S(2)}) collective-permute-start(bf16[256,1152]{1,0:T(8,128)(2,1)S(1)} %shard_map.56.refs_0_), channel_id=1, source_target_pairs={{0,4},{4,0},{8,12},{12,8},{16,20},{20,16},{24,28},{28,24},{1,5},{5... | collective-permute-start | bytes 1769480 | tf_op jit(solution)/shard_map/ppermute | solution.py:108
  16.1 11.4 %collective-permute-start.11 = (bf16[2,80,1152]{2,1,0:T(8,128)(2,1)S(1)}, bf16[2,80,1152]{2,1,0:T(8,128)(2,1)S(1)}, u32[]{:S(2)}, u32[]{:S(2)}) collective-permute-start(bf16[2,80,1152]{2,1,0:T(8,128)(2,1)S(1)} %constant_dynamic-update-slice_fusion.5), channel_id=1, source_target_pairs={{0,8},{4,20},{8,0},{12,28},{16,24},{20,4},{24,16},{28,12},{1,9},{5... | collective-permute-start | bytes 1105928 | tf_op jit(solution)/shard_map/ppermute | solution.py:108
  17.6 9.4 %collective-permute-start.3 = (bf16[1,80,1152]{2,1,0:T(8,128)(2,1)S(1)}, bf16[1,80,1152]{2,1,0:T(8,128)(2,1)S(1)}, u32[]{:S(2)}, u32[]{:S(2)}) collective-permute-start(bf16[1,80,1152]{2,1,0:T(8,128)(2,1)S(1)} %collective-permute-done), channel_id=1, source_target_pairs={{0,1},{1,2},{2,3},{3,0},{4,5},{5,6},{6,7},{7,4},{8,9},{9,10},{10,1... | collective-permute-start | bytes 552968 | tf_op jit(solution)/shard_map/ppermute | solution.py:104
  19.2 16.9 %collective-permute-start.2 = (bf16[2,64,1152]{2,1,0:T(8,128)(2,1)S(1)}, bf16[2,64,1152]{2,1,0:T(8,128)(2,1)S(1)}, u32[]{:S(2)}, u32[]{:S(2)}) collective-permute-start(bf16[2,64,1152]{2,1,0:T(8,128)(2,1)S(1)} %copy-done.5), channel_id=1, source_target_pairs={{0,1},{1,2},{2,3},{3,0},{4,5},{5,6},{6,7},{7,4},{8,9},{9,10},{10,1... | collective-permute-start | bytes 884744 | tf_op jit(solution)/shard_map/ppermute | solution.py:104
  27.0 7.6 %collective-permute-start.4 = (bf16[1,80,1152]{2,1,0:T(8,128)(2,1)S(1)}, bf16[1,80,1152]{2,1,0:T(8,128)(2,1)S(1)}, u32[]{:S(2)}, u32[]{:S(2)}) collective-permute-start(bf16[1,80,1152]{2,1,0:T(8,128)(2,1)S(1)} %collective-permute-done.3), channel_id=1, source_target_pairs={{0,8},{4,20},{8,0},{12,28},{16,24},{20,4},{24,16},{28,12},{1,9},{5... | collective-permute-start | bytes 552968 | tf_op jit(solution)/shard_map/ppermute | solution.py:108
  27.5 18.5 %collective-permute-start.12 = (bf16[4,80,1152]{2,1,0:T(8,128)(2,1)S(1)}, bf16[4,80,1152]{2,1,0:T(8,128)(2,1)S(1)}, u32[]{:S(2)}, u32[]{:S(2)}) collective-permute-start(bf16[4,80,1152]{2,1,0:T(8,128)(2,1)S(1)} %constant_dynamic-update-slice_fusion.7.refs_3_), channel_id=1, source_target_pairs={{0,16},{4,12},{8,24},{12,4},{16,0},{20,28},{24,8},{28,20},{1,17},{... | collective-permute-start | bytes 2211848 | tf_op jit(solution)/shard_map/ppermute | solution.py:108
  34.6 11.5 %collective-permute-start.13 = (bf16[2,80,1152]{2,1,0:T(8,128)(2,1)S(1)}, bf16[2,80,1152]{2,1,0:T(8,128)(2,1)S(1)}, u32[]{:S(2)}, u32[]{:S(2)}) collective-permute-start(bf16[2,80,1152]{2,1,0:T(8,128)(2,1)S(1)} %constant_dynamic-update-slice_fusion.refs_5_), channel_id=1, source_target_pairs={{0,16},{4,12},{8,24},{12,4},{16,0},{20,28},{24,8},{28,20},{1,17},{... | collective-permute-start | bytes 1105928 | tf_op jit(solution)/shard_map/ppermute | solution.py:108
  36.2 9.9 %collective-permute-start.6 = (bf16[2,64,1152]{2,1,0:T(8,128)(2,1)S(1)}, bf16[2,64,1152]{2,1,0:T(8,128)(2,1)S(1)}, u32[]{:S(2)}, u32[]{:S(2)}) collective-permute-start(bf16[2,64,1152]{2,1,0:T(8,128)(2,1)S(1)} %copy-done.5), channel_id=1, source_target_pairs={{0,3},{1,0},{2,1},{3,2},{4,7},{5,4},{6,5},{7,6},{8,11},{9,8},{10,9... | collective-permute-start | bytes 884744 | tf_op jit(solution)/shard_map/ppermute | solution.py:104
  36.2 12.0 %collective-permute-start.5 = (bf16[2,64,1152]{2,1,0:T(8,128)(2,1)S(1)}, bf16[2,64,1152]{2,1,0:T(8,128)(2,1)S(1)}, u32[]{:S(2)}, u32[]{:S(2)}) collective-permute-start(bf16[2,64,1152]{2,1,0:T(8,128)(2,1)S(1)} %collective-permute-done.2), channel_id=1, source_target_pairs={{0,1},{1,2},{2,3},{3,0},{4,5},{5,6},{6,7},{7,4},{8,9},{9,10},{10,1... | collective-permute-start | bytes 884744 | tf_op jit(solution)/shard_map/ppermute | solution.py:104
  48.2 3.2 %collective-permute-start.14 = (bf16[608,1152]{1,0:T(8,128)(2,1)S(1)}, bf16[608,1152]{1,0:T(8,128)(2,1)S(1)}, u32[]{:S(2)}, u32[]{:S(2)}) collective-permute-start(bf16[608,1152]{1,0:T(8,128)(2,1)S(1)} %shard_map.57.mine_ref.refs_7_), channel_id=1, source_target_pairs={{0,4},{4,0},{8,12},{12,8},{16,20},{20,16},{24,28},{28,24},{1,5},{5... | collective-permute-start | bytes 4202504 | tf_op jit(solution)/shard_map/ppermute | solution.py:108
  48.4 4.3 %collective-permute-start.7 = (bf16[6,64,1152]{2,1,0:T(8,128)(2,1)S(1)}, bf16[6,64,1152]{2,1,0:T(8,128)(2,1)S(1)}, u32[]{:S(2)}, u32[]{:S(2)}) collective-permute-start(bf16[6,64,1152]{2,1,0:T(8,128)(2,1)S(1)} %constant_dynamic-update-slice_fusion.2.refs_3_), channel_id=1, source_target_pairs={{0,4},{4,0},{8,12},{12,8},{16,20},{20,16},{24,28},{28,24},{1,5},{5... | collective-permute-start | bytes 2654216 | tf_op jit(solution)/shard_map/ppermute | solution.py:108
  49.1 12.4 %collective-permute-start.9 = (bf16[3,64,1152]{2,1,0:T(8,128)(2,1)S(1)}, bf16[3,64,1152]{2,1,0:T(8,128)(2,1)S(1)}, u32[]{:S(2)}, u32[]{:S(2)}) collective-permute-start(bf16[3,64,1152]{2,1,0:T(8,128)(2,1)S(1)} %pad_maximum_fusion), channel_id=1, source_target_pairs={{0,16},{4,12},{8,24},{12,4},{16,0},{20,28},{24,8},{28,20},{1,17},{... | collective-permute-start | bytes 1327112 | tf_op jit(solution)/shard_map/ppermute | solution.py:108
  49.7 12.4 %collective-permute-start.8 = (bf16[3,64,1152]{2,1,0:T(8,128)(2,1)S(1)}, bf16[3,64,1152]{2,1,0:T(8,128)(2,1)S(1)}, u32[]{:S(2)}, u32[]{:S(2)}) collective-permute-start(bf16[3,64,1152]{2,1,0:T(8,128)(2,1)S(1)} %pad_maximum_fusion), channel_id=1, source_target_pairs={{0,8},{4,20},{8,0},{12,28},{16,24},{20,4},{24,16},{28,12},{1,9},{5... | collective-permute-start | bytes 1327112 | tf_op jit(solution)/shard_map/ppermute | solution.py:108
  52.3 10.5 %copy-start.2 = (f32[3,3,1152]{2,1,0:T(4,128)S(1)}, f32[3,3,1152]{2,1,0:T(4,128)}, u32[]{:S(2)}) copy-start(f32[3,3,1152]{2,1,0:T(4,128)} %refs_6_.1) | copy-start | bytes 124420
  52.7 9.4 %collective-permute-start.17 = (bf16[9,32,128]{2,1,0:T(8,128)(2,1)S(1)}, bf16[9,32,128]{2,1,0:T(8,128)(2,1)S(1)}, u32[]{:S(2)}, u32[]{:S(2)}) collective-permute-start(bf16[9,32,128]{2,1,0:T(8,128)(2,1)S(1)} %get-tuple-element.45), channel_id=1, source_target_pairs={{0,24},{4,28},{8,16},{12,20},{1,25},{5,29},{9,17},{13,21},{2,26},{... | collective-permute-start | bytes 221192 | tf_op jit(solution)/shard_map/ppermute | solution.py:546
  55.5 7.1 %collective-permute-start.16 = (bf16[9,32,128]{2,1,0:T(8,128)(2,1)S(1)}, bf16[9,32,128]{2,1,0:T(8,128)(2,1)S(1)}, u32[]{:S(2)}, u32[]{:S(2)}) collective-permute-start(bf16[9,32,128]{2,1,0:T(8,128)(2,1)S(1)} %get-tuple-element.45), channel_id=1, source_target_pairs={{0,16},{4,20},{8,24},{12,28},{1,17},{5,21},{9,25},{13,29},{2,18},{... | collective-permute-start | bytes 221192 | tf_op jit(solution)/shard_map/ppermute | solution.py:546
  56.8 5.8 %collective-permute-start.15 = (bf16[9,32,128]{2,1,0:T(8,128)(2,1)S(1)}, bf16[9,32,128]{2,1,0:T(8,128)(2,1)S(1)}, u32[]{:S(2)}, u32[]{:S(2)}) collective-permute-start(bf16[9,32,128]{2,1,0:T(8,128)(2,1)S(1)} %get-tuple-element.45), channel_id=1, source_target_pairs={{0,8},{4,12},{16,24},{20,28},{1,9},{5,13},{17,25},{21,29},{2,10},{... | collective-permute-start | bytes 221192 | tf_op jit(solution)/shard_map/ppermute | solution.py:546
  62.1 5.4 %copy-start.4 = (f32[1152]{0:T(1024)S(1)}, f32[1152]{0:T(1024)}, u32[]{:S(2)}) copy-start(f32[1152]{0:T(1024)} %param.9) | copy-start | bytes 13828
  62.6 11.2 %copy-start.1 = (bf16[288,1152]{1,0:T(8,128)(2,1)S(1)}, bf16[288,1152]{1,0:T(8,128)(2,1)}, u32[]{:S(2)}) copy-start(bf16[288,1152]{1,0:T(8,128)(2,1)} %refs_2_.3) | copy-start | bytes 1990660
  62.7 11.1 %collective-permute-start.18 = (bf16[6,64,1152]{2,1,0:T(8,128)(2,1)S(1)}, bf16[6,64,1152]{2,1,0:T(8,128)(2,1)S(1)}, u32[]{:S(2)}, u32[]{:S(2)}) collective-permute-start(bf16[6,64,1152]{2,1,0:T(8,128)(2,1)S(1)} %constant_dynamic-update-slice_fusion.9.refs_5_), channel_id=1, source_target_pairs={{0,4},{4,0},{8,12},{12,8},{16,20},{20,16},{24,28},{28,24},{1,5},{5... | collective-permute-start | bytes 2654216 | tf_op jit(solution)/shard_map/ppermute | solution.py:108
  62.7 4.7 %collective-permute-start.19 = (bf16[9,32,128]{2,1,0:T(8,128)(2,1)S(1)}, bf16[9,32,128]{2,1,0:T(8,128)(2,1)S(1)}, u32[]{:S(2)}, u32[]{:S(2)}) collective-permute-start(bf16[9,32,128]{2,1,0:T(8,128)(2,1)S(1)} %convert_add_fusion.1), channel_id=1, source_target_pairs={{0,1},{1,0},{2,3},{3,2},{4,5},{5,4},{6,7},{7,6},{8,9},{9,8},{10,11... | collective-permute-start | bytes 221192 | tf_op jit(solution)/shard_map/ppermute | solution.py:554
  67.5 6.3 %collective-permute-start.20 = (bf16[9,32,128]{2,1,0:T(8,128)(2,1)S(1)}, bf16[9,32,128]{2,1,0:T(8,128)(2,1)S(1)}, u32[]{:S(2)}, u32[]{:S(2)}) collective-permute-start(bf16[9,32,128]{2,1,0:T(8,128)(2,1)S(1)} %add_convert_fusion), channel_id=1, source_target_pairs={{0,2},{1,3},{2,0},{3,1},{4,6},{5,7},{6,4},{7,5},{8,10},{9,11},{10,... | collective-permute-start | bytes 221192 | tf_op jit(solution)/shard_map/ppermute | solution.py:557
  67.6 7.7 %collective-permute-start.21 = (bf16[1,64,1152]{2,1,0:T(8,128)(2,1)S(1)}, bf16[1,64,1152]{2,1,0:T(8,128)(2,1)S(1)}, u32[]{:S(2)}, u32[]{:S(2)}) collective-permute-start(bf16[1,64,1152]{2,1,0:T(8,128)(2,1)S(1)} %get-tuple-element.57), channel_id=1, source_target_pairs={{0,1},{1,2},{2,3},{4,5},{5,6},{6,7},{8,9},{9,10},{10,11},{12,13},{... | collective-permute-start | bytes 442376 | tf_op jit(solution)/shard_map/ppermute | solution.py:559
  69.7 8.2 %collective-permute-start.22 = (bf16[1,64,1152]{2,1,0:T(8,128)(2,1)S(1)}, bf16[1,64,1152]{2,1,0:T(8,128)(2,1)S(1)}, u32[]{:S(2)}, u32[]{:S(2)}) collective-permute-start(bf16[1,64,1152]{2,1,0:T(8,128)(2,1)S(1)} %get-tuple-element.58), channel_id=1, source_target_pairs={{1,0},{2,1},{3,2},{5,4},{6,5},{7,6},{9,8},{10,9},{11,10},{13,12},{... | collective-permute-start | bytes 442376 | tf_op jit(solution)/shard_map/ppermute | solution.py:560

commit v10 on v9

--- a/solution.py
+++ b/solution.py
@@ -315,10 +315,11 @@
     return rows == columns
 
 
-def state_kernel(mine_ref, other_ref, values_ref, top_ref, bottom_ref, upto_ref, total_ref):
+def state_kernel(mine_ref, other_ref, values_ref, near_ref, next_ref, upto_ref, total_ref):
+    even = lax.rem(lax.axis_index("space"), 2) == 0
     _, _, core = coordinates()
     mask = diagonal_mask()
-    columns = top_ref.shape[1]
+    columns = near_ref.shape[1]
     count = values_ref.shape[0]
     later = jnp.where(core == 1, 1.0, 0.0).astype(jnp.float32)
     for group in range(mine_ref.shape[1] // LANES):
@@ -340,8 +341,9 @@
         here, values = state(mine_ref[low, at], other_ref[high, at])
         there, _ = state(mine_ref[high, at], other_ref[low, at])
         values_ref[:, at] = values
-        top_ref[0, :, at] = values[:columns]
-        bottom_ref[0, :, at] = values[-columns:]
+        top, bottom = values[:columns], values[-columns:]
+        near_ref[0, :, at] = jnp.where(even, bottom, top)
+        next_ref[0, :, at] = jnp.where(even, top, bottom)
         upto_ref[group] = here + later * there
         total_ref[group] = (here + there).astype(jnp.bfloat16)
 
@@ -458,10 +460,11 @@
 
 
 def finish_kernel(*refs):
-    queries_ref, weight_ref, state_ref, local_ref, above_ref, below_ref, *refs = refs
+    queries_ref, weight_ref, state_ref, local_ref, near_ref, next_ref, *refs = refs
     conv_ref, gain_ref, result_ref, read_ref, mixture_ref = refs
     count, depth = queries_ref.shape
-    columns = above_ref.shape[1]
+    columns = near_ref.shape[1]
+    even = lax.rem(lax.axis_index("space"), 2) == 0
     mask = diagonal_mask()
     square = jnp.zeros((count, LANES), jnp.float32)
     for group in range(depth // LANES):
@@ -476,8 +479,10 @@
         lanes = slice(at, at + LANES)
         taps = conv_ref[:, :, lanes]
         mixture = read_ref[:, lanes] * scale * gain_ref[:, lanes] + local_ref[:, lanes]
-        above = column_taps(above_ref[:, :, lanes].astype(jnp.float32), taps[0])[0]
-        below = column_taps(below_ref[:, :, lanes].astype(jnp.float32), taps[2])[0]
+        near = near_ref[:, :, lanes].astype(jnp.float32)
+        beyond = next_ref[:, :, lanes].astype(jnp.float32)
+        above = column_taps(jnp.where(even, beyond, near), taps[0])[0]
+        below = column_taps(jnp.where(even, near, beyond), taps[2])[0]
         middle = mixture[columns : count - columns]
         mixture = jnp.concatenate(
             [mixture[:columns] + above, middle, mixture[count - columns :] + below], axis=0
@@ -534,7 +539,7 @@
     other = flipped(after(mine, second_two), (1, 1))
     straight = jnp.concatenate([second_one, second_two, second_three])
     swapped_straight = flipped(straight, (1, 1))
-    values, top, bottom, upto, total = state_call(mine, other, tokens.shape[0], col_count)
+    values, edge_near, edge_next, upto, total = state_call(mine, other, tokens.shape[0], col_count)
     total = after(total, swapped_straight)
 
     second_own = jnp.stack([second_one[0], second_two[0], second_three[0]])
@@ -545,8 +550,6 @@
         pairs = [(t, t ^ bit) for t in range(8) if not t & guard]
         upto = upto + lax.ppermute(total, "tm", pairs).astype(jnp.float32)
     count = lax.axis_size("space")
-    forward = [(i, i + 1) for i in range(count - 1)]
-    backward = [(target, source) for source, target in forward]
     state = after(upto, second_first, second_second)
     share = state.astype(jnp.bfloat16)
     grid = values.reshape(row_count, col_count, depth)
@@ -554,10 +557,12 @@
     arrived = lax.ppermute(share, "space", [(i, i ^ 1) for i in range(count)])
     arrived = after(arrived, local_term)
     share = (share.astype(jnp.float32) + arrived.astype(jnp.float32)).astype(jnp.bfloat16)
-    arrived = lax.ppermute(share, "space", [(i, i ^ 2) for i in range(count)])
-    top, bottom = after((top, bottom), share)
-    above = lax.ppermute(bottom, "space", forward)
-    below = lax.ppermute(top, "space", backward)
+    arrived = lax.ppermute(share, "space", [(i, count - 1 - i) for i in range(count)])
+    edge_near, edge_next = after((edge_near, edge_next), share)
+    edge_near = lax.ppermute(edge_near, "space", [(i, i ^ 1) for i in range(count)])
+    between = [(i, i + 1) for i in range(1, count - 1, 2)]
+    between += [(target, source) for source, target in between]
+    edge_next = lax.ppermute(edge_next, "space", between)
 
     turned = jnp.concatenate(after((second_first, second_second), total))
     swapped_turned = flipped(after(turned, upto), (1, 1))
@@ -573,14 +578,14 @@
         other,
     )
     state = share.astype(jnp.float32) + arrived.astype(jnp.float32)
-    above, below = after((above, below), queries, weight)
+    edge_near, edge_next = after((edge_near, edge_next), queries, weight)
     result = finish_call(
         queries,
         weight,
         state,
         local_term,
-        above,
-        below,
+        edge_near,
+        edge_next,
         conv_weight,
         norm_gain[None],
     )

time: 80.7 us -> 78.8 us (0.976)
  starting transfers between devices: 26.5 us -> 24 us
    ppermute x3, starting transfers between devices: 3.54 us -> 1.06 us  [the longest x1 0.66 us: plane_form(): edge_next = lax.ppermute(edge_next, 'space', between)]
  transfers between devices with their start and end apart: 23 -> 23, of which waited for: 13 -> 12; matrix products, arithmetic and copies ran while one was open for 1% -> 1% of each run, Pallas kernels for 8% -> 8%
where the time goes in v10:
time: 78.8 us; the launch traced here: 78.6 us
  waiting for transfers between devices  42.7 us (54%)
  starting transfers between devices  24 us (30%)
  Pallas kernels  11 us (14%)
    ppermute x6, waiting for transfers between devices, shifted(): lax.ppermute(value, 'space', [(i, (i + step) % count) for i in range(coun...  23.3 us
    pallas_call x7, Pallas kernels, kernel_call(): pl.pallas_call(body, out_shape=outputs, in_specs=in_specs, out_specs=jax....  11 us
    ppermute x10, waiting for transfers between devices, flipped(): lax.ppermute(value, 'tm', [(t, t ^ bit_on_core[t % 2]) for t in range(8)])  9.33 us
    ppermute x6, starting transfers between devices, shifted(): lax.ppermute(value, 'space', [(i, (i + step) % count) for i in range(coun...  8.78 us
    ppermute x3, starting transfers between devices, plane_form(): upto = upto + lax.ppermute(total, 'tm', pairs).astype(jnp.float32)  7.07 us
    ppermute x10, starting transfers between devices, flipped(): lax.ppermute(value, 'tm', [(t, t ^ bit_on_core[t % 2]) for t in range(8)])  7.06 us
    ppermute x1, waiting for transfers between devices, plane_form(): lax.ppermute(share, 'space', [(i, count - 1 - i) for i in range(count)])  5.94 us
    ppermute x1, waiting for transfers between devices, plane_form(): arrived = lax.ppermute(share, 'space', [(i, i ^ 1) for i in range(count)])  3.73 us
  transfers between devices with their start and end apart: 23, of which 12 were waited for; matrix products, arithmetic and copies ran while one was open for 1% of the time, Pallas kernels for 8%

profile of v10, /device:TPU:0, one launch (start us, length us, event | category | flops | bytes accessed | tf_op | source)
XLA Modules:
  0.0 78.6 jit_solution(12546529057530129216)
XLA Ops:
  0.0 0.0 copy-start.3
  0.0 1.9 %shard_map.55 = (bf16[80,1152]{1,0:T(8,128)(2,1)}, bf16[2,64,1152]{2,1,0:T(8,128)(2,1)}) custom-call(bf16[288,3456]{1,0:T(8,128)(2,1)} %refs_1_.1, bf16[288,1152]{1,0:T(8,128)(2,1)} %refs_2_.3), custom_call_target="tpu_custom_call" | custom-call | bytes 958464 | tf_op jit(solution)/shard_map/pallas_call | solution.py:164
  2.0 5.1 %collective-permute-start.1 = (bf16[1,80,1152]{2,1,0:T(8,128)(2,1)}, bf16[1,80,1152]{2,1,0:T(8,128)(2,1)S(1)}, u32[]{:S(2)}, u32[]{:S(2)}) collective-permute-start(bf16[1,80,1152]{2,1,0:T(8,128)(2,1)} %bitcast.8), channel_id=1, source_target_pairs={{0,3},{1,0},{2,1},{3,2},{4,7},{5,4},{6,5},{7,6},{8,11},{9,8},{10,9... | collective-permute-start | bytes 552968 | tf_op jit(solution)/shard_map/ppermute | solution.py:104
  7.1 0.0 collective-permute-start
  7.1 0.0 copy-done.3
  7.1 1.2 %shard_map.56.refs_0_ = bf16[256,1152]{1,0:T(8,128)(2,1)S(1)} custom-call(bf16[256,1152]{1,0:T(8,128)(2,1)S(1)} %bitcast.7), custom_call_target="tpu_custom_call" | custom-call | flops 679477248 | bytes 589824 | tf_op jit(solution)/shard_map/pallas_call | solution.py:164
  8.2 0.0 copy-start
  8.3 0.1 collective-permute-start.10
  8.3 4.1 %collective-permute-done.1 = bf16[1,80,1152]{2,1,0:T(8,128)(2,1)S(1)} collective-permute-done((bf16[1,80,1152]{2,1,0:T(8,128)(2,1)}, bf16[1,80,1152]{2,1,0:T(8,128)(2,1)S(1)}, u32[]{:S(2)}, u32[]{:S(2)}) %collective-permute-start.1) | collective-permute-done | bytes 184352 | tf_op jit(solution)/shard_map/ppermute | solution.py:104
  12.4 3.6 %collective-permute-done = bf16[1,80,1152]{2,1,0:T(8,128)(2,1)S(1)} collective-permute-done((bf16[1,80,1152]{2,1,0:T(8,128)(2,1)}, bf16[1,80,1152]{2,1,0:T(8,128)(2,1)S(1)}, u32[]{:S(2)}, u32[]{:S(2)}) %collective-permute-start) | collective-permute-done | bytes 184352 | tf_op jit(solution)/shard_map/ppermute | solution.py:104
  16.1 1.6 %collective-permute-start.11 = (bf16[2,80,1152]{2,1,0:T(8,128)(2,1)S(1)}, bf16[2,80,1152]{2,1,0:T(8,128)(2,1)S(1)}, u32[]{:S(2)}, u32[]{:S(2)}) collective-permute-start(bf16[2,80,1152]{2,1,0:T(8,128)(2,1)S(1)} %constant_dynamic-update-slice_fusion.5), channel_id=1, source_target_pairs={{0,8},{4,20},{8,0},{12,28},{16,24},{20,4},{24,16},{28,12},{1,9},{5... | collective-permute-start | bytes 1105928 | tf_op jit(solution)/shard_map/ppermute | solution.py:108
  17.6 1.6 %collective-permute-start.3 = (bf16[1,80,1152]{2,1,0:T(8,128)(2,1)S(1)}, bf16[1,80,1152]{2,1,0:T(8,128)(2,1)S(1)}, u32[]{:S(2)}, u32[]{:S(2)}) collective-permute-start(bf16[1,80,1152]{2,1,0:T(8,128)(2,1)S(1)} %collective-permute-done), channel_id=1, source_target_pairs={{0,1},{1,2},{2,3},{3,0},{4,5},{5,6},{6,7},{7,4},{8,9},{9,10},{10,1... | collective-permute-start | bytes 552968 | tf_op jit(solution)/shard_map/ppermute | solution.py:104
  19.2 0.0 copy-done.5
  19.2 0.0 collective-permute-start.2
  19.3 7.7 %collective-permute-done.3 = bf16[1,80,1152]{2,1,0:T(8,128)(2,1)S(1)} collective-permute-done((bf16[1,80,1152]{2,1,0:T(8,128)(2,1)S(1)}, bf16[1,80,1152]{2,1,0:T(8,128)(2,1)S(1)}, u32[]{:S(2)}, u32[]{:S(2)}) %collective-permute-start.3) | collective-permute-done | bytes 184352 | tf_op jit(solution)/shard_map/ppermute | solution.py:104
  27.0 0.5 collective-permute-start.4
  27.5 0.0 collective-permute-done.11
  27.5 0.0 collective-permute-done.10.refs_1_
  27.5 1.7 %collective-permute-start.12 = (bf16[4,80,1152]{2,1,0:T(8,128)(2,1)S(1)}, bf16[4,80,1152]{2,1,0:T(8,128)(2,1)S(1)}, u32[]{:S(2)}, u32[]{:S(2)}) collective-permute-start(bf16[4,80,1152]{2,1,0:T(8,128)(2,1)S(1)} %constant_dynamic-update-slice_fusion.7.refs_3_), channel_id=1, source_target_pairs={{0,16},{4,12},{8,24},{12,4},{16,0},{20,28},{24,8},{28,20},{1,17},{... | collective-permute-start | bytes 2211848 | tf_op jit(solution)/shard_map/ppermute | solution.py:108
  29.2 5.4 %collective-permute-done.4 = bf16[1,80,1152]{2,1,0:T(8,128)(2,1)S(1)} collective-permute-done((bf16[1,80,1152]{2,1,0:T(8,128)(2,1)S(1)}, bf16[1,80,1152]{2,1,0:T(8,128)(2,1)S(1)}, u32[]{:S(2)}, u32[]{:S(2)}) %collective-permute-start.4) | collective-permute-done | bytes 184352 | tf_op jit(solution)/shard_map/ppermute | solution.py:108
  34.6 1.6 %collective-permute-start.13 = (bf16[2,80,1152]{2,1,0:T(8,128)(2,1)S(1)}, bf16[2,80,1152]{2,1,0:T(8,128)(2,1)S(1)}, u32[]{:S(2)}, u32[]{:S(2)}) collective-permute-start(bf16[2,80,1152]{2,1,0:T(8,128)(2,1)S(1)} %constant_dynamic-update-slice_fusion.refs_5_), channel_id=1, source_target_pairs={{0,16},{4,12},{8,24},{12,4},{16,0},{20,28},{24,8},{28,20},{1,17},{... | collective-permute-start | bytes 1105928 | tf_op jit(solution)/shard_map/ppermute | solution.py:108
  36.2 0.0 collective-permute-start.6
  36.2 0.0 collective-permute-done.2
  36.2 2.0 %collective-permute-start.5 = (bf16[2,64,1152]{2,1,0:T(8,128)(2,1)S(1)}, bf16[2,64,1152]{2,1,0:T(8,128)(2,1)S(1)}, u32[]{:S(2)}, u32[]{:S(2)}) collective-permute-start(bf16[2,64,1152]{2,1,0:T(8,128)(2,1)S(1)} %collective-permute-done.2), channel_id=1, source_target_pairs={{0,1},{1,2},{2,3},{3,0},{4,5},{5,6},{6,7},{7,4},{8,9},{9,10},{10,1... | collective-permute-start | bytes 884744 | tf_op jit(solution)/shard_map/ppermute | solution.py:104
  38.2 7.9 %collective-permute-done.6 = bf16[2,64,1152]{2,1,0:T(8,128)(2,1)S(1)} collective-permute-done((bf16[2,64,1152]{2,1,0:T(8,128)(2,1)S(1)}, bf16[2,64,1152]{2,1,0:T(8,128)(2,1)S(1)}, u32[]{:S(2)}, u32[]{:S(2)}) %collective-permute-start.6) | collective-permute-done | bytes 294944 | tf_op jit(solution)/shard_map/ppermute | solution.py:104
  46.1 0.0 collective-permute-done.13.refs_6_
  46.1 0.0 collective-permute-done.12.refs_4_
  46.1 0.0 copy-done
  46.1 2.1 %shard_map.57.mine_ref.refs_7_ = bf16[608,1152]{1,0:T(8,128)(2,1)S(1)} custom-call(bf16[256,1152]{1,0:T(8,128)(2,1)S(1)} %shard_map.56.refs_0_, bf16[256,1152]{1,0:T(8,128)(2,1)S(1)} %collective-permute-done.10.refs_1_, bf16[288,3456]{1,0:T(8,128)(2,1)S(1)} %copy-done, bf16[4,80,1152]{2,1,0:T(8,128)(2,1)S(1)} %constant_dynamic-update-slice_fusion.7.refs_3_, ...), custom_call_target="tpu_custom_call" | custom-call | flops 1358954496 | bytes 2654208 | tf_op jit(solution)/shard_map/pallas_call | solution.py:164
  48.2 0.0 collective-permute-done.5
  48.2 0.1 collective-permute-start.14
  48.4 0.6 collective-permute-start.7
  49.0 0.1 pad_maximum_fusion
  49.1 0.6 collective-permute-start.9
  49.7 0.5 collective-permute-start.8
  50.1 1.3 %collective-permute-done.14.other_ref.refs_8_ = bf16[608,1152]{1,0:T(8,128)(2,1)S(1)} collective-permute-done((bf16[608,1152]{1,0:T(8,128)(2,1)S(1)}, bf16[608,1152]{1,0:T(8,128)(2,1)S(1)}, u32[]{:S(2)}, u32[]{:S(2)}) %collective-permute-start.14) | collective-permute-done | bytes 1400864 | tf_op jit(solution)/shard_map/ppermute | solution.py:108
  51.4 0.8 %shard_map.58 = (bf16[256,1152]{1,0:T(8,128)(2,1)S(1)}, bf16[1,64,1152]{2,1,0:T(8,128)(2,1)S(1)}, bf16[1,64,1152]{2,1,0:T(8,128)(2,1)S(1)}, f32[9,32,128]{2,1,0:T(8,128)S(1)}, bf16[9,32,128]{2,1,0:T(8,128)(2,1)S(1)}) custom-call(bf16[608,1152]{1,0:T(8,128)(2,1)S(1)} %shard_map.57.mine_ref.refs_7_, bf16[608,1152]{1,0:T(8,128)(2,1)S(1)} %collective-permute-done.14.other_ref.refs_8_), custom_call_target="tpu_custom_call" | custom-call | flops 150994944 | bytes 2359296 | tf_op jit(solution)/shard_map/pallas_call | solution.py:164
  52.3 0.0 copy-start.2
  52.3 0.4 collective-permute-done.7.refs_4_
  52.7 2.7 %collective-permute-start.17 = (bf16[9,32,128]{2,1,0:T(8,128)(2,1)S(1)}, bf16[9,32,128]{2,1,0:T(8,128)(2,1)S(1)}, u32[]{:S(2)}, u32[]{:S(2)}) collective-permute-start(bf16[9,32,128]{2,1,0:T(8,128)(2,1)S(1)} %get-tuple-element.45), channel_id=1, source_target_pairs={{0,24},{4,28},{8,16},{12,20},{1,25},{5,29},{9,17},{13,21},{2,26},{... | collective-permute-start | bytes 221192 | tf_op jit(solution)/shard_map/ppermute | solution.py:551
  55.4 1.3 %collective-permute-start.16 = (bf16[9,32,128]{2,1,0:T(8,128)(2,1)S(1)}, bf16[9,32,128]{2,1,0:T(8,128)(2,1)S(1)}, u32[]{:S(2)}, u32[]{:S(2)}) collective-permute-start(bf16[9,32,128]{2,1,0:T(8,128)(2,1)S(1)} %get-tuple-element.45), channel_id=1, source_target_pairs={{0,16},{4,20},{8,24},{12,28},{1,17},{5,21},{9,25},{13,29},{2,18},{... | collective-permute-start | bytes 221192 | tf_op jit(solution)/shard_map/ppermute | solution.py:551
  56.7 3.1 %collective-permute-start.15 = (bf16[9,32,128]{2,1,0:T(8,128)(2,1)S(1)}, bf16[9,32,128]{2,1,0:T(8,128)(2,1)S(1)}, u32[]{:S(2)}, u32[]{:S(2)}) collective-permute-start(bf16[9,32,128]{2,1,0:T(8,128)(2,1)S(1)} %get-tuple-element.45), channel_id=1, source_target_pairs={{0,8},{4,12},{16,24},{20,28},{1,9},{5,13},{17,25},{21,29},{2,10},{... | collective-permute-start | bytes 221192 | tf_op jit(solution)/shard_map/ppermute | solution.py:551
  59.8 1.7 %collective-permute-done.9 = bf16[3,64,1152]{2,1,0:T(8,128)(2,1)S(1)} collective-permute-done((bf16[3,64,1152]{2,1,0:T(8,128)(2,1)S(1)}, bf16[3,64,1152]{2,1,0:T(8,128)(2,1)S(1)}, u32[]{:S(2)}, u32[]{:S(2)}) %collective-permute-start.9) | collective-permute-done | bytes 442400 | tf_op jit(solution)/shard_map/ppermute | solution.py:108
  61.5 0.5 collective-permute-done.8
  62.1 0.0 copy-start.4
  62.1 0.0 collective-permute-done.17
  62.2 0.5 collective-permute-done.16
  62.6 0.0 collective-permute-done.15
  62.7 0.1 collective-permute-start.18
  62.7 0.1 collective-permute-start.19
  62.8 0.0 copy-done.2
  62.8 0.9 %shard_map.60 = f32[4,64,1152]{2,1,0:T(8,128)S(1)} custom-call(bf16[4,64,1152]{2,1,0:T(8,128)(2,1)S(1)} %bitcast.6, f32[3,3,1152]{2,1,0:T(4,128)S(1)} %copy-done.2), custom_call_target="tpu_custom_call" | custom-call | flops 5308416 | bytes 1769472 | tf_op jit(solution)/shard_map/pallas_call | solution.py:164
  63.7 3.7 %collective-permute-done.19 = bf16[9,32,128]{2,1,0:T(8,128)(2,1)S(1)} collective-permute-done((bf16[9,32,128]{2,1,0:T(8,128)(2,1)S(1)}, bf16[9,32,128]{2,1,0:T(8,128)(2,1)S(1)}, u32[]{:S(2)}, u32[]{:S(2)}) %collective-permute-start.19) | collective-permute-done | bytes 73760 | tf_op jit(solution)/shard_map/ppermute | solution.py:557
  67.5 0.1 collective-permute-start.20
  67.5 0.0 copy-done.4
  67.6 0.3 collective-permute-start.21
  67.9 0.7 collective-permute-start.22
  68.6 5.9 %collective-permute-done.20 = bf16[9,32,128]{2,1,0:T(8,128)(2,1)S(1)} collective-permute-done((bf16[9,32,128]{2,1,0:T(8,128)(2,1)S(1)}, bf16[9,32,128]{2,1,0:T(8,128)(2,1)S(1)}, u32[]{:S(2)}, u32[]{:S(2)}) %collective-permute-start.20) | collective-permute-done | bytes 73760 | tf_op jit(solution)/shard_map/ppermute | solution.py:560
  74.5 0.0 collective-permute-done.18.refs_6_
  74.5 0.0 copy-done.1
  74.5 1.5 %shard_map.59 = (bf16[256,1152]{1,0:T(8,128)(2,1)S(1)}, bf16[1152,1152]{1,0:T(8,128)(2,1)S(1)}) custom-call(bf16[256,1152]{1,0:T(8,128)(2,1)S(1)} %shard_map.56.refs_0_, bf16[288,3456]{1,0:T(8,128)(2,1)S(1)} %copy-done, bf16[288,1152]{1,0:T(8,128)(2,1)S(1)} %copy-done.1, bf16[6,64,1152]{2,1,0:T(8,128)(2,1)S(1)} %constant_dynamic-update-slice_fusion.2.refs_3_, ...), custom_call_target="tpu_custom_call" | custom-call | flops 679477248 | bytes 5308416 | tf_op jit(solution)/shard_map/pallas_call | solution.py:164
  76.1 0.0 collective-permute-done.21.refs_4_
  76.1 0.0 collective-permute-done.22.refs_5_
  76.1 2.5 %shard_map.61 = bf16[256,1152]{1,0:T(8,128)(2,1)} custom-call(bf16[256,1152]{1,0:T(8,128)(2,1)S(1)} %get-tuple-element.50.refs_0_, bf16[1152,1152]{1,0:T(8,128)(2,1)S(1)} %get-tuple-element.51.refs_1_, f32[9,32,128]{2,1,0:T(8,128)S(1)} %convert_add_fusion.refs_2_, f32[256,1152]{1,0:T(8,128)S(1)} %bitcast.5, ...), custom_call_target="tpu_custom_call" | custom-call | flops 679477248 | bytes 2654208 | tf_op jit(solution)/shard_map/pallas_call | solution.py:164
  (20 shorter events, 0.4 us)
Async XLA Ops:
  0.0 7.1 %copy-start.3 = (bf16[1,4,64,1152]{3,2,1,0:T(8,128)(2,1)S(1)}, bf16[1,4,64,1152]{3,2,1,0:T(8,128)(2,1)}, u32[]{:S(2)}) copy-start(bf16[1,4,64,1152]{3,2,1,0:T(8,128)(2,1)} %param.5) | copy-start | bytes 1769476
  2.0 10.5 %collective-permute-start.1 = (bf16[1,80,1152]{2,1,0:T(8,128)(2,1)}, bf16[1,80,1152]{2,1,0:T(8,128)(2,1)S(1)}, u32[]{:S(2)}, u32[]{:S(2)}) collective-permute-start(bf16[1,80,1152]{2,1,0:T(8,128)(2,1)} %bitcast.8), channel_id=1, source_target_pairs={{0,3},{1,0},{2,1},{3,2},{4,7},{5,4},{6,5},{7,6},{8,11},{9,8},{10,9... | collective-permute-start | bytes 552968 | tf_op jit(solution)/shard_map/ppermute | solution.py:104
  7.1 9.0 %collective-permute-start = (bf16[1,80,1152]{2,1,0:T(8,128)(2,1)}, bf16[1,80,1152]{2,1,0:T(8,128)(2,1)S(1)}, u32[]{:S(2)}, u32[]{:S(2)}) collective-permute-start(bf16[1,80,1152]{2,1,0:T(8,128)(2,1)} %bitcast.9), channel_id=1, source_target_pairs={{0,1},{1,2},{2,3},{3,0},{4,5},{5,6},{6,7},{7,4},{8,9},{9,10},{10,1... | collective-permute-start | bytes 552968 | tf_op jit(solution)/shard_map/ppermute | solution.py:104
  7.1 12.2 %copy-start.5 = (bf16[2,64,1152]{2,1,0:T(8,128)(2,1)S(1)}, bf16[2,64,1152]{2,1,0:T(8,128)(2,1)}, u32[]{:S(2)}) copy-start(bf16[2,64,1152]{2,1,0:T(8,128)(2,1)} %get-tuple-element.38) | copy-start | bytes 884740
  8.2 37.8 %copy-start = (bf16[288,3456]{1,0:T(8,128)(2,1)S(1)}, bf16[288,3456]{1,0:T(8,128)(2,1)}, u32[]{:S(2)}) copy-start(bf16[288,3456]{1,0:T(8,128)(2,1)} %refs_1_.1) | copy-start | bytes 5971972
  8.3 19.2 %collective-permute-start.10 = (bf16[256,1152]{1,0:T(8,128)(2,1)S(1)}, bf16[256,1152]{1,0:T(8,128)(2,1)S(1)}, u32[]{:S(2)}, u32[]{:S(2)}) collective-permute-start(bf16[256,1152]{1,0:T(8,128)(2,1)S(1)} %shard_map.56.refs_0_), channel_id=1, source_target_pairs={{0,4},{4,0},{8,12},{12,8},{16,20},{20,16},{24,28},{28,24},{1,5},{5... | collective-permute-start | bytes 1769480 | tf_op jit(solution)/shard_map/ppermute | solution.py:108
  16.1 11.4 %collective-permute-start.11 = (bf16[2,80,1152]{2,1,0:T(8,128)(2,1)S(1)}, bf16[2,80,1152]{2,1,0:T(8,128)(2,1)S(1)}, u32[]{:S(2)}, u32[]{:S(2)}) collective-permute-start(bf16[2,80,1152]{2,1,0:T(8,128)(2,1)S(1)} %constant_dynamic-update-slice_fusion.5), channel_id=1, source_target_pairs={{0,8},{4,20},{8,0},{12,28},{16,24},{20,4},{24,16},{28,12},{1,9},{5... | collective-permute-start | bytes 1105928 | tf_op jit(solution)/shard_map/ppermute | solution.py:108
  17.6 9.4 %collective-permute-start.3 = (bf16[1,80,1152]{2,1,0:T(8,128)(2,1)S(1)}, bf16[1,80,1152]{2,1,0:T(8,128)(2,1)S(1)}, u32[]{:S(2)}, u32[]{:S(2)}) collective-permute-start(bf16[1,80,1152]{2,1,0:T(8,128)(2,1)S(1)} %collective-permute-done), channel_id=1, source_target_pairs={{0,1},{1,2},{2,3},{3,0},{4,5},{5,6},{6,7},{7,4},{8,9},{9,10},{10,1... | collective-permute-start | bytes 552968 | tf_op jit(solution)/shard_map/ppermute | solution.py:104
  19.2 16.9 %collective-permute-start.2 = (bf16[2,64,1152]{2,1,0:T(8,128)(2,1)S(1)}, bf16[2,64,1152]{2,1,0:T(8,128)(2,1)S(1)}, u32[]{:S(2)}, u32[]{:S(2)}) collective-permute-start(bf16[2,64,1152]{2,1,0:T(8,128)(2,1)S(1)} %copy-done.5), channel_id=1, source_target_pairs={{0,1},{1,2},{2,3},{3,0},{4,5},{5,6},{6,7},{7,4},{8,9},{9,10},{10,1... | collective-permute-start | bytes 884744 | tf_op jit(solution)/shard_map/ppermute | solution.py:104
  27.0 7.6 %collective-permute-start.4 = (bf16[1,80,1152]{2,1,0:T(8,128)(2,1)S(1)}, bf16[1,80,1152]{2,1,0:T(8,128)(2,1)S(1)}, u32[]{:S(2)}, u32[]{:S(2)}) collective-permute-start(bf16[1,80,1152]{2,1,0:T(8,128)(2,1)S(1)} %collective-permute-done.3), channel_id=1, source_target_pairs={{0,8},{4,20},{8,0},{12,28},{16,24},{20,4},{24,16},{28,12},{1,9},{5... | collective-permute-start | bytes 552968 | tf_op jit(solution)/shard_map/ppermute | solution.py:108
  27.5 18.5 %collective-permute-start.12 = (bf16[4,80,1152]{2,1,0:T(8,128)(2,1)S(1)}, bf16[4,80,1152]{2,1,0:T(8,128)(2,1)S(1)}, u32[]{:S(2)}, u32[]{:S(2)}) collective-permute-start(bf16[4,80,1152]{2,1,0:T(8,128)(2,1)S(1)} %constant_dynamic-update-slice_fusion.7.refs_3_), channel_id=1, source_target_pairs={{0,16},{4,12},{8,24},{12,4},{16,0},{20,28},{24,8},{28,20},{1,17},{... | collective-permute-start | bytes 2211848 | tf_op jit(solution)/shard_map/ppermute | solution.py:108
  34.6 11.5 %collective-permute-start.13 = (bf16[2,80,1152]{2,1,0:T(8,128)(2,1)S(1)}, bf16[2,80,1152]{2,1,0:T(8,128)(2,1)S(1)}, u32[]{:S(2)}, u32[]{:S(2)}) collective-permute-start(bf16[2,80,1152]{2,1,0:T(8,128)(2,1)S(1)} %constant_dynamic-update-slice_fusion.refs_5_), channel_id=1, source_target_pairs={{0,16},{4,12},{8,24},{12,4},{16,0},{20,28},{24,8},{28,20},{1,17},{... | collective-permute-start | bytes 1105928 | tf_op jit(solution)/shard_map/ppermute | solution.py:108
  36.2 9.9 %collective-permute-start.6 = (bf16[2,64,1152]{2,1,0:T(8,128)(2,1)S(1)}, bf16[2,64,1152]{2,1,0:T(8,128)(2,1)S(1)}, u32[]{:S(2)}, u32[]{:S(2)}) collective-permute-start(bf16[2,64,1152]{2,1,0:T(8,128)(2,1)S(1)} %copy-done.5), channel_id=1, source_target_pairs={{0,3},{1,0},{2,1},{3,2},{4,7},{5,4},{6,5},{7,6},{8,11},{9,8},{10,9... | collective-permute-start | bytes 884744 | tf_op jit(solution)/shard_map/ppermute | solution.py:104
  36.2 12.0 %collective-permute-start.5 = (bf16[2,64,1152]{2,1,0:T(8,128)(2,1)S(1)}, bf16[2,64,1152]{2,1,0:T(8,128)(2,1)S(1)}, u32[]{:S(2)}, u32[]{:S(2)}) collective-permute-start(bf16[2,64,1152]{2,1,0:T(8,128)(2,1)S(1)} %collective-permute-done.2), channel_id=1, source_target_pairs={{0,1},{1,2},{2,3},{3,0},{4,5},{5,6},{6,7},{7,4},{8,9},{9,10},{10,1... | collective-permute-start | bytes 884744 | tf_op jit(solution)/shard_map/ppermute | solution.py:104
  48.2 3.2 %collective-permute-start.14 = (bf16[608,1152]{1,0:T(8,128)(2,1)S(1)}, bf16[608,1152]{1,0:T(8,128)(2,1)S(1)}, u32[]{:S(2)}, u32[]{:S(2)}) collective-permute-start(bf16[608,1152]{1,0:T(8,128)(2,1)S(1)} %shard_map.57.mine_ref.refs_7_), channel_id=1, source_target_pairs={{0,4},{4,0},{8,12},{12,8},{16,20},{20,16},{24,28},{28,24},{1,5},{5... | collective-permute-start | bytes 4202504 | tf_op jit(solution)/shard_map/ppermute | solution.py:108
  48.4 4.3 %collective-permute-start.7 = (bf16[6,64,1152]{2,1,0:T(8,128)(2,1)S(1)}, bf16[6,64,1152]{2,1,0:T(8,128)(2,1)S(1)}, u32[]{:S(2)}, u32[]{:S(2)}) collective-permute-start(bf16[6,64,1152]{2,1,0:T(8,128)(2,1)S(1)} %constant_dynamic-update-slice_fusion.2.refs_3_), channel_id=1, source_target_pairs={{0,4},{4,0},{8,12},{12,8},{16,20},{20,16},{24,28},{28,24},{1,5},{5... | collective-permute-start | bytes 2654216 | tf_op jit(solution)/shard_map/ppermute | solution.py:108
  49.1 12.4 %collective-permute-start.9 = (bf16[3,64,1152]{2,1,0:T(8,128)(2,1)S(1)}, bf16[3,64,1152]{2,1,0:T(8,128)(2,1)S(1)}, u32[]{:S(2)}, u32[]{:S(2)}) collective-permute-start(bf16[3,64,1152]{2,1,0:T(8,128)(2,1)S(1)} %pad_maximum_fusion), channel_id=1, source_target_pairs={{0,16},{4,12},{8,24},{12,4},{16,0},{20,28},{24,8},{28,20},{1,17},{... | collective-permute-start | bytes 1327112 | tf_op jit(solution)/shard_map/ppermute | solution.py:108
  49.7 12.4 %collective-permute-start.8 = (bf16[3,64,1152]{2,1,0:T(8,128)(2,1)S(1)}, bf16[3,64,1152]{2,1,0:T(8,128)(2,1)S(1)}, u32[]{:S(2)}, u32[]{:S(2)}) collective-permute-start(bf16[3,64,1152]{2,1,0:T(8,128)(2,1)S(1)} %pad_maximum_fusion), channel_id=1, source_target_pairs={{0,8},{4,20},{8,0},{12,28},{16,24},{20,4},{24,16},{28,12},{1,9},{5... | collective-permute-start | bytes 1327112 | tf_op jit(solution)/shard_map/ppermute | solution.py:108
  52.3 10.5 %copy-start.2 = (f32[3,3,1152]{2,1,0:T(4,128)S(1)}, f32[3,3,1152]{2,1,0:T(4,128)}, u32[]{:S(2)}) copy-start(f32[3,3,1152]{2,1,0:T(4,128)} %refs_6_.1) | copy-start | bytes 124420
  52.7 9.4 %collective-permute-start.17 = (bf16[9,32,128]{2,1,0:T(8,128)(2,1)S(1)}, bf16[9,32,128]{2,1,0:T(8,128)(2,1)S(1)}, u32[]{:S(2)}, u32[]{:S(2)}) collective-permute-start(bf16[9,32,128]{2,1,0:T(8,128)(2,1)S(1)} %get-tuple-element.45), channel_id=1, source_target_pairs={{0,24},{4,28},{8,16},{12,20},{1,25},{5,29},{9,17},{13,21},{2,26},{... | collective-permute-start | bytes 221192 | tf_op jit(solution)/shard_map/ppermute | solution.py:551
  55.4 7.2 %collective-permute-start.16 = (bf16[9,32,128]{2,1,0:T(8,128)(2,1)S(1)}, bf16[9,32,128]{2,1,0:T(8,128)(2,1)S(1)}, u32[]{:S(2)}, u32[]{:S(2)}) collective-permute-start(bf16[9,32,128]{2,1,0:T(8,128)(2,1)S(1)} %get-tuple-element.45), channel_id=1, source_target_pairs={{0,16},{4,20},{8,24},{12,28},{1,17},{5,21},{9,25},{13,29},{2,18},{... | collective-permute-start | bytes 221192 | tf_op jit(solution)/shard_map/ppermute | solution.py:551
  56.7 5.9 %collective-permute-start.15 = (bf16[9,32,128]{2,1,0:T(8,128)(2,1)S(1)}, bf16[9,32,128]{2,1,0:T(8,128)(2,1)S(1)}, u32[]{:S(2)}, u32[]{:S(2)}) collective-permute-start(bf16[9,32,128]{2,1,0:T(8,128)(2,1)S(1)} %get-tuple-element.45), channel_id=1, source_target_pairs={{0,8},{4,12},{16,24},{20,28},{1,9},{5,13},{17,25},{21,29},{2,10},{... | collective-permute-start | bytes 221192 | tf_op jit(solution)/shard_map/ppermute | solution.py:551
  62.1 5.4 %copy-start.4 = (f32[1152]{0:T(1024)S(1)}, f32[1152]{0:T(1024)}, u32[]{:S(2)}) copy-start(f32[1152]{0:T(1024)} %param.9) | copy-start | bytes 13828
  62.6 11.9 %copy-start.1 = (bf16[288,1152]{1,0:T(8,128)(2,1)S(1)}, bf16[288,1152]{1,0:T(8,128)(2,1)}, u32[]{:S(2)}) copy-start(bf16[288,1152]{1,0:T(8,128)(2,1)} %refs_2_.3) | copy-start | bytes 1990660
  62.7 11.9 %collective-permute-start.18 = (bf16[6,64,1152]{2,1,0:T(8,128)(2,1)S(1)}, bf16[6,64,1152]{2,1,0:T(8,128)(2,1)S(1)}, u32[]{:S(2)}, u32[]{:S(2)}) collective-permute-start(bf16[6,64,1152]{2,1,0:T(8,128)(2,1)S(1)} %constant_dynamic-update-slice_fusion.9.refs_5_), channel_id=1, source_target_pairs={{0,4},{4,0},{8,12},{12,8},{16,20},{20,16},{24,28},{28,24},{1,5},{5... | collective-permute-start | bytes 2654216 | tf_op jit(solution)/shard_map/ppermute | solution.py:108
  62.7 4.7 %collective-permute-start.19 = (bf16[9,32,128]{2,1,0:T(8,128)(2,1)S(1)}, bf16[9,32,128]{2,1,0:T(8,128)(2,1)S(1)}, u32[]{:S(2)}, u32[]{:S(2)}) collective-permute-start(bf16[9,32,128]{2,1,0:T(8,128)(2,1)S(1)} %convert_add_fusion.1), channel_id=1, source_target_pairs={{0,1},{1,0},{2,3},{3,2},{4,5},{5,4},{6,7},{7,6},{8,9},{9,8},{10,11... | collective-permute-start | bytes 221192 | tf_op jit(solution)/shard_map/ppermute | solution.py:557
  67.5 7.0 %collective-permute-start.20 = (bf16[9,32,128]{2,1,0:T(8,128)(2,1)S(1)}, bf16[9,32,128]{2,1,0:T(8,128)(2,1)S(1)}, u32[]{:S(2)}, u32[]{:S(2)}) collective-permute-start(bf16[9,32,128]{2,1,0:T(8,128)(2,1)S(1)} %add_convert_fusion), channel_id=1, source_target_pairs={{0,3},{1,2},{2,1},{3,0},{4,7},{5,6},{6,5},{7,4},{8,11},{9,10},{10,... | collective-permute-start | bytes 221192 | tf_op jit(solution)/shard_map/ppermute | solution.py:560
  67.6 8.5 %collective-permute-start.21 = (bf16[1,64,1152]{2,1,0:T(8,128)(2,1)S(1)}, bf16[1,64,1152]{2,1,0:T(8,128)(2,1)S(1)}, u32[]{:S(2)}, u32[]{:S(2)}) collective-permute-start(bf16[1,64,1152]{2,1,0:T(8,128)(2,1)S(1)} %get-tuple-element.57), channel_id=1, source_target_pairs={{0,1},{1,0},{2,3},{3,2},{4,5},{5,4},{6,7},{7,6},{8,9},{9,8},{10,11... | collective-permute-start | bytes 442376 | tf_op jit(solution)/shard_map/ppermute | solution.py:562
  67.9 8.2 %collective-permute-start.22 = (bf16[1,64,1152]{2,1,0:T(8,128)(2,1)S(1)}, bf16[1,64,1152]{2,1,0:T(8,128)(2,1)S(1)}, u32[]{:S(2)}, u32[]{:S(2)}) collective-permute-start(bf16[1,64,1152]{2,1,0:T(8,128)(2,1)S(1)} %get-tuple-element.58), channel_id=1, source_target_pairs={{1,2},{2,1},{5,6},{6,5},{9,10},{10,9},{13,14},{14,13},{17,18},{18,... | collective-permute-start | bytes 442376 | tf_op jit(solution)/shard_map/ppermute | solution.py:565

commit v11 on v10

--- a/solution.py
+++ b/solution.py
@@ -551,19 +551,6 @@
         upto = upto + lax.ppermute(total, "tm", pairs).astype(jnp.float32)
     count = lax.axis_size("space")
     state = after(upto, second_first, second_second)
-    share = state.astype(jnp.bfloat16)
-    grid = values.reshape(row_count, col_count, depth)
-    local_term = local_call(grid, conv_weight).reshape(-1, depth)
-    arrived = lax.ppermute(share, "space", [(i, i ^ 1) for i in range(count)])
-    arrived = after(arrived, local_term)
-    share = (share.astype(jnp.float32) + arrived.astype(jnp.float32)).astype(jnp.bfloat16)
-    arrived = lax.ppermute(share, "space", [(i, count - 1 - i) for i in range(count)])
-    edge_near, edge_next = after((edge_near, edge_next), share)
-    edge_near = lax.ppermute(edge_near, "space", [(i, i ^ 1) for i in range(count)])
-    between = [(i, i + 1) for i in range(1, count - 1, 2)]
-    between += [(target, source) for source, target in between]
-    edge_next = lax.ppermute(edge_next, "space", between)
-
     turned = jnp.concatenate(after((second_first, second_second), total))
     swapped_turned = flipped(after(turned, upto), (1, 1))
     queries, weight = query_call(
@@ -577,8 +564,21 @@
         mine,
         other,
     )
+    share = state.astype(jnp.bfloat16)
+    grid = values.reshape(row_count, col_count, depth)
+    local_term = local_call(grid, conv_weight).reshape(-1, depth)
+    arrived = lax.ppermute(share, "space", [(i, i ^ 1) for i in range(count)])
+    arrived = after(arrived, local_term, queries, weight)
+    share = (share.astype(jnp.float32) + arrived.astype(jnp.float32)).astype(jnp.bfloat16)
+    arrived = lax.ppermute(share, "space", [(i, count - 1 - i) for i in range(count)])
+    edge_near, edge_next = after((edge_near, edge_next), share)
+    edge_near = lax.ppermute(edge_near, "space", [(i, i ^ 1) for i in range(count)])
+    between = [(i, i + 1) for i in range(1, count - 1, 2)]
+    between += [(target, source) for source, target in between]
+    edge_next = lax.ppermute(edge_next, "space", between)
+
+
     state = share.astype(jnp.float32) + arrived.astype(jnp.float32)
-    edge_near, edge_next = after((edge_near, edge_next), queries, weight)
     result = finish_call(
         queries,
         weight,

time: 78.8 us -> 77.8 us (0.987); the launches traced: 78.6 us -> 76.4 us
  waiting for transfers between devices: 42.7 us -> 40.8 us
    ppermute x1, waiting for transfers between devices: 3.73 us -> 0.74 us  [plane_form(): arrived = lax.ppermute(share, 'space', [(i, i ^ 1) for i in range(count)])]
    ppermute x10, waiting for transfers between devices: 9.33 us -> 11.5 us  [flipped(): lax.ppermute(value, 'tm', [(t, t ^ bit_on_core[t % 2]) for t in range(8)])]
    ppermute x6, waiting for transfers between devices: 23.3 us -> 22.3 us  [shifted(): lax.ppermute(value, 'space', [(i, (i + step) % count) for i in range(coun...]
  transfers between devices with their start and end apart: 23 -> 23, of which waited for: 12 -> 14; matrix products, arithmetic and copies ran while one was open for 1% -> 1% of each run, Pallas kernels for 8% -> 9%
where the time goes in v11:
time: 77.8 us; the launch traced here: 76.4 us
  waiting for transfers between devices  40.8 us (52%)
  starting transfers between devices  23.7 us (30%)
  Pallas kernels  11 us (14%)
    ppermute x6, waiting for transfers between devices, shifted(): lax.ppermute(value, 'space', [(i, (i + step) % count) for i in range(coun...  22.3 us
    ppermute x10, waiting for transfers between devices, flipped(): lax.ppermute(value, 'tm', [(t, t ^ bit_on_core[t % 2]) for t in range(8)])  11.5 us
    pallas_call x7, Pallas kernels, kernel_call(): pl.pallas_call(body, out_shape=outputs, in_specs=in_specs, out_specs=jax....  11 us
    ppermute x6, starting transfers between devices, shifted(): lax.ppermute(value, 'space', [(i, (i + step) % count) for i in range(coun...  9.05 us
    ppermute x10, starting transfers between devices, flipped(): lax.ppermute(value, 'tm', [(t, t ^ bit_on_core[t % 2]) for t in range(8)])  7.06 us
    ppermute x3, starting transfers between devices, plane_form(): upto = upto + lax.ppermute(total, 'tm', pairs).astype(jnp.float32)  6.48 us
    ppermute x1, waiting for transfers between devices, plane_form(): lax.ppermute(share, 'space', [(i, count - 1 - i) for i in range(count)])  5.94 us
  transfers between devices with their start and end apart: 23, of which 14 were waited for; matrix products, arithmetic and copies ran while one was open for 1% of the time, Pallas kernels for 9%

profile of v11, /device:TPU:0, one launch (start us, length us, event | category | flops | bytes accessed | tf_op | source)
XLA Modules:
  0.0 76.4 jit_solution(9270731095452481365)
XLA Ops:
  0.0 1.9 %shard_map.55 = (bf16[80,1152]{1,0:T(8,128)(2,1)}, bf16[2,64,1152]{2,1,0:T(8,128)(2,1)}) custom-call(bf16[288,3456]{1,0:T(8,128)(2,1)} %refs_1_.1, bf16[288,1152]{1,0:T(8,128)(2,1)} %refs_2_.3), custom_call_target="tpu_custom_call" | custom-call | bytes 958464 | tf_op jit(solution)/shard_map/pallas_call | solution.py:164
  2.0 3.1 %collective-permute-start = (bf16[1,80,1152]{2,1,0:T(8,128)(2,1)}, bf16[1,80,1152]{2,1,0:T(8,128)(2,1)S(1)}, u32[]{:S(2)}, u32[]{:S(2)}) collective-permute-start(bf16[1,80,1152]{2,1,0:T(8,128)(2,1)} %bitcast.8), channel_id=1, source_target_pairs={{0,1},{1,2},{2,3},{3,0},{4,5},{5,6},{6,7},{7,4},{8,9},{9,10},{10,1... | collective-permute-start | bytes 552968 | tf_op jit(solution)/shard_map/ppermute | solution.py:104
  5.0 2.1 %collective-permute-start.1 = (bf16[1,80,1152]{2,1,0:T(8,128)(2,1)}, bf16[1,80,1152]{2,1,0:T(8,128)(2,1)S(1)}, u32[]{:S(2)}, u32[]{:S(2)}) collective-permute-start(bf16[1,80,1152]{2,1,0:T(8,128)(2,1)} %bitcast.9), channel_id=1, source_target_pairs={{0,3},{1,0},{2,1},{3,2},{4,7},{5,4},{6,5},{7,6},{8,11},{9,8},{10,9... | collective-permute-start | bytes 552968 | tf_op jit(solution)/shard_map/ppermute | solution.py:104
  7.1 0.0 copy-done.3
  7.1 1.2 %shard_map.56.refs_0_ = bf16[256,1152]{1,0:T(8,128)(2,1)S(1)} custom-call(bf16[256,1152]{1,0:T(8,128)(2,1)S(1)} %bitcast.7), custom_call_target="tpu_custom_call" | custom-call | flops 679477248 | bytes 589824 | tf_op jit(solution)/shard_map/pallas_call | solution.py:164
  8.3 0.0 copy-start
  8.3 0.1 collective-permute-start.10
  8.4 4.4 %collective-permute-done = bf16[1,80,1152]{2,1,0:T(8,128)(2,1)S(1)} collective-permute-done((bf16[1,80,1152]{2,1,0:T(8,128)(2,1)}, bf16[1,80,1152]{2,1,0:T(8,128)(2,1)S(1)}, u32[]{:S(2)}, u32[]{:S(2)}) %collective-permute-start) | collective-permute-done | bytes 184352 | tf_op jit(solution)/shard_map/ppermute | solution.py:104
  12.8 2.5 %collective-permute-done.1 = bf16[1,80,1152]{2,1,0:T(8,128)(2,1)S(1)} collective-permute-done((bf16[1,80,1152]{2,1,0:T(8,128)(2,1)}, bf16[1,80,1152]{2,1,0:T(8,128)(2,1)S(1)}, u32[]{:S(2)}, u32[]{:S(2)}) %collective-permute-start.1) | collective-permute-done | bytes 184352 | tf_op jit(solution)/shard_map/ppermute | solution.py:104
  15.3 1.6 %collective-permute-start.11 = (bf16[2,80,1152]{2,1,0:T(8,128)(2,1)S(1)}, bf16[2,80,1152]{2,1,0:T(8,128)(2,1)S(1)}, u32[]{:S(2)}, u32[]{:S(2)}) collective-permute-start(bf16[2,80,1152]{2,1,0:T(8,128)(2,1)S(1)} %constant_dynamic-update-slice_fusion.5), channel_id=1, source_target_pairs={{0,8},{4,20},{8,0},{12,28},{16,24},{20,4},{24,16},{28,12},{1,9},{5... | collective-permute-start | bytes 1105928 | tf_op jit(solution)/shard_map/ppermute | solution.py:108
  16.9 1.1 %collective-permute-start.3 = (bf16[1,80,1152]{2,1,0:T(8,128)(2,1)S(1)}, bf16[1,80,1152]{2,1,0:T(8,128)(2,1)S(1)}, u32[]{:S(2)}, u32[]{:S(2)}) collective-permute-start(bf16[1,80,1152]{2,1,0:T(8,128)(2,1)S(1)} %collective-permute-done), channel_id=1, source_target_pairs={{0,1},{1,2},{2,3},{3,0},{4,5},{5,6},{6,7},{7,4},{8,9},{9,10},{10,1... | collective-permute-start | bytes 552968 | tf_op jit(solution)/shard_map/ppermute | solution.py:104
  18.0 0.0 copy-done.5
  18.0 0.7 collective-permute-start.2
  18.8 7.5 %collective-permute-done.3 = bf16[1,80,1152]{2,1,0:T(8,128)(2,1)S(1)} collective-permute-done((bf16[1,80,1152]{2,1,0:T(8,128)(2,1)S(1)}, bf16[1,80,1152]{2,1,0:T(8,128)(2,1)S(1)}, u32[]{:S(2)}, u32[]{:S(2)}) %collective-permute-start.3) | collective-permute-done | bytes 184352 | tf_op jit(solution)/shard_map/ppermute | solution.py:104
  26.3 0.4 collective-permute-start.4
  26.7 0.0 collective-permute-done.11
  26.7 0.0 collective-permute-done.10.refs_1_
  26.8 1.7 %collective-permute-start.12 = (bf16[4,80,1152]{2,1,0:T(8,128)(2,1)S(1)}, bf16[4,80,1152]{2,1,0:T(8,128)(2,1)S(1)}, u32[]{:S(2)}, u32[]{:S(2)}) collective-permute-start(bf16[4,80,1152]{2,1,0:T(8,128)(2,1)S(1)} %constant_dynamic-update-slice_fusion.7.refs_3_), channel_id=1, source_target_pairs={{0,16},{4,12},{8,24},{12,4},{16,0},{20,28},{24,8},{28,20},{1,17},{... | collective-permute-start | bytes 2211848 | tf_op jit(solution)/shard_map/ppermute | solution.py:108
  28.5 5.3 %collective-permute-done.4 = bf16[1,80,1152]{2,1,0:T(8,128)(2,1)S(1)} collective-permute-done((bf16[1,80,1152]{2,1,0:T(8,128)(2,1)S(1)}, bf16[1,80,1152]{2,1,0:T(8,128)(2,1)S(1)}, u32[]{:S(2)}, u32[]{:S(2)}) %collective-permute-start.4) | collective-permute-done | bytes 184352 | tf_op jit(solution)/shard_map/ppermute | solution.py:108
  33.9 1.6 %collective-permute-start.13 = (bf16[2,80,1152]{2,1,0:T(8,128)(2,1)S(1)}, bf16[2,80,1152]{2,1,0:T(8,128)(2,1)S(1)}, u32[]{:S(2)}, u32[]{:S(2)}) collective-permute-start(bf16[2,80,1152]{2,1,0:T(8,128)(2,1)S(1)} %constant_dynamic-update-slice_fusion.refs_5_), channel_id=1, source_target_pairs={{0,16},{4,12},{8,24},{12,4},{16,0},{20,28},{24,8},{28,20},{1,17},{... | collective-permute-start | bytes 1105928 | tf_op jit(solution)/shard_map/ppermute | solution.py:108
  35.4 0.1 collective-permute-start.6
  35.6 0.0 collective-permute-done.2
  35.6 1.9 %collective-permute-start.5 = (bf16[2,64,1152]{2,1,0:T(8,128)(2,1)S(1)}, bf16[2,64,1152]{2,1,0:T(8,128)(2,1)S(1)}, u32[]{:S(2)}, u32[]{:S(2)}) collective-permute-start(bf16[2,64,1152]{2,1,0:T(8,128)(2,1)S(1)} %collective-permute-done.2), channel_id=1, source_target_pairs={{0,1},{1,2},{2,3},{3,0},{4,5},{5,6},{6,7},{7,4},{8,9},{9,10},{10,1... | collective-permute-start | bytes 884744 | tf_op jit(solution)/shard_map/ppermute | solution.py:104
  37.5 7.9 %collective-permute-done.6 = bf16[2,64,1152]{2,1,0:T(8,128)(2,1)S(1)} collective-permute-done((bf16[2,64,1152]{2,1,0:T(8,128)(2,1)S(1)}, bf16[2,64,1152]{2,1,0:T(8,128)(2,1)S(1)}, u32[]{:S(2)}, u32[]{:S(2)}) %collective-permute-start.6) | collective-permute-done | bytes 294944 | tf_op jit(solution)/shard_map/ppermute | solution.py:104
  45.3 0.0 collective-permute-done.13.refs_6_
  45.3 0.0 collective-permute-done.12.refs_4_
  45.3 0.0 copy-done
  45.3 2.1 %shard_map.57.mine_ref.refs_7_ = bf16[608,1152]{1,0:T(8,128)(2,1)S(1)} custom-call(bf16[256,1152]{1,0:T(8,128)(2,1)S(1)} %shard_map.56.refs_0_, bf16[256,1152]{1,0:T(8,128)(2,1)S(1)} %collective-permute-done.10.refs_1_, bf16[288,3456]{1,0:T(8,128)(2,1)S(1)} %copy-done, bf16[4,80,1152]{2,1,0:T(8,128)(2,1)S(1)} %constant_dynamic-update-slice_fusion.7.refs_3_, ...), custom_call_target="tpu_custom_call" | custom-call | flops 1358954496 | bytes 2654208 | tf_op jit(solution)/shard_map/pallas_call | solution.py:164
  47.5 0.0 collective-permute-done.5
  47.5 0.1 collective-permute-start.14
  47.7 0.6 collective-permute-start.7
  48.3 0.1 pad_maximum_fusion
  48.4 0.6 collective-permute-start.8
  49.0 0.4 collective-permute-start.9
  49.4 1.3 %collective-permute-done.14.other_ref.refs_8_ = bf16[608,1152]{1,0:T(8,128)(2,1)S(1)} collective-permute-done((bf16[608,1152]{1,0:T(8,128)(2,1)S(1)}, bf16[608,1152]{1,0:T(8,128)(2,1)S(1)}, u32[]{:S(2)}, u32[]{:S(2)}) %collective-permute-start.14) | collective-permute-done | bytes 1400864 | tf_op jit(solution)/shard_map/ppermute | solution.py:108
  50.7 0.8 %shard_map.58 = (bf16[256,1152]{1,0:T(8,128)(2,1)S(1)}, bf16[1,64,1152]{2,1,0:T(8,128)(2,1)S(1)}, bf16[1,64,1152]{2,1,0:T(8,128)(2,1)S(1)}, f32[9,32,128]{2,1,0:T(8,128)S(1)}, bf16[9,32,128]{2,1,0:T(8,128)(2,1)S(1)}) custom-call(bf16[608,1152]{1,0:T(8,128)(2,1)S(1)} %shard_map.57.mine_ref.refs_7_, bf16[608,1152]{1,0:T(8,128)(2,1)S(1)} %collective-permute-done.14.other_ref.refs_8_), custom_call_target="tpu_custom_call" | custom-call | flops 150994944 | bytes 2359296 | tf_op jit(solution)/shard_map/pallas_call | solution.py:164
  51.6 0.0 copy-start.2
  51.6 0.4 collective-permute-done.7.refs_4_
  52.0 2.4 %collective-permute-start.15 = (bf16[9,32,128]{2,1,0:T(8,128)(2,1)S(1)}, bf16[9,32,128]{2,1,0:T(8,128)(2,1)S(1)}, u32[]{:S(2)}, u32[]{:S(2)}) collective-permute-start(bf16[9,32,128]{2,1,0:T(8,128)(2,1)S(1)} %get-tuple-element.43), channel_id=1, source_target_pairs={{0,8},{4,12},{16,24},{20,28},{1,9},{5,13},{17,25},{21,29},{2,10},{... | collective-permute-start | bytes 221192 | tf_op jit(solution)/shard_map/ppermute | solution.py:551
  54.4 2.7 %collective-permute-start.16 = (bf16[9,32,128]{2,1,0:T(8,128)(2,1)S(1)}, bf16[9,32,128]{2,1,0:T(8,128)(2,1)S(1)}, u32[]{:S(2)}, u32[]{:S(2)}) collective-permute-start(bf16[9,32,128]{2,1,0:T(8,128)(2,1)S(1)} %get-tuple-element.43), channel_id=1, source_target_pairs={{0,16},{4,20},{8,24},{12,28},{1,17},{5,21},{9,25},{13,29},{2,18},{... | collective-permute-start | bytes 221192 | tf_op jit(solution)/shard_map/ppermute | solution.py:551
  57.2 1.3 %collective-permute-start.17 = (bf16[9,32,128]{2,1,0:T(8,128)(2,1)S(1)}, bf16[9,32,128]{2,1,0:T(8,128)(2,1)S(1)}, u32[]{:S(2)}, u32[]{:S(2)}) collective-permute-start(bf16[9,32,128]{2,1,0:T(8,128)(2,1)S(1)} %get-tuple-element.43), channel_id=1, source_target_pairs={{0,24},{4,28},{8,16},{12,20},{1,25},{5,29},{9,17},{13,21},{2,26},{... | collective-permute-start | bytes 221192 | tf_op jit(solution)/shard_map/ppermute | solution.py:551
  58.5 2.9 %collective-permute-done.8 = bf16[3,64,1152]{2,1,0:T(8,128)(2,1)S(1)} collective-permute-done((bf16[3,64,1152]{2,1,0:T(8,128)(2,1)S(1)}, bf16[3,64,1152]{2,1,0:T(8,128)(2,1)S(1)}, u32[]{:S(2)}, u32[]{:S(2)}) %collective-permute-start.8) | collective-permute-done | bytes 442400 | tf_op jit(solution)/shard_map/ppermute | solution.py:108
  61.4 0.0 collective-permute-done.9
  61.5 0.0 copy-start.1
  61.5 0.0 collective-permute-done.15
  61.5 0.2 collective-permute-done.16
  61.7 0.1 collective-permute-done.17
  61.9 0.1 collective-permute-start.18
  62.0 0.1 collective-permute-start.19
  62.1 0.0 copy-done.2
  62.1 0.9 %shard_map.60 = f32[4,64,1152]{2,1,0:T(8,128)S(1)} custom-call(bf16[4,64,1152]{2,1,0:T(8,128)(2,1)S(1)} %bitcast.6, f32[3,3,1152]{2,1,0:T(4,128)S(1)} %copy-done.2), custom_call_target="tpu_custom_call" | custom-call | flops 5308416 | bytes 1769472 | tf_op jit(solution)/shard_map/pallas_call | solution.py:164
  63.0 0.0 copy-start.4
  63.0 1.4 %collective-permute-done.18.refs_6_ = bf16[6,64,1152]{2,1,0:T(8,128)(2,1)S(1)} collective-permute-done((bf16[6,64,1152]{2,1,0:T(8,128)(2,1)S(1)}, bf16[6,64,1152]{2,1,0:T(8,128)(2,1)S(1)}, u32[]{:S(2)}, u32[]{:S(2)}) %collective-permute-start.18) | collective-permute-done | bytes 884768 | tf_op jit(solution)/shard_map/ppermute | solution.py:108
  64.4 0.0 copy-done.1
  64.4 1.5 %shard_map.59 = (bf16[256,1152]{1,0:T(8,128)(2,1)S(1)}, bf16[1152,1152]{1,0:T(8,128)(2,1)S(1)}) custom-call(bf16[256,1152]{1,0:T(8,128)(2,1)S(1)} %shard_map.56.refs_0_, bf16[288,3456]{1,0:T(8,128)(2,1)S(1)} %copy-done, bf16[288,1152]{1,0:T(8,128)(2,1)S(1)} %copy-done.1, bf16[6,64,1152]{2,1,0:T(8,128)(2,1)S(1)} %constant_dynamic-update-slice_fusion.2.refs_3_, ...), custom_call_target="tpu_custom_call" | custom-call | flops 679477248 | bytes 5308416 | tf_op jit(solution)/shard_map/pallas_call | solution.py:164
  65.9 0.7 collective-permute-done.19
  66.7 0.1 collective-permute-start.20
  66.8 0.0 copy-done.4
  66.8 0.3 collective-permute-start.21
  67.1 0.7 collective-permute-start.22
  67.8 5.9 %collective-permute-done.20 = bf16[9,32,128]{2,1,0:T(8,128)(2,1)S(1)} collective-permute-done((bf16[9,32,128]{2,1,0:T(8,128)(2,1)S(1)}, bf16[9,32,128]{2,1,0:T(8,128)(2,1)S(1)}, u32[]{:S(2)}, u32[]{:S(2)}) %collective-permute-start.20) | collective-permute-done | bytes 73760 | tf_op jit(solution)/shard_map/ppermute | solution.py:573
  73.8 0.1 collective-permute-done.21.refs_4_
  73.9 0.0 collective-permute-done.22.refs_5_
  73.9 2.5 %shard_map.61 = bf16[256,1152]{1,0:T(8,128)(2,1)} custom-call(bf16[256,1152]{1,0:T(8,128)(2,1)S(1)} %get-tuple-element.48.refs_0_, bf16[1152,1152]{1,0:T(8,128)(2,1)S(1)} %get-tuple-element.49.refs_1_, f32[9,32,128]{2,1,0:T(8,128)S(1)} %convert_add_fusion.refs_2_, f32[256,1152]{1,0:T(8,128)S(1)} %bitcast.5, ...), custom_call_target="tpu_custom_call" | custom-call | flops 679477248 | bytes 2654208 | tf_op jit(solution)/shard_map/pallas_call | solution.py:164
  (20 shorter events, 0.4 us)
Async XLA Ops:
  0.0 7.1 %copy-start.3 = (bf16[1,4,64,1152]{3,2,1,0:T(8,128)(2,1)S(1)}, bf16[1,4,64,1152]{3,2,1,0:T(8,128)(2,1)}, u32[]{:S(2)}) copy-start(bf16[1,4,64,1152]{3,2,1,0:T(8,128)(2,1)} %param.5) | copy-start | bytes 1769476
  2.0 10.8 %collective-permute-start = (bf16[1,80,1152]{2,1,0:T(8,128)(2,1)}, bf16[1,80,1152]{2,1,0:T(8,128)(2,1)S(1)}, u32[]{:S(2)}, u32[]{:S(2)}) collective-permute-start(bf16[1,80,1152]{2,1,0:T(8,128)(2,1)} %bitcast.8), channel_id=1, source_target_pairs={{0,1},{1,2},{2,3},{3,0},{4,5},{5,6},{6,7},{7,4},{8,9},{9,10},{10,1... | collective-permute-start | bytes 552968 | tf_op jit(solution)/shard_map/ppermute | solution.py:104
  5.0 10.3 %collective-permute-start.1 = (bf16[1,80,1152]{2,1,0:T(8,128)(2,1)}, bf16[1,80,1152]{2,1,0:T(8,128)(2,1)S(1)}, u32[]{:S(2)}, u32[]{:S(2)}) collective-permute-start(bf16[1,80,1152]{2,1,0:T(8,128)(2,1)} %bitcast.9), channel_id=1, source_target_pairs={{0,3},{1,0},{2,1},{3,2},{4,7},{5,4},{6,5},{7,6},{8,11},{9,8},{10,9... | collective-permute-start | bytes 552968 | tf_op jit(solution)/shard_map/ppermute | solution.py:104
  7.1 10.9 %copy-start.5 = (bf16[2,64,1152]{2,1,0:T(8,128)(2,1)S(1)}, bf16[2,64,1152]{2,1,0:T(8,128)(2,1)}, u32[]{:S(2)}) copy-start(bf16[2,64,1152]{2,1,0:T(8,128)(2,1)} %get-tuple-element.36) | copy-start | bytes 884740
  8.3 37.0 %copy-start = (bf16[288,3456]{1,0:T(8,128)(2,1)S(1)}, bf16[288,3456]{1,0:T(8,128)(2,1)}, u32[]{:S(2)}) copy-start(bf16[288,3456]{1,0:T(8,128)(2,1)} %refs_1_.1) | copy-start | bytes 5971972
  8.3 18.4 %collective-permute-start.10 = (bf16[256,1152]{1,0:T(8,128)(2,1)S(1)}, bf16[256,1152]{1,0:T(8,128)(2,1)S(1)}, u32[]{:S(2)}, u32[]{:S(2)}) collective-permute-start(bf16[256,1152]{1,0:T(8,128)(2,1)S(1)} %shard_map.56.refs_0_), channel_id=1, source_target_pairs={{0,4},{4,0},{8,12},{12,8},{16,20},{20,16},{24,28},{28,24},{1,5},{5... | collective-permute-start | bytes 1769480 | tf_op jit(solution)/shard_map/ppermute | solution.py:108
  15.3 11.4 %collective-permute-start.11 = (bf16[2,80,1152]{2,1,0:T(8,128)(2,1)S(1)}, bf16[2,80,1152]{2,1,0:T(8,128)(2,1)S(1)}, u32[]{:S(2)}, u32[]{:S(2)}) collective-permute-start(bf16[2,80,1152]{2,1,0:T(8,128)(2,1)S(1)} %constant_dynamic-update-slice_fusion.5), channel_id=1, source_target_pairs={{0,8},{4,20},{8,0},{12,28},{16,24},{20,4},{24,16},{28,12},{1,9},{5... | collective-permute-start | bytes 1105928 | tf_op jit(solution)/shard_map/ppermute | solution.py:108
  16.9 9.4 %collective-permute-start.3 = (bf16[1,80,1152]{2,1,0:T(8,128)(2,1)S(1)}, bf16[1,80,1152]{2,1,0:T(8,128)(2,1)S(1)}, u32[]{:S(2)}, u32[]{:S(2)}) collective-permute-start(bf16[1,80,1152]{2,1,0:T(8,128)(2,1)S(1)} %collective-permute-done), channel_id=1, source_target_pairs={{0,1},{1,2},{2,3},{3,0},{4,5},{5,6},{6,7},{7,4},{8,9},{9,10},{10,1... | collective-permute-start | bytes 552968 | tf_op jit(solution)/shard_map/ppermute | solution.py:104
  18.0 17.6 %collective-permute-start.2 = (bf16[2,64,1152]{2,1,0:T(8,128)(2,1)S(1)}, bf16[2,64,1152]{2,1,0:T(8,128)(2,1)S(1)}, u32[]{:S(2)}, u32[]{:S(2)}) collective-permute-start(bf16[2,64,1152]{2,1,0:T(8,128)(2,1)S(1)} %copy-done.5), channel_id=1, source_target_pairs={{0,1},{1,2},{2,3},{3,0},{4,5},{5,6},{6,7},{7,4},{8,9},{9,10},{10,1... | collective-permute-start | bytes 884744 | tf_op jit(solution)/shard_map/ppermute | solution.py:104
  26.3 7.6 %collective-permute-start.4 = (bf16[1,80,1152]{2,1,0:T(8,128)(2,1)S(1)}, bf16[1,80,1152]{2,1,0:T(8,128)(2,1)S(1)}, u32[]{:S(2)}, u32[]{:S(2)}) collective-permute-start(bf16[1,80,1152]{2,1,0:T(8,128)(2,1)S(1)} %collective-permute-done.3), channel_id=1, source_target_pairs={{0,8},{4,20},{8,0},{12,28},{16,24},{20,4},{24,16},{28,12},{1,9},{5... | collective-permute-start | bytes 552968 | tf_op jit(solution)/shard_map/ppermute | solution.py:108
  26.8 18.5 %collective-permute-start.12 = (bf16[4,80,1152]{2,1,0:T(8,128)(2,1)S(1)}, bf16[4,80,1152]{2,1,0:T(8,128)(2,1)S(1)}, u32[]{:S(2)}, u32[]{:S(2)}) collective-permute-start(bf16[4,80,1152]{2,1,0:T(8,128)(2,1)S(1)} %constant_dynamic-update-slice_fusion.7.refs_3_), channel_id=1, source_target_pairs={{0,16},{4,12},{8,24},{12,4},{16,0},{20,28},{24,8},{28,20},{1,17},{... | collective-permute-start | bytes 2211848 | tf_op jit(solution)/shard_map/ppermute | solution.py:108
  33.9 11.5 %collective-permute-start.13 = (bf16[2,80,1152]{2,1,0:T(8,128)(2,1)S(1)}, bf16[2,80,1152]{2,1,0:T(8,128)(2,1)S(1)}, u32[]{:S(2)}, u32[]{:S(2)}) collective-permute-start(bf16[2,80,1152]{2,1,0:T(8,128)(2,1)S(1)} %constant_dynamic-update-slice_fusion.refs_5_), channel_id=1, source_target_pairs={{0,16},{4,12},{8,24},{12,4},{16,0},{20,28},{24,8},{28,20},{1,17},{... | collective-permute-start | bytes 1105928 | tf_op jit(solution)/shard_map/ppermute | solution.py:108
  35.4 9.9 %collective-permute-start.6 = (bf16[2,64,1152]{2,1,0:T(8,128)(2,1)S(1)}, bf16[2,64,1152]{2,1,0:T(8,128)(2,1)S(1)}, u32[]{:S(2)}, u32[]{:S(2)}) collective-permute-start(bf16[2,64,1152]{2,1,0:T(8,128)(2,1)S(1)} %copy-done.5), channel_id=1, source_target_pairs={{0,3},{1,0},{2,1},{3,2},{4,7},{5,4},{6,5},{7,6},{8,11},{9,8},{10,9... | collective-permute-start | bytes 884744 | tf_op jit(solution)/shard_map/ppermute | solution.py:104
  35.6 11.9 %collective-permute-start.5 = (bf16[2,64,1152]{2,1,0:T(8,128)(2,1)S(1)}, bf16[2,64,1152]{2,1,0:T(8,128)(2,1)S(1)}, u32[]{:S(2)}, u32[]{:S(2)}) collective-permute-start(bf16[2,64,1152]{2,1,0:T(8,128)(2,1)S(1)} %collective-permute-done.2), channel_id=1, source_target_pairs={{0,1},{1,2},{2,3},{3,0},{4,5},{5,6},{6,7},{7,4},{8,9},{9,10},{10,1... | collective-permute-start | bytes 884744 | tf_op jit(solution)/shard_map/ppermute | solution.py:104
  47.5 3.2 %collective-permute-start.14 = (bf16[608,1152]{1,0:T(8,128)(2,1)S(1)}, bf16[608,1152]{1,0:T(8,128)(2,1)S(1)}, u32[]{:S(2)}, u32[]{:S(2)}) collective-permute-start(bf16[608,1152]{1,0:T(8,128)(2,1)S(1)} %shard_map.57.mine_ref.refs_7_), channel_id=1, source_target_pairs={{0,4},{4,0},{8,12},{12,8},{16,20},{20,16},{24,28},{28,24},{1,5},{5... | collective-permute-start | bytes 4202504 | tf_op jit(solution)/shard_map/ppermute | solution.py:108
  47.7 4.3 %collective-permute-start.7 = (bf16[6,64,1152]{2,1,0:T(8,128)(2,1)S(1)}, bf16[6,64,1152]{2,1,0:T(8,128)(2,1)S(1)}, u32[]{:S(2)}, u32[]{:S(2)}) collective-permute-start(bf16[6,64,1152]{2,1,0:T(8,128)(2,1)S(1)} %constant_dynamic-update-slice_fusion.2.refs_3_), channel_id=1, source_target_pairs={{0,4},{4,0},{8,12},{12,8},{16,20},{20,16},{24,28},{28,24},{1,5},{5... | collective-permute-start | bytes 2654216 | tf_op jit(solution)/shard_map/ppermute | solution.py:108
  48.4 13.1 %collective-permute-start.8 = (bf16[3,64,1152]{2,1,0:T(8,128)(2,1)S(1)}, bf16[3,64,1152]{2,1,0:T(8,128)(2,1)S(1)}, u32[]{:S(2)}, u32[]{:S(2)}) collective-permute-start(bf16[3,64,1152]{2,1,0:T(8,128)(2,1)S(1)} %pad_maximum_fusion), channel_id=1, source_target_pairs={{0,8},{4,20},{8,0},{12,28},{16,24},{20,4},{24,16},{28,12},{1,9},{5... | collective-permute-start | bytes 1327112 | tf_op jit(solution)/shard_map/ppermute | solution.py:108
  49.0 12.5 %collective-permute-start.9 = (bf16[3,64,1152]{2,1,0:T(8,128)(2,1)S(1)}, bf16[3,64,1152]{2,1,0:T(8,128)(2,1)S(1)}, u32[]{:S(2)}, u32[]{:S(2)}) collective-permute-start(bf16[3,64,1152]{2,1,0:T(8,128)(2,1)S(1)} %pad_maximum_fusion), channel_id=1, source_target_pairs={{0,16},{4,12},{8,24},{12,4},{16,0},{20,28},{24,8},{28,20},{1,17},{... | collective-permute-start | bytes 1327112 | tf_op jit(solution)/shard_map/ppermute | solution.py:108
  51.6 10.5 %copy-start.2 = (f32[3,3,1152]{2,1,0:T(4,128)S(1)}, f32[3,3,1152]{2,1,0:T(4,128)}, u32[]{:S(2)}) copy-start(f32[3,3,1152]{2,1,0:T(4,128)} %refs_6_.1) | copy-start | bytes 124420
  52.0 9.6 %collective-permute-start.15 = (bf16[9,32,128]{2,1,0:T(8,128)(2,1)S(1)}, bf16[9,32,128]{2,1,0:T(8,128)(2,1)S(1)}, u32[]{:S(2)}, u32[]{:S(2)}) collective-permute-start(bf16[9,32,128]{2,1,0:T(8,128)(2,1)S(1)} %get-tuple-element.43), channel_id=1, source_target_pairs={{0,8},{4,12},{16,24},{20,28},{1,9},{5,13},{17,25},{21,29},{2,10},{... | collective-permute-start | bytes 221192 | tf_op jit(solution)/shard_map/ppermute | solution.py:551
  54.4 7.3 %collective-permute-start.16 = (bf16[9,32,128]{2,1,0:T(8,128)(2,1)S(1)}, bf16[9,32,128]{2,1,0:T(8,128)(2,1)S(1)}, u32[]{:S(2)}, u32[]{:S(2)}) collective-permute-start(bf16[9,32,128]{2,1,0:T(8,128)(2,1)S(1)} %get-tuple-element.43), channel_id=1, source_target_pairs={{0,16},{4,20},{8,24},{12,28},{1,17},{5,21},{9,25},{13,29},{2,18},{... | collective-permute-start | bytes 221192 | tf_op jit(solution)/shard_map/ppermute | solution.py:551
  57.2 4.7 %collective-permute-start.17 = (bf16[9,32,128]{2,1,0:T(8,128)(2,1)S(1)}, bf16[9,32,128]{2,1,0:T(8,128)(2,1)S(1)}, u32[]{:S(2)}, u32[]{:S(2)}) collective-permute-start(bf16[9,32,128]{2,1,0:T(8,128)(2,1)S(1)} %get-tuple-element.43), channel_id=1, source_target_pairs={{0,24},{4,28},{8,16},{12,20},{1,25},{5,29},{9,17},{13,21},{2,26},{... | collective-permute-start | bytes 221192 | tf_op jit(solution)/shard_map/ppermute | solution.py:551
  61.5 2.9 %copy-start.1 = (bf16[288,1152]{1,0:T(8,128)(2,1)S(1)}, bf16[288,1152]{1,0:T(8,128)(2,1)}, u32[]{:S(2)}) copy-start(bf16[288,1152]{1,0:T(8,128)(2,1)} %refs_2_.3) | copy-start | bytes 1990660
  61.9 2.5 %collective-permute-start.18 = (bf16[6,64,1152]{2,1,0:T(8,128)(2,1)S(1)}, bf16[6,64,1152]{2,1,0:T(8,128)(2,1)S(1)}, u32[]{:S(2)}, u32[]{:S(2)}) collective-permute-start(bf16[6,64,1152]{2,1,0:T(8,128)(2,1)S(1)} %constant_dynamic-update-slice_fusion.9.refs_5_), channel_id=1, source_target_pairs={{0,4},{4,0},{8,12},{12,8},{16,20},{20,16},{24,28},{28,24},{1,5},{5... | collective-permute-start | bytes 2654216 | tf_op jit(solution)/shard_map/ppermute | solution.py:108
  62.0 4.7 %collective-permute-start.19 = (bf16[9,32,128]{2,1,0:T(8,128)(2,1)S(1)}, bf16[9,32,128]{2,1,0:T(8,128)(2,1)S(1)}, u32[]{:S(2)}, u32[]{:S(2)}) collective-permute-start(bf16[9,32,128]{2,1,0:T(8,128)(2,1)S(1)} %convert_add_fusion.1), channel_id=1, source_target_pairs={{0,1},{1,0},{2,3},{3,2},{4,5},{5,4},{6,7},{7,6},{8,9},{9,8},{10,11... | collective-permute-start | bytes 221192 | tf_op jit(solution)/shard_map/ppermute | solution.py:570
  63.0 3.8 %copy-start.4 = (f32[1152]{0:T(1024)S(1)}, f32[1152]{0:T(1024)}, u32[]{:S(2)}) copy-start(f32[1152]{0:T(1024)} %param.9) | copy-start | bytes 13828
  66.7 7.0 %collective-permute-start.20 = (bf16[9,32,128]{2,1,0:T(8,128)(2,1)S(1)}, bf16[9,32,128]{2,1,0:T(8,128)(2,1)S(1)}, u32[]{:S(2)}, u32[]{:S(2)}) collective-permute-start(bf16[9,32,128]{2,1,0:T(8,128)(2,1)S(1)} %add_convert_fusion), channel_id=1, source_target_pairs={{0,3},{1,2},{2,1},{3,0},{4,7},{5,6},{6,5},{7,4},{8,11},{9,10},{10,... | collective-permute-start | bytes 221192 | tf_op jit(solution)/shard_map/ppermute | solution.py:573
  66.8 7.1 %collective-permute-start.21 = (bf16[1,64,1152]{2,1,0:T(8,128)(2,1)S(1)}, bf16[1,64,1152]{2,1,0:T(8,128)(2,1)S(1)}, u32[]{:S(2)}, u32[]{:S(2)}) collective-permute-start(bf16[1,64,1152]{2,1,0:T(8,128)(2,1)S(1)} %get-tuple-element.55), channel_id=1, source_target_pairs={{0,1},{1,0},{2,3},{3,2},{4,5},{5,4},{6,7},{7,6},{8,9},{9,8},{10,11... | collective-permute-start | bytes 442376 | tf_op jit(solution)/shard_map/ppermute | solution.py:575
  67.1 6.7 %collective-permute-start.22 = (bf16[1,64,1152]{2,1,0:T(8,128)(2,1)S(1)}, bf16[1,64,1152]{2,1,0:T(8,128)(2,1)S(1)}, u32[]{:S(2)}, u32[]{:S(2)}) collective-permute-start(bf16[1,64,1152]{2,1,0:T(8,128)(2,1)S(1)} %get-tuple-element.56), channel_id=1, source_target_pairs={{1,2},{2,1},{5,6},{6,5},{9,10},{10,9},{13,14},{14,13},{17,18},{18,... | collective-permute-start | bytes 442376 | tf_op jit(solution)/shard_map/ppermute | solution.py:578

commit v12 on v11

--- a/solution.py
+++ b/solution.py
@@ -460,7 +460,7 @@
 
 
 def finish_kernel(*refs):
-    queries_ref, weight_ref, state_ref, local_ref, near_ref, next_ref, *refs = refs
+    queries_ref, weight_ref, share_ref, arrived_ref, local_ref, near_ref, next_ref, *refs = refs
     conv_ref, gain_ref, result_ref, read_ref, mixture_ref = refs
     count, depth = queries_ref.shape
     columns = near_ref.shape[1]
@@ -469,7 +469,8 @@
     square = jnp.zeros((count, LANES), jnp.float32)
     for group in range(depth // LANES):
         lanes = slice(group * LANES, (group + 1) * LANES)
-        spread = jnp.concatenate([state_ref[group]] * (LANES // HEAD_DIM), axis=0)
+        compact = share_ref[group].astype(jnp.float32) + arrived_ref[group].astype(jnp.float32)
+        spread = jnp.concatenate([compact] * (LANES // HEAD_DIM), axis=0)
         spread = jnp.where(mask, spread, 0.0).astype(jnp.bfloat16)
         read = jnp.dot(queries_ref[:, lanes], spread, preferred_element_type=jnp.float32)
         read_ref[:, lanes] = read
@@ -567,10 +568,10 @@
     share = state.astype(jnp.bfloat16)
     grid = values.reshape(row_count, col_count, depth)
     local_term = local_call(grid, conv_weight).reshape(-1, depth)
-    arrived = lax.ppermute(share, "space", [(i, i ^ 1) for i in range(count)])
+    arrived = lax.ppermute(share, "space", [(i, count - 1 - i) for i in range(count)])
     arrived = after(arrived, local_term, queries, weight)
     share = (share.astype(jnp.float32) + arrived.astype(jnp.float32)).astype(jnp.bfloat16)
-    arrived = lax.ppermute(share, "space", [(i, count - 1 - i) for i in range(count)])
+    arrived = lax.ppermute(share, "space", [(i, i ^ 1) for i in range(count)])
     edge_near, edge_next = after((edge_near, edge_next), share)
     edge_near = lax.ppermute(edge_near, "space", [(i, i ^ 1) for i in range(count)])
     between = [(i, i + 1) for i in range(1, count - 1, 2)]
@@ -578,11 +579,11 @@
     edge_next = lax.ppermute(edge_next, "space", between)
 
 
-    state = share.astype(jnp.float32) + arrived.astype(jnp.float32)
     result = finish_call(
         queries,
         weight,
-        state,
+        share,
+        arrived,
         local_term,
         edge_near,
         edge_next,

time: 77.8 us -> 78.3 us (level); the launches traced: 76.4 us -> 78.1 us
  starting transfers between devices: 23.7 us -> 26.7 us
  waiting for transfers between devices: 40.8 us -> 39.6 us
    ppermute x1, waiting for transfers between devices: 5.94 us -> 2.54 us  [plane_form(): lax.ppermute(share, 'space', [(i, count - 1 - i) for i in range(count)])]
    ppermute x1, starting transfers between devices: 0.07 us -> 3.32 us  [plane_form(): arrived = lax.ppermute(share, 'space', [(i, i ^ 1) for i in range(count)])]
    ppermute x1, waiting for transfers between devices: 0.74 us -> 2.98 us  [plane_form(): arrived = lax.ppermute(share, 'space', [(i, i ^ 1) for i in range(count)])]
  transfers between devices with their start and end apart: 23 -> 23, of which waited for: 14 -> 13; matrix products, arithmetic and copies ran while one was open for 1% -> 1% of each run, Pallas kernels for 9% -> 8%
where the time goes in v12:
time: 78.3 us; the launch traced here: 78.1 us
  waiting for transfers between devices  39.6 us (51%)
  starting transfers between devices  26.7 us (34%)
  Pallas kernels  11 us (14%)
    ppermute x6, waiting for transfers between devices, shifted(): lax.ppermute(value, 'space', [(i, (i + step) % count) for i in range(coun...  22.3 us
    ppermute x10, waiting for transfers between devices, flipped(): lax.ppermute(value, 'tm', [(t, t ^ bit_on_core[t % 2]) for t in range(8)])  11.5 us
    pallas_call x7, Pallas kernels, kernel_call(): pl.pallas_call(body, out_shape=outputs, in_specs=in_specs, out_specs=jax....  11 us
    ppermute x6, starting transfers between devices, shifted(): lax.ppermute(value, 'space', [(i, (i + step) % count) for i in range(coun...  9.05 us
    ppermute x10, starting transfers between devices, flipped(): lax.ppermute(value, 'tm', [(t, t ^ bit_on_core[t % 2]) for t in range(8)])  7.06 us
    ppermute x3, starting transfers between devices, plane_form(): upto = upto + lax.ppermute(total, 'tm', pairs).astype(jnp.float32)  6.48 us
    ppermute x1, starting transfers between devices, plane_form(): arrived = lax.ppermute(share, 'space', [(i, i ^ 1) for i in range(count)])  3.32 us
    ppermute x1, waiting for transfers between devices, plane_form(): arrived = lax.ppermute(share, 'space', [(i, i ^ 1) for i in range(count)])  2.98 us
  transfers between devices with their start and end apart: 23, of which 13 were waited for; matrix products, arithmetic and copies ran while one was open for 1% of the time, Pallas kernels for 8%

profile of v12, /device:TPU:0, one launch (start us, length us, event | category | flops | bytes accessed | tf_op | source)
XLA Modules:
  0.0 78.1 jit_solution(9197174405909289400)
XLA Ops:
  0.0 1.9 %shard_map.55 = (bf16[80,1152]{1,0:T(8,128)(2,1)}, bf16[2,64,1152]{2,1,0:T(8,128)(2,1)}) custom-call(bf16[288,3456]{1,0:T(8,128)(2,1)} %refs_1_.1, bf16[288,1152]{1,0:T(8,128)(2,1)} %refs_2_.3), custom_call_target="tpu_custom_call" | custom-call | bytes 958464 | tf_op jit(solution)/shard_map/pallas_call | solution.py:164
  2.0 3.1 %collective-permute-start = (bf16[1,80,1152]{2,1,0:T(8,128)(2,1)}, bf16[1,80,1152]{2,1,0:T(8,128)(2,1)S(1)}, u32[]{:S(2)}, u32[]{:S(2)}) collective-permute-start(bf16[1,80,1152]{2,1,0:T(8,128)(2,1)} %bitcast.8), channel_id=1, source_target_pairs={{0,1},{1,2},{2,3},{3,0},{4,5},{5,6},{6,7},{7,4},{8,9},{9,10},{10,1... | collective-permute-start | bytes 552968 | tf_op jit(solution)/shard_map/ppermute | solution.py:104
  5.0 2.1 %collective-permute-start.1 = (bf16[1,80,1152]{2,1,0:T(8,128)(2,1)}, bf16[1,80,1152]{2,1,0:T(8,128)(2,1)S(1)}, u32[]{:S(2)}, u32[]{:S(2)}) collective-permute-start(bf16[1,80,1152]{2,1,0:T(8,128)(2,1)} %bitcast.9), channel_id=1, source_target_pairs={{0,3},{1,0},{2,1},{3,2},{4,7},{5,4},{6,5},{7,6},{8,11},{9,8},{10,9... | collective-permute-start | bytes 552968 | tf_op jit(solution)/shard_map/ppermute | solution.py:104
  7.1 0.0 copy-done.3
  7.1 1.2 %shard_map.56.refs_0_ = bf16[256,1152]{1,0:T(8,128)(2,1)S(1)} custom-call(bf16[256,1152]{1,0:T(8,128)(2,1)S(1)} %bitcast.7), custom_call_target="tpu_custom_call" | custom-call | flops 679477248 | bytes 589824 | tf_op jit(solution)/shard_map/pallas_call | solution.py:164
  8.3 0.0 copy-start
  8.3 0.1 collective-permute-start.10
  8.4 4.4 %collective-permute-done = bf16[1,80,1152]{2,1,0:T(8,128)(2,1)S(1)} collective-permute-done((bf16[1,80,1152]{2,1,0:T(8,128)(2,1)}, bf16[1,80,1152]{2,1,0:T(8,128)(2,1)S(1)}, u32[]{:S(2)}, u32[]{:S(2)}) %collective-permute-start) | collective-permute-done | bytes 184352 | tf_op jit(solution)/shard_map/ppermute | solution.py:104
  12.8 2.5 %collective-permute-done.1 = bf16[1,80,1152]{2,1,0:T(8,128)(2,1)S(1)} collective-permute-done((bf16[1,80,1152]{2,1,0:T(8,128)(2,1)}, bf16[1,80,1152]{2,1,0:T(8,128)(2,1)S(1)}, u32[]{:S(2)}, u32[]{:S(2)}) %collective-permute-start.1) | collective-permute-done | bytes 184352 | tf_op jit(solution)/shard_map/ppermute | solution.py:104
  15.3 1.6 %collective-permute-start.11 = (bf16[2,80,1152]{2,1,0:T(8,128)(2,1)S(1)}, bf16[2,80,1152]{2,1,0:T(8,128)(2,1)S(1)}, u32[]{:S(2)}, u32[]{:S(2)}) collective-permute-start(bf16[2,80,1152]{2,1,0:T(8,128)(2,1)S(1)} %constant_dynamic-update-slice_fusion.5), channel_id=1, source_target_pairs={{0,8},{4,20},{8,0},{12,28},{16,24},{20,4},{24,16},{28,12},{1,9},{5... | collective-permute-start | bytes 1105928 | tf_op jit(solution)/shard_map/ppermute | solution.py:108
  16.9 1.1 %collective-permute-start.3 = (bf16[1,80,1152]{2,1,0:T(8,128)(2,1)S(1)}, bf16[1,80,1152]{2,1,0:T(8,128)(2,1)S(1)}, u32[]{:S(2)}, u32[]{:S(2)}) collective-permute-start(bf16[1,80,1152]{2,1,0:T(8,128)(2,1)S(1)} %collective-permute-done), channel_id=1, source_target_pairs={{0,1},{1,2},{2,3},{3,0},{4,5},{5,6},{6,7},{7,4},{8,9},{9,10},{10,1... | collective-permute-start | bytes 552968 | tf_op jit(solution)/shard_map/ppermute | solution.py:104
  18.0 0.0 copy-done.5
  18.0 0.7 collective-permute-start.2
  18.8 7.5 %collective-permute-done.3 = bf16[1,80,1152]{2,1,0:T(8,128)(2,1)S(1)} collective-permute-done((bf16[1,80,1152]{2,1,0:T(8,128)(2,1)S(1)}, bf16[1,80,1152]{2,1,0:T(8,128)(2,1)S(1)}, u32[]{:S(2)}, u32[]{:S(2)}) %collective-permute-start.3) | collective-permute-done | bytes 184352 | tf_op jit(solution)/shard_map/ppermute | solution.py:104
  26.3 0.4 collective-permute-start.4
  26.7 0.0 collective-permute-done.11
  26.7 0.0 collective-permute-done.10.refs_1_
  26.8 1.7 %collective-permute-start.12 = (bf16[4,80,1152]{2,1,0:T(8,128)(2,1)S(1)}, bf16[4,80,1152]{2,1,0:T(8,128)(2,1)S(1)}, u32[]{:S(2)}, u32[]{:S(2)}) collective-permute-start(bf16[4,80,1152]{2,1,0:T(8,128)(2,1)S(1)} %constant_dynamic-update-slice_fusion.7.refs_3_), channel_id=1, source_target_pairs={{0,16},{4,12},{8,24},{12,4},{16,0},{20,28},{24,8},{28,20},{1,17},{... | collective-permute-start | bytes 2211848 | tf_op jit(solution)/shard_map/ppermute | solution.py:108
  28.5 5.3 %collective-permute-done.4 = bf16[1,80,1152]{2,1,0:T(8,128)(2,1)S(1)} collective-permute-done((bf16[1,80,1152]{2,1,0:T(8,128)(2,1)S(1)}, bf16[1,80,1152]{2,1,0:T(8,128)(2,1)S(1)}, u32[]{:S(2)}, u32[]{:S(2)}) %collective-permute-start.4) | collective-permute-done | bytes 184352 | tf_op jit(solution)/shard_map/ppermute | solution.py:108
  33.9 1.6 %collective-permute-start.13 = (bf16[2,80,1152]{2,1,0:T(8,128)(2,1)S(1)}, bf16[2,80,1152]{2,1,0:T(8,128)(2,1)S(1)}, u32[]{:S(2)}, u32[]{:S(2)}) collective-permute-start(bf16[2,80,1152]{2,1,0:T(8,128)(2,1)S(1)} %constant_dynamic-update-slice_fusion.refs_5_), channel_id=1, source_target_pairs={{0,16},{4,12},{8,24},{12,4},{16,0},{20,28},{24,8},{28,20},{1,17},{... | collective-permute-start | bytes 1105928 | tf_op jit(solution)/shard_map/ppermute | solution.py:108
  35.4 0.1 collective-permute-start.6
  35.6 0.0 collective-permute-done.2
  35.6 1.9 %collective-permute-start.5 = (bf16[2,64,1152]{2,1,0:T(8,128)(2,1)S(1)}, bf16[2,64,1152]{2,1,0:T(8,128)(2,1)S(1)}, u32[]{:S(2)}, u32[]{:S(2)}) collective-permute-start(bf16[2,64,1152]{2,1,0:T(8,128)(2,1)S(1)} %collective-permute-done.2), channel_id=1, source_target_pairs={{0,1},{1,2},{2,3},{3,0},{4,5},{5,6},{6,7},{7,4},{8,9},{9,10},{10,1... | collective-permute-start | bytes 884744 | tf_op jit(solution)/shard_map/ppermute | solution.py:104
  37.5 7.9 %collective-permute-done.6 = bf16[2,64,1152]{2,1,0:T(8,128)(2,1)S(1)} collective-permute-done((bf16[2,64,1152]{2,1,0:T(8,128)(2,1)S(1)}, bf16[2,64,1152]{2,1,0:T(8,128)(2,1)S(1)}, u32[]{:S(2)}, u32[]{:S(2)}) %collective-permute-start.6) | collective-permute-done | bytes 294944 | tf_op jit(solution)/shard_map/ppermute | solution.py:104
  45.3 0.0 collective-permute-done.13.refs_6_
  45.3 0.0 collective-permute-done.12.refs_4_
  45.3 0.0 copy-done
  45.3 2.1 %shard_map.57.mine_ref.refs_7_ = bf16[608,1152]{1,0:T(8,128)(2,1)S(1)} custom-call(bf16[256,1152]{1,0:T(8,128)(2,1)S(1)} %shard_map.56.refs_0_, bf16[256,1152]{1,0:T(8,128)(2,1)S(1)} %collective-permute-done.10.refs_1_, bf16[288,3456]{1,0:T(8,128)(2,1)S(1)} %copy-done, bf16[4,80,1152]{2,1,0:T(8,128)(2,1)S(1)} %constant_dynamic-update-slice_fusion.7.refs_3_, ...), custom_call_target="tpu_custom_call" | custom-call | flops 1358954496 | bytes 2654208 | tf_op jit(solution)/shard_map/pallas_call | solution.py:164
  47.5 0.0 collective-permute-done.5
  47.5 0.1 collective-permute-start.14
  47.7 0.6 collective-permute-start.7
  48.3 0.1 pad_maximum_fusion
  48.4 0.6 collective-permute-start.8
  49.0 0.4 collective-permute-start.9
  49.4 1.3 %collective-permute-done.14.other_ref.refs_8_ = bf16[608,1152]{1,0:T(8,128)(2,1)S(1)} collective-permute-done((bf16[608,1152]{1,0:T(8,128)(2,1)S(1)}, bf16[608,1152]{1,0:T(8,128)(2,1)S(1)}, u32[]{:S(2)}, u32[]{:S(2)}) %collective-permute-start.14) | collective-permute-done | bytes 1400864 | tf_op jit(solution)/shard_map/ppermute | solution.py:108
  50.7 0.8 %shard_map.58 = (bf16[256,1152]{1,0:T(8,128)(2,1)S(1)}, bf16[1,64,1152]{2,1,0:T(8,128)(2,1)S(1)}, bf16[1,64,1152]{2,1,0:T(8,128)(2,1)S(1)}, f32[9,32,128]{2,1,0:T(8,128)S(1)}, bf16[9,32,128]{2,1,0:T(8,128)(2,1)S(1)}) custom-call(bf16[608,1152]{1,0:T(8,128)(2,1)S(1)} %shard_map.57.mine_ref.refs_7_, bf16[608,1152]{1,0:T(8,128)(2,1)S(1)} %collective-permute-done.14.other_ref.refs_8_), custom_call_target="tpu_custom_call" | custom-call | flops 150994944 | bytes 2359296 | tf_op jit(solution)/shard_map/pallas_call | solution.py:164
  51.6 0.0 copy-start.2
  51.6 0.4 collective-permute-done.7.refs_4_
  52.0 2.4 %collective-permute-start.15 = (bf16[9,32,128]{2,1,0:T(8,128)(2,1)S(1)}, bf16[9,32,128]{2,1,0:T(8,128)(2,1)S(1)}, u32[]{:S(2)}, u32[]{:S(2)}) collective-permute-start(bf16[9,32,128]{2,1,0:T(8,128)(2,1)S(1)} %get-tuple-element.43), channel_id=1, source_target_pairs={{0,8},{4,12},{16,24},{20,28},{1,9},{5,13},{17,25},{21,29},{2,10},{... | collective-permute-start | bytes 221192 | tf_op jit(solution)/shard_map/ppermute | solution.py:552
  54.4 2.8 %collective-permute-start.16 = (bf16[9,32,128]{2,1,0:T(8,128)(2,1)S(1)}, bf16[9,32,128]{2,1,0:T(8,128)(2,1)S(1)}, u32[]{:S(2)}, u32[]{:S(2)}) collective-permute-start(bf16[9,32,128]{2,1,0:T(8,128)(2,1)S(1)} %get-tuple-element.43), channel_id=1, source_target_pairs={{0,16},{4,20},{8,24},{12,28},{1,17},{5,21},{9,25},{13,29},{2,18},{... | collective-permute-start | bytes 221192 | tf_op jit(solution)/shard_map/ppermute | solution.py:552
  57.2 1.3 %collective-permute-start.17 = (bf16[9,32,128]{2,1,0:T(8,128)(2,1)S(1)}, bf16[9,32,128]{2,1,0:T(8,128)(2,1)S(1)}, u32[]{:S(2)}, u32[]{:S(2)}) collective-permute-start(bf16[9,32,128]{2,1,0:T(8,128)(2,1)S(1)} %get-tuple-element.43), channel_id=1, source_target_pairs={{0,24},{4,28},{8,16},{12,20},{1,25},{5,29},{9,17},{13,21},{2,26},{... | collective-permute-start | bytes 221192 | tf_op jit(solution)/shard_map/ppermute | solution.py:552
  58.5 2.9 %collective-permute-done.8 = bf16[3,64,1152]{2,1,0:T(8,128)(2,1)S(1)} collective-permute-done((bf16[3,64,1152]{2,1,0:T(8,128)(2,1)S(1)}, bf16[3,64,1152]{2,1,0:T(8,128)(2,1)S(1)}, u32[]{:S(2)}, u32[]{:S(2)}) %collective-permute-start.8) | collective-permute-done | bytes 442400 | tf_op jit(solution)/shard_map/ppermute | solution.py:108
  61.4 0.0 collective-permute-done.9
  61.5 0.0 copy-start.1
  61.5 0.0 collective-permute-done.15
  61.5 0.2 collective-permute-done.16
  61.7 0.1 collective-permute-done.17
  61.9 0.1 collective-permute-start.18
  62.0 0.1 collective-permute-start.19
  62.1 0.0 copy-done.2
  62.1 0.9 %shard_map.60 = f32[4,64,1152]{2,1,0:T(8,128)S(1)} custom-call(bf16[4,64,1152]{2,1,0:T(8,128)(2,1)S(1)} %bitcast.6, f32[3,3,1152]{2,1,0:T(4,128)S(1)} %copy-done.2), custom_call_target="tpu_custom_call" | custom-call | flops 5308416 | bytes 1769472 | tf_op jit(solution)/shard_map/pallas_call | solution.py:164
  63.0 0.0 copy-start.4
  63.0 1.4 %collective-permute-done.18.refs_6_ = bf16[6,64,1152]{2,1,0:T(8,128)(2,1)S(1)} collective-permute-done((bf16[6,64,1152]{2,1,0:T(8,128)(2,1)S(1)}, bf16[6,64,1152]{2,1,0:T(8,128)(2,1)S(1)}, u32[]{:S(2)}, u32[]{:S(2)}) %collective-permute-start.18) | collective-permute-done | bytes 884768 | tf_op jit(solution)/shard_map/ppermute | solution.py:108
  64.4 0.0 copy-done.1
  64.4 1.5 %shard_map.59 = (bf16[256,1152]{1,0:T(8,128)(2,1)S(1)}, bf16[1152,1152]{1,0:T(8,128)(2,1)S(1)}) custom-call(bf16[256,1152]{1,0:T(8,128)(2,1)S(1)} %shard_map.56.refs_0_, bf16[288,3456]{1,0:T(8,128)(2,1)S(1)} %copy-done, bf16[288,1152]{1,0:T(8,128)(2,1)S(1)} %copy-done.1, bf16[6,64,1152]{2,1,0:T(8,128)(2,1)S(1)} %constant_dynamic-update-slice_fusion.2.refs_3_, ...), custom_call_target="tpu_custom_call" | custom-call | flops 679477248 | bytes 5308416 | tf_op jit(solution)/shard_map/pallas_call | solution.py:164
  65.9 2.5 %collective-permute-done.19 = bf16[9,32,128]{2,1,0:T(8,128)(2,1)S(1)} collective-permute-done((bf16[9,32,128]{2,1,0:T(8,128)(2,1)S(1)}, bf16[9,32,128]{2,1,0:T(8,128)(2,1)S(1)}, u32[]{:S(2)}, u32[]{:S(2)}) %collective-permute-start.19) | collective-permute-done | bytes 73760 | tf_op jit(solution)/shard_map/ppermute | solution.py:571
  68.5 0.1 collective-permute-start.21
  68.6 0.7 collective-permute-start.22
  69.3 3.3 %collective-permute-start.20 = (bf16[9,32,128]{2,1,0:T(8,128)(2,1)S(1)}, bf16[9,32,128]{2,1,0:T(8,128)(2,1)S(1)}, u32[]{:S(2)}, u32[]{:S(2)}) collective-permute-start(bf16[9,32,128]{2,1,0:T(8,128)(2,1)S(1)} %add_convert_fusion.refs_2_), channel_id=1, source_target_pairs={{0,1},{1,0},{2,3},{3,2},{4,5},{5,4},{6,7},{7,6},{8,9},{9,8},{10,11... | collective-permute-start | bytes 221192 | tf_op jit(solution)/shard_map/ppermute | solution.py:574
  72.6 0.0 copy-done.4
  72.6 3.0 %collective-permute-done.20.refs_3_ = bf16[9,32,128]{2,1,0:T(8,128)(2,1)S(1)} collective-permute-done((bf16[9,32,128]{2,1,0:T(8,128)(2,1)S(1)}, bf16[9,32,128]{2,1,0:T(8,128)(2,1)S(1)}, u32[]{:S(2)}, u32[]{:S(2)}) %collective-permute-start.20) | collective-permute-done | bytes 73760 | tf_op jit(solution)/shard_map/ppermute | solution.py:574
  75.6 0.0 collective-permute-done.21.refs_5_
  75.6 0.0 collective-permute-done.22.refs_6_
  75.6 2.5 %shard_map.61 = bf16[256,1152]{1,0:T(8,128)(2,1)} custom-call(bf16[256,1152]{1,0:T(8,128)(2,1)S(1)} %get-tuple-element.48.refs_0_, bf16[1152,1152]{1,0:T(8,128)(2,1)S(1)} %get-tuple-element.49.refs_1_, bf16[9,32,128]{2,1,0:T(8,128)(2,1)S(1)} %add_convert_fusion.refs_2_, bf16[9,32,128]{2,1,0:T(8,128)(2,1)S(1)} %collective-permute-done.20.refs_3_, ...), custom_call_target="tpu_custom_call" | custom-call | flops 679477248 | bytes 2654208 | tf_op jit(solution)/shard_map/pallas_call | solution.py:164
  (19 shorter events, 0.4 us)
Async XLA Ops:
  0.0 7.1 %copy-start.3 = (bf16[1,4,64,1152]{3,2,1,0:T(8,128)(2,1)S(1)}, bf16[1,4,64,1152]{3,2,1,0:T(8,128)(2,1)}, u32[]{:S(2)}) copy-start(bf16[1,4,64,1152]{3,2,1,0:T(8,128)(2,1)} %param.5) | copy-start | bytes 1769476
  2.0 10.8 %collective-permute-start = (bf16[1,80,1152]{2,1,0:T(8,128)(2,1)}, bf16[1,80,1152]{2,1,0:T(8,128)(2,1)S(1)}, u32[]{:S(2)}, u32[]{:S(2)}) collective-permute-start(bf16[1,80,1152]{2,1,0:T(8,128)(2,1)} %bitcast.8), channel_id=1, source_target_pairs={{0,1},{1,2},{2,3},{3,0},{4,5},{5,6},{6,7},{7,4},{8,9},{9,10},{10,1... | collective-permute-start | bytes 552968 | tf_op jit(solution)/shard_map/ppermute | solution.py:104
  5.0 10.3 %collective-permute-start.1 = (bf16[1,80,1152]{2,1,0:T(8,128)(2,1)}, bf16[1,80,1152]{2,1,0:T(8,128)(2,1)S(1)}, u32[]{:S(2)}, u32[]{:S(2)}) collective-permute-start(bf16[1,80,1152]{2,1,0:T(8,128)(2,1)} %bitcast.9), channel_id=1, source_target_pairs={{0,3},{1,0},{2,1},{3,2},{4,7},{5,4},{6,5},{7,6},{8,11},{9,8},{10,9... | collective-permute-start | bytes 552968 | tf_op jit(solution)/shard_map/ppermute | solution.py:104
  7.1 10.9 %copy-start.5 = (bf16[2,64,1152]{2,1,0:T(8,128)(2,1)S(1)}, bf16[2,64,1152]{2,1,0:T(8,128)(2,1)}, u32[]{:S(2)}) copy-start(bf16[2,64,1152]{2,1,0:T(8,128)(2,1)} %get-tuple-element.36) | copy-start | bytes 884740
  8.3 37.0 %copy-start = (bf16[288,3456]{1,0:T(8,128)(2,1)S(1)}, bf16[288,3456]{1,0:T(8,128)(2,1)}, u32[]{:S(2)}) copy-start(bf16[288,3456]{1,0:T(8,128)(2,1)} %refs_1_.1) | copy-start | bytes 5971972
  8.3 18.4 %collective-permute-start.10 = (bf16[256,1152]{1,0:T(8,128)(2,1)S(1)}, bf16[256,1152]{1,0:T(8,128)(2,1)S(1)}, u32[]{:S(2)}, u32[]{:S(2)}) collective-permute-start(bf16[256,1152]{1,0:T(8,128)(2,1)S(1)} %shard_map.56.refs_0_), channel_id=1, source_target_pairs={{0,4},{4,0},{8,12},{12,8},{16,20},{20,16},{24,28},{28,24},{1,5},{5... | collective-permute-start | bytes 1769480 | tf_op jit(solution)/shard_map/ppermute | solution.py:108
  15.3 11.4 %collective-permute-start.11 = (bf16[2,80,1152]{2,1,0:T(8,128)(2,1)S(1)}, bf16[2,80,1152]{2,1,0:T(8,128)(2,1)S(1)}, u32[]{:S(2)}, u32[]{:S(2)}) collective-permute-start(bf16[2,80,1152]{2,1,0:T(8,128)(2,1)S(1)} %constant_dynamic-update-slice_fusion.5), channel_id=1, source_target_pairs={{0,8},{4,20},{8,0},{12,28},{16,24},{20,4},{24,16},{28,12},{1,9},{5... | collective-permute-start | bytes 1105928 | tf_op jit(solution)/shard_map/ppermute | solution.py:108
  16.9 9.4 %collective-permute-start.3 = (bf16[1,80,1152]{2,1,0:T(8,128)(2,1)S(1)}, bf16[1,80,1152]{2,1,0:T(8,128)(2,1)S(1)}, u32[]{:S(2)}, u32[]{:S(2)}) collective-permute-start(bf16[1,80,1152]{2,1,0:T(8,128)(2,1)S(1)} %collective-permute-done), channel_id=1, source_target_pairs={{0,1},{1,2},{2,3},{3,0},{4,5},{5,6},{6,7},{7,4},{8,9},{9,10},{10,1... | collective-permute-start | bytes 552968 | tf_op jit(solution)/shard_map/ppermute | solution.py:104
  18.0 17.6 %collective-permute-start.2 = (bf16[2,64,1152]{2,1,0:T(8,128)(2,1)S(1)}, bf16[2,64,1152]{2,1,0:T(8,128)(2,1)S(1)}, u32[]{:S(2)}, u32[]{:S(2)}) collective-permute-start(bf16[2,64,1152]{2,1,0:T(8,128)(2,1)S(1)} %copy-done.5), channel_id=1, source_target_pairs={{0,1},{1,2},{2,3},{3,0},{4,5},{5,6},{6,7},{7,4},{8,9},{9,10},{10,1... | collective-permute-start | bytes 884744 | tf_op jit(solution)/shard_map/ppermute | solution.py:104
  26.3 7.6 %collective-permute-start.4 = (bf16[1,80,1152]{2,1,0:T(8,128)(2,1)S(1)}, bf16[1,80,1152]{2,1,0:T(8,128)(2,1)S(1)}, u32[]{:S(2)}, u32[]{:S(2)}) collective-permute-start(bf16[1,80,1152]{2,1,0:T(8,128)(2,1)S(1)} %collective-permute-done.3), channel_id=1, source_target_pairs={{0,8},{4,20},{8,0},{12,28},{16,24},{20,4},{24,16},{28,12},{1,9},{5... | collective-permute-start | bytes 552968 | tf_op jit(solution)/shard_map/ppermute | solution.py:108
  26.8 18.5 %collective-permute-start.12 = (bf16[4,80,1152]{2,1,0:T(8,128)(2,1)S(1)}, bf16[4,80,1152]{2,1,0:T(8,128)(2,1)S(1)}, u32[]{:S(2)}, u32[]{:S(2)}) collective-permute-start(bf16[4,80,1152]{2,1,0:T(8,128)(2,1)S(1)} %constant_dynamic-update-slice_fusion.7.refs_3_), channel_id=1, source_target_pairs={{0,16},{4,12},{8,24},{12,4},{16,0},{20,28},{24,8},{28,20},{1,17},{... | collective-permute-start | bytes 2211848 | tf_op jit(solution)/shard_map/ppermute | solution.py:108
  33.9 11.5 %collective-permute-start.13 = (bf16[2,80,1152]{2,1,0:T(8,128)(2,1)S(1)}, bf16[2,80,1152]{2,1,0:T(8,128)(2,1)S(1)}, u32[]{:S(2)}, u32[]{:S(2)}) collective-permute-start(bf16[2,80,1152]{2,1,0:T(8,128)(2,1)S(1)} %constant_dynamic-update-slice_fusion.refs_5_), channel_id=1, source_target_pairs={{0,16},{4,12},{8,24},{12,4},{16,0},{20,28},{24,8},{28,20},{1,17},{... | collective-permute-start | bytes 1105928 | tf_op jit(solution)/shard_map/ppermute | solution.py:108
  35.4 9.9 %collective-permute-start.6 = (bf16[2,64,1152]{2,1,0:T(8,128)(2,1)S(1)}, bf16[2,64,1152]{2,1,0:T(8,128)(2,1)S(1)}, u32[]{:S(2)}, u32[]{:S(2)}) collective-permute-start(bf16[2,64,1152]{2,1,0:T(8,128)(2,1)S(1)} %copy-done.5), channel_id=1, source_target_pairs={{0,3},{1,0},{2,1},{3,2},{4,7},{5,4},{6,5},{7,6},{8,11},{9,8},{10,9... | collective-permute-start | bytes 884744 | tf_op jit(solution)/shard_map/ppermute | solution.py:104
  35.6 11.9 %collective-permute-start.5 = (bf16[2,64,1152]{2,1,0:T(8,128)(2,1)S(1)}, bf16[2,64,1152]{2,1,0:T(8,128)(2,1)S(1)}, u32[]{:S(2)}, u32[]{:S(2)}) collective-permute-start(bf16[2,64,1152]{2,1,0:T(8,128)(2,1)S(1)} %collective-permute-done.2), channel_id=1, source_target_pairs={{0,1},{1,2},{2,3},{3,0},{4,5},{5,6},{6,7},{7,4},{8,9},{9,10},{10,1... | collective-permute-start | bytes 884744 | tf_op jit(solution)/shard_map/ppermute | solution.py:104
  47.5 3.2 %collective-permute-start.14 = (bf16[608,1152]{1,0:T(8,128)(2,1)S(1)}, bf16[608,1152]{1,0:T(8,128)(2,1)S(1)}, u32[]{:S(2)}, u32[]{:S(2)}) collective-permute-start(bf16[608,1152]{1,0:T(8,128)(2,1)S(1)} %shard_map.57.mine_ref.refs_7_), channel_id=1, source_target_pairs={{0,4},{4,0},{8,12},{12,8},{16,20},{20,16},{24,28},{28,24},{1,5},{5... | collective-permute-start | bytes 4202504 | tf_op jit(solution)/shard_map/ppermute | solution.py:108
  47.7 4.3 %collective-permute-start.7 = (bf16[6,64,1152]{2,1,0:T(8,128)(2,1)S(1)}, bf16[6,64,1152]{2,1,0:T(8,128)(2,1)S(1)}, u32[]{:S(2)}, u32[]{:S(2)}) collective-permute-start(bf16[6,64,1152]{2,1,0:T(8,128)(2,1)S(1)} %constant_dynamic-update-slice_fusion.2.refs_3_), channel_id=1, source_target_pairs={{0,4},{4,0},{8,12},{12,8},{16,20},{20,16},{24,28},{28,24},{1,5},{5... | collective-permute-start | bytes 2654216 | tf_op jit(solution)/shard_map/ppermute | solution.py:108
  48.4 13.1 %collective-permute-start.8 = (bf16[3,64,1152]{2,1,0:T(8,128)(2,1)S(1)}, bf16[3,64,1152]{2,1,0:T(8,128)(2,1)S(1)}, u32[]{:S(2)}, u32[]{:S(2)}) collective-permute-start(bf16[3,64,1152]{2,1,0:T(8,128)(2,1)S(1)} %pad_maximum_fusion), channel_id=1, source_target_pairs={{0,8},{4,20},{8,0},{12,28},{16,24},{20,4},{24,16},{28,12},{1,9},{5... | collective-permute-start | bytes 1327112 | tf_op jit(solution)/shard_map/ppermute | solution.py:108
  49.0 12.5 %collective-permute-start.9 = (bf16[3,64,1152]{2,1,0:T(8,128)(2,1)S(1)}, bf16[3,64,1152]{2,1,0:T(8,128)(2,1)S(1)}, u32[]{:S(2)}, u32[]{:S(2)}) collective-permute-start(bf16[3,64,1152]{2,1,0:T(8,128)(2,1)S(1)} %pad_maximum_fusion), channel_id=1, source_target_pairs={{0,16},{4,12},{8,24},{12,4},{16,0},{20,28},{24,8},{28,20},{1,17},{... | collective-permute-start | bytes 1327112 | tf_op jit(solution)/shard_map/ppermute | solution.py:108
  51.6 10.5 %copy-start.2 = (f32[3,3,1152]{2,1,0:T(4,128)S(1)}, f32[3,3,1152]{2,1,0:T(4,128)}, u32[]{:S(2)}) copy-start(f32[3,3,1152]{2,1,0:T(4,128)} %refs_7_.1) | copy-start | bytes 124420
  52.0 9.6 %collective-permute-start.15 = (bf16[9,32,128]{2,1,0:T(8,128)(2,1)S(1)}, bf16[9,32,128]{2,1,0:T(8,128)(2,1)S(1)}, u32[]{:S(2)}, u32[]{:S(2)}) collective-permute-start(bf16[9,32,128]{2,1,0:T(8,128)(2,1)S(1)} %get-tuple-element.43), channel_id=1, source_target_pairs={{0,8},{4,12},{16,24},{20,28},{1,9},{5,13},{17,25},{21,29},{2,10},{... | collective-permute-start | bytes 221192 | tf_op jit(solution)/shard_map/ppermute | solution.py:552
  54.4 7.3 %collective-permute-start.16 = (bf16[9,32,128]{2,1,0:T(8,128)(2,1)S(1)}, bf16[9,32,128]{2,1,0:T(8,128)(2,1)S(1)}, u32[]{:S(2)}, u32[]{:S(2)}) collective-permute-start(bf16[9,32,128]{2,1,0:T(8,128)(2,1)S(1)} %get-tuple-element.43), channel_id=1, source_target_pairs={{0,16},{4,20},{8,24},{12,28},{1,17},{5,21},{9,25},{13,29},{2,18},{... | collective-permute-start | bytes 221192 | tf_op jit(solution)/shard_map/ppermute | solution.py:552
  57.2 4.7 %collective-permute-start.17 = (bf16[9,32,128]{2,1,0:T(8,128)(2,1)S(1)}, bf16[9,32,128]{2,1,0:T(8,128)(2,1)S(1)}, u32[]{:S(2)}, u32[]{:S(2)}) collective-permute-start(bf16[9,32,128]{2,1,0:T(8,128)(2,1)S(1)} %get-tuple-element.43), channel_id=1, source_target_pairs={{0,24},{4,28},{8,16},{12,20},{1,25},{5,29},{9,17},{13,21},{2,26},{... | collective-permute-start | bytes 221192 | tf_op jit(solution)/shard_map/ppermute | solution.py:552
  61.5 2.9 %copy-start.1 = (bf16[288,1152]{1,0:T(8,128)(2,1)S(1)}, bf16[288,1152]{1,0:T(8,128)(2,1)}, u32[]{:S(2)}) copy-start(bf16[288,1152]{1,0:T(8,128)(2,1)} %refs_2_.3) | copy-start | bytes 1990660
  61.9 2.5 %collective-permute-start.18 = (bf16[6,64,1152]{2,1,0:T(8,128)(2,1)S(1)}, bf16[6,64,1152]{2,1,0:T(8,128)(2,1)S(1)}, u32[]{:S(2)}, u32[]{:S(2)}) collective-permute-start(bf16[6,64,1152]{2,1,0:T(8,128)(2,1)S(1)} %constant_dynamic-update-slice_fusion.9.refs_5_), channel_id=1, source_target_pairs={{0,4},{4,0},{8,12},{12,8},{16,20},{20,16},{24,28},{28,24},{1,5},{5... | collective-permute-start | bytes 2654216 | tf_op jit(solution)/shard_map/ppermute | solution.py:108
  62.0 6.5 %collective-permute-start.19 = (bf16[9,32,128]{2,1,0:T(8,128)(2,1)S(1)}, bf16[9,32,128]{2,1,0:T(8,128)(2,1)S(1)}, u32[]{:S(2)}, u32[]{:S(2)}) collective-permute-start(bf16[9,32,128]{2,1,0:T(8,128)(2,1)S(1)} %convert_add_fusion), channel_id=1, source_target_pairs={{0,3},{1,2},{2,1},{3,0},{4,7},{5,6},{6,5},{7,4},{8,11},{9,10},{10,... | collective-permute-start | bytes 221192 | tf_op jit(solution)/shard_map/ppermute | solution.py:571
  63.0 9.6 %copy-start.4 = (f32[1152]{0:T(1024)S(1)}, f32[1152]{0:T(1024)}, u32[]{:S(2)}) copy-start(f32[1152]{0:T(1024)} %param.9) | copy-start | bytes 13828
  68.5 7.1 %collective-permute-start.21 = (bf16[1,64,1152]{2,1,0:T(8,128)(2,1)S(1)}, bf16[1,64,1152]{2,1,0:T(8,128)(2,1)S(1)}, u32[]{:S(2)}, u32[]{:S(2)}) collective-permute-start(bf16[1,64,1152]{2,1,0:T(8,128)(2,1)S(1)} %get-tuple-element.55), channel_id=1, source_target_pairs={{0,1},{1,0},{2,3},{3,2},{4,5},{5,4},{6,7},{7,6},{8,9},{9,8},{10,11... | collective-permute-start | bytes 442376 | tf_op jit(solution)/shard_map/ppermute | solution.py:576
  68.6 7.0 %collective-permute-start.22 = (bf16[1,64,1152]{2,1,0:T(8,128)(2,1)S(1)}, bf16[1,64,1152]{2,1,0:T(8,128)(2,1)S(1)}, u32[]{:S(2)}, u32[]{:S(2)}) collective-permute-start(bf16[1,64,1152]{2,1,0:T(8,128)(2,1)S(1)} %get-tuple-element.56), channel_id=1, source_target_pairs={{1,2},{2,1},{5,6},{6,5},{9,10},{10,9},{13,14},{14,13},{17,18},{18,... | collective-permute-start | bytes 442376 | tf_op jit(solution)/shard_map/ppermute | solution.py:579
  69.3 6.3 %collective-permute-start.20 = (bf16[9,32,128]{2,1,0:T(8,128)(2,1)S(1)}, bf16[9,32,128]{2,1,0:T(8,128)(2,1)S(1)}, u32[]{:S(2)}, u32[]{:S(2)}) collective-permute-start(bf16[9,32,128]{2,1,0:T(8,128)(2,1)S(1)} %add_convert_fusion.refs_2_), channel_id=1, source_target_pairs={{0,1},{1,0},{2,3},{3,2},{4,5},{5,4},{6,7},{7,6},{8,9},{9,8},{10,11... | collective-permute-start | bytes 221192 | tf_op jit(solution)/shard_map/ppermute | solution.py:574

commit v13 on v11

--- a/solution.py
+++ b/solution.py
@@ -567,10 +567,10 @@
     share = state.astype(jnp.bfloat16)
     grid = values.reshape(row_count, col_count, depth)
     local_term = local_call(grid, conv_weight).reshape(-1, depth)
-    arrived = lax.ppermute(share, "space", [(i, i ^ 1) for i in range(count)])
+    arrived = lax.ppermute(share, "space", [(i, count - 1 - i) for i in range(count)])
     arrived = after(arrived, local_term, queries, weight)
     share = (share.astype(jnp.float32) + arrived.astype(jnp.float32)).astype(jnp.bfloat16)
-    arrived = lax.ppermute(share, "space", [(i, count - 1 - i) for i in range(count)])
+    arrived = lax.ppermute(share, "space", [(i, i ^ 1) for i in range(count)])
     edge_near, edge_next = after((edge_near, edge_next), share)
     edge_near = lax.ppermute(edge_near, "space", [(i, i ^ 1) for i in range(count)])
     between = [(i, i + 1) for i in range(1, count - 1, 2)]

time: 77.8 us -> 78.4 us (level); the launches traced: 76.4 us -> 78.1 us
  starting transfers between devices: 23.7 us -> 25.4 us
    ppermute x1, waiting for transfers between devices: 5.94 us -> 2.54 us  [plane_form(): lax.ppermute(share, 'space', [(i, count - 1 - i) for i in range(count)])]
    ppermute x1, waiting for transfers between devices: 0.74 us -> 2.48 us  [plane_form(): arrived = lax.ppermute(share, 'space', [(i, i ^ 1) for i in range(count)])]
    ppermute x1, waiting for transfers between devices: 0.09 us -> 1.79 us  [plane_form(): lax.ppermute(edge_near, 'space', [(i, i ^ 1) for i in range(count)])]
    ppermute x1, starting transfers between devices: 0.33 us -> 2 us  [plane_form(): lax.ppermute(edge_near, 'space', [(i, i ^ 1) for i in range(count)])]
  transfers between devices with their start and end apart: 23 -> 23, of which waited for: 14 -> 14; matrix products, arithmetic and copies ran while one was open for 1% -> 1% of each run, Pallas kernels for 9% -> 8%
where the time goes in v13:
time: 78.4 us; the launch traced here: 78.1 us
  waiting for transfers between devices  40.9 us (52%)
  starting transfers between devices  25.4 us (32%)
  Pallas kernels  11 us (14%)
    ppermute x6, waiting for transfers between devices, shifted(): lax.ppermute(value, 'space', [(i, (i + step) % count) for i in range(coun...  22.3 us
    ppermute x10, waiting for transfers between devices, flipped(): lax.ppermute(value, 'tm', [(t, t ^ bit_on_core[t % 2]) for t in range(8)])  11.5 us
    pallas_call x7, Pallas kernels, kernel_call(): pl.pallas_call(body, out_shape=outputs, in_specs=in_specs, out_specs=jax....  11 us
    ppermute x6, starting transfers between devices, shifted(): lax.ppermute(value, 'space', [(i, (i + step) % count) for i in range(coun...  9.05 us
    ppermute x10, starting transfers between devices, flipped(): lax.ppermute(value, 'tm', [(t, t ^ bit_on_core[t % 2]) for t in range(8)])  7.06 us
    ppermute x3, starting transfers between devices, plane_form(): upto = upto + lax.ppermute(total, 'tm', pairs).astype(jnp.float32)  6.48 us
    ppermute x1, waiting for transfers between devices, plane_form(): lax.ppermute(share, 'space', [(i, count - 1 - i) for i in range(count)])  2.54 us
    ppermute x1, waiting for transfers between devices, plane_form(): arrived = lax.ppermute(share, 'space', [(i, i ^ 1) for i in range(count)])  2.48 us
  transfers between devices with their start and end apart: 23, of which 14 were waited for; matrix products, arithmetic and copies ran while one was open for 1% of the time, Pallas kernels for 8%

profile of v13, /device:TPU:0, one launch (start us, length us, event | category | flops | bytes accessed | tf_op | source)
XLA Modules:
  0.0 78.1 jit_solution(11340322601837116861)
XLA Ops:
  0.0 1.9 %shard_map.55 = (bf16[80,1152]{1,0:T(8,128)(2,1)}, bf16[2,64,1152]{2,1,0:T(8,128)(2,1)}) custom-call(bf16[288,3456]{1,0:T(8,128)(2,1)} %refs_1_.1, bf16[288,1152]{1,0:T(8,128)(2,1)} %refs_2_.3), custom_call_target="tpu_custom_call" | custom-call | bytes 958464 | tf_op jit(solution)/shard_map/pallas_call | solution.py:164
  2.0 3.1 %collective-permute-start = (bf16[1,80,1152]{2,1,0:T(8,128)(2,1)}, bf16[1,80,1152]{2,1,0:T(8,128)(2,1)S(1)}, u32[]{:S(2)}, u32[]{:S(2)}) collective-permute-start(bf16[1,80,1152]{2,1,0:T(8,128)(2,1)} %bitcast.8), channel_id=1, source_target_pairs={{0,1},{1,2},{2,3},{3,0},{4,5},{5,6},{6,7},{7,4},{8,9},{9,10},{10,1... | collective-permute-start | bytes 552968 | tf_op jit(solution)/shard_map/ppermute | solution.py:104
  5.0 2.1 %collective-permute-start.1 = (bf16[1,80,1152]{2,1,0:T(8,128)(2,1)}, bf16[1,80,1152]{2,1,0:T(8,128)(2,1)S(1)}, u32[]{:S(2)}, u32[]{:S(2)}) collective-permute-start(bf16[1,80,1152]{2,1,0:T(8,128)(2,1)} %bitcast.9), channel_id=1, source_target_pairs={{0,3},{1,0},{2,1},{3,2},{4,7},{5,4},{6,5},{7,6},{8,11},{9,8},{10,9... | collective-permute-start | bytes 552968 | tf_op jit(solution)/shard_map/ppermute | solution.py:104
  7.1 0.0 copy-done.3
  7.1 1.2 %shard_map.56.refs_0_ = bf16[256,1152]{1,0:T(8,128)(2,1)S(1)} custom-call(bf16[256,1152]{1,0:T(8,128)(2,1)S(1)} %bitcast.7), custom_call_target="tpu_custom_call" | custom-call | flops 679477248 | bytes 589824 | tf_op jit(solution)/shard_map/pallas_call | solution.py:164
  8.3 0.0 copy-start
  8.3 0.1 collective-permute-start.10
  8.4 4.4 %collective-permute-done = bf16[1,80,1152]{2,1,0:T(8,128)(2,1)S(1)} collective-permute-done((bf16[1,80,1152]{2,1,0:T(8,128)(2,1)}, bf16[1,80,1152]{2,1,0:T(8,128)(2,1)S(1)}, u32[]{:S(2)}, u32[]{:S(2)}) %collective-permute-start) | collective-permute-done | bytes 184352 | tf_op jit(solution)/shard_map/ppermute | solution.py:104
  12.8 2.5 %collective-permute-done.1 = bf16[1,80,1152]{2,1,0:T(8,128)(2,1)S(1)} collective-permute-done((bf16[1,80,1152]{2,1,0:T(8,128)(2,1)}, bf16[1,80,1152]{2,1,0:T(8,128)(2,1)S(1)}, u32[]{:S(2)}, u32[]{:S(2)}) %collective-permute-start.1) | collective-permute-done | bytes 184352 | tf_op jit(solution)/shard_map/ppermute | solution.py:104
  15.3 1.6 %collective-permute-start.11 = (bf16[2,80,1152]{2,1,0:T(8,128)(2,1)S(1)}, bf16[2,80,1152]{2,1,0:T(8,128)(2,1)S(1)}, u32[]{:S(2)}, u32[]{:S(2)}) collective-permute-start(bf16[2,80,1152]{2,1,0:T(8,128)(2,1)S(1)} %constant_dynamic-update-slice_fusion.5), channel_id=1, source_target_pairs={{0,8},{4,20},{8,0},{12,28},{16,24},{20,4},{24,16},{28,12},{1,9},{5... | collective-permute-start | bytes 1105928 | tf_op jit(solution)/shard_map/ppermute | solution.py:108
  16.9 1.1 %collective-permute-start.3 = (bf16[1,80,1152]{2,1,0:T(8,128)(2,1)S(1)}, bf16[1,80,1152]{2,1,0:T(8,128)(2,1)S(1)}, u32[]{:S(2)}, u32[]{:S(2)}) collective-permute-start(bf16[1,80,1152]{2,1,0:T(8,128)(2,1)S(1)} %collective-permute-done), channel_id=1, source_target_pairs={{0,1},{1,2},{2,3},{3,0},{4,5},{5,6},{6,7},{7,4},{8,9},{9,10},{10,1... | collective-permute-start | bytes 552968 | tf_op jit(solution)/shard_map/ppermute | solution.py:104
  18.0 0.0 copy-done.5
  18.0 0.7 collective-permute-start.2
  18.8 7.5 %collective-permute-done.3 = bf16[1,80,1152]{2,1,0:T(8,128)(2,1)S(1)} collective-permute-done((bf16[1,80,1152]{2,1,0:T(8,128)(2,1)S(1)}, bf16[1,80,1152]{2,1,0:T(8,128)(2,1)S(1)}, u32[]{:S(2)}, u32[]{:S(2)}) %collective-permute-start.3) | collective-permute-done | bytes 184352 | tf_op jit(solution)/shard_map/ppermute | solution.py:104
  26.3 0.4 collective-permute-start.4
  26.7 0.0 collective-permute-done.11
  26.7 0.0 collective-permute-done.10.refs_1_
  26.8 1.7 %collective-permute-start.12 = (bf16[4,80,1152]{2,1,0:T(8,128)(2,1)S(1)}, bf16[4,80,1152]{2,1,0:T(8,128)(2,1)S(1)}, u32[]{:S(2)}, u32[]{:S(2)}) collective-permute-start(bf16[4,80,1152]{2,1,0:T(8,128)(2,1)S(1)} %constant_dynamic-update-slice_fusion.7.refs_3_), channel_id=1, source_target_pairs={{0,16},{4,12},{8,24},{12,4},{16,0},{20,28},{24,8},{28,20},{1,17},{... | collective-permute-start | bytes 2211848 | tf_op jit(solution)/shard_map/ppermute | solution.py:108
  28.5 5.3 %collective-permute-done.4 = bf16[1,80,1152]{2,1,0:T(8,128)(2,1)S(1)} collective-permute-done((bf16[1,80,1152]{2,1,0:T(8,128)(2,1)S(1)}, bf16[1,80,1152]{2,1,0:T(8,128)(2,1)S(1)}, u32[]{:S(2)}, u32[]{:S(2)}) %collective-permute-start.4) | collective-permute-done | bytes 184352 | tf_op jit(solution)/shard_map/ppermute | solution.py:108
  33.9 1.6 %collective-permute-start.13 = (bf16[2,80,1152]{2,1,0:T(8,128)(2,1)S(1)}, bf16[2,80,1152]{2,1,0:T(8,128)(2,1)S(1)}, u32[]{:S(2)}, u32[]{:S(2)}) collective-permute-start(bf16[2,80,1152]{2,1,0:T(8,128)(2,1)S(1)} %constant_dynamic-update-slice_fusion.refs_5_), channel_id=1, source_target_pairs={{0,16},{4,12},{8,24},{12,4},{16,0},{20,28},{24,8},{28,20},{1,17},{... | collective-permute-start | bytes 1105928 | tf_op jit(solution)/shard_map/ppermute | solution.py:108
  35.4 0.1 collective-permute-start.6
  35.6 0.0 collective-permute-done.2
  35.6 1.9 %collective-permute-start.5 = (bf16[2,64,1152]{2,1,0:T(8,128)(2,1)S(1)}, bf16[2,64,1152]{2,1,0:T(8,128)(2,1)S(1)}, u32[]{:S(2)}, u32[]{:S(2)}) collective-permute-start(bf16[2,64,1152]{2,1,0:T(8,128)(2,1)S(1)} %collective-permute-done.2), channel_id=1, source_target_pairs={{0,1},{1,2},{2,3},{3,0},{4,5},{5,6},{6,7},{7,4},{8,9},{9,10},{10,1... | collective-permute-start | bytes 884744 | tf_op jit(solution)/shard_map/ppermute | solution.py:104
  37.5 7.9 %collective-permute-done.6 = bf16[2,64,1152]{2,1,0:T(8,128)(2,1)S(1)} collective-permute-done((bf16[2,64,1152]{2,1,0:T(8,128)(2,1)S(1)}, bf16[2,64,1152]{2,1,0:T(8,128)(2,1)S(1)}, u32[]{:S(2)}, u32[]{:S(2)}) %collective-permute-start.6) | collective-permute-done | bytes 294944 | tf_op jit(solution)/shard_map/ppermute | solution.py:104
  45.3 0.0 collective-permute-done.13.refs_6_
  45.3 0.0 collective-permute-done.12.refs_4_
  45.3 0.0 copy-done
  45.3 2.1 %shard_map.57.mine_ref.refs_7_ = bf16[608,1152]{1,0:T(8,128)(2,1)S(1)} custom-call(bf16[256,1152]{1,0:T(8,128)(2,1)S(1)} %shard_map.56.refs_0_, bf16[256,1152]{1,0:T(8,128)(2,1)S(1)} %collective-permute-done.10.refs_1_, bf16[288,3456]{1,0:T(8,128)(2,1)S(1)} %copy-done, bf16[4,80,1152]{2,1,0:T(8,128)(2,1)S(1)} %constant_dynamic-update-slice_fusion.7.refs_3_, ...), custom_call_target="tpu_custom_call" | custom-call | flops 1358954496 | bytes 2654208 | tf_op jit(solution)/shard_map/pallas_call | solution.py:164
  47.5 0.0 collective-permute-done.5
  47.5 0.1 collective-permute-start.14
  47.7 0.6 collective-permute-start.7
  48.3 0.1 pad_maximum_fusion
  48.4 0.6 collective-permute-start.8
  49.0 0.4 collective-permute-start.9
  49.4 1.3 %collective-permute-done.14.other_ref.refs_8_ = bf16[608,1152]{1,0:T(8,128)(2,1)S(1)} collective-permute-done((bf16[608,1152]{1,0:T(8,128)(2,1)S(1)}, bf16[608,1152]{1,0:T(8,128)(2,1)S(1)}, u32[]{:S(2)}, u32[]{:S(2)}) %collective-permute-start.14) | collective-permute-done | bytes 1400864 | tf_op jit(solution)/shard_map/ppermute | solution.py:108
  50.7 0.8 %shard_map.58 = (bf16[256,1152]{1,0:T(8,128)(2,1)S(1)}, bf16[1,64,1152]{2,1,0:T(8,128)(2,1)S(1)}, bf16[1,64,1152]{2,1,0:T(8,128)(2,1)S(1)}, f32[9,32,128]{2,1,0:T(8,128)S(1)}, bf16[9,32,128]{2,1,0:T(8,128)(2,1)S(1)}) custom-call(bf16[608,1152]{1,0:T(8,128)(2,1)S(1)} %shard_map.57.mine_ref.refs_7_, bf16[608,1152]{1,0:T(8,128)(2,1)S(1)} %collective-permute-done.14.other_ref.refs_8_), custom_call_target="tpu_custom_call" | custom-call | flops 150994944 | bytes 2359296 | tf_op jit(solution)/shard_map/pallas_call | solution.py:164
  51.6 0.0 copy-start.2
  51.6 0.4 collective-permute-done.7.refs_4_
  52.0 2.4 %collective-permute-start.15 = (bf16[9,32,128]{2,1,0:T(8,128)(2,1)S(1)}, bf16[9,32,128]{2,1,0:T(8,128)(2,1)S(1)}, u32[]{:S(2)}, u32[]{:S(2)}) collective-permute-start(bf16[9,32,128]{2,1,0:T(8,128)(2,1)S(1)} %get-tuple-element.43), channel_id=1, source_target_pairs={{0,8},{4,12},{16,24},{20,28},{1,9},{5,13},{17,25},{21,29},{2,10},{... | collective-permute-start | bytes 221192 | tf_op jit(solution)/shard_map/ppermute | solution.py:551
  54.4 2.7 %collective-permute-start.16 = (bf16[9,32,128]{2,1,0:T(8,128)(2,1)S(1)}, bf16[9,32,128]{2,1,0:T(8,128)(2,1)S(1)}, u32[]{:S(2)}, u32[]{:S(2)}) collective-permute-start(bf16[9,32,128]{2,1,0:T(8,128)(2,1)S(1)} %get-tuple-element.43), channel_id=1, source_target_pairs={{0,16},{4,20},{8,24},{12,28},{1,17},{5,21},{9,25},{13,29},{2,18},{... | collective-permute-start | bytes 221192 | tf_op jit(solution)/shard_map/ppermute | solution.py:551
  57.2 1.3 %collective-permute-start.17 = (bf16[9,32,128]{2,1,0:T(8,128)(2,1)S(1)}, bf16[9,32,128]{2,1,0:T(8,128)(2,1)S(1)}, u32[]{:S(2)}, u32[]{:S(2)}) collective-permute-start(bf16[9,32,128]{2,1,0:T(8,128)(2,1)S(1)} %get-tuple-element.43), channel_id=1, source_target_pairs={{0,24},{4,28},{8,16},{12,20},{1,25},{5,29},{9,17},{13,21},{2,26},{... | collective-permute-start | bytes 221192 | tf_op jit(solution)/shard_map/ppermute | solution.py:551
  58.5 2.9 %collective-permute-done.8 = bf16[3,64,1152]{2,1,0:T(8,128)(2,1)S(1)} collective-permute-done((bf16[3,64,1152]{2,1,0:T(8,128)(2,1)S(1)}, bf16[3,64,1152]{2,1,0:T(8,128)(2,1)S(1)}, u32[]{:S(2)}, u32[]{:S(2)}) %collective-permute-start.8) | collective-permute-done | bytes 442400 | tf_op jit(solution)/shard_map/ppermute | solution.py:108
  61.4 0.0 collective-permute-done.9
  61.5 0.0 copy-start.1
  61.5 0.0 collective-permute-done.15
  61.5 0.2 collective-permute-done.16
  61.7 0.1 collective-permute-done.17
  61.9 0.1 collective-permute-start.18
  62.0 0.1 collective-permute-start.19
  62.1 0.0 copy-done.2
  62.1 0.9 %shard_map.60 = f32[4,64,1152]{2,1,0:T(8,128)S(1)} custom-call(bf16[4,64,1152]{2,1,0:T(8,128)(2,1)S(1)} %bitcast.6, f32[3,3,1152]{2,1,0:T(4,128)S(1)} %copy-done.2), custom_call_target="tpu_custom_call" | custom-call | flops 5308416 | bytes 1769472 | tf_op jit(solution)/shard_map/pallas_call | solution.py:164
  63.0 0.0 copy-start.4
  63.0 1.4 %collective-permute-done.18.refs_6_ = bf16[6,64,1152]{2,1,0:T(8,128)(2,1)S(1)} collective-permute-done((bf16[6,64,1152]{2,1,0:T(8,128)(2,1)S(1)}, bf16[6,64,1152]{2,1,0:T(8,128)(2,1)S(1)}, u32[]{:S(2)}, u32[]{:S(2)}) %collective-permute-start.18) | collective-permute-done | bytes 884768 | tf_op jit(solution)/shard_map/ppermute | solution.py:108
  64.4 0.0 copy-done.1
  64.4 1.5 %shard_map.59 = (bf16[256,1152]{1,0:T(8,128)(2,1)S(1)}, bf16[1152,1152]{1,0:T(8,128)(2,1)S(1)}) custom-call(bf16[256,1152]{1,0:T(8,128)(2,1)S(1)} %shard_map.56.refs_0_, bf16[288,3456]{1,0:T(8,128)(2,1)S(1)} %copy-done, bf16[288,1152]{1,0:T(8,128)(2,1)S(1)} %copy-done.1, bf16[6,64,1152]{2,1,0:T(8,128)(2,1)S(1)} %constant_dynamic-update-slice_fusion.2.refs_3_, ...), custom_call_target="tpu_custom_call" | custom-call | flops 679477248 | bytes 5308416 | tf_op jit(solution)/shard_map/pallas_call | solution.py:164
  65.9 2.5 %collective-permute-done.19 = bf16[9,32,128]{2,1,0:T(8,128)(2,1)S(1)} collective-permute-done((bf16[9,32,128]{2,1,0:T(8,128)(2,1)S(1)}, bf16[9,32,128]{2,1,0:T(8,128)(2,1)S(1)}, u32[]{:S(2)}, u32[]{:S(2)}) %collective-permute-start.19) | collective-permute-done | bytes 73760 | tf_op jit(solution)/shard_map/ppermute | solution.py:570
  68.5 0.1 collective-permute-start.20
  68.6 0.0 copy-done.4
  68.6 2.0 %collective-permute-start.21 = (bf16[1,64,1152]{2,1,0:T(8,128)(2,1)S(1)}, bf16[1,64,1152]{2,1,0:T(8,128)(2,1)S(1)}, u32[]{:S(2)}, u32[]{:S(2)}) collective-permute-start(bf16[1,64,1152]{2,1,0:T(8,128)(2,1)S(1)} %get-tuple-element.55), channel_id=1, source_target_pairs={{0,1},{1,0},{2,3},{3,2},{4,5},{5,4},{6,7},{7,6},{8,9},{9,8},{10,11... | collective-permute-start | bytes 442376 | tf_op jit(solution)/shard_map/ppermute | solution.py:575
  70.6 0.7 collective-permute-start.22
  71.3 2.5 %collective-permute-done.20 = bf16[9,32,128]{2,1,0:T(8,128)(2,1)S(1)} collective-permute-done((bf16[9,32,128]{2,1,0:T(8,128)(2,1)S(1)}, bf16[9,32,128]{2,1,0:T(8,128)(2,1)S(1)}, u32[]{:S(2)}, u32[]{:S(2)}) %collective-permute-start.20) | collective-permute-done | bytes 73760 | tf_op jit(solution)/shard_map/ppermute | solution.py:573
  73.8 1.8 %collective-permute-done.21.refs_4_ = bf16[1,64,1152]{2,1,0:T(8,128)(2,1)S(1)} collective-permute-done((bf16[1,64,1152]{2,1,0:T(8,128)(2,1)S(1)}, bf16[1,64,1152]{2,1,0:T(8,128)(2,1)S(1)}, u32[]{:S(2)}, u32[]{:S(2)}) %collective-permute-start.21) | collective-permute-done | bytes 147488 | tf_op jit(solution)/shard_map/ppermute | solution.py:575
  75.6 0.0 collective-permute-done.22.refs_5_
  75.6 2.5 %shard_map.61 = bf16[256,1152]{1,0:T(8,128)(2,1)} custom-call(bf16[256,1152]{1,0:T(8,128)(2,1)S(1)} %get-tuple-element.48.refs_0_, bf16[1152,1152]{1,0:T(8,128)(2,1)S(1)} %get-tuple-element.49.refs_1_, f32[9,32,128]{2,1,0:T(8,128)S(1)} %convert_add_fusion.refs_2_, f32[256,1152]{1,0:T(8,128)S(1)} %bitcast.5, ...), custom_call_target="tpu_custom_call" | custom-call | flops 679477248 | bytes 2654208 | tf_op jit(solution)/shard_map/pallas_call | solution.py:164
  (20 shorter events, 0.4 us)
Async XLA Ops:
  0.0 7.1 %copy-start.3 = (bf16[1,4,64,1152]{3,2,1,0:T(8,128)(2,1)S(1)}, bf16[1,4,64,1152]{3,2,1,0:T(8,128)(2,1)}, u32[]{:S(2)}) copy-start(bf16[1,4,64,1152]{3,2,1,0:T(8,128)(2,1)} %param.5) | copy-start | bytes 1769476
  2.0 10.8 %collective-permute-start = (bf16[1,80,1152]{2,1,0:T(8,128)(2,1)}, bf16[1,80,1152]{2,1,0:T(8,128)(2,1)S(1)}, u32[]{:S(2)}, u32[]{:S(2)}) collective-permute-start(bf16[1,80,1152]{2,1,0:T(8,128)(2,1)} %bitcast.8), channel_id=1, source_target_pairs={{0,1},{1,2},{2,3},{3,0},{4,5},{5,6},{6,7},{7,4},{8,9},{9,10},{10,1... | collective-permute-start | bytes 552968 | tf_op jit(solution)/shard_map/ppermute | solution.py:104
  5.0 10.3 %collective-permute-start.1 = (bf16[1,80,1152]{2,1,0:T(8,128)(2,1)}, bf16[1,80,1152]{2,1,0:T(8,128)(2,1)S(1)}, u32[]{:S(2)}, u32[]{:S(2)}) collective-permute-start(bf16[1,80,1152]{2,1,0:T(8,128)(2,1)} %bitcast.9), channel_id=1, source_target_pairs={{0,3},{1,0},{2,1},{3,2},{4,7},{5,4},{6,5},{7,6},{8,11},{9,8},{10,9... | collective-permute-start | bytes 552968 | tf_op jit(solution)/shard_map/ppermute | solution.py:104
  7.1 10.9 %copy-start.5 = (bf16[2,64,1152]{2,1,0:T(8,128)(2,1)S(1)}, bf16[2,64,1152]{2,1,0:T(8,128)(2,1)}, u32[]{:S(2)}) copy-start(bf16[2,64,1152]{2,1,0:T(8,128)(2,1)} %get-tuple-element.36) | copy-start | bytes 884740
  8.3 37.0 %copy-start = (bf16[288,3456]{1,0:T(8,128)(2,1)S(1)}, bf16[288,3456]{1,0:T(8,128)(2,1)}, u32[]{:S(2)}) copy-start(bf16[288,3456]{1,0:T(8,128)(2,1)} %refs_1_.1) | copy-start | bytes 5971972
  8.3 18.4 %collective-permute-start.10 = (bf16[256,1152]{1,0:T(8,128)(2,1)S(1)}, bf16[256,1152]{1,0:T(8,128)(2,1)S(1)}, u32[]{:S(2)}, u32[]{:S(2)}) collective-permute-start(bf16[256,1152]{1,0:T(8,128)(2,1)S(1)} %shard_map.56.refs_0_), channel_id=1, source_target_pairs={{0,4},{4,0},{8,12},{12,8},{16,20},{20,16},{24,28},{28,24},{1,5},{5... | collective-permute-start | bytes 1769480 | tf_op jit(solution)/shard_map/ppermute | solution.py:108
  15.3 11.4 %collective-permute-start.11 = (bf16[2,80,1152]{2,1,0:T(8,128)(2,1)S(1)}, bf16[2,80,1152]{2,1,0:T(8,128)(2,1)S(1)}, u32[]{:S(2)}, u32[]{:S(2)}) collective-permute-start(bf16[2,80,1152]{2,1,0:T(8,128)(2,1)S(1)} %constant_dynamic-update-slice_fusion.5), channel_id=1, source_target_pairs={{0,8},{4,20},{8,0},{12,28},{16,24},{20,4},{24,16},{28,12},{1,9},{5... | collective-permute-start | bytes 1105928 | tf_op jit(solution)/shard_map/ppermute | solution.py:108
  16.9 9.4 %collective-permute-start.3 = (bf16[1,80,1152]{2,1,0:T(8,128)(2,1)S(1)}, bf16[1,80,1152]{2,1,0:T(8,128)(2,1)S(1)}, u32[]{:S(2)}, u32[]{:S(2)}) collective-permute-start(bf16[1,80,1152]{2,1,0:T(8,128)(2,1)S(1)} %collective-permute-done), channel_id=1, source_target_pairs={{0,1},{1,2},{2,3},{3,0},{4,5},{5,6},{6,7},{7,4},{8,9},{9,10},{10,1... | collective-permute-start | bytes 552968 | tf_op jit(solution)/shard_map/ppermute | solution.py:104
  18.0 17.6 %collective-permute-start.2 = (bf16[2,64,1152]{2,1,0:T(8,128)(2,1)S(1)}, bf16[2,64,1152]{2,1,0:T(8,128)(2,1)S(1)}, u32[]{:S(2)}, u32[]{:S(2)}) collective-permute-start(bf16[2,64,1152]{2,1,0:T(8,128)(2,1)S(1)} %copy-done.5), channel_id=1, source_target_pairs={{0,1},{1,2},{2,3},{3,0},{4,5},{5,6},{6,7},{7,4},{8,9},{9,10},{10,1... | collective-permute-start | bytes 884744 | tf_op jit(solution)/shard_map/ppermute | solution.py:104
  26.3 7.6 %collective-permute-start.4 = (bf16[1,80,1152]{2,1,0:T(8,128)(2,1)S(1)}, bf16[1,80,1152]{2,1,0:T(8,128)(2,1)S(1)}, u32[]{:S(2)}, u32[]{:S(2)}) collective-permute-start(bf16[1,80,1152]{2,1,0:T(8,128)(2,1)S(1)} %collective-permute-done.3), channel_id=1, source_target_pairs={{0,8},{4,20},{8,0},{12,28},{16,24},{20,4},{24,16},{28,12},{1,9},{5... | collective-permute-start | bytes 552968 | tf_op jit(solution)/shard_map/ppermute | solution.py:108
  26.8 18.5 %collective-permute-start.12 = (bf16[4,80,1152]{2,1,0:T(8,128)(2,1)S(1)}, bf16[4,80,1152]{2,1,0:T(8,128)(2,1)S(1)}, u32[]{:S(2)}, u32[]{:S(2)}) collective-permute-start(bf16[4,80,1152]{2,1,0:T(8,128)(2,1)S(1)} %constant_dynamic-update-slice_fusion.7.refs_3_), channel_id=1, source_target_pairs={{0,16},{4,12},{8,24},{12,4},{16,0},{20,28},{24,8},{28,20},{1,17},{... | collective-permute-start | bytes 2211848 | tf_op jit(solution)/shard_map/ppermute | solution.py:108
  33.9 11.5 %collective-permute-start.13 = (bf16[2,80,1152]{2,1,0:T(8,128)(2,1)S(1)}, bf16[2,80,1152]{2,1,0:T(8,128)(2,1)S(1)}, u32[]{:S(2)}, u32[]{:S(2)}) collective-permute-start(bf16[2,80,1152]{2,1,0:T(8,128)(2,1)S(1)} %constant_dynamic-update-slice_fusion.refs_5_), channel_id=1, source_target_pairs={{0,16},{4,12},{8,24},{12,4},{16,0},{20,28},{24,8},{28,20},{1,17},{... | collective-permute-start | bytes 1105928 | tf_op jit(solution)/shard_map/ppermute | solution.py:108
  35.4 9.9 %collective-permute-start.6 = (bf16[2,64,1152]{2,1,0:T(8,128)(2,1)S(1)}, bf16[2,64,1152]{2,1,0:T(8,128)(2,1)S(1)}, u32[]{:S(2)}, u32[]{:S(2)}) collective-permute-start(bf16[2,64,1152]{2,1,0:T(8,128)(2,1)S(1)} %copy-done.5), channel_id=1, source_target_pairs={{0,3},{1,0},{2,1},{3,2},{4,7},{5,4},{6,5},{7,6},{8,11},{9,8},{10,9... | collective-permute-start | bytes 884744 | tf_op jit(solution)/shard_map/ppermute | solution.py:104
  35.6 11.9 %collective-permute-start.5 = (bf16[2,64,1152]{2,1,0:T(8,128)(2,1)S(1)}, bf16[2,64,1152]{2,1,0:T(8,128)(2,1)S(1)}, u32[]{:S(2)}, u32[]{:S(2)}) collective-permute-start(bf16[2,64,1152]{2,1,0:T(8,128)(2,1)S(1)} %collective-permute-done.2), channel_id=1, source_target_pairs={{0,1},{1,2},{2,3},{3,0},{4,5},{5,6},{6,7},{7,4},{8,9},{9,10},{10,1... | collective-permute-start | bytes 884744 | tf_op jit(solution)/shard_map/ppermute | solution.py:104
  47.5 3.2 %collective-permute-start.14 = (bf16[608,1152]{1,0:T(8,128)(2,1)S(1)}, bf16[608,1152]{1,0:T(8,128)(2,1)S(1)}, u32[]{:S(2)}, u32[]{:S(2)}) collective-permute-start(bf16[608,1152]{1,0:T(8,128)(2,1)S(1)} %shard_map.57.mine_ref.refs_7_), channel_id=1, source_target_pairs={{0,4},{4,0},{8,12},{12,8},{16,20},{20,16},{24,28},{28,24},{1,5},{5... | collective-permute-start | bytes 4202504 | tf_op jit(solution)/shard_map/ppermute | solution.py:108
  47.7 4.3 %collective-permute-start.7 = (bf16[6,64,1152]{2,1,0:T(8,128)(2,1)S(1)}, bf16[6,64,1152]{2,1,0:T(8,128)(2,1)S(1)}, u32[]{:S(2)}, u32[]{:S(2)}) collective-permute-start(bf16[6,64,1152]{2,1,0:T(8,128)(2,1)S(1)} %constant_dynamic-update-slice_fusion.2.refs_3_), channel_id=1, source_target_pairs={{0,4},{4,0},{8,12},{12,8},{16,20},{20,16},{24,28},{28,24},{1,5},{5... | collective-permute-start | bytes 2654216 | tf_op jit(solution)/shard_map/ppermute | solution.py:108
  48.4 13.1 %collective-permute-start.8 = (bf16[3,64,1152]{2,1,0:T(8,128)(2,1)S(1)}, bf16[3,64,1152]{2,1,0:T(8,128)(2,1)S(1)}, u32[]{:S(2)}, u32[]{:S(2)}) collective-permute-start(bf16[3,64,1152]{2,1,0:T(8,128)(2,1)S(1)} %pad_maximum_fusion), channel_id=1, source_target_pairs={{0,8},{4,20},{8,0},{12,28},{16,24},{20,4},{24,16},{28,12},{1,9},{5... | collective-permute-start | bytes 1327112 | tf_op jit(solution)/shard_map/ppermute | solution.py:108
  49.0 12.5 %collective-permute-start.9 = (bf16[3,64,1152]{2,1,0:T(8,128)(2,1)S(1)}, bf16[3,64,1152]{2,1,0:T(8,128)(2,1)S(1)}, u32[]{:S(2)}, u32[]{:S(2)}) collective-permute-start(bf16[3,64,1152]{2,1,0:T(8,128)(2,1)S(1)} %pad_maximum_fusion), channel_id=1, source_target_pairs={{0,16},{4,12},{8,24},{12,4},{16,0},{20,28},{24,8},{28,20},{1,17},{... | collective-permute-start | bytes 1327112 | tf_op jit(solution)/shard_map/ppermute | solution.py:108
  51.6 10.5 %copy-start.2 = (f32[3,3,1152]{2,1,0:T(4,128)S(1)}, f32[3,3,1152]{2,1,0:T(4,128)}, u32[]{:S(2)}) copy-start(f32[3,3,1152]{2,1,0:T(4,128)} %refs_6_.1) | copy-start | bytes 124420
  52.0 9.6 %collective-permute-start.15 = (bf16[9,32,128]{2,1,0:T(8,128)(2,1)S(1)}, bf16[9,32,128]{2,1,0:T(8,128)(2,1)S(1)}, u32[]{:S(2)}, u32[]{:S(2)}) collective-permute-start(bf16[9,32,128]{2,1,0:T(8,128)(2,1)S(1)} %get-tuple-element.43), channel_id=1, source_target_pairs={{0,8},{4,12},{16,24},{20,28},{1,9},{5,13},{17,25},{21,29},{2,10},{... | collective-permute-start | bytes 221192 | tf_op jit(solution)/shard_map/ppermute | solution.py:551
  54.4 7.3 %collective-permute-start.16 = (bf16[9,32,128]{2,1,0:T(8,128)(2,1)S(1)}, bf16[9,32,128]{2,1,0:T(8,128)(2,1)S(1)}, u32[]{:S(2)}, u32[]{:S(2)}) collective-permute-start(bf16[9,32,128]{2,1,0:T(8,128)(2,1)S(1)} %get-tuple-element.43), channel_id=1, source_target_pairs={{0,16},{4,20},{8,24},{12,28},{1,17},{5,21},{9,25},{13,29},{2,18},{... | collective-permute-start | bytes 221192 | tf_op jit(solution)/shard_map/ppermute | solution.py:551
  57.2 4.7 %collective-permute-start.17 = (bf16[9,32,128]{2,1,0:T(8,128)(2,1)S(1)}, bf16[9,32,128]{2,1,0:T(8,128)(2,1)S(1)}, u32[]{:S(2)}, u32[]{:S(2)}) collective-permute-start(bf16[9,32,128]{2,1,0:T(8,128)(2,1)S(1)} %get-tuple-element.43), channel_id=1, source_target_pairs={{0,24},{4,28},{8,16},{12,20},{1,25},{5,29},{9,17},{13,21},{2,26},{... | collective-permute-start | bytes 221192 | tf_op jit(solution)/shard_map/ppermute | solution.py:551
  61.5 2.9 %copy-start.1 = (bf16[288,1152]{1,0:T(8,128)(2,1)S(1)}, bf16[288,1152]{1,0:T(8,128)(2,1)}, u32[]{:S(2)}) copy-start(bf16[288,1152]{1,0:T(8,128)(2,1)} %refs_2_.3) | copy-start | bytes 1990660
  61.9 2.5 %collective-permute-start.18 = (bf16[6,64,1152]{2,1,0:T(8,128)(2,1)S(1)}, bf16[6,64,1152]{2,1,0:T(8,128)(2,1)S(1)}, u32[]{:S(2)}, u32[]{:S(2)}) collective-permute-start(bf16[6,64,1152]{2,1,0:T(8,128)(2,1)S(1)} %constant_dynamic-update-slice_fusion.9.refs_5_), channel_id=1, source_target_pairs={{0,4},{4,0},{8,12},{12,8},{16,20},{20,16},{24,28},{28,24},{1,5},{5... | collective-permute-start | bytes 2654216 | tf_op jit(solution)/shard_map/ppermute | solution.py:108
  62.0 6.5 %collective-permute-start.19 = (bf16[9,32,128]{2,1,0:T(8,128)(2,1)S(1)}, bf16[9,32,128]{2,1,0:T(8,128)(2,1)S(1)}, u32[]{:S(2)}, u32[]{:S(2)}) collective-permute-start(bf16[9,32,128]{2,1,0:T(8,128)(2,1)S(1)} %convert_add_fusion.1), channel_id=1, source_target_pairs={{0,3},{1,2},{2,1},{3,0},{4,7},{5,6},{6,5},{7,4},{8,11},{9,10},{10,... | collective-permute-start | bytes 221192 | tf_op jit(solution)/shard_map/ppermute | solution.py:570
  63.0 5.6 %copy-start.4 = (f32[1152]{0:T(1024)S(1)}, f32[1152]{0:T(1024)}, u32[]{:S(2)}) copy-start(f32[1152]{0:T(1024)} %param.9) | copy-start | bytes 13828
  68.5 5.2 %collective-permute-start.20 = (bf16[9,32,128]{2,1,0:T(8,128)(2,1)S(1)}, bf16[9,32,128]{2,1,0:T(8,128)(2,1)S(1)}, u32[]{:S(2)}, u32[]{:S(2)}) collective-permute-start(bf16[9,32,128]{2,1,0:T(8,128)(2,1)S(1)} %add_convert_fusion), channel_id=1, source_target_pairs={{0,1},{1,0},{2,3},{3,2},{4,5},{5,4},{6,7},{7,6},{8,9},{9,8},{10,11... | collective-permute-start | bytes 221192 | tf_op jit(solution)/shard_map/ppermute | solution.py:573
  68.6 7.0 %collective-permute-start.21 = (bf16[1,64,1152]{2,1,0:T(8,128)(2,1)S(1)}, bf16[1,64,1152]{2,1,0:T(8,128)(2,1)S(1)}, u32[]{:S(2)}, u32[]{:S(2)}) collective-permute-start(bf16[1,64,1152]{2,1,0:T(8,128)(2,1)S(1)} %get-tuple-element.55), channel_id=1, source_target_pairs={{0,1},{1,0},{2,3},{3,2},{4,5},{5,4},{6,7},{7,6},{8,9},{9,8},{10,11... | collective-permute-start | bytes 442376 | tf_op jit(solution)/shard_map/ppermute | solution.py:575
  70.6 5.0 %collective-permute-start.22 = (bf16[1,64,1152]{2,1,0:T(8,128)(2,1)S(1)}, bf16[1,64,1152]{2,1,0:T(8,128)(2,1)S(1)}, u32[]{:S(2)}, u32[]{:S(2)}) collective-permute-start(bf16[1,64,1152]{2,1,0:T(8,128)(2,1)S(1)} %get-tuple-element.56), channel_id=1, source_target_pairs={{1,2},{2,1},{5,6},{6,5},{9,10},{10,9},{13,14},{14,13},{17,18},{18,... | collective-permute-start | bytes 442376 | tf_op jit(solution)/shard_map/ppermute | solution.py:578

commit v14 on v11

--- a/solution.py
+++ b/solution.py
@@ -365,6 +365,27 @@
         [whole_vmem()] * 2,
         flops=4 * count * depth * LANES,
         bytes_accessed=8 * count * depth,
+    )
+
+
+def row_kernel(upto_ref, total_ref, beside_ref, prefix_ref, row_ref):
+    _, x, _ = coordinates()
+    beside = beside_ref[...].astype(jnp.float32)
+    prefix_ref[...] = upto_ref[...] + jnp.where(x == 1, beside, 0.0)
+    row_ref[...] = (total_ref[...].astype(jnp.float32) + beside).astype(jnp.bfloat16)
+
+
+def row_call(upto, total, beside):
+    return kernel_call(
+        row_kernel,
+        [
+            jax.ShapeDtypeStruct(upto.shape, jnp.float32),
+            jax.ShapeDtypeStruct(upto.shape, jnp.bfloat16),
+        ],
+        (upto, total, beside),
+        [whole_vmem()] * 3,
+        flops=2 * upto.size,
+        bytes_accessed=12 * upto.size,
     )
 
 
@@ -546,12 +567,11 @@
     second_first = flipped(second_own, (2, 4))
     second_second = flipped(second_own, (4, 2))
 
-    for bit, guard in ((2, 2), (4, 4), (6, 4)):
-        pairs = [(t, t ^ bit) for t in range(8) if not t & guard]
-        upto = upto + lax.ppermute(total, "tm", pairs).astype(jnp.float32)
+    upto, row_total = row_call(upto, total, flipped(total, (2, 2)))
+    upto = upto + lax.ppermute(row_total, "tm", [(t, t ^ 4) for t in range(4)]).astype(jnp.float32)
     count = lax.axis_size("space")
     state = after(upto, second_first, second_second)
-    turned = jnp.concatenate(after((second_first, second_second), total))
+    turned = jnp.concatenate(after((second_first, second_second), upto))
     swapped_turned = flipped(after(turned, upto), (1, 1))
     queries, weight = query_call(
         tokens,

time: 77.8 us -> 83.1 us (1.068)
  waiting for transfers between devices: 40.8 us -> 49.3 us
  starting transfers between devices: 23.7 us -> 20.6 us
    ppermute x10 -> x11, waiting for transfers between devices: 11.5 us -> 18.3 us  [flipped(): lax.ppermute(value, 'tm', [(t, t ^ bit_on_core[t % 2]) for t in range(8)])]
    ppermute x3 -> x1, starting transfers between devices: 6.48 us -> 2.84 us  [plane_form(): lax.ppermute(row_total, 'tm', [(t, t ^ 4) for t in range(4)])]
    ppermute x3 -> x1, waiting for transfers between devices: 0.32 us -> 1.96 us  [plane_form(): lax.ppermute(row_total, 'tm', [(t, t ^ 4) for t in range(4)])]
    ppermute x10 -> x11, starting transfers between devices: 7.06 us -> 7.59 us  [flipped(): lax.ppermute(value, 'tm', [(t, t ^ bit_on_core[t % 2]) for t in range(8)])]
    pallas_call x7 -> x8, Pallas kernels: 11 us -> 11.1 us  [kernel_call(): pl.pallas_call(body, out_shape=outputs, in_specs=in_specs, out_specs=jax....]
  transfers between devices with their start and end apart: 23 -> 22, of which waited for: 14 -> 13; matrix products, arithmetic and copies ran while one was open for 1% -> 0% of each run, Pallas kernels for 9% -> 8%
where the time goes in v14:
time: 83.1 us; the launch traced here: 81.8 us
  waiting for transfers between devices  49.3 us (59%)
  starting transfers between devices  20.6 us (25%)
  Pallas kernels  11.1 us (13%)
    ppermute x6, waiting for transfers between devices, shifted(): lax.ppermute(value, 'space', [(i, (i + step) % count) for i in range(coun...  22.3 us
    ppermute x11, waiting for transfers between devices, flipped(): lax.ppermute(value, 'tm', [(t, t ^ bit_on_core[t % 2]) for t in range(8)])  18.3 us
    pallas_call x8, Pallas kernels, kernel_call(): pl.pallas_call(body, out_shape=outputs, in_specs=in_specs, out_specs=jax....  11.1 us
    ppermute x6, starting transfers between devices, shifted(): lax.ppermute(value, 'space', [(i, (i + step) % count) for i in range(coun...  9.05 us
    ppermute x11, starting transfers between devices, flipped(): lax.ppermute(value, 'tm', [(t, t ^ bit_on_core[t % 2]) for t in range(8)])  7.59 us
    ppermute x1, waiting for transfers between devices, plane_form(): lax.ppermute(share, 'space', [(i, count - 1 - i) for i in range(count)])  5.94 us
    ppermute x1, starting transfers between devices, plane_form(): lax.ppermute(row_total, 'tm', [(t, t ^ 4) for t in range(4)])  2.84 us
    ppermute x1, waiting for transfers between devices, plane_form(): lax.ppermute(row_total, 'tm', [(t, t ^ 4) for t in range(4)])  1.96 us
  transfers between devices with their start and end apart: 22, of which 13 were waited for; matrix products, arithmetic and copies ran while one was open for 0% of the time, Pallas kernels for 8%

profile of v14, /device:TPU:0, one launch (start us, length us, event | category | flops | bytes accessed | tf_op | source)
XLA Modules:
  0.0 81.8 jit_solution(10189897563532732829)
XLA Ops:
  0.0 0.0 copy-start.3
  0.0 1.9 %shard_map.55 = (bf16[80,1152]{1,0:T(8,128)(2,1)}, bf16[2,64,1152]{2,1,0:T(8,128)(2,1)}) custom-call(bf16[288,3456]{1,0:T(8,128)(2,1)} %refs_1_.1, bf16[288,1152]{1,0:T(8,128)(2,1)} %refs_2_.3), custom_call_target="tpu_custom_call" | custom-call | bytes 958464 | tf_op jit(solution)/shard_map/pallas_call | solution.py:164
  2.0 3.1 %collective-permute-start = (bf16[1,80,1152]{2,1,0:T(8,128)(2,1)}, bf16[1,80,1152]{2,1,0:T(8,128)(2,1)S(1)}, u32[]{:S(2)}, u32[]{:S(2)}) collective-permute-start(bf16[1,80,1152]{2,1,0:T(8,128)(2,1)} %bitcast.8), channel_id=1, source_target_pairs={{0,1},{1,2},{2,3},{3,0},{4,5},{5,6},{6,7},{7,4},{8,9},{9,10},{10,1... | collective-permute-start | bytes 552968 | tf_op jit(solution)/shard_map/ppermute | solution.py:104
  5.0 2.1 %collective-permute-start.1 = (bf16[1,80,1152]{2,1,0:T(8,128)(2,1)}, bf16[1,80,1152]{2,1,0:T(8,128)(2,1)S(1)}, u32[]{:S(2)}, u32[]{:S(2)}) collective-permute-start(bf16[1,80,1152]{2,1,0:T(8,128)(2,1)} %bitcast.9), channel_id=1, source_target_pairs={{0,3},{1,0},{2,1},{3,2},{4,7},{5,4},{6,5},{7,6},{8,11},{9,8},{10,9... | collective-permute-start | bytes 552968 | tf_op jit(solution)/shard_map/ppermute | solution.py:104
  7.1 0.0 copy-done.3
  7.1 0.0 copy-start.5
  7.1 1.2 %shard_map.56.refs_0_ = bf16[256,1152]{1,0:T(8,128)(2,1)S(1)} custom-call(bf16[256,1152]{1,0:T(8,128)(2,1)S(1)} %bitcast.7), custom_call_target="tpu_custom_call" | custom-call | flops 679477248 | bytes 589824 | tf_op jit(solution)/shard_map/pallas_call | solution.py:164
  8.3 0.0 copy-start
  8.3 0.1 collective-permute-start.10
  8.4 4.4 %collective-permute-done = bf16[1,80,1152]{2,1,0:T(8,128)(2,1)S(1)} collective-permute-done((bf16[1,80,1152]{2,1,0:T(8,128)(2,1)}, bf16[1,80,1152]{2,1,0:T(8,128)(2,1)S(1)}, u32[]{:S(2)}, u32[]{:S(2)}) %collective-permute-start) | collective-permute-done | bytes 184352 | tf_op jit(solution)/shard_map/ppermute | solution.py:104
  12.8 2.5 %collective-permute-done.1 = bf16[1,80,1152]{2,1,0:T(8,128)(2,1)S(1)} collective-permute-done((bf16[1,80,1152]{2,1,0:T(8,128)(2,1)}, bf16[1,80,1152]{2,1,0:T(8,128)(2,1)S(1)}, u32[]{:S(2)}, u32[]{:S(2)}) %collective-permute-start.1) | collective-permute-done | bytes 184352 | tf_op jit(solution)/shard_map/ppermute | solution.py:104
  15.3 1.6 %collective-permute-start.11 = (bf16[2,80,1152]{2,1,0:T(8,128)(2,1)S(1)}, bf16[2,80,1152]{2,1,0:T(8,128)(2,1)S(1)}, u32[]{:S(2)}, u32[]{:S(2)}) collective-permute-start(bf16[2,80,1152]{2,1,0:T(8,128)(2,1)S(1)} %constant_dynamic-update-slice_fusion.5), channel_id=1, source_target_pairs={{0,8},{4,20},{8,0},{12,28},{16,24},{20,4},{24,16},{28,12},{1,9},{5... | collective-permute-start | bytes 1105928 | tf_op jit(solution)/shard_map/ppermute | solution.py:108
  16.9 1.1 %collective-permute-start.3 = (bf16[1,80,1152]{2,1,0:T(8,128)(2,1)S(1)}, bf16[1,80,1152]{2,1,0:T(8,128)(2,1)S(1)}, u32[]{:S(2)}, u32[]{:S(2)}) collective-permute-start(bf16[1,80,1152]{2,1,0:T(8,128)(2,1)S(1)} %collective-permute-done), channel_id=1, source_target_pairs={{0,1},{1,2},{2,3},{3,0},{4,5},{5,6},{6,7},{7,4},{8,9},{9,10},{10,1... | collective-permute-start | bytes 552968 | tf_op jit(solution)/shard_map/ppermute | solution.py:104
  18.0 0.0 copy-done.5
  18.0 0.7 collective-permute-start.2
  18.8 7.5 %collective-permute-done.3 = bf16[1,80,1152]{2,1,0:T(8,128)(2,1)S(1)} collective-permute-done((bf16[1,80,1152]{2,1,0:T(8,128)(2,1)S(1)}, bf16[1,80,1152]{2,1,0:T(8,128)(2,1)S(1)}, u32[]{:S(2)}, u32[]{:S(2)}) %collective-permute-start.3) | collective-permute-done | bytes 184352 | tf_op jit(solution)/shard_map/ppermute | solution.py:104
  26.3 0.4 collective-permute-start.4
  26.7 0.0 collective-permute-done.11
  26.7 0.0 collective-permute-done.10.refs_1_
  26.8 1.7 %collective-permute-start.12 = (bf16[4,80,1152]{2,1,0:T(8,128)(2,1)S(1)}, bf16[4,80,1152]{2,1,0:T(8,128)(2,1)S(1)}, u32[]{:S(2)}, u32[]{:S(2)}) collective-permute-start(bf16[4,80,1152]{2,1,0:T(8,128)(2,1)S(1)} %constant_dynamic-update-slice_fusion.7.refs_3_), channel_id=1, source_target_pairs={{0,16},{4,12},{8,24},{12,4},{16,0},{20,28},{24,8},{28,20},{1,17},{... | collective-permute-start | bytes 2211848 | tf_op jit(solution)/shard_map/ppermute | solution.py:108
  28.5 5.3 %collective-permute-done.4 = bf16[1,80,1152]{2,1,0:T(8,128)(2,1)S(1)} collective-permute-done((bf16[1,80,1152]{2,1,0:T(8,128)(2,1)S(1)}, bf16[1,80,1152]{2,1,0:T(8,128)(2,1)S(1)}, u32[]{:S(2)}, u32[]{:S(2)}) %collective-permute-start.4) | collective-permute-done | bytes 184352 | tf_op jit(solution)/shard_map/ppermute | solution.py:108
  33.9 1.6 %collective-permute-start.13 = (bf16[2,80,1152]{2,1,0:T(8,128)(2,1)S(1)}, bf16[2,80,1152]{2,1,0:T(8,128)(2,1)S(1)}, u32[]{:S(2)}, u32[]{:S(2)}) collective-permute-start(bf16[2,80,1152]{2,1,0:T(8,128)(2,1)S(1)} %constant_dynamic-update-slice_fusion.refs_5_), channel_id=1, source_target_pairs={{0,16},{4,12},{8,24},{12,4},{16,0},{20,28},{24,8},{28,20},{1,17},{... | collective-permute-start | bytes 1105928 | tf_op jit(solution)/shard_map/ppermute | solution.py:108
  35.4 0.1 collective-permute-start.6
  35.6 0.0 collective-permute-done.2
  35.6 1.9 %collective-permute-start.5 = (bf16[2,64,1152]{2,1,0:T(8,128)(2,1)S(1)}, bf16[2,64,1152]{2,1,0:T(8,128)(2,1)S(1)}, u32[]{:S(2)}, u32[]{:S(2)}) collective-permute-start(bf16[2,64,1152]{2,1,0:T(8,128)(2,1)S(1)} %collective-permute-done.2), channel_id=1, source_target_pairs={{0,1},{1,2},{2,3},{3,0},{4,5},{5,6},{6,7},{7,4},{8,9},{9,10},{10,1... | collective-permute-start | bytes 884744 | tf_op jit(solution)/shard_map/ppermute | solution.py:104
  37.5 7.9 %collective-permute-done.6 = bf16[2,64,1152]{2,1,0:T(8,128)(2,1)S(1)} collective-permute-done((bf16[2,64,1152]{2,1,0:T(8,128)(2,1)S(1)}, bf16[2,64,1152]{2,1,0:T(8,128)(2,1)S(1)}, u32[]{:S(2)}, u32[]{:S(2)}) %collective-permute-start.6) | collective-permute-done | bytes 294944 | tf_op jit(solution)/shard_map/ppermute | solution.py:104
  45.3 0.0 collective-permute-done.13.refs_6_
  45.3 0.0 collective-permute-done.12.refs_4_
  45.3 0.0 copy-done
  45.3 2.1 %shard_map.57.mine_ref.refs_7_ = bf16[608,1152]{1,0:T(8,128)(2,1)S(1)} custom-call(bf16[256,1152]{1,0:T(8,128)(2,1)S(1)} %shard_map.56.refs_0_, bf16[256,1152]{1,0:T(8,128)(2,1)S(1)} %collective-permute-done.10.refs_1_, bf16[288,3456]{1,0:T(8,128)(2,1)S(1)} %copy-done, bf16[4,80,1152]{2,1,0:T(8,128)(2,1)S(1)} %constant_dynamic-update-slice_fusion.7.refs_3_, ...), custom_call_target="tpu_custom_call" | custom-call | flops 1358954496 | bytes 2654208 | tf_op jit(solution)/shard_map/pallas_call | solution.py:164
  47.5 0.0 collective-permute-done.5
  47.5 0.1 collective-permute-start.14
  47.7 0.6 collective-permute-start.7
  48.3 0.1 pad_maximum_fusion
  48.4 0.6 collective-permute-start.8
  49.0 0.4 collective-permute-start.9
  49.4 1.3 %collective-permute-done.14.other_ref.refs_8_ = bf16[608,1152]{1,0:T(8,128)(2,1)S(1)} collective-permute-done((bf16[608,1152]{1,0:T(8,128)(2,1)S(1)}, bf16[608,1152]{1,0:T(8,128)(2,1)S(1)}, u32[]{:S(2)}, u32[]{:S(2)}) %collective-permute-start.14) | collective-permute-done | bytes 1400864 | tf_op jit(solution)/shard_map/ppermute | solution.py:108
  50.7 0.8 %shard_map.58 = (bf16[256,1152]{1,0:T(8,128)(2,1)S(1)}, bf16[1,64,1152]{2,1,0:T(8,128)(2,1)S(1)}, bf16[1,64,1152]{2,1,0:T(8,128)(2,1)S(1)}, f32[9,32,128]{2,1,0:T(8,128)S(1)}, bf16[9,32,128]{2,1,0:T(8,128)(2,1)S(1)}) custom-call(bf16[608,1152]{1,0:T(8,128)(2,1)S(1)} %shard_map.57.mine_ref.refs_7_, bf16[608,1152]{1,0:T(8,128)(2,1)S(1)} %collective-permute-done.14.other_ref.refs_8_), custom_call_target="tpu_custom_call" | custom-call | flops 150994944 | bytes 2359296 | tf_op jit(solution)/shard_map/pallas_call | solution.py:164
  51.6 0.0 copy-start.2
  51.6 0.4 collective-permute-done.7.refs_4_
  52.0 0.5 collective-permute-start.15
  52.5 9.8 %collective-permute-done.15.beside_ref = bf16[9,32,128]{2,1,0:T(8,128)(2,1)S(1)} collective-permute-done((bf16[9,32,128]{2,1,0:T(8,128)(2,1)S(1)}, bf16[9,32,128]{2,1,0:T(8,128)(2,1)S(1)}, u32[]{:S(2)}, u32[]{:S(2)}) %collective-permute-start.15) | collective-permute-done | bytes 73760 | tf_op jit(solution)/shard_map/ppermute | solution.py:108
  62.4 2.8 %collective-permute-start.16 = (bf16[9,32,128]{2,1,0:T(8,128)(2,1)S(1)}, bf16[9,32,128]{2,1,0:T(8,128)(2,1)S(1)}, u32[]{:S(2)}, u32[]{:S(2)}) collective-permute-start(bf16[9,32,128]{2,1,0:T(8,128)(2,1)S(1)} %get-tuple-element.48), channel_id=1, source_target_pairs={{0,16},{4,20},{8,24},{12,28},{1,17},{5,21},{9,25},{13,29},{2,18},{... | collective-permute-start | bytes 221192 | tf_op jit(solution)/shard_map/ppermute | solution.py:571
  65.2 2.0 %collective-permute-done.16 = bf16[9,32,128]{2,1,0:T(8,128)(2,1)S(1)} collective-permute-done((bf16[9,32,128]{2,1,0:T(8,128)(2,1)S(1)}, bf16[9,32,128]{2,1,0:T(8,128)(2,1)S(1)}, u32[]{:S(2)}, u32[]{:S(2)}) %collective-permute-start.16) | collective-permute-done | bytes 73760 | tf_op jit(solution)/shard_map/ppermute | solution.py:571
  67.2 0.0 collective-permute-done.8
  67.2 0.0 collective-permute-done.9
  67.3 0.0 copy-start.1
  67.3 0.1 collective-permute-start.17
  67.4 0.1 collective-permute-start.18
  67.5 0.0 copy-done.2
  67.5 0.9 %shard_map.61 = f32[4,64,1152]{2,1,0:T(8,128)S(1)} custom-call(bf16[4,64,1152]{2,1,0:T(8,128)(2,1)S(1)} %bitcast.6, f32[3,3,1152]{2,1,0:T(4,128)S(1)} %copy-done.2), custom_call_target="tpu_custom_call" | custom-call | flops 5308416 | bytes 1769472 | tf_op jit(solution)/shard_map/pallas_call | solution.py:164
  68.4 0.0 copy-start.4
  68.4 1.4 %collective-permute-done.17.refs_6_ = bf16[6,64,1152]{2,1,0:T(8,128)(2,1)S(1)} collective-permute-done((bf16[6,64,1152]{2,1,0:T(8,128)(2,1)S(1)}, bf16[6,64,1152]{2,1,0:T(8,128)(2,1)S(1)}, u32[]{:S(2)}, u32[]{:S(2)}) %collective-permute-start.17) | collective-permute-done | bytes 884768 | tf_op jit(solution)/shard_map/ppermute | solution.py:108
  69.8 0.0 copy-done.1
  69.8 1.5 %shard_map.60 = (bf16[256,1152]{1,0:T(8,128)(2,1)S(1)}, bf16[1152,1152]{1,0:T(8,128)(2,1)S(1)}) custom-call(bf16[256,1152]{1,0:T(8,128)(2,1)S(1)} %shard_map.56.refs_0_, bf16[288,3456]{1,0:T(8,128)(2,1)S(1)} %copy-done, bf16[288,1152]{1,0:T(8,128)(2,1)S(1)} %copy-done.1, bf16[6,64,1152]{2,1,0:T(8,128)(2,1)S(1)} %constant_dynamic-update-slice_fusion.2.refs_3_, ...), custom_call_target="tpu_custom_call" | custom-call | flops 679477248 | bytes 5308416 | tf_op jit(solution)/shard_map/pallas_call | solution.py:164
  71.3 0.7 collective-permute-done.18
  72.1 0.1 collective-permute-start.19
  72.2 0.0 copy-done.4
  72.2 0.3 collective-permute-start.20
  72.6 0.7 collective-permute-start.21
  73.2 5.9 %collective-permute-done.19 = bf16[9,32,128]{2,1,0:T(8,128)(2,1)S(1)} collective-permute-done((bf16[9,32,128]{2,1,0:T(8,128)(2,1)S(1)}, bf16[9,32,128]{2,1,0:T(8,128)(2,1)S(1)}, u32[]{:S(2)}, u32[]{:S(2)}) %collective-permute-start.19) | collective-permute-done | bytes 73760 | tf_op jit(solution)/shard_map/ppermute | solution.py:593
  79.2 0.1 collective-permute-done.20.refs_4_
  79.3 0.0 collective-permute-done.21.refs_5_
  79.3 2.5 %shard_map.62 = bf16[256,1152]{1,0:T(8,128)(2,1)} custom-call(bf16[256,1152]{1,0:T(8,128)(2,1)S(1)} %get-tuple-element.52.refs_0_, bf16[1152,1152]{1,0:T(8,128)(2,1)S(1)} %get-tuple-element.53.refs_1_, f32[9,32,128]{2,1,0:T(8,128)S(1)} %convert_add_fusion.refs_2_, f32[256,1152]{1,0:T(8,128)S(1)} %bitcast.5, ...), custom_call_target="tpu_custom_call" | custom-call | flops 679477248 | bytes 2654208 | tf_op jit(solution)/shard_map/pallas_call | solution.py:164
  (19 shorter events, 0.5 us)
Async XLA Ops:
  0.0 7.1 %copy-start.3 = (bf16[1,4,64,1152]{3,2,1,0:T(8,128)(2,1)S(1)}, bf16[1,4,64,1152]{3,2,1,0:T(8,128)(2,1)}, u32[]{:S(2)}) copy-start(bf16[1,4,64,1152]{3,2,1,0:T(8,128)(2,1)} %param.5) | copy-start | bytes 1769476
  2.0 10.8 %collective-permute-start = (bf16[1,80,1152]{2,1,0:T(8,128)(2,1)}, bf16[1,80,1152]{2,1,0:T(8,128)(2,1)S(1)}, u32[]{:S(2)}, u32[]{:S(2)}) collective-permute-start(bf16[1,80,1152]{2,1,0:T(8,128)(2,1)} %bitcast.8), channel_id=1, source_target_pairs={{0,1},{1,2},{2,3},{3,0},{4,5},{5,6},{6,7},{7,4},{8,9},{9,10},{10,1... | collective-permute-start | bytes 552968 | tf_op jit(solution)/shard_map/ppermute | solution.py:104
  5.0 10.3 %collective-permute-start.1 = (bf16[1,80,1152]{2,1,0:T(8,128)(2,1)}, bf16[1,80,1152]{2,1,0:T(8,128)(2,1)S(1)}, u32[]{:S(2)}, u32[]{:S(2)}) collective-permute-start(bf16[1,80,1152]{2,1,0:T(8,128)(2,1)} %bitcast.9), channel_id=1, source_target_pairs={{0,3},{1,0},{2,1},{3,2},{4,7},{5,4},{6,5},{7,6},{8,11},{9,8},{10,9... | collective-permute-start | bytes 552968 | tf_op jit(solution)/shard_map/ppermute | solution.py:104
  7.1 10.9 %copy-start.5 = (bf16[2,64,1152]{2,1,0:T(8,128)(2,1)S(1)}, bf16[2,64,1152]{2,1,0:T(8,128)(2,1)}, u32[]{:S(2)}) copy-start(bf16[2,64,1152]{2,1,0:T(8,128)(2,1)} %get-tuple-element.38) | copy-start | bytes 884740
  8.3 37.0 %copy-start = (bf16[288,3456]{1,0:T(8,128)(2,1)S(1)}, bf16[288,3456]{1,0:T(8,128)(2,1)}, u32[]{:S(2)}) copy-start(bf16[288,3456]{1,0:T(8,128)(2,1)} %refs_1_.1) | copy-start | bytes 5971972
  8.3 18.4 %collective-permute-start.10 = (bf16[256,1152]{1,0:T(8,128)(2,1)S(1)}, bf16[256,1152]{1,0:T(8,128)(2,1)S(1)}, u32[]{:S(2)}, u32[]{:S(2)}) collective-permute-start(bf16[256,1152]{1,0:T(8,128)(2,1)S(1)} %shard_map.56.refs_0_), channel_id=1, source_target_pairs={{0,4},{4,0},{8,12},{12,8},{16,20},{20,16},{24,28},{28,24},{1,5},{5... | collective-permute-start | bytes 1769480 | tf_op jit(solution)/shard_map/ppermute | solution.py:108
  15.3 11.4 %collective-permute-start.11 = (bf16[2,80,1152]{2,1,0:T(8,128)(2,1)S(1)}, bf16[2,80,1152]{2,1,0:T(8,128)(2,1)S(1)}, u32[]{:S(2)}, u32[]{:S(2)}) collective-permute-start(bf16[2,80,1152]{2,1,0:T(8,128)(2,1)S(1)} %constant_dynamic-update-slice_fusion.5), channel_id=1, source_target_pairs={{0,8},{4,20},{8,0},{12,28},{16,24},{20,4},{24,16},{28,12},{1,9},{5... | collective-permute-start | bytes 1105928 | tf_op jit(solution)/shard_map/ppermute | solution.py:108
  16.9 9.4 %collective-permute-start.3 = (bf16[1,80,1152]{2,1,0:T(8,128)(2,1)S(1)}, bf16[1,80,1152]{2,1,0:T(8,128)(2,1)S(1)}, u32[]{:S(2)}, u32[]{:S(2)}) collective-permute-start(bf16[1,80,1152]{2,1,0:T(8,128)(2,1)S(1)} %collective-permute-done), channel_id=1, source_target_pairs={{0,1},{1,2},{2,3},{3,0},{4,5},{5,6},{6,7},{7,4},{8,9},{9,10},{10,1... | collective-permute-start | bytes 552968 | tf_op jit(solution)/shard_map/ppermute | solution.py:104
  18.0 17.6 %collective-permute-start.2 = (bf16[2,64,1152]{2,1,0:T(8,128)(2,1)S(1)}, bf16[2,64,1152]{2,1,0:T(8,128)(2,1)S(1)}, u32[]{:S(2)}, u32[]{:S(2)}) collective-permute-start(bf16[2,64,1152]{2,1,0:T(8,128)(2,1)S(1)} %copy-done.5), channel_id=1, source_target_pairs={{0,1},{1,2},{2,3},{3,0},{4,5},{5,6},{6,7},{7,4},{8,9},{9,10},{10,1... | collective-permute-start | bytes 884744 | tf_op jit(solution)/shard_map/ppermute | solution.py:104
  26.3 7.6 %collective-permute-start.4 = (bf16[1,80,1152]{2,1,0:T(8,128)(2,1)S(1)}, bf16[1,80,1152]{2,1,0:T(8,128)(2,1)S(1)}, u32[]{:S(2)}, u32[]{:S(2)}) collective-permute-start(bf16[1,80,1152]{2,1,0:T(8,128)(2,1)S(1)} %collective-permute-done.3), channel_id=1, source_target_pairs={{0,8},{4,20},{8,0},{12,28},{16,24},{20,4},{24,16},{28,12},{1,9},{5... | collective-permute-start | bytes 552968 | tf_op jit(solution)/shard_map/ppermute | solution.py:108
  26.8 18.5 %collective-permute-start.12 = (bf16[4,80,1152]{2,1,0:T(8,128)(2,1)S(1)}, bf16[4,80,1152]{2,1,0:T(8,128)(2,1)S(1)}, u32[]{:S(2)}, u32[]{:S(2)}) collective-permute-start(bf16[4,80,1152]{2,1,0:T(8,128)(2,1)S(1)} %constant_dynamic-update-slice_fusion.7.refs_3_), channel_id=1, source_target_pairs={{0,16},{4,12},{8,24},{12,4},{16,0},{20,28},{24,8},{28,20},{1,17},{... | collective-permute-start | bytes 2211848 | tf_op jit(solution)/shard_map/ppermute | solution.py:108
  33.9 11.5 %collective-permute-start.13 = (bf16[2,80,1152]{2,1,0:T(8,128)(2,1)S(1)}, bf16[2,80,1152]{2,1,0:T(8,128)(2,1)S(1)}, u32[]{:S(2)}, u32[]{:S(2)}) collective-permute-start(bf16[2,80,1152]{2,1,0:T(8,128)(2,1)S(1)} %constant_dynamic-update-slice_fusion.refs_5_), channel_id=1, source_target_pairs={{0,16},{4,12},{8,24},{12,4},{16,0},{20,28},{24,8},{28,20},{1,17},{... | collective-permute-start | bytes 1105928 | tf_op jit(solution)/shard_map/ppermute | solution.py:108
  35.4 9.9 %collective-permute-start.6 = (bf16[2,64,1152]{2,1,0:T(8,128)(2,1)S(1)}, bf16[2,64,1152]{2,1,0:T(8,128)(2,1)S(1)}, u32[]{:S(2)}, u32[]{:S(2)}) collective-permute-start(bf16[2,64,1152]{2,1,0:T(8,128)(2,1)S(1)} %copy-done.5), channel_id=1, source_target_pairs={{0,3},{1,0},{2,1},{3,2},{4,7},{5,4},{6,5},{7,6},{8,11},{9,8},{10,9... | collective-permute-start | bytes 884744 | tf_op jit(solution)/shard_map/ppermute | solution.py:104
  35.6 11.9 %collective-permute-start.5 = (bf16[2,64,1152]{2,1,0:T(8,128)(2,1)S(1)}, bf16[2,64,1152]{2,1,0:T(8,128)(2,1)S(1)}, u32[]{:S(2)}, u32[]{:S(2)}) collective-permute-start(bf16[2,64,1152]{2,1,0:T(8,128)(2,1)S(1)} %collective-permute-done.2), channel_id=1, source_target_pairs={{0,1},{1,2},{2,3},{3,0},{4,5},{5,6},{6,7},{7,4},{8,9},{9,10},{10,1... | collective-permute-start | bytes 884744 | tf_op jit(solution)/shard_map/ppermute | solution.py:104
  47.5 3.2 %collective-permute-start.14 = (bf16[608,1152]{1,0:T(8,128)(2,1)S(1)}, bf16[608,1152]{1,0:T(8,128)(2,1)S(1)}, u32[]{:S(2)}, u32[]{:S(2)}) collective-permute-start(bf16[608,1152]{1,0:T(8,128)(2,1)S(1)} %shard_map.57.mine_ref.refs_7_), channel_id=1, source_target_pairs={{0,4},{4,0},{8,12},{12,8},{16,20},{20,16},{24,28},{28,24},{1,5},{5... | collective-permute-start | bytes 4202504 | tf_op jit(solution)/shard_map/ppermute | solution.py:108
  47.7 4.3 %collective-permute-start.7 = (bf16[6,64,1152]{2,1,0:T(8,128)(2,1)S(1)}, bf16[6,64,1152]{2,1,0:T(8,128)(2,1)S(1)}, u32[]{:S(2)}, u32[]{:S(2)}) collective-permute-start(bf16[6,64,1152]{2,1,0:T(8,128)(2,1)S(1)} %constant_dynamic-update-slice_fusion.2.refs_3_), channel_id=1, source_target_pairs={{0,4},{4,0},{8,12},{12,8},{16,20},{20,16},{24,28},{28,24},{1,5},{5... | collective-permute-start | bytes 2654216 | tf_op jit(solution)/shard_map/ppermute | solution.py:108
  48.4 18.8 %collective-permute-start.8 = (bf16[3,64,1152]{2,1,0:T(8,128)(2,1)S(1)}, bf16[3,64,1152]{2,1,0:T(8,128)(2,1)S(1)}, u32[]{:S(2)}, u32[]{:S(2)}) collective-permute-start(bf16[3,64,1152]{2,1,0:T(8,128)(2,1)S(1)} %pad_maximum_fusion), channel_id=1, source_target_pairs={{0,8},{4,20},{8,0},{12,28},{16,24},{20,4},{24,16},{28,12},{1,9},{5... | collective-permute-start | bytes 1327112 | tf_op jit(solution)/shard_map/ppermute | solution.py:108
  49.0 18.2 %collective-permute-start.9 = (bf16[3,64,1152]{2,1,0:T(8,128)(2,1)S(1)}, bf16[3,64,1152]{2,1,0:T(8,128)(2,1)S(1)}, u32[]{:S(2)}, u32[]{:S(2)}) collective-permute-start(bf16[3,64,1152]{2,1,0:T(8,128)(2,1)S(1)} %pad_maximum_fusion), channel_id=1, source_target_pairs={{0,16},{4,12},{8,24},{12,4},{16,0},{20,28},{24,8},{28,20},{1,17},{... | collective-permute-start | bytes 1327112 | tf_op jit(solution)/shard_map/ppermute | solution.py:108
  51.6 15.9 %copy-start.2 = (f32[3,3,1152]{2,1,0:T(4,128)S(1)}, f32[3,3,1152]{2,1,0:T(4,128)}, u32[]{:S(2)}) copy-start(f32[3,3,1152]{2,1,0:T(4,128)} %refs_6_.1) | copy-start | bytes 124420
  52.0 10.3 %collective-permute-start.15 = (bf16[9,32,128]{2,1,0:T(8,128)(2,1)S(1)}, bf16[9,32,128]{2,1,0:T(8,128)(2,1)S(1)}, u32[]{:S(2)}, u32[]{:S(2)}) collective-permute-start(bf16[9,32,128]{2,1,0:T(8,128)(2,1)S(1)} %get-tuple-element.46.total_ref), channel_id=1, source_target_pairs={{0,8},{4,12},{8,0},{12,4},{16,24},{20,28},{24,16},{28,20},{1,9},{5... | collective-permute-start | bytes 221192 | tf_op jit(solution)/shard_map/ppermute | solution.py:108
  62.4 4.8 %collective-permute-start.16 = (bf16[9,32,128]{2,1,0:T(8,128)(2,1)S(1)}, bf16[9,32,128]{2,1,0:T(8,128)(2,1)S(1)}, u32[]{:S(2)}, u32[]{:S(2)}) collective-permute-start(bf16[9,32,128]{2,1,0:T(8,128)(2,1)S(1)} %get-tuple-element.48), channel_id=1, source_target_pairs={{0,16},{4,20},{8,24},{12,28},{1,17},{5,21},{9,25},{13,29},{2,18},{... | collective-permute-start | bytes 221192 | tf_op jit(solution)/shard_map/ppermute | solution.py:571
  67.3 2.6 %copy-start.1 = (bf16[288,1152]{1,0:T(8,128)(2,1)S(1)}, bf16[288,1152]{1,0:T(8,128)(2,1)}, u32[]{:S(2)}) copy-start(bf16[288,1152]{1,0:T(8,128)(2,1)} %refs_2_.3) | copy-start | bytes 1990660
  67.3 2.5 %collective-permute-start.17 = (bf16[6,64,1152]{2,1,0:T(8,128)(2,1)S(1)}, bf16[6,64,1152]{2,1,0:T(8,128)(2,1)S(1)}, u32[]{:S(2)}, u32[]{:S(2)}) collective-permute-start(bf16[6,64,1152]{2,1,0:T(8,128)(2,1)S(1)} %constant_dynamic-update-slice_fusion.9.refs_5_), channel_id=1, source_target_pairs={{0,4},{4,0},{8,12},{12,8},{16,20},{20,16},{24,28},{28,24},{1,5},{5... | collective-permute-start | bytes 2654216 | tf_op jit(solution)/shard_map/ppermute | solution.py:108
  67.4 4.7 %collective-permute-start.18 = (bf16[9,32,128]{2,1,0:T(8,128)(2,1)S(1)}, bf16[9,32,128]{2,1,0:T(8,128)(2,1)S(1)}, u32[]{:S(2)}, u32[]{:S(2)}) collective-permute-start(bf16[9,32,128]{2,1,0:T(8,128)(2,1)S(1)} %convert_add_fusion.1), channel_id=1, source_target_pairs={{0,1},{1,0},{2,3},{3,2},{4,5},{5,4},{6,7},{7,6},{8,9},{9,8},{10,11... | collective-permute-start | bytes 221192 | tf_op jit(solution)/shard_map/ppermute | solution.py:590
  68.4 3.8 %copy-start.4 = (f32[1152]{0:T(1024)S(1)}, f32[1152]{0:T(1024)}, u32[]{:S(2)}) copy-start(f32[1152]{0:T(1024)} %param.9) | copy-start | bytes 13828
  72.1 7.0 %collective-permute-start.19 = (bf16[9,32,128]{2,1,0:T(8,128)(2,1)S(1)}, bf16[9,32,128]{2,1,0:T(8,128)(2,1)S(1)}, u32[]{:S(2)}, u32[]{:S(2)}) collective-permute-start(bf16[9,32,128]{2,1,0:T(8,128)(2,1)S(1)} %add_convert_fusion), channel_id=1, source_target_pairs={{0,3},{1,2},{2,1},{3,0},{4,7},{5,6},{6,5},{7,4},{8,11},{9,10},{10,... | collective-permute-start | bytes 221192 | tf_op jit(solution)/shard_map/ppermute | solution.py:593
  72.2 7.1 %collective-permute-start.20 = (bf16[1,64,1152]{2,1,0:T(8,128)(2,1)S(1)}, bf16[1,64,1152]{2,1,0:T(8,128)(2,1)S(1)}, u32[]{:S(2)}, u32[]{:S(2)}) collective-permute-start(bf16[1,64,1152]{2,1,0:T(8,128)(2,1)S(1)} %get-tuple-element.59), channel_id=1, source_target_pairs={{0,1},{1,0},{2,3},{3,2},{4,5},{5,4},{6,7},{7,6},{8,9},{9,8},{10,11... | collective-permute-start | bytes 442376 | tf_op jit(solution)/shard_map/ppermute | solution.py:595
  72.6 6.7 %collective-permute-start.21 = (bf16[1,64,1152]{2,1,0:T(8,128)(2,1)S(1)}, bf16[1,64,1152]{2,1,0:T(8,128)(2,1)S(1)}, u32[]{:S(2)}, u32[]{:S(2)}) collective-permute-start(bf16[1,64,1152]{2,1,0:T(8,128)(2,1)S(1)} %get-tuple-element.60), channel_id=1, source_target_pairs={{1,2},{2,1},{5,6},{6,5},{9,10},{10,9},{13,14},{14,13},{17,18},{18,... | collective-permute-start | bytes 442376 | tf_op jit(solution)/shard_map/ppermute | solution.py:598

commit v15 on v11

--- a/solution.py
+++ b/solution.py
@@ -10,6 +10,7 @@
 HEADS = 36
 HEAD_DIM = 32
 LANES = 128
+WIDE = 2 * LANES
 MAIN = 64
 REST = 16
 STEPS = (1, 2, 3)
@@ -267,9 +268,8 @@
     _, x, core = coordinates()
     count, depth = tokens_ref.shape
     floor = jnp.where(core == 0, 0.0, -jnp.inf).astype(jnp.float32)
-    width = 3 * LANES
-
-    for at in range(0, depth, width):
+    for at in range(0, depth, WIDE):
+        width = min(WIDE, depth - at)
         lanes = slice(at, at + width)
 
         def slot(k, low, high):
@@ -407,7 +407,6 @@
     steps = len(STEPS)
     rest_at = ours_ref.shape[0] - 2 * steps * REST
     places = chip_places(y, x)
-    width = 3 * LANES
 
     def block(of_core, index, lanes):
         pack, k = index
@@ -421,8 +420,8 @@
     def put(row, value, lanes):
         weight_ref[pl.ds(pl.multiple_of(row, REST), value.shape[0]), lanes] = value
 
-    for at in range(0, depth, width):
-        lanes = slice(at, at + width)
+    for at in range(0, depth, WIDE):
+        lanes = slice(at, min(at + WIDE, depth))
         order = [(0, 2 * k) for k in range(steps)] + [(1, k) for k in range(2 * steps)]
         order += [(0, 2 * k + 1) for k in range(steps)]
         columns = [qkv_ref[:, lanes]] + [block(0, k, lanes) for k in order] + [rest(0, lanes)]
@@ -488,9 +487,8 @@
             [mixture[:columns] + above, middle, mixture[count - columns :] + below], axis=0
         )
         mixture_ref[:, lanes] = mixture.astype(jnp.bfloat16)
-    width = 3 * LANES
-    for at in range(0, depth, width):
-        lanes = slice(at, at + width)
+    for at in range(0, depth, WIDE):
+        lanes = slice(at, min(at + WIDE, depth))
         product = jnp.dot(
             mixture_ref[...], weight_ref[:, lanes], preferred_element_type=jnp.float32
         )

time: 77.8 us -> 77.4 us (level)
  transfers between devices with their start and end apart: 23 -> 23, of which waited for: 14 -> 14; matrix products, arithmetic and copies ran while one was open for 1% -> 1% of each run, Pallas kernels for 9% -> 8%
where the time goes in v15:
time: 77.4 us; the launch traced here: 76 us
  waiting for transfers between devices  41 us (53%)
  starting transfers between devices  23.7 us (31%)
  Pallas kernels  10.4 us (13%)
    ppermute x6, waiting for transfers between devices, shifted(): lax.ppermute(value, 'space', [(i, (i + step) % count) for i in range(coun...  22.3 us
    ppermute x10, waiting for transfers between devices, flipped(): lax.ppermute(value, 'tm', [(t, t ^ bit_on_core[t % 2]) for t in range(8)])  11.5 us
    pallas_call x7, Pallas kernels, kernel_call(): pl.pallas_call(body, out_shape=outputs, in_specs=in_specs, out_specs=jax....  10.4 us
    ppermute x6, starting transfers between devices, shifted(): lax.ppermute(value, 'space', [(i, (i + step) % count) for i in range(coun...  9.05 us
    ppermute x10, starting transfers between devices, flipped(): lax.ppermute(value, 'tm', [(t, t ^ bit_on_core[t % 2]) for t in range(8)])  7.06 us
    ppermute x3, starting transfers between devices, plane_form(): upto = upto + lax.ppermute(total, 'tm', pairs).astype(jnp.float32)  6.48 us
    ppermute x1, waiting for transfers between devices, plane_form(): lax.ppermute(share, 'space', [(i, count - 1 - i) for i in range(count)])  5.94 us
  transfers between devices with their start and end apart: 23, of which 14 were waited for; matrix products, arithmetic and copies ran while one was open for 1% of the time, Pallas kernels for 8%

profile of v15, /device:TPU:0, one launch (start us, length us, event | category | flops | bytes accessed | tf_op | source)
XLA Modules:
  0.0 76.0 jit_solution(9436428664170520361)
XLA Ops:
  0.0 1.9 %shard_map.55 = (bf16[80,1152]{1,0:T(8,128)(2,1)}, bf16[2,64,1152]{2,1,0:T(8,128)(2,1)}) custom-call(bf16[288,3456]{1,0:T(8,128)(2,1)} %refs_1_.1, bf16[288,1152]{1,0:T(8,128)(2,1)} %refs_2_.3), custom_call_target="tpu_custom_call" | custom-call | bytes 958464 | tf_op jit(solution)/shard_map/pallas_call | solution.py:165
  2.0 3.1 %collective-permute-start = (bf16[1,80,1152]{2,1,0:T(8,128)(2,1)}, bf16[1,80,1152]{2,1,0:T(8,128)(2,1)S(1)}, u32[]{:S(2)}, u32[]{:S(2)}) collective-permute-start(bf16[1,80,1152]{2,1,0:T(8,128)(2,1)} %bitcast.8), channel_id=1, source_target_pairs={{0,1},{1,2},{2,3},{3,0},{4,5},{5,6},{6,7},{7,4},{8,9},{9,10},{10,1... | collective-permute-start | bytes 552968 | tf_op jit(solution)/shard_map/ppermute | solution.py:105
  5.0 2.1 %collective-permute-start.1 = (bf16[1,80,1152]{2,1,0:T(8,128)(2,1)}, bf16[1,80,1152]{2,1,0:T(8,128)(2,1)S(1)}, u32[]{:S(2)}, u32[]{:S(2)}) collective-permute-start(bf16[1,80,1152]{2,1,0:T(8,128)(2,1)} %bitcast.9), channel_id=1, source_target_pairs={{0,3},{1,0},{2,1},{3,2},{4,7},{5,4},{6,5},{7,6},{8,11},{9,8},{10,9... | collective-permute-start | bytes 552968 | tf_op jit(solution)/shard_map/ppermute | solution.py:105
  7.1 0.0 copy-done.3
  7.1 1.2 %shard_map.56.refs_0_ = bf16[256,1152]{1,0:T(8,128)(2,1)S(1)} custom-call(bf16[256,1152]{1,0:T(8,128)(2,1)S(1)} %bitcast.7), custom_call_target="tpu_custom_call" | custom-call | flops 679477248 | bytes 589824 | tf_op jit(solution)/shard_map/pallas_call | solution.py:165
  8.3 0.0 copy-start
  8.3 0.1 collective-permute-start.10
  8.4 4.4 %collective-permute-done = bf16[1,80,1152]{2,1,0:T(8,128)(2,1)S(1)} collective-permute-done((bf16[1,80,1152]{2,1,0:T(8,128)(2,1)}, bf16[1,80,1152]{2,1,0:T(8,128)(2,1)S(1)}, u32[]{:S(2)}, u32[]{:S(2)}) %collective-permute-start) | collective-permute-done | bytes 184352 | tf_op jit(solution)/shard_map/ppermute | solution.py:105
  12.8 2.5 %collective-permute-done.1 = bf16[1,80,1152]{2,1,0:T(8,128)(2,1)S(1)} collective-permute-done((bf16[1,80,1152]{2,1,0:T(8,128)(2,1)}, bf16[1,80,1152]{2,1,0:T(8,128)(2,1)S(1)}, u32[]{:S(2)}, u32[]{:S(2)}) %collective-permute-start.1) | collective-permute-done | bytes 184352 | tf_op jit(solution)/shard_map/ppermute | solution.py:105
  15.3 1.6 %collective-permute-start.11 = (bf16[2,80,1152]{2,1,0:T(8,128)(2,1)S(1)}, bf16[2,80,1152]{2,1,0:T(8,128)(2,1)S(1)}, u32[]{:S(2)}, u32[]{:S(2)}) collective-permute-start(bf16[2,80,1152]{2,1,0:T(8,128)(2,1)S(1)} %constant_dynamic-update-slice_fusion.5), channel_id=1, source_target_pairs={{0,8},{4,20},{8,0},{12,28},{16,24},{20,4},{24,16},{28,12},{1,9},{5... | collective-permute-start | bytes 1105928 | tf_op jit(solution)/shard_map/ppermute | solution.py:109
  16.9 1.1 %collective-permute-start.3 = (bf16[1,80,1152]{2,1,0:T(8,128)(2,1)S(1)}, bf16[1,80,1152]{2,1,0:T(8,128)(2,1)S(1)}, u32[]{:S(2)}, u32[]{:S(2)}) collective-permute-start(bf16[1,80,1152]{2,1,0:T(8,128)(2,1)S(1)} %collective-permute-done), channel_id=1, source_target_pairs={{0,1},{1,2},{2,3},{3,0},{4,5},{5,6},{6,7},{7,4},{8,9},{9,10},{10,1... | collective-permute-start | bytes 552968 | tf_op jit(solution)/shard_map/ppermute | solution.py:105
  18.0 0.0 copy-done.5
  18.0 0.7 collective-permute-start.2
  18.8 7.5 %collective-permute-done.3 = bf16[1,80,1152]{2,1,0:T(8,128)(2,1)S(1)} collective-permute-done((bf16[1,80,1152]{2,1,0:T(8,128)(2,1)S(1)}, bf16[1,80,1152]{2,1,0:T(8,128)(2,1)S(1)}, u32[]{:S(2)}, u32[]{:S(2)}) %collective-permute-start.3) | collective-permute-done | bytes 184352 | tf_op jit(solution)/shard_map/ppermute | solution.py:105
  26.3 0.4 collective-permute-start.4
  26.7 0.0 collective-permute-done.11
  26.7 0.0 collective-permute-done.10.refs_1_
  26.8 1.7 %collective-permute-start.12 = (bf16[4,80,1152]{2,1,0:T(8,128)(2,1)S(1)}, bf16[4,80,1152]{2,1,0:T(8,128)(2,1)S(1)}, u32[]{:S(2)}, u32[]{:S(2)}) collective-permute-start(bf16[4,80,1152]{2,1,0:T(8,128)(2,1)S(1)} %constant_dynamic-update-slice_fusion.7.refs_3_), channel_id=1, source_target_pairs={{0,16},{4,12},{8,24},{12,4},{16,0},{20,28},{24,8},{28,20},{1,17},{... | collective-permute-start | bytes 2211848 | tf_op jit(solution)/shard_map/ppermute | solution.py:109
  28.5 5.3 %collective-permute-done.4 = bf16[1,80,1152]{2,1,0:T(8,128)(2,1)S(1)} collective-permute-done((bf16[1,80,1152]{2,1,0:T(8,128)(2,1)S(1)}, bf16[1,80,1152]{2,1,0:T(8,128)(2,1)S(1)}, u32[]{:S(2)}, u32[]{:S(2)}) %collective-permute-start.4) | collective-permute-done | bytes 184352 | tf_op jit(solution)/shard_map/ppermute | solution.py:109
  33.9 1.6 %collective-permute-start.13 = (bf16[2,80,1152]{2,1,0:T(8,128)(2,1)S(1)}, bf16[2,80,1152]{2,1,0:T(8,128)(2,1)S(1)}, u32[]{:S(2)}, u32[]{:S(2)}) collective-permute-start(bf16[2,80,1152]{2,1,0:T(8,128)(2,1)S(1)} %constant_dynamic-update-slice_fusion.refs_5_), channel_id=1, source_target_pairs={{0,16},{4,12},{8,24},{12,4},{16,0},{20,28},{24,8},{28,20},{1,17},{... | collective-permute-start | bytes 1105928 | tf_op jit(solution)/shard_map/ppermute | solution.py:109
  35.4 0.1 collective-permute-start.6
  35.6 0.0 collective-permute-done.2
  35.6 1.9 %collective-permute-start.5 = (bf16[2,64,1152]{2,1,0:T(8,128)(2,1)S(1)}, bf16[2,64,1152]{2,1,0:T(8,128)(2,1)S(1)}, u32[]{:S(2)}, u32[]{:S(2)}) collective-permute-start(bf16[2,64,1152]{2,1,0:T(8,128)(2,1)S(1)} %collective-permute-done.2), channel_id=1, source_target_pairs={{0,1},{1,2},{2,3},{3,0},{4,5},{5,6},{6,7},{7,4},{8,9},{9,10},{10,1... | collective-permute-start | bytes 884744 | tf_op jit(solution)/shard_map/ppermute | solution.py:105
  37.5 7.9 %collective-permute-done.6 = bf16[2,64,1152]{2,1,0:T(8,128)(2,1)S(1)} collective-permute-done((bf16[2,64,1152]{2,1,0:T(8,128)(2,1)S(1)}, bf16[2,64,1152]{2,1,0:T(8,128)(2,1)S(1)}, u32[]{:S(2)}, u32[]{:S(2)}) %collective-permute-start.6) | collective-permute-done | bytes 294944 | tf_op jit(solution)/shard_map/ppermute | solution.py:105
  45.3 0.0 collective-permute-done.13.refs_6_
  45.3 0.0 collective-permute-done.12.refs_4_
  45.3 0.0 copy-done
  45.3 1.9 %shard_map.57.mine_ref.refs_7_ = bf16[608,1152]{1,0:T(8,128)(2,1)S(1)} custom-call(bf16[256,1152]{1,0:T(8,128)(2,1)S(1)} %shard_map.56.refs_0_, bf16[256,1152]{1,0:T(8,128)(2,1)S(1)} %collective-permute-done.10.refs_1_, bf16[288,3456]{1,0:T(8,128)(2,1)S(1)} %copy-done, bf16[4,80,1152]{2,1,0:T(8,128)(2,1)S(1)} %constant_dynamic-update-slice_fusion.7.refs_3_, ...), custom_call_target="tpu_custom_call" | custom-call | flops 1358954496 | bytes 2654208 | tf_op jit(solution)/shard_map/pallas_call | solution.py:165
  47.2 0.0 collective-permute-done.5
  47.2 0.1 collective-permute-start.14
  47.4 0.6 collective-permute-start.7
  48.0 0.1 pad_maximum_fusion
  48.1 0.6 collective-permute-start.8
  48.7 0.4 collective-permute-start.9
  49.1 1.3 %collective-permute-done.14.other_ref.refs_8_ = bf16[608,1152]{1,0:T(8,128)(2,1)S(1)} collective-permute-done((bf16[608,1152]{1,0:T(8,128)(2,1)S(1)}, bf16[608,1152]{1,0:T(8,128)(2,1)S(1)}, u32[]{:S(2)}, u32[]{:S(2)}) %collective-permute-start.14) | collective-permute-done | bytes 1400864 | tf_op jit(solution)/shard_map/ppermute | solution.py:109
  50.4 0.8 %shard_map.58 = (bf16[256,1152]{1,0:T(8,128)(2,1)S(1)}, bf16[1,64,1152]{2,1,0:T(8,128)(2,1)S(1)}, bf16[1,64,1152]{2,1,0:T(8,128)(2,1)S(1)}, f32[9,32,128]{2,1,0:T(8,128)S(1)}, bf16[9,32,128]{2,1,0:T(8,128)(2,1)S(1)}) custom-call(bf16[608,1152]{1,0:T(8,128)(2,1)S(1)} %shard_map.57.mine_ref.refs_7_, bf16[608,1152]{1,0:T(8,128)(2,1)S(1)} %collective-permute-done.14.other_ref.refs_8_), custom_call_target="tpu_custom_call" | custom-call | flops 150994944 | bytes 2359296 | tf_op jit(solution)/shard_map/pallas_call | solution.py:165
  51.3 0.0 copy-start.2
  51.3 0.4 collective-permute-done.7.refs_4_
  51.7 2.4 %collective-permute-start.15 = (bf16[9,32,128]{2,1,0:T(8,128)(2,1)S(1)}, bf16[9,32,128]{2,1,0:T(8,128)(2,1)S(1)}, u32[]{:S(2)}, u32[]{:S(2)}) collective-permute-start(bf16[9,32,128]{2,1,0:T(8,128)(2,1)S(1)} %get-tuple-element.43), channel_id=1, source_target_pairs={{0,8},{4,12},{16,24},{20,28},{1,9},{5,13},{17,25},{21,29},{2,10},{... | collective-permute-start | bytes 221192 | tf_op jit(solution)/shard_map/ppermute | solution.py:549
  54.2 2.8 %collective-permute-start.16 = (bf16[9,32,128]{2,1,0:T(8,128)(2,1)S(1)}, bf16[9,32,128]{2,1,0:T(8,128)(2,1)S(1)}, u32[]{:S(2)}, u32[]{:S(2)}) collective-permute-start(bf16[9,32,128]{2,1,0:T(8,128)(2,1)S(1)} %get-tuple-element.43), channel_id=1, source_target_pairs={{0,16},{4,20},{8,24},{12,28},{1,17},{5,21},{9,25},{13,29},{2,18},{... | collective-permute-start | bytes 221192 | tf_op jit(solution)/shard_map/ppermute | solution.py:549
  56.9 1.3 %collective-permute-start.17 = (bf16[9,32,128]{2,1,0:T(8,128)(2,1)S(1)}, bf16[9,32,128]{2,1,0:T(8,128)(2,1)S(1)}, u32[]{:S(2)}, u32[]{:S(2)}) collective-permute-start(bf16[9,32,128]{2,1,0:T(8,128)(2,1)S(1)} %get-tuple-element.43), channel_id=1, source_target_pairs={{0,24},{4,28},{8,16},{12,20},{1,25},{5,29},{9,17},{13,21},{2,26},{... | collective-permute-start | bytes 221192 | tf_op jit(solution)/shard_map/ppermute | solution.py:549
  58.2 2.9 %collective-permute-done.8 = bf16[3,64,1152]{2,1,0:T(8,128)(2,1)S(1)} collective-permute-done((bf16[3,64,1152]{2,1,0:T(8,128)(2,1)S(1)}, bf16[3,64,1152]{2,1,0:T(8,128)(2,1)S(1)}, u32[]{:S(2)}, u32[]{:S(2)}) %collective-permute-start.8) | collective-permute-done | bytes 442400 | tf_op jit(solution)/shard_map/ppermute | solution.py:109
  61.2 0.0 collective-permute-done.9
  61.2 0.0 copy-start.1
  61.3 0.0 collective-permute-done.15
  61.3 0.2 collective-permute-done.16
  61.5 0.1 collective-permute-done.17
  61.6 0.1 collective-permute-start.18
  61.7 0.1 collective-permute-start.19
  61.8 0.0 copy-done.2
  61.8 0.9 %shard_map.60 = f32[4,64,1152]{2,1,0:T(8,128)S(1)} custom-call(bf16[4,64,1152]{2,1,0:T(8,128)(2,1)S(1)} %bitcast.6, f32[3,3,1152]{2,1,0:T(4,128)S(1)} %copy-done.2), custom_call_target="tpu_custom_call" | custom-call | flops 5308416 | bytes 1769472 | tf_op jit(solution)/shard_map/pallas_call | solution.py:165
  62.7 0.0 copy-start.4
  62.7 1.4 %collective-permute-done.18.refs_6_ = bf16[6,64,1152]{2,1,0:T(8,128)(2,1)S(1)} collective-permute-done((bf16[6,64,1152]{2,1,0:T(8,128)(2,1)S(1)}, bf16[6,64,1152]{2,1,0:T(8,128)(2,1)S(1)}, u32[]{:S(2)}, u32[]{:S(2)}) %collective-permute-start.18) | collective-permute-done | bytes 884768 | tf_op jit(solution)/shard_map/ppermute | solution.py:109
  64.1 0.0 copy-done.1
  64.1 1.4 %shard_map.59 = (bf16[256,1152]{1,0:T(8,128)(2,1)S(1)}, bf16[1152,1152]{1,0:T(8,128)(2,1)S(1)}) custom-call(bf16[256,1152]{1,0:T(8,128)(2,1)S(1)} %shard_map.56.refs_0_, bf16[288,3456]{1,0:T(8,128)(2,1)S(1)} %copy-done, bf16[288,1152]{1,0:T(8,128)(2,1)S(1)} %copy-done.1, bf16[6,64,1152]{2,1,0:T(8,128)(2,1)S(1)} %constant_dynamic-update-slice_fusion.2.refs_3_, ...), custom_call_target="tpu_custom_call" | custom-call | flops 679477248 | bytes 5308416 | tf_op jit(solution)/shard_map/pallas_call | solution.py:165
  65.5 0.9 %collective-permute-done.19 = bf16[9,32,128]{2,1,0:T(8,128)(2,1)S(1)} collective-permute-done((bf16[9,32,128]{2,1,0:T(8,128)(2,1)S(1)}, bf16[9,32,128]{2,1,0:T(8,128)(2,1)S(1)}, u32[]{:S(2)}, u32[]{:S(2)}) %collective-permute-start.19) | collective-permute-done | bytes 73760 | tf_op jit(solution)/shard_map/ppermute | solution.py:568
  66.4 0.1 collective-permute-start.20
  66.5 0.0 copy-done.4
  66.5 0.3 collective-permute-start.21
  66.9 0.7 collective-permute-start.22
  67.5 5.9 %collective-permute-done.20 = bf16[9,32,128]{2,1,0:T(8,128)(2,1)S(1)} collective-permute-done((bf16[9,32,128]{2,1,0:T(8,128)(2,1)S(1)}, bf16[9,32,128]{2,1,0:T(8,128)(2,1)S(1)}, u32[]{:S(2)}, u32[]{:S(2)}) %collective-permute-start.20) | collective-permute-done | bytes 73760 | tf_op jit(solution)/shard_map/ppermute | solution.py:571
  73.5 0.1 collective-permute-done.21.refs_4_
  73.6 0.0 collective-permute-done.22.refs_5_
  73.6 2.4 %shard_map.61 = bf16[256,1152]{1,0:T(8,128)(2,1)} custom-call(bf16[256,1152]{1,0:T(8,128)(2,1)S(1)} %get-tuple-element.48.refs_0_, bf16[1152,1152]{1,0:T(8,128)(2,1)S(1)} %get-tuple-element.49.refs_1_, f32[9,32,128]{2,1,0:T(8,128)S(1)} %convert_add_fusion.refs_2_, f32[256,1152]{1,0:T(8,128)S(1)} %bitcast.5, ...), custom_call_target="tpu_custom_call" | custom-call | flops 679477248 | bytes 2654208 | tf_op jit(solution)/shard_map/pallas_call | solution.py:165
  (20 shorter events, 0.4 us)
Async XLA Ops:
  0.0 7.1 %copy-start.3 = (bf16[1,4,64,1152]{3,2,1,0:T(8,128)(2,1)S(1)}, bf16[1,4,64,1152]{3,2,1,0:T(8,128)(2,1)}, u32[]{:S(2)}) copy-start(bf16[1,4,64,1152]{3,2,1,0:T(8,128)(2,1)} %param.5) | copy-start | bytes 1769476
  2.0 10.8 %collective-permute-start = (bf16[1,80,1152]{2,1,0:T(8,128)(2,1)}, bf16[1,80,1152]{2,1,0:T(8,128)(2,1)S(1)}, u32[]{:S(2)}, u32[]{:S(2)}) collective-permute-start(bf16[1,80,1152]{2,1,0:T(8,128)(2,1)} %bitcast.8), channel_id=1, source_target_pairs={{0,1},{1,2},{2,3},{3,0},{4,5},{5,6},{6,7},{7,4},{8,9},{9,10},{10,1... | collective-permute-start | bytes 552968 | tf_op jit(solution)/shard_map/ppermute | solution.py:105
  5.0 10.3 %collective-permute-start.1 = (bf16[1,80,1152]{2,1,0:T(8,128)(2,1)}, bf16[1,80,1152]{2,1,0:T(8,128)(2,1)S(1)}, u32[]{:S(2)}, u32[]{:S(2)}) collective-permute-start(bf16[1,80,1152]{2,1,0:T(8,128)(2,1)} %bitcast.9), channel_id=1, source_target_pairs={{0,3},{1,0},{2,1},{3,2},{4,7},{5,4},{6,5},{7,6},{8,11},{9,8},{10,9... | collective-permute-start | bytes 552968 | tf_op jit(solution)/shard_map/ppermute | solution.py:105
  7.1 10.9 %copy-start.5 = (bf16[2,64,1152]{2,1,0:T(8,128)(2,1)S(1)}, bf16[2,64,1152]{2,1,0:T(8,128)(2,1)}, u32[]{:S(2)}) copy-start(bf16[2,64,1152]{2,1,0:T(8,128)(2,1)} %get-tuple-element.36) | copy-start | bytes 884740
  8.3 37.0 %copy-start = (bf16[288,3456]{1,0:T(8,128)(2,1)S(1)}, bf16[288,3456]{1,0:T(8,128)(2,1)}, u32[]{:S(2)}) copy-start(bf16[288,3456]{1,0:T(8,128)(2,1)} %refs_1_.1) | copy-start | bytes 5971972
  8.3 18.4 %collective-permute-start.10 = (bf16[256,1152]{1,0:T(8,128)(2,1)S(1)}, bf16[256,1152]{1,0:T(8,128)(2,1)S(1)}, u32[]{:S(2)}, u32[]{:S(2)}) collective-permute-start(bf16[256,1152]{1,0:T(8,128)(2,1)S(1)} %shard_map.56.refs_0_), channel_id=1, source_target_pairs={{0,4},{4,0},{8,12},{12,8},{16,20},{20,16},{24,28},{28,24},{1,5},{5... | collective-permute-start | bytes 1769480 | tf_op jit(solution)/shard_map/ppermute | solution.py:109
  15.3 11.4 %collective-permute-start.11 = (bf16[2,80,1152]{2,1,0:T(8,128)(2,1)S(1)}, bf16[2,80,1152]{2,1,0:T(8,128)(2,1)S(1)}, u32[]{:S(2)}, u32[]{:S(2)}) collective-permute-start(bf16[2,80,1152]{2,1,0:T(8,128)(2,1)S(1)} %constant_dynamic-update-slice_fusion.5), channel_id=1, source_target_pairs={{0,8},{4,20},{8,0},{12,28},{16,24},{20,4},{24,16},{28,12},{1,9},{5... | collective-permute-start | bytes 1105928 | tf_op jit(solution)/shard_map/ppermute | solution.py:109
  16.9 9.4 %collective-permute-start.3 = (bf16[1,80,1152]{2,1,0:T(8,128)(2,1)S(1)}, bf16[1,80,1152]{2,1,0:T(8,128)(2,1)S(1)}, u32[]{:S(2)}, u32[]{:S(2)}) collective-permute-start(bf16[1,80,1152]{2,1,0:T(8,128)(2,1)S(1)} %collective-permute-done), channel_id=1, source_target_pairs={{0,1},{1,2},{2,3},{3,0},{4,5},{5,6},{6,7},{7,4},{8,9},{9,10},{10,1... | collective-permute-start | bytes 552968 | tf_op jit(solution)/shard_map/ppermute | solution.py:105
  18.0 17.6 %collective-permute-start.2 = (bf16[2,64,1152]{2,1,0:T(8,128)(2,1)S(1)}, bf16[2,64,1152]{2,1,0:T(8,128)(2,1)S(1)}, u32[]{:S(2)}, u32[]{:S(2)}) collective-permute-start(bf16[2,64,1152]{2,1,0:T(8,128)(2,1)S(1)} %copy-done.5), channel_id=1, source_target_pairs={{0,1},{1,2},{2,3},{3,0},{4,5},{5,6},{6,7},{7,4},{8,9},{9,10},{10,1... | collective-permute-start | bytes 884744 | tf_op jit(solution)/shard_map/ppermute | solution.py:105
  26.3 7.6 %collective-permute-start.4 = (bf16[1,80,1152]{2,1,0:T(8,128)(2,1)S(1)}, bf16[1,80,1152]{2,1,0:T(8,128)(2,1)S(1)}, u32[]{:S(2)}, u32[]{:S(2)}) collective-permute-start(bf16[1,80,1152]{2,1,0:T(8,128)(2,1)S(1)} %collective-permute-done.3), channel_id=1, source_target_pairs={{0,8},{4,20},{8,0},{12,28},{16,24},{20,4},{24,16},{28,12},{1,9},{5... | collective-permute-start | bytes 552968 | tf_op jit(solution)/shard_map/ppermute | solution.py:109
  26.8 18.5 %collective-permute-start.12 = (bf16[4,80,1152]{2,1,0:T(8,128)(2,1)S(1)}, bf16[4,80,1152]{2,1,0:T(8,128)(2,1)S(1)}, u32[]{:S(2)}, u32[]{:S(2)}) collective-permute-start(bf16[4,80,1152]{2,1,0:T(8,128)(2,1)S(1)} %constant_dynamic-update-slice_fusion.7.refs_3_), channel_id=1, source_target_pairs={{0,16},{4,12},{8,24},{12,4},{16,0},{20,28},{24,8},{28,20},{1,17},{... | collective-permute-start | bytes 2211848 | tf_op jit(solution)/shard_map/ppermute | solution.py:109
  33.9 11.5 %collective-permute-start.13 = (bf16[2,80,1152]{2,1,0:T(8,128)(2,1)S(1)}, bf16[2,80,1152]{2,1,0:T(8,128)(2,1)S(1)}, u32[]{:S(2)}, u32[]{:S(2)}) collective-permute-start(bf16[2,80,1152]{2,1,0:T(8,128)(2,1)S(1)} %constant_dynamic-update-slice_fusion.refs_5_), channel_id=1, source_target_pairs={{0,16},{4,12},{8,24},{12,4},{16,0},{20,28},{24,8},{28,20},{1,17},{... | collective-permute-start | bytes 1105928 | tf_op jit(solution)/shard_map/ppermute | solution.py:109
  35.4 9.9 %collective-permute-start.6 = (bf16[2,64,1152]{2,1,0:T(8,128)(2,1)S(1)}, bf16[2,64,1152]{2,1,0:T(8,128)(2,1)S(1)}, u32[]{:S(2)}, u32[]{:S(2)}) collective-permute-start(bf16[2,64,1152]{2,1,0:T(8,128)(2,1)S(1)} %copy-done.5), channel_id=1, source_target_pairs={{0,3},{1,0},{2,1},{3,2},{4,7},{5,4},{6,5},{7,6},{8,11},{9,8},{10,9... | collective-permute-start | bytes 884744 | tf_op jit(solution)/shard_map/ppermute | solution.py:105
  35.6 11.6 %collective-permute-start.5 = (bf16[2,64,1152]{2,1,0:T(8,128)(2,1)S(1)}, bf16[2,64,1152]{2,1,0:T(8,128)(2,1)S(1)}, u32[]{:S(2)}, u32[]{:S(2)}) collective-permute-start(bf16[2,64,1152]{2,1,0:T(8,128)(2,1)S(1)} %collective-permute-done.2), channel_id=1, source_target_pairs={{0,1},{1,2},{2,3},{3,0},{4,5},{5,6},{6,7},{7,4},{8,9},{9,10},{10,1... | collective-permute-start | bytes 884744 | tf_op jit(solution)/shard_map/ppermute | solution.py:105
  47.2 3.2 %collective-permute-start.14 = (bf16[608,1152]{1,0:T(8,128)(2,1)S(1)}, bf16[608,1152]{1,0:T(8,128)(2,1)S(1)}, u32[]{:S(2)}, u32[]{:S(2)}) collective-permute-start(bf16[608,1152]{1,0:T(8,128)(2,1)S(1)} %shard_map.57.mine_ref.refs_7_), channel_id=1, source_target_pairs={{0,4},{4,0},{8,12},{12,8},{16,20},{20,16},{24,28},{28,24},{1,5},{5... | collective-permute-start | bytes 4202504 | tf_op jit(solution)/shard_map/ppermute | solution.py:109
  47.4 4.3 %collective-permute-start.7 = (bf16[6,64,1152]{2,1,0:T(8,128)(2,1)S(1)}, bf16[6,64,1152]{2,1,0:T(8,128)(2,1)S(1)}, u32[]{:S(2)}, u32[]{:S(2)}) collective-permute-start(bf16[6,64,1152]{2,1,0:T(8,128)(2,1)S(1)} %constant_dynamic-update-slice_fusion.2.refs_3_), channel_id=1, source_target_pairs={{0,4},{4,0},{8,12},{12,8},{16,20},{20,16},{24,28},{28,24},{1,5},{5... | collective-permute-start | bytes 2654216 | tf_op jit(solution)/shard_map/ppermute | solution.py:109
  48.1 13.1 %collective-permute-start.8 = (bf16[3,64,1152]{2,1,0:T(8,128)(2,1)S(1)}, bf16[3,64,1152]{2,1,0:T(8,128)(2,1)S(1)}, u32[]{:S(2)}, u32[]{:S(2)}) collective-permute-start(bf16[3,64,1152]{2,1,0:T(8,128)(2,1)S(1)} %pad_maximum_fusion), channel_id=1, source_target_pairs={{0,8},{4,20},{8,0},{12,28},{16,24},{20,4},{24,16},{28,12},{1,9},{5... | collective-permute-start | bytes 1327112 | tf_op jit(solution)/shard_map/ppermute | solution.py:109
  48.7 12.5 %collective-permute-start.9 = (bf16[3,64,1152]{2,1,0:T(8,128)(2,1)S(1)}, bf16[3,64,1152]{2,1,0:T(8,128)(2,1)S(1)}, u32[]{:S(2)}, u32[]{:S(2)}) collective-permute-start(bf16[3,64,1152]{2,1,0:T(8,128)(2,1)S(1)} %pad_maximum_fusion), channel_id=1, source_target_pairs={{0,16},{4,12},{8,24},{12,4},{16,0},{20,28},{24,8},{28,20},{1,17},{... | collective-permute-start | bytes 1327112 | tf_op jit(solution)/shard_map/ppermute | solution.py:109
  51.3 10.5 %copy-start.2 = (f32[3,3,1152]{2,1,0:T(4,128)S(1)}, f32[3,3,1152]{2,1,0:T(4,128)}, u32[]{:S(2)}) copy-start(f32[3,3,1152]{2,1,0:T(4,128)} %refs_6_.1) | copy-start | bytes 124420
  51.7 9.6 %collective-permute-start.15 = (bf16[9,32,128]{2,1,0:T(8,128)(2,1)S(1)}, bf16[9,32,128]{2,1,0:T(8,128)(2,1)S(1)}, u32[]{:S(2)}, u32[]{:S(2)}) collective-permute-start(bf16[9,32,128]{2,1,0:T(8,128)(2,1)S(1)} %get-tuple-element.43), channel_id=1, source_target_pairs={{0,8},{4,12},{16,24},{20,28},{1,9},{5,13},{17,25},{21,29},{2,10},{... | collective-permute-start | bytes 221192 | tf_op jit(solution)/shard_map/ppermute | solution.py:549
  54.2 7.3 %collective-permute-start.16 = (bf16[9,32,128]{2,1,0:T(8,128)(2,1)S(1)}, bf16[9,32,128]{2,1,0:T(8,128)(2,1)S(1)}, u32[]{:S(2)}, u32[]{:S(2)}) collective-permute-start(bf16[9,32,128]{2,1,0:T(8,128)(2,1)S(1)} %get-tuple-element.43), channel_id=1, source_target_pairs={{0,16},{4,20},{8,24},{12,28},{1,17},{5,21},{9,25},{13,29},{2,18},{... | collective-permute-start | bytes 221192 | tf_op jit(solution)/shard_map/ppermute | solution.py:549
  56.9 4.7 %collective-permute-start.17 = (bf16[9,32,128]{2,1,0:T(8,128)(2,1)S(1)}, bf16[9,32,128]{2,1,0:T(8,128)(2,1)S(1)}, u32[]{:S(2)}, u32[]{:S(2)}) collective-permute-start(bf16[9,32,128]{2,1,0:T(8,128)(2,1)S(1)} %get-tuple-element.43), channel_id=1, source_target_pairs={{0,24},{4,28},{8,16},{12,20},{1,25},{5,29},{9,17},{13,21},{2,26},{... | collective-permute-start | bytes 221192 | tf_op jit(solution)/shard_map/ppermute | solution.py:549
  61.2 2.9 %copy-start.1 = (bf16[288,1152]{1,0:T(8,128)(2,1)S(1)}, bf16[288,1152]{1,0:T(8,128)(2,1)}, u32[]{:S(2)}) copy-start(bf16[288,1152]{1,0:T(8,128)(2,1)} %refs_2_.3) | copy-start | bytes 1990660
  61.6 2.5 %collective-permute-start.18 = (bf16[6,64,1152]{2,1,0:T(8,128)(2,1)S(1)}, bf16[6,64,1152]{2,1,0:T(8,128)(2,1)S(1)}, u32[]{:S(2)}, u32[]{:S(2)}) collective-permute-start(bf16[6,64,1152]{2,1,0:T(8,128)(2,1)S(1)} %constant_dynamic-update-slice_fusion.9.refs_5_), channel_id=1, source_target_pairs={{0,4},{4,0},{8,12},{12,8},{16,20},{20,16},{24,28},{28,24},{1,5},{5... | collective-permute-start | bytes 2654216 | tf_op jit(solution)/shard_map/ppermute | solution.py:109
  61.7 4.7 %collective-permute-start.19 = (bf16[9,32,128]{2,1,0:T(8,128)(2,1)S(1)}, bf16[9,32,128]{2,1,0:T(8,128)(2,1)S(1)}, u32[]{:S(2)}, u32[]{:S(2)}) collective-permute-start(bf16[9,32,128]{2,1,0:T(8,128)(2,1)S(1)} %convert_add_fusion.1), channel_id=1, source_target_pairs={{0,1},{1,0},{2,3},{3,2},{4,5},{5,4},{6,7},{7,6},{8,9},{9,8},{10,11... | collective-permute-start | bytes 221192 | tf_op jit(solution)/shard_map/ppermute | solution.py:568
  62.7 3.8 %copy-start.4 = (f32[1152]{0:T(1024)S(1)}, f32[1152]{0:T(1024)}, u32[]{:S(2)}) copy-start(f32[1152]{0:T(1024)} %param.9) | copy-start | bytes 13828
  66.4 7.0 %collective-permute-start.20 = (bf16[9,32,128]{2,1,0:T(8,128)(2,1)S(1)}, bf16[9,32,128]{2,1,0:T(8,128)(2,1)S(1)}, u32[]{:S(2)}, u32[]{:S(2)}) collective-permute-start(bf16[9,32,128]{2,1,0:T(8,128)(2,1)S(1)} %add_convert_fusion), channel_id=1, source_target_pairs={{0,3},{1,2},{2,1},{3,0},{4,7},{5,6},{6,5},{7,4},{8,11},{9,10},{10,... | collective-permute-start | bytes 221192 | tf_op jit(solution)/shard_map/ppermute | solution.py:571
  66.5 7.1 %collective-permute-start.21 = (bf16[1,64,1152]{2,1,0:T(8,128)(2,1)S(1)}, bf16[1,64,1152]{2,1,0:T(8,128)(2,1)S(1)}, u32[]{:S(2)}, u32[]{:S(2)}) collective-permute-start(bf16[1,64,1152]{2,1,0:T(8,128)(2,1)S(1)} %get-tuple-element.55), channel_id=1, source_target_pairs={{0,1},{1,0},{2,3},{3,2},{4,5},{5,4},{6,7},{7,6},{8,9},{9,8},{10,11... | collective-permute-start | bytes 442376 | tf_op jit(solution)/shard_map/ppermute | solution.py:573
  66.9 6.7 %collective-permute-start.22 = (bf16[1,64,1152]{2,1,0:T(8,128)(2,1)S(1)}, bf16[1,64,1152]{2,1,0:T(8,128)(2,1)S(1)}, u32[]{:S(2)}, u32[]{:S(2)}) collective-permute-start(bf16[1,64,1152]{2,1,0:T(8,128)(2,1)S(1)} %get-tuple-element.56), channel_id=1, source_target_pairs={{1,2},{2,1},{5,6},{6,5},{9,10},{10,9},{13,14},{14,13},{17,18},{18,... | collective-permute-start | bytes 442376 | tf_op jit(solution)/shard_map/ppermute | solution.py:576

commit v16 on v15

--- a/solution.py
+++ b/solution.py
@@ -466,13 +466,23 @@
     even = lax.rem(lax.axis_index("space"), 2) == 0
     mask = diagonal_mask()
     square = jnp.zeros((count, LANES), jnp.float32)
-    for group in range(depth // LANES):
-        lanes = slice(group * LANES, (group + 1) * LANES)
-        spread = jnp.concatenate([state_ref[group]] * (LANES // HEAD_DIM), axis=0)
-        spread = jnp.where(mask, spread, 0.0).astype(jnp.bfloat16)
-        read = jnp.dot(queries_ref[:, lanes], spread, preferred_element_type=jnp.float32)
+    empty = jnp.zeros((LANES, LANES), jnp.bfloat16)
+
+    def spread(group):
+        tall = jnp.concatenate([state_ref[group]] * (LANES // HEAD_DIM), axis=0)
+        return jnp.where(mask, tall, 0.0).astype(jnp.bfloat16)
+
+    for at in range(0, depth, WIDE):
+        lanes = slice(at, min(at + WIDE, depth))
+        block = spread(at // LANES)
+        if at + WIDE <= depth:
+            right = jnp.concatenate([empty, spread(at // LANES + 1)], axis=0)
+            block = jnp.concatenate([jnp.concatenate([block, empty], axis=0), right], axis=1)
+        read = jnp.dot(queries_ref[:, lanes], block, preferred_element_type=jnp.float32)
         read_ref[:, lanes] = read
-        square = square + read * read
+        for k in range(read.shape[1] // LANES):
+            part = read[:, k * LANES : (k + 1) * LANES]
+            square = square + part * part
     scale = lax.rsqrt(jnp.sum(square, axis=1, keepdims=True) / depth + 1e-06)
     for at in range(0, depth, LANES):
         lanes = slice(at, at + LANES)

time: 77.4 us -> 77.4 us (level)
  no operation moved by 1% of the time
where the time goes in v16:
time: 77.4 us; the launch traced here: 76 us
  waiting for transfers between devices  41 us (53%)
  starting transfers between devices  23.7 us (31%)
  Pallas kernels  10.4 us (13%)
    ppermute x6, waiting for transfers between devices, shifted(): lax.ppermute(value, 'space', [(i, (i + step) % count) for i in range(coun...  22.3 us
    ppermute x10, waiting for transfers between devices, flipped(): lax.ppermute(value, 'tm', [(t, t ^ bit_on_core[t % 2]) for t in range(8)])  11.5 us
    pallas_call x7, Pallas kernels, kernel_call(): pl.pallas_call(body, out_shape=outputs, in_specs=in_specs, out_specs=jax....  10.4 us
    ppermute x6, starting transfers between devices, shifted(): lax.ppermute(value, 'space', [(i, (i + step) % count) for i in range(coun...  9.05 us
    ppermute x10, starting transfers between devices, flipped(): lax.ppermute(value, 'tm', [(t, t ^ bit_on_core[t % 2]) for t in range(8)])  7.06 us
    ppermute x3, starting transfers between devices, plane_form(): upto = upto + lax.ppermute(total, 'tm', pairs).astype(jnp.float32)  6.48 us
    ppermute x1, waiting for transfers between devices, plane_form(): lax.ppermute(share, 'space', [(i, count - 1 - i) for i in range(count)])  5.94 us
  transfers between devices with their start and end apart: 23, of which 14 were waited for; matrix products, arithmetic and copies ran while one was open for 1% of the time, Pallas kernels for 8%

profile of v16, /device:TPU:0, one launch (start us, length us, event | category | flops | bytes accessed | tf_op | source)
XLA Modules:
  0.0 76.0 jit_solution(15584630555525588901)
XLA Ops:
  0.0 1.9 %shard_map.55 = (bf16[80,1152]{1,0:T(8,128)(2,1)}, bf16[2,64,1152]{2,1,0:T(8,128)(2,1)}) custom-call(bf16[288,3456]{1,0:T(8,128)(2,1)} %refs_1_.1, bf16[288,1152]{1,0:T(8,128)(2,1)} %refs_2_.3), custom_call_target="tpu_custom_call" | custom-call | bytes 958464 | tf_op jit(solution)/shard_map/pallas_call | solution.py:165
  2.0 3.1 %collective-permute-start = (bf16[1,80,1152]{2,1,0:T(8,128)(2,1)}, bf16[1,80,1152]{2,1,0:T(8,128)(2,1)S(1)}, u32[]{:S(2)}, u32[]{:S(2)}) collective-permute-start(bf16[1,80,1152]{2,1,0:T(8,128)(2,1)} %bitcast.8), channel_id=1, source_target_pairs={{0,1},{1,2},{2,3},{3,0},{4,5},{5,6},{6,7},{7,4},{8,9},{9,10},{10,1... | collective-permute-start | bytes 552968 | tf_op jit(solution)/shard_map/ppermute | solution.py:105
  5.0 2.1 %collective-permute-start.1 = (bf16[1,80,1152]{2,1,0:T(8,128)(2,1)}, bf16[1,80,1152]{2,1,0:T(8,128)(2,1)S(1)}, u32[]{:S(2)}, u32[]{:S(2)}) collective-permute-start(bf16[1,80,1152]{2,1,0:T(8,128)(2,1)} %bitcast.9), channel_id=1, source_target_pairs={{0,3},{1,0},{2,1},{3,2},{4,7},{5,4},{6,5},{7,6},{8,11},{9,8},{10,9... | collective-permute-start | bytes 552968 | tf_op jit(solution)/shard_map/ppermute | solution.py:105
  7.1 0.0 copy-done.3
  7.1 1.2 %shard_map.56.refs_0_ = bf16[256,1152]{1,0:T(8,128)(2,1)S(1)} custom-call(bf16[256,1152]{1,0:T(8,128)(2,1)S(1)} %bitcast.7), custom_call_target="tpu_custom_call" | custom-call | flops 679477248 | bytes 589824 | tf_op jit(solution)/shard_map/pallas_call | solution.py:165
  8.3 0.0 copy-start
  8.3 0.1 collective-permute-start.10
  8.4 4.4 %collective-permute-done = bf16[1,80,1152]{2,1,0:T(8,128)(2,1)S(1)} collective-permute-done((bf16[1,80,1152]{2,1,0:T(8,128)(2,1)}, bf16[1,80,1152]{2,1,0:T(8,128)(2,1)S(1)}, u32[]{:S(2)}, u32[]{:S(2)}) %collective-permute-start) | collective-permute-done | bytes 184352 | tf_op jit(solution)/shard_map/ppermute | solution.py:105
  12.8 2.5 %collective-permute-done.1 = bf16[1,80,1152]{2,1,0:T(8,128)(2,1)S(1)} collective-permute-done((bf16[1,80,1152]{2,1,0:T(8,128)(2,1)}, bf16[1,80,1152]{2,1,0:T(8,128)(2,1)S(1)}, u32[]{:S(2)}, u32[]{:S(2)}) %collective-permute-start.1) | collective-permute-done | bytes 184352 | tf_op jit(solution)/shard_map/ppermute | solution.py:105
  15.3 1.6 %collective-permute-start.11 = (bf16[2,80,1152]{2,1,0:T(8,128)(2,1)S(1)}, bf16[2,80,1152]{2,1,0:T(8,128)(2,1)S(1)}, u32[]{:S(2)}, u32[]{:S(2)}) collective-permute-start(bf16[2,80,1152]{2,1,0:T(8,128)(2,1)S(1)} %constant_dynamic-update-slice_fusion.5), channel_id=1, source_target_pairs={{0,8},{4,20},{8,0},{12,28},{16,24},{20,4},{24,16},{28,12},{1,9},{5... | collective-permute-start | bytes 1105928 | tf_op jit(solution)/shard_map/ppermute | solution.py:109
  16.9 1.1 %collective-permute-start.3 = (bf16[1,80,1152]{2,1,0:T(8,128)(2,1)S(1)}, bf16[1,80,1152]{2,1,0:T(8,128)(2,1)S(1)}, u32[]{:S(2)}, u32[]{:S(2)}) collective-permute-start(bf16[1,80,1152]{2,1,0:T(8,128)(2,1)S(1)} %collective-permute-done), channel_id=1, source_target_pairs={{0,1},{1,2},{2,3},{3,0},{4,5},{5,6},{6,7},{7,4},{8,9},{9,10},{10,1... | collective-permute-start | bytes 552968 | tf_op jit(solution)/shard_map/ppermute | solution.py:105
  18.0 0.0 copy-done.5
  18.0 0.7 collective-permute-start.2
  18.8 7.5 %collective-permute-done.3 = bf16[1,80,1152]{2,1,0:T(8,128)(2,1)S(1)} collective-permute-done((bf16[1,80,1152]{2,1,0:T(8,128)(2,1)S(1)}, bf16[1,80,1152]{2,1,0:T(8,128)(2,1)S(1)}, u32[]{:S(2)}, u32[]{:S(2)}) %collective-permute-start.3) | collective-permute-done | bytes 184352 | tf_op jit(solution)/shard_map/ppermute | solution.py:105
  26.3 0.4 collective-permute-start.4
  26.7 0.0 collective-permute-done.11
  26.7 0.0 collective-permute-done.10.refs_1_
  26.8 1.7 %collective-permute-start.12 = (bf16[4,80,1152]{2,1,0:T(8,128)(2,1)S(1)}, bf16[4,80,1152]{2,1,0:T(8,128)(2,1)S(1)}, u32[]{:S(2)}, u32[]{:S(2)}) collective-permute-start(bf16[4,80,1152]{2,1,0:T(8,128)(2,1)S(1)} %constant_dynamic-update-slice_fusion.7.refs_3_), channel_id=1, source_target_pairs={{0,16},{4,12},{8,24},{12,4},{16,0},{20,28},{24,8},{28,20},{1,17},{... | collective-permute-start | bytes 2211848 | tf_op jit(solution)/shard_map/ppermute | solution.py:109
  28.5 5.3 %collective-permute-done.4 = bf16[1,80,1152]{2,1,0:T(8,128)(2,1)S(1)} collective-permute-done((bf16[1,80,1152]{2,1,0:T(8,128)(2,1)S(1)}, bf16[1,80,1152]{2,1,0:T(8,128)(2,1)S(1)}, u32[]{:S(2)}, u32[]{:S(2)}) %collective-permute-start.4) | collective-permute-done | bytes 184352 | tf_op jit(solution)/shard_map/ppermute | solution.py:109
  33.9 1.6 %collective-permute-start.13 = (bf16[2,80,1152]{2,1,0:T(8,128)(2,1)S(1)}, bf16[2,80,1152]{2,1,0:T(8,128)(2,1)S(1)}, u32[]{:S(2)}, u32[]{:S(2)}) collective-permute-start(bf16[2,80,1152]{2,1,0:T(8,128)(2,1)S(1)} %constant_dynamic-update-slice_fusion.refs_5_), channel_id=1, source_target_pairs={{0,16},{4,12},{8,24},{12,4},{16,0},{20,28},{24,8},{28,20},{1,17},{... | collective-permute-start | bytes 1105928 | tf_op jit(solution)/shard_map/ppermute | solution.py:109
  35.4 0.1 collective-permute-start.6
  35.6 0.0 collective-permute-done.2
  35.6 1.9 %collective-permute-start.5 = (bf16[2,64,1152]{2,1,0:T(8,128)(2,1)S(1)}, bf16[2,64,1152]{2,1,0:T(8,128)(2,1)S(1)}, u32[]{:S(2)}, u32[]{:S(2)}) collective-permute-start(bf16[2,64,1152]{2,1,0:T(8,128)(2,1)S(1)} %collective-permute-done.2), channel_id=1, source_target_pairs={{0,1},{1,2},{2,3},{3,0},{4,5},{5,6},{6,7},{7,4},{8,9},{9,10},{10,1... | collective-permute-start | bytes 884744 | tf_op jit(solution)/shard_map/ppermute | solution.py:105
  37.5 7.9 %collective-permute-done.6 = bf16[2,64,1152]{2,1,0:T(8,128)(2,1)S(1)} collective-permute-done((bf16[2,64,1152]{2,1,0:T(8,128)(2,1)S(1)}, bf16[2,64,1152]{2,1,0:T(8,128)(2,1)S(1)}, u32[]{:S(2)}, u32[]{:S(2)}) %collective-permute-start.6) | collective-permute-done | bytes 294944 | tf_op jit(solution)/shard_map/ppermute | solution.py:105
  45.3 0.0 collective-permute-done.13.refs_6_
  45.3 0.0 collective-permute-done.12.refs_4_
  45.3 0.0 copy-done
  45.3 1.9 %shard_map.57.mine_ref.refs_7_ = bf16[608,1152]{1,0:T(8,128)(2,1)S(1)} custom-call(bf16[256,1152]{1,0:T(8,128)(2,1)S(1)} %shard_map.56.refs_0_, bf16[256,1152]{1,0:T(8,128)(2,1)S(1)} %collective-permute-done.10.refs_1_, bf16[288,3456]{1,0:T(8,128)(2,1)S(1)} %copy-done, bf16[4,80,1152]{2,1,0:T(8,128)(2,1)S(1)} %constant_dynamic-update-slice_fusion.7.refs_3_, ...), custom_call_target="tpu_custom_call" | custom-call | flops 1358954496 | bytes 2654208 | tf_op jit(solution)/shard_map/pallas_call | solution.py:165
  47.2 0.0 collective-permute-done.5
  47.2 0.1 collective-permute-start.14
  47.4 0.6 collective-permute-start.7
  48.0 0.1 pad_maximum_fusion
  48.1 0.6 collective-permute-start.8
  48.7 0.4 collective-permute-start.9
  49.1 1.3 %collective-permute-done.14.other_ref.refs_8_ = bf16[608,1152]{1,0:T(8,128)(2,1)S(1)} collective-permute-done((bf16[608,1152]{1,0:T(8,128)(2,1)S(1)}, bf16[608,1152]{1,0:T(8,128)(2,1)S(1)}, u32[]{:S(2)}, u32[]{:S(2)}) %collective-permute-start.14) | collective-permute-done | bytes 1400864 | tf_op jit(solution)/shard_map/ppermute | solution.py:109
  50.4 0.8 %shard_map.58 = (bf16[256,1152]{1,0:T(8,128)(2,1)S(1)}, bf16[1,64,1152]{2,1,0:T(8,128)(2,1)S(1)}, bf16[1,64,1152]{2,1,0:T(8,128)(2,1)S(1)}, f32[9,32,128]{2,1,0:T(8,128)S(1)}, bf16[9,32,128]{2,1,0:T(8,128)(2,1)S(1)}) custom-call(bf16[608,1152]{1,0:T(8,128)(2,1)S(1)} %shard_map.57.mine_ref.refs_7_, bf16[608,1152]{1,0:T(8,128)(2,1)S(1)} %collective-permute-done.14.other_ref.refs_8_), custom_call_target="tpu_custom_call" | custom-call | flops 150994944 | bytes 2359296 | tf_op jit(solution)/shard_map/pallas_call | solution.py:165
  51.3 0.0 copy-start.2
  51.3 0.4 collective-permute-done.7.refs_4_
  51.7 2.4 %collective-permute-start.15 = (bf16[9,32,128]{2,1,0:T(8,128)(2,1)S(1)}, bf16[9,32,128]{2,1,0:T(8,128)(2,1)S(1)}, u32[]{:S(2)}, u32[]{:S(2)}) collective-permute-start(bf16[9,32,128]{2,1,0:T(8,128)(2,1)S(1)} %get-tuple-element.43), channel_id=1, source_target_pairs={{0,8},{4,12},{16,24},{20,28},{1,9},{5,13},{17,25},{21,29},{2,10},{... | collective-permute-start | bytes 221192 | tf_op jit(solution)/shard_map/ppermute | solution.py:559
  54.2 2.8 %collective-permute-start.16 = (bf16[9,32,128]{2,1,0:T(8,128)(2,1)S(1)}, bf16[9,32,128]{2,1,0:T(8,128)(2,1)S(1)}, u32[]{:S(2)}, u32[]{:S(2)}) collective-permute-start(bf16[9,32,128]{2,1,0:T(8,128)(2,1)S(1)} %get-tuple-element.43), channel_id=1, source_target_pairs={{0,16},{4,20},{8,24},{12,28},{1,17},{5,21},{9,25},{13,29},{2,18},{... | collective-permute-start | bytes 221192 | tf_op jit(solution)/shard_map/ppermute | solution.py:559
  56.9 1.3 %collective-permute-start.17 = (bf16[9,32,128]{2,1,0:T(8,128)(2,1)S(1)}, bf16[9,32,128]{2,1,0:T(8,128)(2,1)S(1)}, u32[]{:S(2)}, u32[]{:S(2)}) collective-permute-start(bf16[9,32,128]{2,1,0:T(8,128)(2,1)S(1)} %get-tuple-element.43), channel_id=1, source_target_pairs={{0,24},{4,28},{8,16},{12,20},{1,25},{5,29},{9,17},{13,21},{2,26},{... | collective-permute-start | bytes 221192 | tf_op jit(solution)/shard_map/ppermute | solution.py:559
  58.2 2.9 %collective-permute-done.8 = bf16[3,64,1152]{2,1,0:T(8,128)(2,1)S(1)} collective-permute-done((bf16[3,64,1152]{2,1,0:T(8,128)(2,1)S(1)}, bf16[3,64,1152]{2,1,0:T(8,128)(2,1)S(1)}, u32[]{:S(2)}, u32[]{:S(2)}) %collective-permute-start.8) | collective-permute-done | bytes 442400 | tf_op jit(solution)/shard_map/ppermute | solution.py:109
  61.2 0.0 collective-permute-done.9
  61.2 0.0 copy-start.1
  61.3 0.0 collective-permute-done.15
  61.3 0.2 collective-permute-done.16
  61.5 0.1 collective-permute-done.17
  61.6 0.1 collective-permute-start.18
  61.7 0.1 collective-permute-start.19
  61.8 0.0 copy-done.2
  61.8 0.9 %shard_map.60 = f32[4,64,1152]{2,1,0:T(8,128)S(1)} custom-call(bf16[4,64,1152]{2,1,0:T(8,128)(2,1)S(1)} %bitcast.6, f32[3,3,1152]{2,1,0:T(4,128)S(1)} %copy-done.2), custom_call_target="tpu_custom_call" | custom-call | flops 5308416 | bytes 1769472 | tf_op jit(solution)/shard_map/pallas_call | solution.py:165
  62.7 0.0 copy-start.4
  62.7 1.4 %collective-permute-done.18.refs_6_ = bf16[6,64,1152]{2,1,0:T(8,128)(2,1)S(1)} collective-permute-done((bf16[6,64,1152]{2,1,0:T(8,128)(2,1)S(1)}, bf16[6,64,1152]{2,1,0:T(8,128)(2,1)S(1)}, u32[]{:S(2)}, u32[]{:S(2)}) %collective-permute-start.18) | collective-permute-done | bytes 884768 | tf_op jit(solution)/shard_map/ppermute | solution.py:109
  64.1 0.0 copy-done.1
  64.1 1.4 %shard_map.59 = (bf16[256,1152]{1,0:T(8,128)(2,1)S(1)}, bf16[1152,1152]{1,0:T(8,128)(2,1)S(1)}) custom-call(bf16[256,1152]{1,0:T(8,128)(2,1)S(1)} %shard_map.56.refs_0_, bf16[288,3456]{1,0:T(8,128)(2,1)S(1)} %copy-done, bf16[288,1152]{1,0:T(8,128)(2,1)S(1)} %copy-done.1, bf16[6,64,1152]{2,1,0:T(8,128)(2,1)S(1)} %constant_dynamic-update-slice_fusion.2.refs_3_, ...), custom_call_target="tpu_custom_call" | custom-call | flops 679477248 | bytes 5308416 | tf_op jit(solution)/shard_map/pallas_call | solution.py:165
  65.5 0.9 %collective-permute-done.19 = bf16[9,32,128]{2,1,0:T(8,128)(2,1)S(1)} collective-permute-done((bf16[9,32,128]{2,1,0:T(8,128)(2,1)S(1)}, bf16[9,32,128]{2,1,0:T(8,128)(2,1)S(1)}, u32[]{:S(2)}, u32[]{:S(2)}) %collective-permute-start.19) | collective-permute-done | bytes 73760 | tf_op jit(solution)/shard_map/ppermute | solution.py:578
  66.4 0.1 collective-permute-start.20
  66.5 0.0 copy-done.4
  66.5 0.3 collective-permute-start.21
  66.9 0.7 collective-permute-start.22
  67.5 5.9 %collective-permute-done.20 = bf16[9,32,128]{2,1,0:T(8,128)(2,1)S(1)} collective-permute-done((bf16[9,32,128]{2,1,0:T(8,128)(2,1)S(1)}, bf16[9,32,128]{2,1,0:T(8,128)(2,1)S(1)}, u32[]{:S(2)}, u32[]{:S(2)}) %collective-permute-start.20) | collective-permute-done | bytes 73760 | tf_op jit(solution)/shard_map/ppermute | solution.py:581
  73.5 0.1 collective-permute-done.21.refs_4_
  73.6 0.0 collective-permute-done.22.refs_5_
  73.6 2.4 %shard_map.61 = bf16[256,1152]{1,0:T(8,128)(2,1)} custom-call(bf16[256,1152]{1,0:T(8,128)(2,1)S(1)} %get-tuple-element.48.refs_0_, bf16[1152,1152]{1,0:T(8,128)(2,1)S(1)} %get-tuple-element.49.refs_1_, f32[9,32,128]{2,1,0:T(8,128)S(1)} %convert_add_fusion.refs_2_, f32[256,1152]{1,0:T(8,128)S(1)} %bitcast.5, ...), custom_call_target="tpu_custom_call" | custom-call | flops 679477248 | bytes 2654208 | tf_op jit(solution)/shard_map/pallas_call | solution.py:165
  (20 shorter events, 0.4 us)
Async XLA Ops:
  0.0 7.1 %copy-start.3 = (bf16[1,4,64,1152]{3,2,1,0:T(8,128)(2,1)S(1)}, bf16[1,4,64,1152]{3,2,1,0:T(8,128)(2,1)}, u32[]{:S(2)}) copy-start(bf16[1,4,64,1152]{3,2,1,0:T(8,128)(2,1)} %param.5) | copy-start | bytes 1769476
  2.0 10.8 %collective-permute-start = (bf16[1,80,1152]{2,1,0:T(8,128)(2,1)}, bf16[1,80,1152]{2,1,0:T(8,128)(2,1)S(1)}, u32[]{:S(2)}, u32[]{:S(2)}) collective-permute-start(bf16[1,80,1152]{2,1,0:T(8,128)(2,1)} %bitcast.8), channel_id=1, source_target_pairs={{0,1},{1,2},{2,3},{3,0},{4,5},{5,6},{6,7},{7,4},{8,9},{9,10},{10,1... | collective-permute-start | bytes 552968 | tf_op jit(solution)/shard_map/ppermute | solution.py:105
  5.0 10.3 %collective-permute-start.1 = (bf16[1,80,1152]{2,1,0:T(8,128)(2,1)}, bf16[1,80,1152]{2,1,0:T(8,128)(2,1)S(1)}, u32[]{:S(2)}, u32[]{:S(2)}) collective-permute-start(bf16[1,80,1152]{2,1,0:T(8,128)(2,1)} %bitcast.9), channel_id=1, source_target_pairs={{0,3},{1,0},{2,1},{3,2},{4,7},{5,4},{6,5},{7,6},{8,11},{9,8},{10,9... | collective-permute-start | bytes 552968 | tf_op jit(solution)/shard_map/ppermute | solution.py:105
  7.1 10.9 %copy-start.5 = (bf16[2,64,1152]{2,1,0:T(8,128)(2,1)S(1)}, bf16[2,64,1152]{2,1,0:T(8,128)(2,1)}, u32[]{:S(2)}) copy-start(bf16[2,64,1152]{2,1,0:T(8,128)(2,1)} %get-tuple-element.36) | copy-start | bytes 884740
  8.3 37.0 %copy-start = (bf16[288,3456]{1,0:T(8,128)(2,1)S(1)}, bf16[288,3456]{1,0:T(8,128)(2,1)}, u32[]{:S(2)}) copy-start(bf16[288,3456]{1,0:T(8,128)(2,1)} %refs_1_.1) | copy-start | bytes 5971972
  8.3 18.4 %collective-permute-start.10 = (bf16[256,1152]{1,0:T(8,128)(2,1)S(1)}, bf16[256,1152]{1,0:T(8,128)(2,1)S(1)}, u32[]{:S(2)}, u32[]{:S(2)}) collective-permute-start(bf16[256,1152]{1,0:T(8,128)(2,1)S(1)} %shard_map.56.refs_0_), channel_id=1, source_target_pairs={{0,4},{4,0},{8,12},{12,8},{16,20},{20,16},{24,28},{28,24},{1,5},{5... | collective-permute-start | bytes 1769480 | tf_op jit(solution)/shard_map/ppermute | solution.py:109
  15.3 11.4 %collective-permute-start.11 = (bf16[2,80,1152]{2,1,0:T(8,128)(2,1)S(1)}, bf16[2,80,1152]{2,1,0:T(8,128)(2,1)S(1)}, u32[]{:S(2)}, u32[]{:S(2)}) collective-permute-start(bf16[2,80,1152]{2,1,0:T(8,128)(2,1)S(1)} %constant_dynamic-update-slice_fusion.5), channel_id=1, source_target_pairs={{0,8},{4,20},{8,0},{12,28},{16,24},{20,4},{24,16},{28,12},{1,9},{5... | collective-permute-start | bytes 1105928 | tf_op jit(solution)/shard_map/ppermute | solution.py:109
  16.9 9.4 %collective-permute-start.3 = (bf16[1,80,1152]{2,1,0:T(8,128)(2,1)S(1)}, bf16[1,80,1152]{2,1,0:T(8,128)(2,1)S(1)}, u32[]{:S(2)}, u32[]{:S(2)}) collective-permute-start(bf16[1,80,1152]{2,1,0:T(8,128)(2,1)S(1)} %collective-permute-done), channel_id=1, source_target_pairs={{0,1},{1,2},{2,3},{3,0},{4,5},{5,6},{6,7},{7,4},{8,9},{9,10},{10,1... | collective-permute-start | bytes 552968 | tf_op jit(solution)/shard_map/ppermute | solution.py:105
  18.0 17.6 %collective-permute-start.2 = (bf16[2,64,1152]{2,1,0:T(8,128)(2,1)S(1)}, bf16[2,64,1152]{2,1,0:T(8,128)(2,1)S(1)}, u32[]{:S(2)}, u32[]{:S(2)}) collective-permute-start(bf16[2,64,1152]{2,1,0:T(8,128)(2,1)S(1)} %copy-done.5), channel_id=1, source_target_pairs={{0,1},{1,2},{2,3},{3,0},{4,5},{5,6},{6,7},{7,4},{8,9},{9,10},{10,1... | collective-permute-start | bytes 884744 | tf_op jit(solution)/shard_map/ppermute | solution.py:105
  26.3 7.6 %collective-permute-start.4 = (bf16[1,80,1152]{2,1,0:T(8,128)(2,1)S(1)}, bf16[1,80,1152]{2,1,0:T(8,128)(2,1)S(1)}, u32[]{:S(2)}, u32[]{:S(2)}) collective-permute-start(bf16[1,80,1152]{2,1,0:T(8,128)(2,1)S(1)} %collective-permute-done.3), channel_id=1, source_target_pairs={{0,8},{4,20},{8,0},{12,28},{16,24},{20,4},{24,16},{28,12},{1,9},{5... | collective-permute-start | bytes 552968 | tf_op jit(solution)/shard_map/ppermute | solution.py:109
  26.8 18.5 %collective-permute-start.12 = (bf16[4,80,1152]{2,1,0:T(8,128)(2,1)S(1)}, bf16[4,80,1152]{2,1,0:T(8,128)(2,1)S(1)}, u32[]{:S(2)}, u32[]{:S(2)}) collective-permute-start(bf16[4,80,1152]{2,1,0:T(8,128)(2,1)S(1)} %constant_dynamic-update-slice_fusion.7.refs_3_), channel_id=1, source_target_pairs={{0,16},{4,12},{8,24},{12,4},{16,0},{20,28},{24,8},{28,20},{1,17},{... | collective-permute-start | bytes 2211848 | tf_op jit(solution)/shard_map/ppermute | solution.py:109
  33.9 11.5 %collective-permute-start.13 = (bf16[2,80,1152]{2,1,0:T(8,128)(2,1)S(1)}, bf16[2,80,1152]{2,1,0:T(8,128)(2,1)S(1)}, u32[]{:S(2)}, u32[]{:S(2)}) collective-permute-start(bf16[2,80,1152]{2,1,0:T(8,128)(2,1)S(1)} %constant_dynamic-update-slice_fusion.refs_5_), channel_id=1, source_target_pairs={{0,16},{4,12},{8,24},{12,4},{16,0},{20,28},{24,8},{28,20},{1,17},{... | collective-permute-start | bytes 1105928 | tf_op jit(solution)/shard_map/ppermute | solution.py:109
  35.4 9.9 %collective-permute-start.6 = (bf16[2,64,1152]{2,1,0:T(8,128)(2,1)S(1)}, bf16[2,64,1152]{2,1,0:T(8,128)(2,1)S(1)}, u32[]{:S(2)}, u32[]{:S(2)}) collective-permute-start(bf16[2,64,1152]{2,1,0:T(8,128)(2,1)S(1)} %copy-done.5), channel_id=1, source_target_pairs={{0,3},{1,0},{2,1},{3,2},{4,7},{5,4},{6,5},{7,6},{8,11},{9,8},{10,9... | collective-permute-start | bytes 884744 | tf_op jit(solution)/shard_map/ppermute | solution.py:105
  35.6 11.6 %collective-permute-start.5 = (bf16[2,64,1152]{2,1,0:T(8,128)(2,1)S(1)}, bf16[2,64,1152]{2,1,0:T(8,128)(2,1)S(1)}, u32[]{:S(2)}, u32[]{:S(2)}) collective-permute-start(bf16[2,64,1152]{2,1,0:T(8,128)(2,1)S(1)} %collective-permute-done.2), channel_id=1, source_target_pairs={{0,1},{1,2},{2,3},{3,0},{4,5},{5,6},{6,7},{7,4},{8,9},{9,10},{10,1... | collective-permute-start | bytes 884744 | tf_op jit(solution)/shard_map/ppermute | solution.py:105
  47.2 3.2 %collective-permute-start.14 = (bf16[608,1152]{1,0:T(8,128)(2,1)S(1)}, bf16[608,1152]{1,0:T(8,128)(2,1)S(1)}, u32[]{:S(2)}, u32[]{:S(2)}) collective-permute-start(bf16[608,1152]{1,0:T(8,128)(2,1)S(1)} %shard_map.57.mine_ref.refs_7_), channel_id=1, source_target_pairs={{0,4},{4,0},{8,12},{12,8},{16,20},{20,16},{24,28},{28,24},{1,5},{5... | collective-permute-start | bytes 4202504 | tf_op jit(solution)/shard_map/ppermute | solution.py:109
  47.4 4.3 %collective-permute-start.7 = (bf16[6,64,1152]{2,1,0:T(8,128)(2,1)S(1)}, bf16[6,64,1152]{2,1,0:T(8,128)(2,1)S(1)}, u32[]{:S(2)}, u32[]{:S(2)}) collective-permute-start(bf16[6,64,1152]{2,1,0:T(8,128)(2,1)S(1)} %constant_dynamic-update-slice_fusion.2.refs_3_), channel_id=1, source_target_pairs={{0,4},{4,0},{8,12},{12,8},{16,20},{20,16},{24,28},{28,24},{1,5},{5... | collective-permute-start | bytes 2654216 | tf_op jit(solution)/shard_map/ppermute | solution.py:109
  48.1 13.1 %collective-permute-start.8 = (bf16[3,64,1152]{2,1,0:T(8,128)(2,1)S(1)}, bf16[3,64,1152]{2,1,0:T(8,128)(2,1)S(1)}, u32[]{:S(2)}, u32[]{:S(2)}) collective-permute-start(bf16[3,64,1152]{2,1,0:T(8,128)(2,1)S(1)} %pad_maximum_fusion), channel_id=1, source_target_pairs={{0,8},{4,20},{8,0},{12,28},{16,24},{20,4},{24,16},{28,12},{1,9},{5... | collective-permute-start | bytes 1327112 | tf_op jit(solution)/shard_map/ppermute | solution.py:109
  48.7 12.5 %collective-permute-start.9 = (bf16[3,64,1152]{2,1,0:T(8,128)(2,1)S(1)}, bf16[3,64,1152]{2,1,0:T(8,128)(2,1)S(1)}, u32[]{:S(2)}, u32[]{:S(2)}) collective-permute-start(bf16[3,64,1152]{2,1,0:T(8,128)(2,1)S(1)} %pad_maximum_fusion), channel_id=1, source_target_pairs={{0,16},{4,12},{8,24},{12,4},{16,0},{20,28},{24,8},{28,20},{1,17},{... | collective-permute-start | bytes 1327112 | tf_op jit(solution)/shard_map/ppermute | solution.py:109
  51.3 10.5 %copy-start.2 = (f32[3,3,1152]{2,1,0:T(4,128)S(1)}, f32[3,3,1152]{2,1,0:T(4,128)}, u32[]{:S(2)}) copy-start(f32[3,3,1152]{2,1,0:T(4,128)} %refs_6_.1) | copy-start | bytes 124420
  51.7 9.6 %collective-permute-start.15 = (bf16[9,32,128]{2,1,0:T(8,128)(2,1)S(1)}, bf16[9,32,128]{2,1,0:T(8,128)(2,1)S(1)}, u32[]{:S(2)}, u32[]{:S(2)}) collective-permute-start(bf16[9,32,128]{2,1,0:T(8,128)(2,1)S(1)} %get-tuple-element.43), channel_id=1, source_target_pairs={{0,8},{4,12},{16,24},{20,28},{1,9},{5,13},{17,25},{21,29},{2,10},{... | collective-permute-start | bytes 221192 | tf_op jit(solution)/shard_map/ppermute | solution.py:559
  54.2 7.3 %collective-permute-start.16 = (bf16[9,32,128]{2,1,0:T(8,128)(2,1)S(1)}, bf16[9,32,128]{2,1,0:T(8,128)(2,1)S(1)}, u32[]{:S(2)}, u32[]{:S(2)}) collective-permute-start(bf16[9,32,128]{2,1,0:T(8,128)(2,1)S(1)} %get-tuple-element.43), channel_id=1, source_target_pairs={{0,16},{4,20},{8,24},{12,28},{1,17},{5,21},{9,25},{13,29},{2,18},{... | collective-permute-start | bytes 221192 | tf_op jit(solution)/shard_map/ppermute | solution.py:559
  56.9 4.7 %collective-permute-start.17 = (bf16[9,32,128]{2,1,0:T(8,128)(2,1)S(1)}, bf16[9,32,128]{2,1,0:T(8,128)(2,1)S(1)}, u32[]{:S(2)}, u32[]{:S(2)}) collective-permute-start(bf16[9,32,128]{2,1,0:T(8,128)(2,1)S(1)} %get-tuple-element.43), channel_id=1, source_target_pairs={{0,24},{4,28},{8,16},{12,20},{1,25},{5,29},{9,17},{13,21},{2,26},{... | collective-permute-start | bytes 221192 | tf_op jit(solution)/shard_map/ppermute | solution.py:559
  61.2 2.9 %copy-start.1 = (bf16[288,1152]{1,0:T(8,128)(2,1)S(1)}, bf16[288,1152]{1,0:T(8,128)(2,1)}, u32[]{:S(2)}) copy-start(bf16[288,1152]{1,0:T(8,128)(2,1)} %refs_2_.3) | copy-start | bytes 1990660
  61.6 2.5 %collective-permute-start.18 = (bf16[6,64,1152]{2,1,0:T(8,128)(2,1)S(1)}, bf16[6,64,1152]{2,1,0:T(8,128)(2,1)S(1)}, u32[]{:S(2)}, u32[]{:S(2)}) collective-permute-start(bf16[6,64,1152]{2,1,0:T(8,128)(2,1)S(1)} %constant_dynamic-update-slice_fusion.9.refs_5_), channel_id=1, source_target_pairs={{0,4},{4,0},{8,12},{12,8},{16,20},{20,16},{24,28},{28,24},{1,5},{5... | collective-permute-start | bytes 2654216 | tf_op jit(solution)/shard_map/ppermute | solution.py:109
  61.7 4.7 %collective-permute-start.19 = (bf16[9,32,128]{2,1,0:T(8,128)(2,1)S(1)}, bf16[9,32,128]{2,1,0:T(8,128)(2,1)S(1)}, u32[]{:S(2)}, u32[]{:S(2)}) collective-permute-start(bf16[9,32,128]{2,1,0:T(8,128)(2,1)S(1)} %convert_add_fusion.1), channel_id=1, source_target_pairs={{0,1},{1,0},{2,3},{3,2},{4,5},{5,4},{6,7},{7,6},{8,9},{9,8},{10,11... | collective-permute-start | bytes 221192 | tf_op jit(solution)/shard_map/ppermute | solution.py:578
  62.7 3.8 %copy-start.4 = (f32[1152]{0:T(1024)S(1)}, f32[1152]{0:T(1024)}, u32[]{:S(2)}) copy-start(f32[1152]{0:T(1024)} %param.9) | copy-start | bytes 13828
  66.4 7.0 %collective-permute-start.20 = (bf16[9,32,128]{2,1,0:T(8,128)(2,1)S(1)}, bf16[9,32,128]{2,1,0:T(8,128)(2,1)S(1)}, u32[]{:S(2)}, u32[]{:S(2)}) collective-permute-start(bf16[9,32,128]{2,1,0:T(8,128)(2,1)S(1)} %add_convert_fusion), channel_id=1, source_target_pairs={{0,3},{1,2},{2,1},{3,0},{4,7},{5,6},{6,5},{7,4},{8,11},{9,10},{10,... | collective-permute-start | bytes 221192 | tf_op jit(solution)/shard_map/ppermute | solution.py:581
  66.5 7.1 %collective-permute-start.21 = (bf16[1,64,1152]{2,1,0:T(8,128)(2,1)S(1)}, bf16[1,64,1152]{2,1,0:T(8,128)(2,1)S(1)}, u32[]{:S(2)}, u32[]{:S(2)}) collective-permute-start(bf16[1,64,1152]{2,1,0:T(8,128)(2,1)S(1)} %get-tuple-element.55), channel_id=1, source_target_pairs={{0,1},{1,0},{2,3},{3,2},{4,5},{5,4},{6,7},{7,6},{8,9},{9,8},{10,11... | collective-permute-start | bytes 442376 | tf_op jit(solution)/shard_map/ppermute | solution.py:583
  66.9 6.7 %collective-permute-start.22 = (bf16[1,64,1152]{2,1,0:T(8,128)(2,1)S(1)}, bf16[1,64,1152]{2,1,0:T(8,128)(2,1)S(1)}, u32[]{:S(2)}, u32[]{:S(2)}) collective-permute-start(bf16[1,64,1152]{2,1,0:T(8,128)(2,1)S(1)} %get-tuple-element.56), channel_id=1, source_target_pairs={{1,2},{2,1},{5,6},{6,5},{9,10},{10,9},{13,14},{14,13},{17,18},{18,... | collective-permute-start | bytes 442376 | tf_op jit(solution)/shard_map/ppermute | solution.py:586
